TPU v7x, 32 devices: a whole 2x2x4 slice. The times are simulated.
32 devices in a mesh: dp: 16 (over z, y, x), tensor: 2 (over core).
Axes of the slice: x: 2, y: 2, z: 4, core: 2. Of those that a mesh axis runs over, the one named last changes fastest.
Arguments:
- tokens: bfloat16 [8192, 2048], P(('dp', 'tensor')), may hold values from -6 to 6
- lengths: int32 [16], P('dp'), may hold values from 257 to 512, as said below
- w_query: bfloat16 [2048, 2048], P('dp', 'tensor'), may hold values from -0.125 to 0.125
- w_key: bfloat16 [2048, 2048], P('dp', 'tensor'), may hold values from -0.125 to 0.125
- w_value: bfloat16 [2048, 4096], P('dp', 'tensor'), may hold values from -0.125 to 0.125
- w_gate: bfloat16 [2048, 4096], P('dp', 'tensor'), may hold values from -0.125 to 0.125
- w_out: bfloat16 [4096, 2048], P('tensor', 'dp'), may hold values from -0.125 to 0.125
- w_ffgate: bfloat16 [2048, 4096], P('dp', 'tensor'), may hold values from -0.125 to 0.125
- w_ffup: bfloat16 [2048, 4096], P('dp', 'tensor'), may hold values from -0.125 to 0.125
- w_ffdown: bfloat16 [4096, 2048], P('tensor', 'dp'), may hold values from -0.125 to 0.125
- gain_attn: bfloat16 [2048], P('dp'), may hold values from 0.099609375 to 1.8984375
- gain_mlp: bfloat16 [2048], P('dp'), may hold values from 0.099609375 to 1.8984375
- cotangent: bfloat16 [8192, 2048], P(('dp', 'tensor')), may hold values from -6 to 6
Outputs:
- output: bfloat16 [8192, 2048], P(('dp', 'tensor'))
- tokens_grad: bfloat16 [8192, 2048], P(('dp', 'tensor'))
- grad_query: float32 [2048, 2048], P('dp', 'tensor')
- grad_key: float32 [2048, 2048], P('dp', 'tensor')
- grad_value: float32 [2048, 4096], P('dp', 'tensor')
- gate_weight_gradient: float32 [2048, 4096], P('dp', 'tensor')
- grad_out: float32 [4096, 2048], P('tensor', 'dp')
- grad_ffgate: float32 [2048, 4096], P('dp', 'tensor')
- grad_ffup: float32 [2048, 4096], P('dp', 'tensor')
- grad_ffdown: float32 [4096, 2048], P('tensor', 'dp')
- grad_gain_attn: float32 [2048], P(('dp', 'tensor'))
- grad_gain_mlp: float32 [2048], P(('dp', 'tensor'))
Inputs may be any that keep to these rules, and one draw needn't show every extreme that they name: `lengths`: one slot of every draw is full; each slot is used past its middle.
All inputs are finite; a program needn't handle non-finite values.
Results may differ from a plain program's by a relative error of at most 0.015.
The roundings to bfloat16 on the way count: a program that leaves them out, or rounds other values in their place, can miss the bound.
Values may be sent and summed in bfloat16 or wider, within the bound.
No kernel may reach another device: no remote copies, remote signals or barrier semaphores. Data moves between devices by JAX's collectives and lax.ppermute only.
A program may use at most 256 MiB of HBM per device.

v0:
```python
import jax
import jax.numpy as jnp
from jax import lax
from jax.sharding import PartitionSpec as P

DK = 256
DV = 512


norm_eps = 1e-06
group_floor = 1.0


def rms_scale(rows, gain):
    factor = lax.rsqrt(jnp.mean(rows * rows, axis=-1, keepdims=True) + norm_eps)
    return rows * factor * gain


def gate_norm(gate_pre, retained):
    normed = retained * lax.rsqrt(
        jnp.mean(retained * retained, axis=-1, keepdims=True) + group_floor
    )
    return jax.nn.silu(gate_pre) * normed.reshape(gate_pre.shape)


def mlp_inner(gate_up, value_up):
    return jax.nn.gelu(gate_up, approximate=True) * value_up


def decay_table(count, heads, first_head):
    positions = jnp.arange(count, dtype=jnp.int32)
    spacing = positions[:, None] - positions[None, :]
    head_ids = (jnp.arange(heads, dtype=jnp.int32) + first_head).astype(jnp.float32)
    log_rates = jnp.log1p(-jnp.exp2(-5.0 - head_ids))
    kept_spacing = jnp.where(spacing >= 0, spacing, jnp.zeros_like(spacing)).astype(jnp.float32)
    powers = jnp.exp(kept_spacing[None] * log_rates[:, None, None])
    return jnp.where(spacing[None] >= 0, powers, jnp.zeros_like(powers))


def spread_rows(rows):
    return lax.all_gather(rows, "tensor", axis=0, tiled=True)


def fold_rows(terms):
    return lax.psum_scatter(terms, "tensor", scatter_dimension=0, tiled=True)


def spread_grads(rows):
    return lax.all_gather(rows, "tensor", axis=0, tiled=True)


def fold_grads(terms):
    return lax.psum_scatter(terms, "tensor", scatter_dimension=0, tiled=True)


def on_device(
    tokens,
    lengths,
    w_query,
    w_key,
    w_value,
    w_gate,
    w_out,
    w_ffgate,
    w_ffup,
    w_ffdown,
    gain_attn,
    gain_mlp,
    cotangent,
):
    piece_rows = tokens.shape[0]
    tensor_place = lax.axis_index("tensor")
    positions = tensor_place * piece_rows + jnp.arange(piece_rows, dtype=jnp.int32)
    valid_rows = (positions < lengths[0]).astype(jnp.float32)[:, None]
    attn_full = (
        lax.all_gather(w_query, "dp", axis=0, tiled=True),
        lax.all_gather(w_key, "dp", axis=0, tiled=True),
        lax.all_gather(w_value, "dp", axis=0, tiled=True),
        lax.all_gather(w_gate, "dp", axis=0, tiled=True),
        lax.all_gather(w_out, "dp", axis=1, tiled=True),
        lax.all_gather(gain_attn, "dp", axis=0, tiled=True),
    )
    query_full, key_full, value_full, gate_full, out_full, gain_one = attn_full
    input_rows = tokens.astype(jnp.float32)
    gain_first = gain_one.astype(jnp.float32)
    normed_attn = rms_scale(input_rows, gain_first).astype(jnp.bfloat16)
    attn_all = spread_rows(normed_attn)
    slot_len = attn_all.shape[0]
    head_keys = w_query.shape[1]
    heads_here = head_keys // DK
    query_matrix = (
        jnp.dot(attn_all, query_full, preferred_element_type=jnp.float32)
        .astype(jnp.bfloat16)
        .reshape(slot_len, heads_here, DK)
    )
    key_matrix_rows = (
        jnp.dot(attn_all, key_full, preferred_element_type=jnp.float32)
        .astype(jnp.bfloat16)
        .reshape(slot_len, heads_here, DK)
    )
    value_rows = (
        jnp.dot(attn_all, value_full, preferred_element_type=jnp.float32)
        .astype(jnp.bfloat16)
        .reshape(slot_len, heads_here, DV)
    )
    gate_pre = jnp.dot(attn_all, gate_full, preferred_element_type=jnp.float32)
    decays = decay_table(slot_len, heads_here, tensor_place * heads_here)
    unscaled_scores = jnp.einsum(
        "wjk,bjk->jwb", query_matrix, key_matrix_rows, preferred_element_type=jnp.float32
    )
    scores = (unscaled_scores * decays).astype(jnp.bfloat16)
    retained = jnp.einsum("hnm,mhe->nhe", scores, value_rows, preferred_element_type=jnp.float32)
    gated_rows = gate_norm(gate_pre, retained).astype(jnp.bfloat16)
    attn_rows = fold_rows(jnp.dot(gated_rows, out_full, preferred_element_type=jnp.float32))
    hidden = input_rows + attn_rows
    ffn_full = (
        lax.all_gather(w_ffgate, "dp", axis=0, tiled=True),
        lax.all_gather(w_ffup, "dp", axis=0, tiled=True),
        lax.all_gather(w_ffdown, "dp", axis=1, tiled=True),
        lax.all_gather(gain_mlp, "dp", axis=0, tiled=True),
    )
    ffgate_full, ffup_full, ffdown_full, gain_two = ffn_full
    gain_second = gain_two.astype(jnp.float32)
    normed_mlp = rms_scale(hidden, gain_second).astype(jnp.bfloat16)
    mlp_all = spread_rows(normed_mlp)
    gate_up = jnp.dot(mlp_all, ffgate_full, preferred_element_type=jnp.float32)
    value_up = jnp.dot(mlp_all, ffup_full, preferred_element_type=jnp.float32)
    inner_act = mlp_inner(gate_up, value_up).astype(jnp.bfloat16)
    mlp_rows = fold_rows(jnp.dot(inner_act, ffdown_full, preferred_element_type=jnp.float32))
    output = (valid_rows * (hidden + mlp_rows)).astype(jnp.bfloat16)
    back_rows = valid_rows * cotangent.astype(jnp.float32)
    ffgate_back, ffup_back, ffdown_back, unused_gain = (
        lax.all_gather(w_ffgate, "dp", axis=0, tiled=True),
        lax.all_gather(w_ffup, "dp", axis=0, tiled=True),
        lax.all_gather(w_ffdown, "dp", axis=1, tiled=True),
        lax.all_gather(gain_mlp, "dp", axis=0, tiled=True),
    )
    back_all = spread_grads(back_rows.astype(jnp.bfloat16))
    grad_down = jnp.einsum("tf,td->fd", inner_act, back_all, preferred_element_type=jnp.float32)
    grad_inner = jnp.einsum("td,fd->tf", back_all, ffdown_back, preferred_element_type=jnp.float32)
    unused_inner, inner_back = jax.vjp(mlp_inner, gate_up, value_up)
    grad_gate_up, grad_value_up = inner_back(grad_inner)
    grad_gate_up = grad_gate_up.astype(jnp.bfloat16)
    grad_value_up = grad_value_up.astype(jnp.bfloat16)
    grad_ffgate = jnp.einsum("td,tf->df", mlp_all, grad_gate_up, preferred_element_type=jnp.float32)
    grad_ffup = jnp.einsum("td,tf->df", mlp_all, grad_value_up, preferred_element_type=jnp.float32)
    mlp_terms = jnp.einsum(
        "tf,df->td", grad_gate_up, ffgate_back, preferred_element_type=jnp.float32
    )
    mlp_terms = mlp_terms + jnp.einsum(
        "tf,df->td", grad_value_up, ffup_back, preferred_element_type=jnp.float32
    )
    grad_mlp_norm = fold_grads(mlp_terms)
    unused_norm, norm_back = jax.vjp(rms_scale, hidden, gain_second)
    hidden_add, grad_gain_mlp = norm_back(grad_mlp_norm)
    grad_hidden = back_rows + hidden_add
    ffn_sums = (
        lax.psum_scatter(grad_ffgate, "dp", scatter_dimension=0, tiled=True),
        lax.psum_scatter(grad_ffup, "dp", scatter_dimension=0, tiled=True),
        lax.psum_scatter(grad_down, "dp", scatter_dimension=1, tiled=True),
    )
    query_back, key_back, value_back, gate_back, out_back, spare_gain = (
        lax.all_gather(w_query, "dp", axis=0, tiled=True),
        lax.all_gather(w_key, "dp", axis=0, tiled=True),
        lax.all_gather(w_value, "dp", axis=0, tiled=True),
        lax.all_gather(w_gate, "dp", axis=0, tiled=True),
        lax.all_gather(w_out, "dp", axis=1, tiled=True),
        lax.all_gather(gain_attn, "dp", axis=0, tiled=True),
    )
    attn_grad_all = spread_grads(grad_hidden.astype(jnp.bfloat16))
    grad_out = jnp.einsum(
        "tv,td->vd", gated_rows, attn_grad_all, preferred_element_type=jnp.float32
    )
    grad_gated = jnp.einsum(
        "td,vd->tv", attn_grad_all, out_back, preferred_element_type=jnp.float32
    )
    unused_gated, gated_back = jax.vjp(gate_norm, gate_pre, retained)
    grad_gate_pre, grad_retained = gated_back(grad_gated)
    grad_gate_pre = grad_gate_pre.astype(jnp.bfloat16)
    grad_retained = grad_retained.astype(jnp.bfloat16)
    grad_scores = jnp.einsum(
        "nhe,mhe->hnm", grad_retained, value_rows, preferred_element_type=jnp.float32
    )
    unscaled_score_gradient = (grad_scores * decays).astype(jnp.bfloat16)
    grad_queries = (
        jnp.einsum(
            "ptf,fpa->tpa",
            unscaled_score_gradient,
            key_matrix_rows,
            preferred_element_type=jnp.float32,
        )
        .astype(jnp.bfloat16)
        .reshape(slot_len, head_keys)
    )
    grad_keys = (
        jnp.einsum(
            "jfu,fji->uji",
            unscaled_score_gradient,
            query_matrix,
            preferred_element_type=jnp.float32,
        )
        .astype(jnp.bfloat16)
        .reshape(slot_len, head_keys)
    )
    grad_values = (
        jnp.einsum("hnm,nhe->mhe", scores, grad_retained, preferred_element_type=jnp.float32)
        .astype(jnp.bfloat16)
        .reshape(slot_len, w_value.shape[1])
    )
    grad_query = jnp.einsum("td,tk->dk", attn_all, grad_queries, preferred_element_type=jnp.float32)
    grad_key = jnp.einsum("td,tk->dk", attn_all, grad_keys, preferred_element_type=jnp.float32)
    grad_value = jnp.einsum("td,tv->dv", attn_all, grad_values, preferred_element_type=jnp.float32)
    gate_weight_gradient = jnp.einsum(
        "td,tv->dv", attn_all, grad_gate_pre, preferred_element_type=jnp.float32
    )
    attn_terms = jnp.einsum(
        "tk,dk->td", grad_queries, query_back, preferred_element_type=jnp.float32
    )
    attn_terms = attn_terms + jnp.einsum(
        "tk,dk->td", grad_keys, key_back, preferred_element_type=jnp.float32
    )
    attn_terms = attn_terms + jnp.einsum(
        "tv,dv->td", grad_values, value_back, preferred_element_type=jnp.float32
    )
    attn_terms = attn_terms + jnp.einsum(
        "tv,dv->td", grad_gate_pre, gate_back, preferred_element_type=jnp.float32
    )
    grad_attn_norm = fold_grads(attn_terms)
    unused_first, first_back = jax.vjp(rms_scale, input_rows, gain_first)
    input_add, grad_gain_attn = first_back(grad_attn_norm)
    tokens_grad = (grad_hidden + input_add).astype(jnp.bfloat16)
    attn_sums = (
        lax.psum_scatter(grad_query, "dp", scatter_dimension=0, tiled=True),
        lax.psum_scatter(grad_key, "dp", scatter_dimension=0, tiled=True),
        lax.psum_scatter(grad_value, "dp", scatter_dimension=0, tiled=True),
        lax.psum_scatter(gate_weight_gradient, "dp", scatter_dimension=0, tiled=True),
        lax.psum_scatter(grad_out, "dp", scatter_dimension=1, tiled=True),
    )
    weight_sums = (
        attn_sums[0],
        attn_sums[1],
        attn_sums[2],
        attn_sums[3],
        attn_sums[4],
        ffn_sums[0],
        ffn_sums[1],
        ffn_sums[2],
    )
    gain_totals_rows = (
        lax.psum_scatter(grad_gain_attn, ("dp", "tensor"), scatter_dimension=0, tiled=True),
        lax.psum_scatter(grad_gain_mlp, ("dp", "tensor"), scatter_dimension=0, tiled=True),
    )
    return (
        output,
        tokens_grad,
        weight_sums[0],
        weight_sums[1],
        weight_sums[2],
        weight_sums[3],
        weight_sums[4],
        weight_sums[5],
        weight_sums[6],
        weight_sums[7],
        gain_totals_rows[0],
        gain_totals_rows[1],
    )


def solution(mesh):
    return jax.shard_map(
        on_device,
        mesh=mesh,
        in_specs=(
            P(("dp", "tensor"), None),
            P("dp"),
            P("dp", "tensor"),
            P("dp", "tensor"),
            P("dp", "tensor"),
            P("dp", "tensor"),
            P("tensor", "dp"),
            P("dp", "tensor"),
            P("dp", "tensor"),
            P("tensor", "dp"),
            P("dp"),
            P("dp"),
            P(("dp", "tensor"), None),
        ),
        out_specs=(
            P(("dp", "tensor"), None),
            P(("dp", "tensor"), None),
            P("dp", "tensor"),
            P("dp", "tensor"),
            P("dp", "tensor"),
            P("dp", "tensor"),
            P("tensor", "dp"),
            P("dp", "tensor"),
            P("dp", "tensor"),
            P("tensor", "dp"),
            P(("dp", "tensor")),
            P(("dp", "tensor")),
        ),
        check_vma=False,
    )
```

profile of v0, /device:TPU:0, one launch (start us, length us, event | category | flops | bytes accessed | tf_op | source)
XLA Modules:
  0.0 3659.4 jit_solution(17885185547728505244)
XLA Ops:
  8.8 42.4 %all-gather = bf16[16,1,128]{2,1,0:T(2,128)(2,1)S(1)} all-gather(bf16[1,1,128]{2,1,0:T(2,128)(2,1)} %bitcast.113), channel_id=1, replica_groups=mesh['dp'=16,'tensor'=2] {'dp'}, dimensions={0}, use_global_device_ids=true | all-gather | bytes 4352 | tf_op jit(solution)/shard_map/all_gather | solution.py:81
  60.9 80.1 %all-gather.21.cloned.1.call-done = bf16[2048,1024]{1,0:T(8,128)(2,1)} async-done(((bf16[128,1024]{1,0:T(8,128)(2,1)}), bf16[2048,1024]{1,0:T(8,128)(2,1)}) %all-gather.21.cloned.1.call-update) | async-done | bytes 4194320 | tf_op jit(solution)/shard_map/all_gather | solution.py:76
  140.9 5.2 convolution_convert_fusion.5
  146.9 71.5 %all-gather.23.cloned.1.call-done = bf16[2048,1024]{1,0:T(8,128)(2,1)} async-done(((bf16[128,1024]{1,0:T(8,128)(2,1)}), bf16[2048,1024]{1,0:T(8,128)(2,1)}) %all-gather.23.cloned.1.call-update) | async-done | bytes 4194320 | tf_op jit(solution)/shard_map/all_gather | solution.py:77
  218.4 6.1 convolution_convert_fusion.4
  228.8 103.7 %all-gather.19.cloned.1.call-done = bf16[2048,2048]{1,0:T(8,128)(2,1)} async-done(((bf16[128,2048]{1,0:T(8,128)(2,1)}), bf16[2048,2048]{1,0:T(8,128)(2,1)}) %all-gather.19.cloned.1.call-update) | async-done | bytes 8388624 | tf_op jit(solution)/shard_map/all_gather | solution.py:78
  332.5 8.7 convolution_convert_fusion
  346.0 5.6 copy.46
  351.5 94.7 %all-gather.17.cloned.1.call-done = bf16[2048,2048]{1,0:T(8,128)(2,1)} async-done(((bf16[128,2048]{1,0:T(8,128)(2,1)}), bf16[2048,2048]{1,0:T(8,128)(2,1)}) %all-gather.17.cloned.1.call-update) | async-done | bytes 8388624 | tf_op jit(solution)/shard_map/all_gather | solution.py:79
  446.2 11.1 multiply_convert_fusion.3
  457.2 132.1 %all-gather.25.cloned.1.call-done = bf16[2048,2048]{1,0:T(8,128)(2,1)} async-done(((bf16[2048,128]{1,0:T(8,128)(2,1)}), bf16[2048,2048]{1,0:T(8,128)(2,1)}) %all-gather.25.cloned.1.call-update) | async-done | bytes 8388624 | tf_op jit(solution)/shard_map/all_gather | solution.py:80
  589.3 10.6 fusion.36
  600.8 37.7 %all-gather.1 = bf16[16,1,128]{2,1,0:T(2,128)(2,1)S(1)} all-gather(bf16[1,1,128]{2,1,0:T(2,128)(2,1)S(1)} %bitcast.114), channel_id=1, replica_groups=mesh['dp'=16,'tensor'=2] {'dp'}, dimensions={0}, use_global_device_ids=true | all-gather | bytes 4352 | tf_op jit(solution)/shard_map/all_gather | solution.py:120
  644.9 82.7 %all-gather.29.cloned.1.call-done = bf16[2048,2048]{1,0:T(8,128)(2,1)} async-done(((bf16[128,2048]{1,0:T(8,128)(2,1)}), bf16[2048,2048]{1,0:T(8,128)(2,1)}) %all-gather.29.cloned.1.call-update) | async-done | bytes 8388624 | tf_op jit(solution)/shard_map/all_gather | solution.py:117
  727.7 11.0 all-gather.27.cloned.1.call-done
  738.7 10.5 fusion.37
  749.2 106.5 %all-gather.31.cloned.1.call-done = bf16[2048,2048]{1,0:T(8,128)(2,1)} async-done(((bf16[128,2048]{1,0:T(8,128)(2,1)}), bf16[2048,2048]{1,0:T(8,128)(2,1)}) %all-gather.31.cloned.1.call-update) | async-done | bytes 8388624 | tf_op jit(solution)/shard_map/all_gather | solution.py:118
  855.7 10.6 fusion.38
  866.7 146.5 %all-gather.33.cloned.1.call-done = bf16[2048,2048]{1,0:T(8,128)(2,1)} async-done(((bf16[2048,128]{1,0:T(8,128)(2,1)}), bf16[2048,2048]{1,0:T(8,128)(2,1)}) %all-gather.33.cloned.1.call-update) | async-done | bytes 8388624 | tf_op jit(solution)/shard_map/all_gather | solution.py:119
  1013.2 13.4 multiply_convert_fusion.1
  1026.6 8.5 fusion.40
  1035.1 6.2 convolution_add_fusion
  1041.4 10.5 fusion.39
  1054.1 13.1 reduce-scatter.15.cloned.1.call-done
  1067.3 5.1 fusion.34
  1072.4 12.0 all-gather.37.cloned.1.call-done
  1084.4 14.6 fusion.10
  1099.0 5.7 copy.47
  1122.4 4.4 fusion.41
  1126.8 6.3 fusion.43
  1133.1 13.3 add_add_fusion.1
  1146.5 7.3 fusion.45
  1155.6 5.7 fusion.44
  1161.6 12.7 fusion.49
  1174.4 12.6 fusion.50
  1187.2 12.6 fusion.51
  1199.9 12.6 fusion.48
  1212.6 9.9 fusion.46
  1222.9 9.9 fusion.47
  1236.5 46.1 %all-reduce.2 = (f32[2048]{0:T(1024)S(1)}, f32[2048]{0:T(1024)S(1)}) all-reduce(f32[2048]{0:T(1024)S(1)} %get-tuple-element.14, f32[2048]{0:T(1024)S(1)} %get-tuple-element.12), channel_id=14, replica_groups=mesh['dp'=16,'tensor'=2] {'dp','tensor'}, use_global_device_ids=true, to_apply=%region_19.20.clone | all-reduce | flops 4096 | bytes 32768
  1287.0 56.2 %reduce-scatter.23.cloned.1.call-done = f32[128,1024]{1,0:T(8,128)} async-done(((f32[2048,1024]{1,0:T(8,128)}), f32[128,1024]{1,0:T(8,128)}) %reduce-scatter.23.cloned.1.call-update) | async-done | bytes 524304 | tf_op jit(solution)/shard_map/reduce_scatter | solution.py:234
  1343.2 183.0 %reduce-scatter.21.cloned.1.call-done = f32[128,1024]{1,0:T(8,128)} async-done(((f32[2048,1024]{1,0:T(8,128)}), f32[128,1024]{1,0:T(8,128)}) %reduce-scatter.21.cloned.1.call-update) | async-done | bytes 524304 | tf_op jit(solution)/shard_map/reduce_scatter | solution.py:233
  1526.2 351.7 %reduce-scatter.31.cloned.1.call-done = f32[128,2048]{1,0:T(8,128)} async-done(((f32[2048,2048]{1,0:T(8,128)}), f32[128,2048]{1,0:T(8,128)}) %reduce-scatter.31.cloned.1.call-update) | async-done | bytes 1048592 | tf_op jit(solution)/shard_map/reduce_scatter | solution.py:158
  1877.8 354.7 %reduce-scatter.33.cloned.1.call-done = f32[128,2048]{1,0:T(8,128)} async-done(((f32[2048,2048]{1,0:T(8,128)}), f32[128,2048]{1,0:T(8,128)}) %reduce-scatter.33.cloned.1.call-update) | async-done | bytes 1048592 | tf_op jit(solution)/shard_map/reduce_scatter | solution.py:159
  2232.6 354.9 %reduce-scatter.35.cloned.1.call-done = f32[2048,128]{1,0:T(8,128)} async-done(((f32[2048,2048]{1,0:T(8,128)}), f32[2048,128]{1,0:T(8,128)}) %reduce-scatter.35.cloned.1.call-update) | async-done | bytes 1048592 | tf_op jit(solution)/shard_map/reduce_scatter | solution.py:160
  2587.5 354.9 %reduce-scatter.29.cloned.1.call-done = f32[2048,128]{1,0:T(8,128)} async-done(((f32[2048,2048]{1,0:T(8,128)}), f32[2048,128]{1,0:T(8,128)}) %reduce-scatter.29.cloned.1.call-update) | async-done | bytes 1048592 | tf_op jit(solution)/shard_map/reduce_scatter | solution.py:237
  2942.4 354.9 %reduce-scatter.25.cloned.1.call-done = f32[128,2048]{1,0:T(8,128)} async-done(((f32[2048,2048]{1,0:T(8,128)}), f32[128,2048]{1,0:T(8,128)}) %reduce-scatter.25.cloned.1.call-update) | async-done | bytes 1048592 | tf_op jit(solution)/shard_map/reduce_scatter | solution.py:235
  3297.3 354.7 %reduce-scatter.27.cloned.1.call-done = f32[128,2048]{1,0:T(8,128)} async-done(((f32[2048,2048]{1,0:T(8,128)}), f32[128,2048]{1,0:T(8,128)}) %reduce-scatter.27.cloned.1.call-update) | async-done | bytes 1048592 | tf_op jit(solution)/shard_map/reduce_scatter | solution.py:236
  (156 shorter events, 58.5 us)
Async XLA Ops:
  7.2 53.7 %all-gather.15.cloned.1.call-start = ((), (), s32[]{:S(2)}) async-start(), calls=%async_computation.12 | async-start | bytes 3145728 | tf_op jit(solution)/shard_map/all_gather | solution.py:41
  8.7 42.4 %copy-start.17 = (f32[256]{0:T(256)}, f32[256]{0:T(256)S(1)}, u32[]{:S(2)}) copy-start(f32[256]{0:T(256)S(1)} %fusion.21) | copy-start | bytes 3076
  8.8 42.4 %copy-start.15 = (f32[256]{0:T(256)}, f32[256]{0:T(256)S(1)}, u32[]{:S(2)}) copy-start(f32[256]{0:T(256)S(1)} %fusion.32) | copy-start | bytes 3076
  54.3 86.7 %all-gather.21.cloned.1.call-start = ((), (), s32[]{:S(2)}) async-start(), calls=%async_computation.15 | async-start | bytes 4456448 | tf_op jit(solution)/shard_map/all_gather | solution.py:76
  55.0 163.4 %all-gather.23.cloned.1.call-start = ((), (), s32[]{:S(2)}) async-start(), calls=%async_computation.16 | async-start | bytes 4456448 | tf_op jit(solution)/shard_map/all_gather | solution.py:77
  55.8 276.8 %all-gather.19.cloned.1.call-start = ((), (), s32[]{:S(2)}) async-start(), calls=%async_computation.14 | async-start | bytes 8912896 | tf_op jit(solution)/shard_map/all_gather | solution.py:78
  56.3 389.8 %all-gather.17.cloned.1.call-start = ((), (), s32[]{:S(2)}) async-start(), calls=%async_computation.13 | async-start | bytes 8912896 | tf_op jit(solution)/shard_map/all_gather | solution.py:79
  56.9 532.4 %all-gather.25.cloned.1.call-start = ((), (), s32[]{:S(2)}) async-start(), calls=%async_computation.17 | async-start | bytes 8912896 | tf_op jit(solution)/shard_map/all_gather | solution.py:80
  57.5 581.0 %reduce-scatter.13.cloned.1.call-start = ((), (), s32[]{:S(2)}) async-start(), calls=%async_computation.18 | async-start | bytes 6291456 | tf_op jit(solution)/shard_map/reduce_scatter | solution.py:45
  57.8 168.3 %copy-start.11 = (f32[512,512]{1,0:T(8,128)}, f32[512,512]{1,0:T(8,128)S(1)}, u32[]{:S(2)}) copy-start(f32[512,512]{1,0:T(8,128)S(1)} %select_convert_fusion) | copy-start | bytes 3145732
  146.9 79.2 %copy-start.7 = (bf16[512,1024]{0,1:T(8,128)(2,1)}, bf16[512,1024]{0,1:T(8,128)(2,1)S(1)}, u32[]{:S(2)}) copy-start(bf16[512,1024]{0,1:T(8,128)(2,1)S(1)} %copy.48) | copy-start | bytes 3145732
  226.0 2.7 copy-start.9
  332.5 8.7 copy-start.28
  342.7 3.3 copy-start
  346.0 100.2 %copy-start.23 = (bf16[512,2048]{1,0:T(8,128)(2,1)S(1)}, bf16[512,2048]{1,0:T(8,128)(2,1)}, u32[]{:S(2)}) copy-start(bf16[512,2048]{1,0:T(8,128)(2,1)} %all-gather.15.cloned.1.call-done) | copy-start | bytes 6291460
  599.9 38.6 %copy-start.3 = (bf16[256,2048]{1,0:T(8,128)(2,1)S(1)}, bf16[256,2048]{1,0:T(8,128)(2,1)}, u32[]{:S(2)}) copy-start(bf16[256,2048]{1,0:T(8,128)(2,1)} %param.13) | copy-start | bytes 3145732
  600.0 127.7 %all-gather.29.cloned.1.call-start = ((), (), s32[]{:S(2)}) async-start(), calls=%async_computation.20 | async-start | bytes 8912896 | tf_op jit(solution)/shard_map/all_gather | solution.py:117
  600.7 137.9 %all-gather.27.cloned.1.call-start = ((), (), s32[]{:S(2)}) async-start(), calls=%async_computation.19 | async-start | bytes 3145728 | tf_op jit(solution)/shard_map/all_gather | solution.py:41
  640.5 2.5 copy-start.6
  641.8 213.9 %all-gather.31.cloned.1.call-start = ((), (), s32[]{:S(2)}) async-start(), calls=%async_computation.21 | async-start | bytes 8912896 | tf_op jit(solution)/shard_map/all_gather | solution.py:118
  642.3 224.4 %all-gather.35.cloned.1.call-start = ((), (), s32[]{:S(2)}) async-start(), calls=%async_computation.24 | async-start | bytes 3145728 | tf_op jit(solution)/shard_map/all_gather | solution.py:49
  644.3 368.9 %all-gather.33.cloned.1.call-start = ((), (), s32[]{:S(2)}) async-start(), calls=%async_computation.22 | async-start | bytes 8912896 | tf_op jit(solution)/shard_map/all_gather | solution.py:119
  644.9 407.1 %reduce-scatter.17.cloned.1.call-start = ((), (), s32[]{:S(2)}) async-start(), calls=%async_computation.25 | async-start | bytes 6291456 | tf_op jit(solution)/shard_map/reduce_scatter | solution.py:53
  1026.6 8.5 copy-start.31
  1026.6 8.6 copy-start.30
  1026.6 8.6 copy-start.20
  1041.4 25.9 reduce-scatter.15.cloned.1.call-start
  1051.9 32.5 all-gather.37.cloned.1.call-start
  1072.3 160.5 %reduce-scatter.19.cloned.1.call-start = ((), (), s32[]{:S(2)}) async-start(), calls=%async_computation.27 | async-start | bytes 6291456 | tf_op jit(solution)/shard_map/reduce_scatter | solution.py:53
  1104.7 4.6 copy-start.1
  1104.7 5.9 copy-start.2
  1110.6 1.9 copy-start.26
  1112.6 2.3 copy-start.8
  1117.7 2.2 copy-start.22
  1119.0 7.8 copy-start.27
  1119.9 2.4 copy-start.21
  1119.9 6.9 slice-start
  1122.4 4.4 slice-start.1
  1146.5 196.7 %reduce-scatter.23.cloned.1.call-start = ((), (), s32[]{:S(2)}) async-start(), calls=%async_computation.29 | async-start | bytes 8912896 | tf_op jit(solution)/shard_map/reduce_scatter | solution.py:234
  1153.9 372.3 %reduce-scatter.21.cloned.1.call-start = ((), (), s32[]{:S(2)}) async-start(), calls=%async_computation.28 | async-start | bytes 8912896 | tf_op jit(solution)/shard_map/reduce_scatter | solution.py:233
  1161.3 716.6 %reduce-scatter.31.cloned.1.call-start = ((), (), s32[]{:S(2)}) async-start(), calls=%async_computation.33 | async-start | bytes 17825792 | tf_op jit(solution)/shard_map/reduce_scatter | solution.py:158
  1174.3 1058.3 %reduce-scatter.33.cloned.1.call-start = ((), (), s32[]{:S(2)}) async-start(), calls=%async_computation.34 | async-start | bytes 17825792 | tf_op jit(solution)/shard_map/reduce_scatter | solution.py:159
  1186.9 1400.6 %reduce-scatter.35.cloned.1.call-start = ((), (), s32[]{:S(2)}) async-start(), calls=%async_computation.35 | async-start | bytes 17825792 | tf_op jit(solution)/shard_map/reduce_scatter | solution.py:160
  1199.9 1742.5 %reduce-scatter.29.cloned.1.call-start = ((), (), s32[]{:S(2)}) async-start(), calls=%async_computation.32 | async-start | bytes 17825792 | tf_op jit(solution)/shard_map/reduce_scatter | solution.py:237
  1212.5 2084.8 %reduce-scatter.25.cloned.1.call-start = ((), (), s32[]{:S(2)}) async-start(), calls=%async_computation.30 | async-start | bytes 17825792 | tf_op jit(solution)/shard_map/reduce_scatter | solution.py:235
  1222.5 2429.5 %reduce-scatter.27.cloned.1.call-start = ((), (), s32[]{:S(2)}) async-start(), calls=%async_computation.31 | async-start | bytes 17825792 | tf_op jit(solution)/shard_map/reduce_scatter | solution.py:236
  1232.8 50.9 %copy-start.18 = (f32[256]{0:T(256)S(1)}, f32[256]{0:T(256)}, u32[]{:S(2)}) copy-start(f32[256]{0:T(256)} %copy-done.17) | copy-start | bytes 3076
  1234.0 49.8 %copy-start.5 = (f32[256,2048]{1,0:T(8,128)S(1)}, f32[256,2048]{1,0:T(8,128)}, u32[]{:S(2)}) copy-start(f32[256,2048]{1,0:T(8,128)} %reduce-scatter.19.cloned.1.call-done) | copy-start | bytes 6291460
  (10 other events, 12.4 us)
Sparse Core Ops, SparseCore 0:
  54.4 6.4 all-gather.14
  63.6 77.2 all-gather.20
  143.7 74.6 all-gather.22
  221.0 111.4 all-gather.18
  335.1 111.0 all-gather.16
  448.7 140.5 all-gather.24
  600.1 10.2 reduce-scatter.12
  613.5 114.1 all-gather.28
  729.9 8.7 all-gather.26
  741.7 113.9 all-gather.30
  857.9 8.7 all-gather.34
  869.6 143.5 all-gather.32
  1041.5 10.2 reduce-scatter.16
  1053.9 13.3 reduce-scatter.14
  1072.5 11.8 all-gather.36
  1146.6 13.1 reduce-scatter.18
  1162.6 180.5 reduce-scatter.22
  1345.9 180.2 reduce-scatter.20
  1529.0 348.7 reduce-scatter.30
  1880.6 351.9 reduce-scatter.32
  2235.5 351.9 reduce-scatter.34
  2590.4 351.9 reduce-scatter.28
  2945.3 351.9 reduce-scatter.24
  3300.0 351.9 reduce-scatter.26
where the time goes:
time: 3670 us; the launch traced here: 3660 us
  waiting for transfers between devices  3230 us (88%)
  matrix products  235 us (6%)
  blocking collectives  126 us (3%)
    reduce_scatter x1, waiting for transfers between devices, on_device(): lax.psum_scatter(grad_value, 'dp', scatter_dimension=0, tiled=True)  355 us
    reduce_scatter x1, waiting for transfers between devices, on_device(): lax.psum_scatter(grad_down, 'dp', scatter_dimension=1, tiled=True)  355 us
    reduce_scatter x1, waiting for transfers between devices, on_device(): lax.psum_scatter(grad_out, 'dp', scatter_dimension=1, tiled=True)  355 us
    reduce_scatter x1, waiting for transfers between devices, on_device(): lax.psum_scatter(grad_ffup, 'dp', scatter_dimension=0, tiled=True)  355 us
    reduce_scatter x1, waiting for transfers between devices, on_device(): lax.psum_scatter(gate_weight_gradient, 'dp', scatter_dimension=0, tiled=T...  355 us
    reduce_scatter x1, waiting for transfers between devices, on_device(): lax.psum_scatter(grad_ffgate, 'dp', scatter_dimension=0, tiled=True)  352 us
    reduce_scatter x1, waiting for transfers between devices, on_device(): lax.psum_scatter(grad_query, 'dp', scatter_dimension=0, tiled=True)  183 us
    all_gather x1, waiting for transfers between devices, on_device(): lax.all_gather(w_ffdown, 'dp', axis=1, tiled=True)  146 us
  transfers between devices with their start and end apart: 24, of which 21 were waited for; matrix products, arithmetic and copies ran while one was open for 5% of the time, Pallas kernels for 0%

commit v1 on v0

v1 whole, which is shorter than its diff:
```python
import jax
import jax.numpy as jnp
from jax import lax
from jax.sharding import PartitionSpec as P

DK = 256
DV = 512
PLANE = 4

norm_eps = 1e-06
group_floor = 1.0

bf16 = jnp.bfloat16
f32 = jnp.float32


def decay_table(positions, head):
    spacing = positions[:, None] - positions[None, :]
    log_rate = jnp.log1p(-jnp.exp2(-5.0 - head.astype(f32)))
    kept_spacing = jnp.where(spacing >= 0, spacing, jnp.zeros_like(spacing)).astype(f32)
    powers = jnp.exp(kept_spacing * log_rate)
    return jnp.where(spacing >= 0, powers, jnp.zeros_like(powers))


def dot(left, right):
    return jnp.dot(left, right, preferred_element_type=f32)


def dot_nt(left, right):
    return lax.dot_general(left, right, (((1,), (1,)), ((), ())), preferred_element_type=f32)


def dot_tn(left, right):
    return lax.dot_general(left, right, (((0,), (0,)), ((), ())), preferred_element_type=f32)


def hop(value, bits, count):
    return lax.ppermute(value, "dp", [(i, i ^ bits) for i in range(count)])


def swap(value):
    return lax.ppermute(value, "tensor", [(0, 1), (1, 0)])


def natural(blocks, me):
    stacked = jnp.stack(blocks)
    return [lax.dynamic_index_in_dim(stacked, me ^ j, 0, keepdims=False) for j in range(PLANE)]


def plane_gather(mine, count):
    half = mine.shape[0] // 2
    from_x = hop(mine, 1, count)
    from_y = hop(mine, 2, count)
    far_a = hop(from_x[:half], 2, count)
    far_b = hop(from_y[half:], 1, count)
    return [mine, from_x, from_y, jnp.concatenate([far_a, far_b])]


def spread(mine, count):
    blocks = plane_gather(mine, count)
    near = jnp.stack(blocks)
    other = swap(near)
    return jnp.stack([near, other], axis=1).reshape(8 * mine.shape[0], mine.shape[1])


def fold(terms, rows, count):
    parts = terms.reshape(PLANE, 2, rows, terms.shape[1])
    arrived = swap(parts[:, 1].astype(bf16))
    mine = parts[:, 0] + arrived.astype(f32)
    half = rows // 2
    first, second = mine[:, :half], mine[:, half:]
    from_x = hop(jnp.stack([first[1], first[3]]).astype(bf16), 1, count).astype(f32)
    from_y = hop(jnp.stack([second[2], second[3]]).astype(bf16), 2, count).astype(f32)
    last_y = hop((first[2] + from_x[1]).astype(bf16), 2, count).astype(f32)
    last_x = hop((second[1] + from_y[1]).astype(bf16), 1, count).astype(f32)
    return jnp.concatenate([first[0] + from_x[0] + last_y, second[0] + from_y[0] + last_x])


def on_device(
    tokens,
    lengths,
    w_query,
    w_key,
    w_value,
    w_gate,
    w_out,
    w_ffgate,
    w_ffup,
    w_ffdown,
    gain_attn,
    gain_mlp,
    cotangent,
):
    count = lax.axis_size("dp")
    depth = count // PLANE
    columns = [[q + PLANE * z for z in range(depth)] for q in range(PLANE)]
    place = lax.axis_index("dp")
    me = place % PLANE
    core = lax.axis_index("tensor")
    rows, width = tokens.shape
    shard = w_query.shape[0]

    gains = jnp.stack([gain_attn, gain_mlp])[None]
    step = 1
    while step < count:
        gains = jnp.concatenate([gains, hop(gains, step, count)])
        step *= 2
    order = place ^ jnp.arange(count)
    gains = jnp.take(gains, order, axis=0).astype(f32)
    gain_first = gains[:, 0].reshape(1, width)
    gain_second = gains[:, 1].reshape(1, width)

    def cut_columns(weight):
        part = weight.shape[1] // PLANE
        return [lax.dynamic_slice_in_dim(weight, (me ^ k) * part, part, 1) for k in range(PLANE)]

    def cut_rows(weight):
        part = weight.shape[0] // PLANE
        return [lax.dynamic_slice_in_dim(weight, (me ^ k) * part, part, 0) for k in range(PLANE)]

    def gather_depth(block):
        return lax.all_gather(block, "dp", axis=0, tiled=False, axis_index_groups=columns)

    wide = [cut_columns(w) for w in (w_query, w_key, w_value, w_gate)]
    wide_cuts = [jnp.concatenate([w[k] for w in wide], axis=1) for k in range(PLANE)]
    wide_blocks = [wide_cuts[0]] + [hop(wide_cuts[k], k, count) for k in range(1, PLANE)]
    out_cuts = cut_rows(w_out)
    out_blocks = [out_cuts[0]] + [hop(out_cuts[k], k, count) for k in range(1, PLANE)]
    ff = [cut_columns(w) for w in (w_ffgate, w_ffup)]
    ff_cuts = [jnp.concatenate([w[k] for w in ff], axis=1) for k in range(PLANE)]
    ff_blocks = [ff_cuts[0]] + [hop(ff_cuts[k], k, count) for k in range(1, PLANE)]
    down_cuts = cut_rows(w_ffdown)
    down_blocks = [down_cuts[0]] + [hop(down_cuts[k], k, count) for k in range(1, PLANE)]

    def full_columns(blocks):
        block = jnp.concatenate(natural(blocks, me), axis=0)
        return gather_depth(block).reshape(width, block.shape[1])

    def full_rows(blocks):
        block = jnp.concatenate(natural(blocks, me), axis=1)
        gathered = gather_depth(block)
        return jnp.moveaxis(gathered, 0, 1).reshape(block.shape[0], width)

    wide_full = full_columns(wide_blocks)
    out_full = full_rows(out_blocks)
    ff_full = full_columns(ff_blocks)
    down_full = full_rows(down_blocks)
    key_cols = w_query.shape[1] // PLANE
    value_cols = w_value.shape[1] // PLANE
    heads = key_cols // DK
    assert heads == 1
    inner = w_ffgate.shape[1] // PLANE

    input_rows = tokens.astype(f32)
    first_scale = lax.rsqrt(jnp.mean(input_rows * input_rows, axis=-1, keepdims=True) + norm_eps)
    normed_attn = (input_rows * first_scale * gain_first).astype(bf16)
    attn_all = spread(normed_attn, count)
    total = attn_all.shape[0]
    slot_len = 2 * rows

    query_key = dot(attn_all, wide_full[:, : 2 * key_cols]).astype(bf16)
    query = query_key[:, :key_cols].reshape(PLANE, slot_len, key_cols)
    key = query_key[:, key_cols:].reshape(PLANE, slot_len, key_cols)
    value = dot(attn_all, wide_full[:, 2 * key_cols : 2 * key_cols + value_cols]).astype(bf16)
    value = value.reshape(PLANE, slot_len, value_cols)
    gate_pre = dot(attn_all, wide_full[:, 2 * key_cols + value_cols :])

    local = jnp.arange(rows, dtype=jnp.int32)
    positions = jnp.concatenate([core * rows + local, (1 - core) * rows + local])
    decays = decay_table(positions, core * PLANE + me)
    scores = jnp.einsum("snd,smd->snm", query, key, preferred_element_type=f32)
    scores = (scores * decays).astype(bf16)
    retained = jnp.einsum("snm,sme->sne", scores, value, preferred_element_type=f32)
    retained = retained.reshape(total, value_cols)
    group_scale = lax.rsqrt(jnp.mean(retained * retained, axis=-1, keepdims=True) + group_floor)
    normed = retained * group_scale
    sigma = jax.nn.sigmoid(gate_pre)
    gated = (gate_pre * sigma * normed).astype(bf16)
    hidden = input_rows + fold(dot(gated, out_full), rows, count)

    second_scale = lax.rsqrt(jnp.mean(hidden * hidden, axis=-1, keepdims=True) + norm_eps)
    normed_mlp = (hidden * second_scale * gain_second).astype(bf16)
    mlp_all = spread(normed_mlp, count)
    up = dot(mlp_all, ff_full)
    gate_up, value_up = up[:, :inner], up[:, inner:]
    gelu, gelu_back = jax.vjp(lambda u: jax.nn.gelu(u, approximate=True), gate_up)
    inner_act = (gelu * value_up).astype(bf16)
    valid_rows = ((core * rows + local) < lengths[0]).astype(f32)[:, None]
    mlp_rows = fold(dot(inner_act, down_full), rows, count)
    output = (valid_rows * (hidden + mlp_rows)).astype(bf16)

    back_rows = valid_rows * cotangent.astype(f32)
    back_all = spread(back_rows.astype(bf16), count)
    grad_down = dot_tn(inner_act, back_all).astype(bf16)
    grad_inner = dot_nt(back_all, down_full)
    grad_gate_up = gelu_back(grad_inner * value_up)[0].astype(bf16)
    grad_value_up = (grad_inner * gelu).astype(bf16)
    grad_up = jnp.concatenate([grad_gate_up, grad_value_up], axis=1)
    grad_ff = dot_tn(mlp_all, grad_up).astype(bf16)
    grad_normed = fold(dot_nt(grad_up, ff_full), rows, count)
    gain_term_mlp = jnp.sum(grad_normed * hidden * second_scale, axis=0)
    scaled = grad_normed * gain_second
    grad_hidden = back_rows + second_scale * (
        scaled
        - hidden * (second_scale * second_scale) * jnp.mean(hidden * scaled, axis=-1, keepdims=True)
    )

    attn_grad_all = spread(grad_hidden.astype(bf16), count)
    grad_out = dot_tn(gated, attn_grad_all).astype(bf16)
    grad_gated = dot_nt(attn_grad_all, out_full)
    grad_gate_pre = (
        grad_gated * normed * (sigma * (1.0 + gate_pre * (1.0 - sigma)))
    ).astype(bf16)
    grad_normed_head = grad_gated * (gate_pre * sigma)
    grad_retained = (
        group_scale
        * (
            grad_normed_head
            - normed * group_scale * jnp.mean(retained * grad_normed_head, axis=-1, keepdims=True)
        )
    ).astype(bf16)
    grad_retained = grad_retained.reshape(PLANE, slot_len, value_cols)
    grad_scores = jnp.einsum("sne,sme->snm", grad_retained, value, preferred_element_type=f32)
    grad_scores = (grad_scores * decays).astype(bf16)
    grad_query = jnp.einsum("snm,smd->snd", grad_scores, key, preferred_element_type=f32)
    grad_key = jnp.einsum("snm,snd->smd", grad_scores, query, preferred_element_type=f32)
    grad_value = jnp.einsum("snm,sne->sme", scores, grad_retained, preferred_element_type=f32)
    grad_wide = jnp.concatenate(
        [
            grad_query.astype(bf16).reshape(total, key_cols),
            grad_key.astype(bf16).reshape(total, key_cols),
            grad_value.astype(bf16).reshape(total, value_cols),
            grad_gate_pre,
        ],
        axis=1,
    )
    grad_wide_weights = dot_tn(attn_all, grad_wide).astype(bf16)
    grad_normed_attn = fold(dot_nt(grad_wide, wide_full), rows, count)
    gain_term_attn = jnp.sum(grad_normed_attn * input_rows * first_scale, axis=0)
    scaled_first = grad_normed_attn * gain_first
    tokens_grad = grad_hidden + first_scale * (
        scaled_first
        - input_rows
        * (first_scale * first_scale)
        * jnp.mean(input_rows * scaled_first, axis=-1, keepdims=True)
    )
    tokens_grad = tokens_grad.astype(bf16)

    def sum_depth(block):
        return lax.psum_scatter(
            block, "dp", scatter_dimension=0, tiled=True, axis_index_groups=columns
        )

    def back_columns(block):
        cuts = [lax.dynamic_slice_in_dim(block, (me ^ k) * shard, shard, 0) for k in range(PLANE)]
        blocks = [cuts[0]] + [hop(cuts[k], k, count) for k in range(1, PLANE)]
        return natural(blocks, me)

    def back_rows_of(block):
        cuts = [lax.dynamic_slice_in_dim(block, (me ^ k) * shard, shard, 1) for k in range(PLANE)]
        blocks = [cuts[0]] + [hop(cuts[k], k, count) for k in range(1, PLANE)]
        return jnp.concatenate(natural(blocks, me), axis=0).astype(f32)

    def depth_first(block):
        cut = block.reshape(block.shape[0], depth, width // depth)
        return jnp.moveaxis(cut, 1, 0).reshape(depth * block.shape[0], width // depth)

    down_sum = back_rows_of(sum_depth(depth_first(grad_down)))
    ff_sums = back_columns(sum_depth(grad_ff))
    ffgate_sum = jnp.concatenate([b[:, :inner] for b in ff_sums], axis=1).astype(f32)
    ffup_sum = jnp.concatenate([b[:, inner:] for b in ff_sums], axis=1).astype(f32)
    out_sum = back_rows_of(sum_depth(depth_first(grad_out)))
    wide_sums = back_columns(sum_depth(grad_wide_weights))
    edges = (0, key_cols, 2 * key_cols, 2 * key_cols + value_cols, 2 * key_cols + 2 * value_cols)
    wide_out = [
        jnp.concatenate([b[:, lo:hi] for b in wide_sums], axis=1).astype(f32)
        for lo, hi in zip(edges[:-1], edges[1:])
    ]

    gain_terms = jnp.stack([gain_term_attn, gain_term_mlp])
    bit = count // 2
    while bit >= 1:
        side = (place // bit) % 2
        cut = gain_terms.reshape(2, 2, -1)
        kept = lax.dynamic_index_in_dim(cut, side, 1, keepdims=False)
        sent = lax.dynamic_index_in_dim(cut, 1 - side, 1, keepdims=False)
        gain_terms = kept + hop(sent, bit, count)
        bit //= 2
    cut = gain_terms.reshape(2, 2, -1)
    kept = lax.dynamic_index_in_dim(cut, core, 1, keepdims=False)
    sent = lax.dynamic_index_in_dim(cut, 1 - core, 1, keepdims=False)
    gain_terms = kept + swap(sent)

    return (
        output,
        tokens_grad,
        wide_out[0],
        wide_out[1],
        wide_out[2],
        wide_out[3],
        out_sum,
        ffgate_sum,
        ffup_sum,
        down_sum,
        gain_terms[0],
        gain_terms[1],
    )


def solution(mesh):
    return jax.shard_map(
        on_device,
        mesh=mesh,
        in_specs=(
            P(("dp", "tensor"), None),
            P("dp"),
            P("dp", "tensor"),
            P("dp", "tensor"),
            P("dp", "tensor"),
            P("dp", "tensor"),
            P("tensor", "dp"),
            P("dp", "tensor"),
            P("dp", "tensor"),
            P("tensor", "dp"),
            P("dp"),
            P("dp"),
            P(("dp", "tensor"), None),
        ),
        out_specs=(
            P(("dp", "tensor"), None),
            P(("dp", "tensor"), None),
            P("dp", "tensor"),
            P("dp", "tensor"),
            P("dp", "tensor"),
            P("dp", "tensor"),
            P("tensor", "dp"),
            P("dp", "tensor"),
            P("dp", "tensor"),
            P("tensor", "dp"),
            P(("dp", "tensor")),
            P(("dp", "tensor")),
        ),
        check_vma=False,
    )
```

time: 3670 us -> 896 us (0.24)
  waiting for transfers between devices: 3230 us -> 367 us
  blocking collectives: 126 us -> 0 us
  other arithmetic: 30 us -> 154 us
  local copies, waits for them, and re-layouts: 23 us -> 126 us
  matrix products: 235 us -> 149 us
  starting transfers between devices: 1.73 us -> 77.5 us
    reduce_scatter x12 -> x4, waiting for transfers between devices: 2380 us -> 19.8 us  [sum_depth(): lax.psum_scatter(block, 'dp', scatter_dimension=0, tiled=True, axis_index...]
    all_gather x12 -> x4, waiting for transfers between devices: 844 us -> 61.3 us  [gather_depth(): lax.all_gather(block, 'dp', axis=0, tiled=False, axis_index_groups=columns)]
    ppermute x0 -> x73, waiting for transfers between devices: none -> 286 us  [the longest x64 273 us: hop(): return lax.ppermute(value, 'dp', [(i, i ^ bits) for i in range(count)])]
    another operation x0 -> x33, other arithmetic: none -> 95.6 us
    dot_general x30 -> x20, matrix products: 235 us -> 149 us  [the longest x4 51.5 us: dot_nt(): lax.dot_general(left, right, (((1,), (1,)), ((), ())), preferred_element_...]
    all_gather x2 -> x0, blocking collectives: 80.1 us -> none  [the longest x1 42.4 us: on_device(): lax.all_gather(gain_attn, 'dp', axis=0, tiled=True)]
    ppermute x0 -> x73, starting transfers between devices: none -> 76.3 us  [the longest x64 75 us: hop(): return lax.ppermute(value, 'dp', [(i, i ^ bits) for i in range(count)])]
    another operation x0 -> x17, local copies, waits for them, and re-layouts: none -> 48.3 us  [the longest x4 33.5 us: spread(): jnp.stack([near, other], axis=1).reshape(8 * mine.shape[0], mine.shape[1])]
  transfers between devices with their start and end apart: 24 -> 81, of which waited for: 21 -> 46; matrix products, arithmetic and copies ran while one was open for 5% -> 33% of each run, Pallas kernels for 0% -> 0%
where the time goes in v1:
time: 896 us; the launch traced here: 891 us
  waiting for transfers between devices  367 us (41%)
  other arithmetic  154 us (17%)
  matrix products  149 us (17%)
  local copies, waits for them, and re-layouts  126 us (14%)
  starting transfers between devices  77.5 us (9%)
  between operations  16.7 us (2%)
    ppermute x64, waiting for transfers between devices, hop(): return lax.ppermute(value, 'dp', [(i, i ^ bits) for i in range(count)])  273 us
    ppermute x64, starting transfers between devices, hop(): return lax.ppermute(value, 'dp', [(i, i ^ bits) for i in range(count)])  75 us
    all_gather x4, waiting for transfers between devices, gather_depth(): lax.all_gather(block, 'dp', axis=0, tiled=False, axis_index_groups=columns)  61.3 us
    dot_general x4, matrix products, dot_nt(): lax.dot_general(left, right, (((1,), (1,)), ((), ())), preferred_element_...  51.5 us
    dot_general x6, matrix products, dot(): return jnp.dot(left, right, preferred_element_type=f32)  45.1 us
    dot_general x4, matrix products, dot_tn(): lax.dot_general(left, right, (((0,), (0,)), ((), ())), preferred_element_...  44.6 us
    another operation x4, other arithmetic  42.3 us
    another operation x8, other arithmetic, spread(): jnp.stack([near, other], axis=1).reshape(8 * mine.shape[0], mine.shape[1])  41.8 us
  transfers between devices with their start and end apart: 81, of which 46 were waited for; matrix products, arithmetic and copies ran while one was open for 33% of the time, Pallas kernels for 0%

profile of v1, /device:TPU:0, one launch (start us, length us, event | category | flops | bytes accessed | tf_op | source)
XLA Modules:
  0.0 890.7 jit_solution(10042839093234165826)
XLA Ops:
  32.0 14.8 %collective-permute-done.10 = bf16[128,1536]{1,0:T(8,128)(2,1)S(1)} collective-permute-done((bf16[128,1536]{1,0:T(8,128)(2,1)S(1)}, bf16[128,1536]{1,0:T(8,128)(2,1)S(1)}, u32[]{:S(2)}, u32[]{:S(2)}) %collective-permute-start.10) | collective-permute-done | bytes 393248 | tf_op jit(solution)/shard_map/ppermute | solution.py:38
  69.1 19.8 %collective-permute-done.4 = bf16[256,2048]{1,0:T(8,128)(2,1)S(1)} collective-permute-done((bf16[256,2048]{1,0:T(8,128)(2,1)S(1)}, bf16[256,2048]{1,0:T(8,128)(2,1)S(1)}, u32[]{:S(2)}, u32[]{:S(2)}) %collective-permute-start.4) | collective-permute-done | bytes 1048608 | tf_op jit(solution)/shard_map/ppermute | solution.py:38
  92.7 6.5 collective-permute-done.6
  112.9 7.6 pad_maximum_fusion
  120.5 8.3 copy.36
  128.8 61.3 %all-gather.9.cloned.1.call-done = bf16[2048,1536]{1,0:T(8,128)(2,1)} async-done(((bf16[512,1536]{1,0:T(8,128)(2,1)}), bf16[2048,1536]{1,0:T(8,128)(2,1)}) %all-gather.9.cloned.1.call-update) | async-done | bytes 6291472 | tf_op jit(solution)/shard_map/all_gather | solution.py:122
  190.1 8.6 convolution_convert_fusion.5
  207.9 7.5 multiply_convert_fusion.5
  220.2 5.8 copy-done.10
  229.3 6.8 collective-permute-done.15
  236.1 11.6 %fusion.109 = (bf16[4,256,2048]{2,1,0:T(8,128)(2,1)}, f32[4,256,2048]{2,1,0:T(8,128)}) fusion(bf16[4,256,2048]{2,1,0:T(8,128)(2,1)} %collective-permute-done.15, f32[4,2,256,2048]{3,2,1,0:T(8,128)} %copy-done.10), kind=kLoop, calls=%fused_computation.343 | loop fusion | flops 6291456 | bytes 25165824 | tf_op jit(solution)/shard_map/convert.22
  262.6 16.3 %collective-permute-done.16 = bf16[2,128,2048]{2,1,0:T(8,128)(2,1)} collective-permute-done((bf16[2,128,2048]{2,1,0:T(8,128)(2,1)}, bf16[2,128,2048]{2,1,0:T(8,128)(2,1)}, u32[]{:S(2)}, u32[]{:S(2)}) %collective-permute-start.16) | collective-permute-done | bytes 1048608 | tf_op jit(solution)/shard_map/ppermute | solution.py:38
  288.0 13.2 %collective-permute-done.36 = bf16[256,2048]{1,0:T(8,128)(2,1)S(1)} collective-permute-done((bf16[256,2048]{1,0:T(8,128)(2,1)}, bf16[256,2048]{1,0:T(8,128)(2,1)S(1)}, u32[]{:S(2)}, u32[]{:S(2)}) %collective-permute-start.36) | collective-permute-done | bytes 1048608 | tf_op jit(solution)/shard_map/ppermute | solution.py:38
  306.8 17.2 %collective-permute-done.17 = bf16[128,2048]{1,0:T(8,128)(2,1)S(1)} collective-permute-done((bf16[128,2048]{1,0:T(8,128)(2,1)S(1)}, bf16[128,2048]{1,0:T(8,128)(2,1)S(1)}, u32[]{:S(2)}, u32[]{:S(2)}) %collective-permute-start.17) | collective-permute-done | bytes 524320 | tf_op jit(solution)/shard_map/ppermute | solution.py:38
  346.9 14.0 %collective-permute-done.20 = bf16[256,2048]{1,0:T(8,128)(2,1)} collective-permute-done((bf16[256,2048]{1,0:T(8,128)(2,1)}, bf16[256,2048]{1,0:T(8,128)(2,1)}, u32[]{:S(2)}, u32[]{:S(2)}) %collective-permute-start.20) | collective-permute-done | bytes 1048608 | tf_op jit(solution)/shard_map/ppermute | solution.py:38
  364.5 9.1 %collective-permute-done.22 = bf16[128,2048]{1,0:T(8,128)(2,1)S(1)} collective-permute-done((bf16[128,2048]{1,0:T(8,128)(2,1)S(1)}, bf16[128,2048]{1,0:T(8,128)(2,1)S(1)}, u32[]{:S(2)}, u32[]{:S(2)}) %collective-permute-start.22) | collective-permute-done | bytes 524320 | tf_op jit(solution)/shard_map/ppermute | solution.py:38
  392.5 6.2 pad_maximum_fusion.2
  398.7 8.4 copy.43
  407.1 6.3 pad_maximum_fusion.1
  413.4 8.3 copy.39
  421.7 12.6 %fusion.129 = f32[2048,1024]{1,0:T(8,128)S(1)} fusion(bf16[2048,2048]{1,0:T(8,128)(2,1)} %bitcast.367, bf16[2048,1024]{1,0:T(8,128)(2,1)} %all-gather.13.cloned.1.call-done), kind=kOutput, calls=%fused_computation.362 | convolution fusion | flops 8589934592 | bytes 20971520 | tf_op jit(solution)/shard_map/dot_general | solution.py:26
  434.3 11.2 %fusion.20 = (bf16[2048,512]{1,0:T(8,128)(2,1)S(1)}, bf16[2048,512]{1,0:T(8,128)(2,1)S(1)}, bf16[2048,512]{1,0:T(8,128)(2,1)}) fusion(f32[2048,1024]{1,0:T(8,128)S(1)} %fusion.129, bf16[2048,2048]{1,0:T(8,128)(2,1)} %bitcast.371, bf16[512,2048]{1,0:T(8,128)(2,1)S(1)} %bitcast.396), kind=kOutput, calls=%fused_computation.43 | convolution fusion | flops 4322230272 | bytes 25165824 | tf_op jit(solution)/shard_map/dot_general | solution.py:30
  448.7 12.6 %fusion.25 = f32[4,2,256,2048]{3,2,0,1:T(8,128)S(1)} fusion(bf16[2048,1024]{1,0:T(8,128)(2,1)} %all-gather.13.cloned.1.call-done, bf16[4,2,256,1024]{3,2,1,0:T(8,128)(2,1)} %bitcast.384), kind=kOutput, calls=%fused_computation.53 | convolution fusion | flops 8589934592 | bytes 25165824 | tf_op jit(solution)/shard_map/dot_general | solution.py:30
  468.9 6.3 fusion.49
  484.3 10.2 %fusion.105 = (bf16[4,256,2048]{2,1,0:T(8,128)(2,1)S(1)}, f32[4,256,2048]{2,1,0:T(8,128)}) fusion(bf16[4,256,2048]{2,1,0:T(8,128)(2,1)} %collective-permute-done.41, f32[4,2,256,2048]{3,2,0,1:T(8,128)} %copy-done.9), kind=kLoop, calls=%fused_computation.341 | loop fusion | flops 6291456 | bytes 25165824 | tf_op jit(solution)/shard_map/convert.10
  496.5 10.2 %fusion.107 = (bf16[4,256,2048]{2,1,0:T(8,128)(2,1)S(1)}, f32[4,256,2048]{2,1,0:T(8,128)}) fusion(bf16[4,256,2048]{2,1,0:T(8,128)(2,1)} %collective-permute-done.31, f32[4,2,256,2048]{3,2,0,1:T(8,128)} %copy-done.8), kind=kLoop, calls=%fused_computation.342 | loop fusion | flops 6291456 | bytes 25165824 | tf_op jit(solution)/shard_map/convert.16
  514.5 8.1 convolution_convert_fusion.2
  524.4 11.3 %collective-permute-done.42 = bf16[2,128,2048]{2,1,0:T(8,128)(2,1)} collective-permute-done((bf16[2,128,2048]{2,1,0:T(8,128)(2,1)}, bf16[2,128,2048]{2,1,0:T(8,128)(2,1)}, u32[]{:S(2)}, u32[]{:S(2)}) %collective-permute-start.42) | collective-permute-done | bytes 1048608 | tf_op jit(solution)/shard_map/ppermute | solution.py:38
  542.9 15.3 %collective-permute-done.32 = bf16[2,128,2048]{2,1,0:T(8,128)(2,1)} collective-permute-done((bf16[2,128,2048]{2,1,0:T(8,128)(2,1)}, bf16[2,128,2048]{2,1,0:T(8,128)(2,1)}, u32[]{:S(2)}, u32[]{:S(2)}) %collective-permute-start.32) | collective-permute-done | bytes 1048608 | tf_op jit(solution)/shard_map/ppermute | solution.py:38
  562.3 7.6 collective-permute-done.43
  572.0 7.9 collective-permute-done.33
  586.8 21.0 %collective-permute-done.47 = bf16[256,2048]{1,0:T(8,128)(2,1)S(1)} collective-permute-done((bf16[256,2048]{1,0:T(8,128)(2,1)S(1)}, bf16[256,2048]{1,0:T(8,128)(2,1)S(1)}, u32[]{:S(2)}, u32[]{:S(2)}) %collective-permute-start.47) | collective-permute-done | bytes 1048608 | tf_op jit(solution)/shard_map/ppermute | solution.py:38
  613.4 11.1 %convolution_convert_fusion.1 = bf16[2048,1024]{1,0:T(8,128)(2,1)} fusion(bf16[2048,2048]{1,0:T(8,128)(2,1)S(1)} %bitcast.370, bf16[2048,512]{1,0:T(8,128)(2,1)S(1)} %copy-done.40, bf16[2048,512]{1,0:T(8,128)(2,1)S(1)} %copy-done.38), kind=kOutput, calls=%fused_computation.70 | convolution fusion | flops 8600420352 | bytes 16777216 | tf_op jit(solution)/shard_map/dot_general | solution.py:34
  629.0 6.4 collective-permute-done.50
  637.4 6.2 pad_maximum_fusion.3
  643.6 8.5 copy.48
  652.1 8.3 convolution_convert_fusion.3
  663.4 7.5 fusion.27
  671.3 6.2 multiply_convert_fusion.2
  684.1 17.1 %convolution_convert_fusion = bf16[2048,1536]{1,0:T(8,128)(2,1)} fusion(bf16[2048,2048]{1,0:T(8,128)(2,1)S(1)} %bitcast.366, bf16[2048,512]{1,0:T(8,128)(2,1)S(1)} %get-tuple-element.31, bf16[2048,512]{1,0:T(8,128)(2,1)S(1)} %bitcast.394, bf16[2048,256]{1,0:T(8,128)(2,1)S(1)} %bitcast.400, bf16[2048,256]{1,0:T(8,128)(2,1)} %bitcast.444), kind=kOutput, calls=%fused_computation.17 | convolution fusion | flops 12913213440 | bytes 20971520 | tf_op jit(solution)/shard_map/dot_general | solution.py:34
  701.2 20.2 %fusion.11 = f32[4,2,256,2048]{3,2,0,1:T(8,128)} fusion(bf16[2048,1536]{1,0:T(8,128)(2,1)} %all-gather.9.cloned.1.call-done, bf16[4,2,256,512]{3,2,1,0:T(8,128)(2,1)S(1)} %bitcast.393, bf16[4,2,256,512]{3,2,1,0:T(8,128)(2,1)} %bitcast.395, bf16[4,2,256,256]{3,2,1,0:T(8,128)(2,1)S(1)} %bitcast.401, bf16[4,2,256,256]{3,2,1,0:T(8,128)(2,1)} %bitcast.445), kind=kOutput, calls=%fused_computation.26 | convolution fusion | flops 12910067712 | bytes 29360128 | tf_op jit(solution)/shard_map/dot_general | solution.py:30
  721.4 6.1 fusion.24
  753.8 10.3 %fusion.102 = (bf16[4,256,2048]{2,1,0:T(8,128)(2,1)S(1)}, f32[4,256,2048]{2,1,0:T(8,128)}) fusion(bf16[4,256,2048]{2,1,0:T(8,128)(2,1)} %collective-permute-done.51, f32[4,2,256,2048]{3,2,0,1:T(8,128)} %fusion.11), kind=kLoop, calls=%fused_computation.339 | loop fusion | flops 6291456 | bytes 25165824 | tf_op jit(solution)/shard_map/convert.4
  767.0 22.3 %collective-permute-done.52 = bf16[2,128,2048]{2,1,0:T(8,128)(2,1)S(1)} collective-permute-done((bf16[2,128,2048]{2,1,0:T(8,128)(2,1)S(1)}, bf16[2,128,2048]{2,1,0:T(8,128)(2,1)S(1)}, u32[]{:S(2)}, u32[]{:S(2)}) %collective-permute-start.52) | collective-permute-done | bytes 1048608 | tf_op jit(solution)/shard_map/ppermute | solution.py:38
  803.2 6.1 collective-permute-done.53
  837.5 19.8 %reduce-scatter.5.cloned.1.call-done = bf16[512,1536]{1,0:T(8,128)(2,1)} async-done(((bf16[2048,1536]{1,0:T(8,128)(2,1)}), bf16[512,1536]{1,0:T(8,128)(2,1)}) %reduce-scatter.5.cloned.1.call-update) | async-done | bytes 1572880 | tf_op jit(solution)/shard_map/reduce_scatter | solution.py:250
  864.7 7.2 collective-permute-done.58
  871.9 7.3 collective-permute-done.57
  (490 shorter events, 311.7 us)
Async XLA Ops:
  7.2 99.7 %all-gather.11.cloned.1.call-start = ((), (), s32[]{:S(2)}) async-start(), calls=%async_computation.9 | async-start | bytes 2621440 | tf_op jit(solution)/shard_map/all_gather | solution.py:122
  27.9 162.2 %all-gather.9.cloned.1.call-start = ((), (), s32[]{:S(2)}) async-start(), calls=%async_computation.8 | async-start | bytes 7864320 | tf_op jit(solution)/shard_map/all_gather | solution.py:122
  28.2 18.6 %collective-permute-start.10 = (bf16[128,1536]{1,0:T(8,128)(2,1)S(1)}, bf16[128,1536]{1,0:T(8,128)(2,1)S(1)}, u32[]{:S(2)}, u32[]{:S(2)}) collective-permute-start(bf16[128,1536]{1,0:T(8,128)(2,1)S(1)} %pad_maximum_fusion.29), channel_id=1, source_target_pairs={{0,4},{2,6},{4,0},{6,2},{8,12},{10,14},{12,8},{14,10},{16,20},{18,... | collective-permute-start | bytes 1179656 | tf_op jit(solution)/shard_map/ppermute | solution.py:38
  28.7 18.2 %collective-permute-start.11 = (bf16[128,1536]{1,0:T(8,128)(2,1)S(1)}, bf16[128,1536]{1,0:T(8,128)(2,1)S(1)}, u32[]{:S(2)}, u32[]{:S(2)}) collective-permute-start(bf16[128,1536]{1,0:T(8,128)(2,1)S(1)} %pad_maximum_fusion.30), channel_id=1, source_target_pairs={{0,6},{2,4},{4,2},{6,0},{8,14},{10,12},{12,10},{14,8},{16,22},{18,... | collective-permute-start | bytes 1179656 | tf_op jit(solution)/shard_map/ppermute | solution.py:38
  31.4 16.8 %collective-permute-start.9 = (bf16[128,1536]{1,0:T(8,128)(2,1)S(1)}, bf16[128,1536]{1,0:T(8,128)(2,1)S(1)}, u32[]{:S(2)}, u32[]{:S(2)}) collective-permute-start(bf16[128,1536]{1,0:T(8,128)(2,1)S(1)} %pad_maximum_fusion.28), channel_id=1, source_target_pairs={{0,2},{2,0},{4,6},{6,4},{8,10},{10,8},{12,14},{14,12},{16,18},{18,... | collective-permute-start | bytes 1179656 | tf_op jit(solution)/shard_map/ppermute | solution.py:38
  49.8 330.2 %all-gather.15.cloned.1.call-start = ((), (), s32[]{:S(2)}) async-start(), calls=%async_computation.11 | async-start | bytes 2621440 | tf_op jit(solution)/shard_map/all_gather | solution.py:122
  66.5 22.4 %collective-permute-start.4 = (bf16[256,2048]{1,0:T(8,128)(2,1)S(1)}, bf16[256,2048]{1,0:T(8,128)(2,1)S(1)}, u32[]{:S(2)}, u32[]{:S(2)}) collective-permute-start(bf16[256,2048]{1,0:T(8,128)(2,1)S(1)} %fusion.32), channel_id=1, source_target_pairs={{0,2},{2,0},{4,6},{6,4},{8,10},{10,8},{12,14},{14,12},{16,18},{18,... | collective-permute-start | bytes 3145736 | tf_op jit(solution)/shard_map/ppermute | solution.py:38
  68.1 24.1 %collective-permute-start.5 = (bf16[256,2048]{1,0:T(8,128)(2,1)S(1)}, bf16[256,2048]{1,0:T(8,128)(2,1)S(1)}, u32[]{:S(2)}, u32[]{:S(2)}) collective-permute-start(bf16[256,2048]{1,0:T(8,128)(2,1)S(1)} %fusion.32), channel_id=1, source_target_pairs={{0,4},{2,6},{4,0},{6,2},{8,12},{10,14},{12,8},{14,10},{16,20},{18,... | collective-permute-start | bytes 3145736 | tf_op jit(solution)/shard_map/ppermute | solution.py:38
  252.5 26.3 %collective-permute-start.16 = (bf16[2,128,2048]{2,1,0:T(8,128)(2,1)}, bf16[2,128,2048]{2,1,0:T(8,128)(2,1)}, u32[]{:S(2)}, u32[]{:S(2)}) collective-permute-start(bf16[2,128,2048]{2,1,0:T(8,128)(2,1)} %pad_maximum_fusion.15), channel_id=1, source_target_pairs={{0,2},{2,0},{4,6},{6,4},{8,10},{10,8},{12,14},{14,12},{16,18},{18,... | collective-permute-start | bytes 3145736 | tf_op jit(solution)/shard_map/ppermute | solution.py:38
  254.0 26.4 %collective-permute-start.18 = (bf16[2,128,2048]{2,1,0:T(8,128)(2,1)}, bf16[2,128,2048]{2,1,0:T(8,128)(2,1)}, u32[]{:S(2)}, u32[]{:S(2)}) collective-permute-start(bf16[2,128,2048]{2,1,0:T(8,128)(2,1)} %stack.348), channel_id=1, source_target_pairs={{0,4},{2,6},{4,0},{6,2},{8,12},{10,14},{12,8},{14,10},{16,20},{18,... | collective-permute-start | bytes 3145736 | tf_op jit(solution)/shard_map/ppermute | solution.py:38
  256.7 44.5 %collective-permute-start.36 = (bf16[256,2048]{1,0:T(8,128)(2,1)}, bf16[256,2048]{1,0:T(8,128)(2,1)S(1)}, u32[]{:S(2)}, u32[]{:S(2)}) collective-permute-start(bf16[256,2048]{1,0:T(8,128)(2,1)} %fusion.51), channel_id=1, source_target_pairs={{0,2},{2,0},{4,6},{6,4},{8,10},{10,8},{12,14},{14,12},{16,18},{18,... | collective-permute-start | bytes 3145736 | tf_op jit(solution)/shard_map/ppermute | solution.py:38
  257.2 47.2 %collective-permute-start.37 = (bf16[256,2048]{1,0:T(8,128)(2,1)}, bf16[256,2048]{1,0:T(8,128)(2,1)}, u32[]{:S(2)}, u32[]{:S(2)}) collective-permute-start(bf16[256,2048]{1,0:T(8,128)(2,1)} %fusion.51), channel_id=1, source_target_pairs={{0,4},{2,6},{4,0},{6,2},{8,12},{10,14},{12,8},{14,10},{16,20},{18,... | collective-permute-start | bytes 3145736 | tf_op jit(solution)/shard_map/ppermute | solution.py:38
  259.3 70.5 %collective-permute-start.26 = (bf16[128,1024]{1,0:T(8,128)(2,1)}, bf16[128,1024]{1,0:T(8,128)(2,1)}, u32[]{:S(2)}, u32[]{:S(2)}) collective-permute-start(bf16[128,1024]{1,0:T(8,128)(2,1)} %pad_maximum_fusion.32), channel_id=1, source_target_pairs={{0,4},{2,6},{4,0},{6,2},{8,12},{10,14},{12,8},{14,10},{16,20},{18,... | collective-permute-start | bytes 786440 | tf_op jit(solution)/shard_map/ppermute | solution.py:38
  262.4 159.3 %all-gather.13.cloned.1.call-start = ((), (), s32[]{:S(2)}) async-start(), calls=%async_computation.10 | async-start | bytes 5242880 | tf_op jit(solution)/shard_map/all_gather | solution.py:122
  283.8 40.3 %collective-permute-start.17 = (bf16[128,2048]{1,0:T(8,128)(2,1)S(1)}, bf16[128,2048]{1,0:T(8,128)(2,1)S(1)}, u32[]{:S(2)}, u32[]{:S(2)}) collective-permute-start(bf16[128,2048]{1,0:T(8,128)(2,1)S(1)} %get-tuple-element.49), channel_id=1, source_target_pairs={{0,4},{2,6},{4,0},{6,2},{8,12},{10,14},{12,8},{14,10},{16,20},{18,... | collective-permute-start | bytes 1572872 | tf_op jit(solution)/shard_map/ppermute | solution.py:38
  285.3 40.2 %collective-permute-start.19 = (bf16[128,2048]{1,0:T(8,128)(2,1)S(1)}, bf16[128,2048]{1,0:T(8,128)(2,1)S(1)}, u32[]{:S(2)}, u32[]{:S(2)}) collective-permute-start(bf16[128,2048]{1,0:T(8,128)(2,1)S(1)} %get-tuple-element.50), channel_id=1, source_target_pairs={{0,2},{2,0},{4,6},{6,4},{8,10},{10,8},{12,14},{14,12},{16,18},{18,... | collective-permute-start | bytes 1572872 | tf_op jit(solution)/shard_map/ppermute | solution.py:38
  301.2 30.1 %collective-permute-start.27 = (bf16[128,1024]{1,0:T(8,128)(2,1)S(1)}, bf16[128,1024]{1,0:T(8,128)(2,1)S(1)}, u32[]{:S(2)}, u32[]{:S(2)}) collective-permute-start(bf16[128,1024]{1,0:T(8,128)(2,1)S(1)} %pad_maximum_fusion.33), channel_id=1, source_target_pairs={{0,6},{2,4},{4,2},{6,0},{8,14},{10,12},{12,10},{14,8},{16,22},{18,... | collective-permute-start | bytes 786440 | tf_op jit(solution)/shard_map/ppermute | solution.py:38
  304.4 27.4 %collective-permute-start.25 = (bf16[128,1024]{1,0:T(8,128)(2,1)S(1)}, bf16[128,1024]{1,0:T(8,128)(2,1)S(1)}, u32[]{:S(2)}, u32[]{:S(2)}) collective-permute-start(bf16[128,1024]{1,0:T(8,128)(2,1)S(1)} %copy-done.53), channel_id=1, source_target_pairs={{0,2},{2,0},{4,6},{6,4},{8,10},{10,8},{12,14},{14,12},{16,18},{18,... | collective-permute-start | bytes 786440 | tf_op jit(solution)/shard_map/ppermute | solution.py:38
  329.8 31.1 %collective-permute-start.20 = (bf16[256,2048]{1,0:T(8,128)(2,1)}, bf16[256,2048]{1,0:T(8,128)(2,1)}, u32[]{:S(2)}, u32[]{:S(2)}) collective-permute-start(bf16[256,2048]{1,0:T(8,128)(2,1)} %multiply_convert_fusion.7), channel_id=1, source_target_pairs={{0,2},{2,0},{4,6},{6,4},{8,10},{10,8},{12,14},{14,12},{16,18},{18,... | collective-permute-start | bytes 3145736 | tf_op jit(solution)/shard_map/ppermute | solution.py:38
  331.3 31.3 %collective-permute-start.21 = (bf16[256,2048]{1,0:T(8,128)(2,1)}, bf16[256,2048]{1,0:T(8,128)(2,1)}, u32[]{:S(2)}, u32[]{:S(2)}) collective-permute-start(bf16[256,2048]{1,0:T(8,128)(2,1)} %multiply_convert_fusion.7), channel_id=1, source_target_pairs={{0,4},{2,6},{4,0},{6,2},{8,12},{10,14},{12,8},{14,10},{16,20},{18,... | collective-permute-start | bytes 3145736 | tf_op jit(solution)/shard_map/ppermute | solution.py:38
  334.1 393.5 %reduce-scatter.11.cloned.1.call-start = ((), (), s32[]{:S(2)}) async-start(), calls=%async_computation.7 | async-start | bytes 2621440 | tf_op jit(solution)/shard_map/reduce_scatter | solution.py:250
  346.9 45.6 %collective-permute-start.40 = (bf16[4,256,2048]{2,1,0:T(8,128)(2,1)}, bf16[4,256,2048]{2,1,0:T(8,128)(2,1)}, u32[]{:S(2)}, u32[]{:S(2)}) collective-permute-start(bf16[4,256,2048]{2,1,0:T(8,128)(2,1)} %get-tuple-element.58), channel_id=1, source_target_pairs={{0,1},{1,0},{2,3},{3,2},{4,5},{5,4},{6,7},{7,6},{8,9},{9,8},{10,11... | collective-permute-start | bytes 12582920 | tf_op jit(solution)/shard_map/ppermute | solution.py:42
  380.0 27.1 %collective-permute-start.24 = (bf16[4,256,2048]{2,1,0:T(8,128)(2,1)}, bf16[4,256,2048]{2,1,0:T(8,128)(2,1)}, u32[]{:S(2)}, u32[]{:S(2)}) collective-permute-start(bf16[4,256,2048]{2,1,0:T(8,128)(2,1)} %get-tuple-element.62), channel_id=1, source_target_pairs={{0,1},{1,0},{2,3},{3,2},{4,5},{5,4},{6,7},{7,6},{8,9},{9,8},{10,11... | collective-permute-start | bytes 12582920 | tf_op jit(solution)/shard_map/ppermute | solution.py:42
  464.0 20.4 %collective-permute-start.41 = (bf16[4,256,2048]{2,1,0:T(8,128)(2,1)}, bf16[4,256,2048]{2,1,0:T(8,128)(2,1)}, u32[]{:S(2)}, u32[]{:S(2)}) collective-permute-start(bf16[4,256,2048]{2,1,0:T(8,128)(2,1)} %fusion.23), channel_id=1, source_target_pairs={{0,1},{1,0},{2,3},{3,2},{4,5},{5,4},{6,7},{7,6},{8,9},{9,8},{10,11... | collective-permute-start | bytes 12582920 | tf_op jit(solution)/shard_map/ppermute | solution.py:42
  509.4 26.3 %collective-permute-start.42 = (bf16[2,128,2048]{2,1,0:T(8,128)(2,1)}, bf16[2,128,2048]{2,1,0:T(8,128)(2,1)}, u32[]{:S(2)}, u32[]{:S(2)}) collective-permute-start(bf16[2,128,2048]{2,1,0:T(8,128)(2,1)} %pad_maximum_fusion.19), channel_id=1, source_target_pairs={{0,2},{2,0},{4,6},{6,4},{8,10},{10,8},{12,14},{14,12},{16,18},{18,... | collective-permute-start | bytes 3145736 | tf_op jit(solution)/shard_map/ppermute | solution.py:38
  509.9 27.4 %collective-permute-start.44 = (bf16[2,128,2048]{2,1,0:T(8,128)(2,1)}, bf16[2,128,2048]{2,1,0:T(8,128)(2,1)}, u32[]{:S(2)}, u32[]{:S(2)}) collective-permute-start(bf16[2,128,2048]{2,1,0:T(8,128)(2,1)} %stack.350), channel_id=1, source_target_pairs={{0,4},{2,6},{4,0},{6,2},{8,12},{10,14},{12,8},{14,10},{16,20},{18,... | collective-permute-start | bytes 3145736 | tf_op jit(solution)/shard_map/ppermute | solution.py:38
  512.5 45.7 %collective-permute-start.32 = (bf16[2,128,2048]{2,1,0:T(8,128)(2,1)}, bf16[2,128,2048]{2,1,0:T(8,128)(2,1)}, u32[]{:S(2)}, u32[]{:S(2)}) collective-permute-start(bf16[2,128,2048]{2,1,0:T(8,128)(2,1)} %pad_maximum_fusion.18), channel_id=1, source_target_pairs={{0,2},{2,0},{4,6},{6,4},{8,10},{10,8},{12,14},{14,12},{16,18},{18,... | collective-permute-start | bytes 3145736 | tf_op jit(solution)/shard_map/ppermute | solution.py:38
  514.0 45.7 %collective-permute-start.34 = (bf16[2,128,2048]{2,1,0:T(8,128)(2,1)}, bf16[2,128,2048]{2,1,0:T(8,128)(2,1)S(1)}, u32[]{:S(2)}, u32[]{:S(2)}) collective-permute-start(bf16[2,128,2048]{2,1,0:T(8,128)(2,1)} %stack.349), channel_id=1, source_target_pairs={{0,4},{2,6},{4,0},{6,2},{8,12},{10,14},{12,8},{14,10},{16,20},{18,... | collective-permute-start | bytes 3145736 | tf_op jit(solution)/shard_map/ppermute | solution.py:38
  524.2 213.6 %reduce-scatter.9.cloned.1.call-start = ((), (), s32[]{:S(2)}) async-start(), calls=%async_computation.6 | async-start | bytes 5242880 | tf_op jit(solution)/shard_map/reduce_scatter | solution.py:250
  540.9 29.0 %collective-permute-start.43 = (bf16[128,2048]{1,0:T(8,128)(2,1)S(1)}, bf16[128,2048]{1,0:T(8,128)(2,1)S(1)}, u32[]{:S(2)}, u32[]{:S(2)}) collective-permute-start(bf16[128,2048]{1,0:T(8,128)(2,1)S(1)} %get-tuple-element.40), channel_id=1, source_target_pairs={{0,4},{2,6},{4,0},{6,2},{8,12},{10,14},{12,8},{14,10},{16,20},{18,... | collective-permute-start | bytes 1572872 | tf_op jit(solution)/shard_map/ppermute | solution.py:38
  542.4 27.5 %collective-permute-start.45 = (bf16[128,2048]{1,0:T(8,128)(2,1)S(1)}, bf16[128,2048]{1,0:T(8,128)(2,1)S(1)}, u32[]{:S(2)}, u32[]{:S(2)}) collective-permute-start(bf16[128,2048]{1,0:T(8,128)(2,1)S(1)} %get-tuple-element.41), channel_id=1, source_target_pairs={{0,2},{2,0},{4,6},{6,4},{8,10},{10,8},{12,14},{14,12},{16,18},{18,... | collective-permute-start | bytes 1572872 | tf_op jit(solution)/shard_map/ppermute | solution.py:38
  560.3 19.6 %collective-permute-start.33 = (bf16[128,2048]{1,0:T(8,128)(2,1)S(1)}, bf16[128,2048]{1,0:T(8,128)(2,1)S(1)}, u32[]{:S(2)}, u32[]{:S(2)}) collective-permute-start(bf16[128,2048]{1,0:T(8,128)(2,1)S(1)} %get-tuple-element.45), channel_id=1, source_target_pairs={{0,4},{2,6},{4,0},{6,2},{8,12},{10,14},{12,8},{14,10},{16,20},{18,... | collective-permute-start | bytes 1572872 | tf_op jit(solution)/shard_map/ppermute | solution.py:38
  561.8 18.1 %collective-permute-start.35 = (bf16[128,2048]{1,0:T(8,128)(2,1)S(1)}, bf16[128,2048]{1,0:T(8,128)(2,1)S(1)}, u32[]{:S(2)}, u32[]{:S(2)}) collective-permute-start(bf16[128,2048]{1,0:T(8,128)(2,1)S(1)} %get-tuple-element.46), channel_id=1, source_target_pairs={{0,2},{2,0},{4,6},{6,4},{8,10},{10,8},{12,14},{14,12},{16,18},{18,... | collective-permute-start | bytes 1572872 | tf_op jit(solution)/shard_map/ppermute | solution.py:38
  583.9 23.9 %collective-permute-start.47 = (bf16[256,2048]{1,0:T(8,128)(2,1)S(1)}, bf16[256,2048]{1,0:T(8,128)(2,1)S(1)}, u32[]{:S(2)}, u32[]{:S(2)}) collective-permute-start(bf16[256,2048]{1,0:T(8,128)(2,1)S(1)} %get-tuple-element.18), channel_id=1, source_target_pairs={{0,4},{2,6},{4,0},{6,2},{8,12},{10,14},{12,8},{14,10},{16,20},{18,... | collective-permute-start | bytes 3145736 | tf_op jit(solution)/shard_map/ppermute | solution.py:38
  585.3 24.7 %collective-permute-start.46 = (bf16[256,2048]{1,0:T(8,128)(2,1)S(1)}, bf16[256,2048]{1,0:T(8,128)(2,1)S(1)}, u32[]{:S(2)}, u32[]{:S(2)}) collective-permute-start(bf16[256,2048]{1,0:T(8,128)(2,1)S(1)} %get-tuple-element.18), channel_id=1, source_target_pairs={{0,2},{2,0},{4,6},{6,4},{8,10},{10,8},{12,14},{14,12},{16,18},{18,... | collective-permute-start | bytes 3145736 | tf_op jit(solution)/shard_map/ppermute | solution.py:38
  608.6 16.1 %collective-permute-start.49 = (bf16[128,2048]{1,0:T(8,128)(2,1)}, bf16[128,2048]{1,0:T(8,128)(2,1)}, u32[]{:S(2)}, u32[]{:S(2)}) collective-permute-start(bf16[128,2048]{1,0:T(8,128)(2,1)} %slice.486), channel_id=1, source_target_pairs={{0,2},{2,0},{4,6},{6,4},{8,10},{10,8},{12,14},{14,12},{16,18},{18,... | collective-permute-start | bytes 1572872 | tf_op jit(solution)/shard_map/ppermute | solution.py:38
  624.5 173.3 %reduce-scatter.7.cloned.1.call-start = ((), (), s32[]{:S(2)}) async-start(), calls=%async_computation.5 | async-start | bytes 2621440 | tf_op jit(solution)/shard_map/reduce_scatter | solution.py:250
  670.9 186.4 %reduce-scatter.5.cloned.1.call-start = ((), (), s32[]{:S(2)}) async-start(), calls=%async_computation.4 | async-start | bytes 7864320 | tf_op jit(solution)/shard_map/reduce_scatter | solution.py:250
  727.5 26.3 %collective-permute-start.51 = (bf16[4,256,2048]{2,1,0:T(8,128)(2,1)}, bf16[4,256,2048]{2,1,0:T(8,128)(2,1)}, u32[]{:S(2)}, u32[]{:S(2)}) collective-permute-start(bf16[4,256,2048]{2,1,0:T(8,128)(2,1)} %fusion.24), channel_id=1, source_target_pairs={{0,1},{1,0},{2,3},{3,2},{4,5},{5,4},{6,7},{7,6},{8,9},{9,8},{10,11... | collective-permute-start | bytes 12582920 | tf_op jit(solution)/shard_map/ppermute | solution.py:42
  764.4 24.9 %collective-permute-start.52 = (bf16[2,128,2048]{2,1,0:T(8,128)(2,1)S(1)}, bf16[2,128,2048]{2,1,0:T(8,128)(2,1)S(1)}, u32[]{:S(2)}, u32[]{:S(2)}) collective-permute-start(bf16[2,128,2048]{2,1,0:T(8,128)(2,1)S(1)} %pad_maximum_fusion.20), channel_id=1, source_target_pairs={{0,2},{2,0},{4,6},{6,4},{8,10},{10,8},{12,14},{14,12},{16,18},{18,... | collective-permute-start | bytes 3145736 | tf_op jit(solution)/shard_map/ppermute | solution.py:38
  765.9 24.8 %collective-permute-start.54 = (bf16[2,128,2048]{2,1,0:T(8,128)(2,1)S(1)}, bf16[2,128,2048]{2,1,0:T(8,128)(2,1)S(1)}, u32[]{:S(2)}, u32[]{:S(2)}) collective-permute-start(bf16[2,128,2048]{2,1,0:T(8,128)(2,1)S(1)} %stack.351), channel_id=1, source_target_pairs={{0,4},{2,6},{4,0},{6,2},{8,12},{10,14},{12,8},{14,10},{16,20},{18,... | collective-permute-start | bytes 3145736 | tf_op jit(solution)/shard_map/ppermute | solution.py:38
  793.6 15.7 %collective-permute-start.53 = (bf16[128,2048]{1,0:T(8,128)(2,1)S(1)}, bf16[128,2048]{1,0:T(8,128)(2,1)S(1)}, u32[]{:S(2)}, u32[]{:S(2)}) collective-permute-start(bf16[128,2048]{1,0:T(8,128)(2,1)S(1)} %get-tuple-element.36), channel_id=1, source_target_pairs={{0,4},{2,6},{4,0},{6,2},{8,12},{10,14},{12,8},{14,10},{16,20},{18,... | collective-permute-start | bytes 1572872 | tf_op jit(solution)/shard_map/ppermute | solution.py:38
  799.7 18.1 %collective-permute-start.61 = (bf16[512,128]{1,0:T(8,128)(2,1)}, bf16[512,128]{1,0:T(8,128)(2,1)S(1)}, u32[]{:S(2)}, u32[]{:S(2)}) collective-permute-start(bf16[512,128]{1,0:T(8,128)(2,1)} %get-tuple-element.107), channel_id=1, source_target_pairs={{0,6},{2,4},{4,2},{6,0},{8,14},{10,12},{12,10},{14,8},{16,22},{18,... | collective-permute-start | bytes 393224 | tf_op jit(solution)/shard_map/ppermute | solution.py:38
  801.3 16.6 %collective-permute-start.60 = (bf16[512,128]{1,0:T(8,128)(2,1)}, bf16[512,128]{1,0:T(8,128)(2,1)}, u32[]{:S(2)}, u32[]{:S(2)}) collective-permute-start(bf16[512,128]{1,0:T(8,128)(2,1)} %get-tuple-element.108), channel_id=1, source_target_pairs={{0,4},{2,6},{4,0},{6,2},{8,12},{10,14},{12,8},{14,10},{16,20},{18,... | collective-permute-start | bytes 393224 | tf_op jit(solution)/shard_map/ppermute | solution.py:38
  802.2 15.7 %collective-permute-start.59 = (bf16[512,128]{1,0:T(8,128)(2,1)S(1)}, bf16[512,128]{1,0:T(8,128)(2,1)}, u32[]{:S(2)}, u32[]{:S(2)}) collective-permute-start(bf16[512,128]{1,0:T(8,128)(2,1)S(1)} %get-tuple-element.109), channel_id=1, source_target_pairs={{0,2},{2,0},{4,6},{6,4},{8,10},{10,8},{12,14},{14,12},{16,18},{18,... | collective-permute-start | bytes 393224 | tf_op jit(solution)/shard_map/ppermute | solution.py:38
  837.5 26.7 %collective-permute-start.72 = (f32[2,64]{1,0:T(2,128)S(1)}, f32[2,64]{1,0:T(2,128)S(1)}, u32[]{:S(2)}, u32[]{:S(2)}) collective-permute-start(f32[2,64]{1,0:T(2,128)S(1)} %bitcast.437), channel_id=1, source_target_pairs={{0,1},{1,0},{2,3},{3,2},{4,5},{5,4},{6,7},{7,6},{8,9},{9,8},{10,11... | collective-permute-start | bytes 1544 | tf_op jit(solution)/shard_map/ppermute | solution.py:42
  861.4 17.9 %collective-permute-start.57 = (bf16[128,1536]{1,0:T(8,128)(2,1)S(1)}, bf16[128,1536]{1,0:T(8,128)(2,1)S(1)}, u32[]{:S(2)}, u32[]{:S(2)}) collective-permute-start(bf16[128,1536]{1,0:T(8,128)(2,1)S(1)} %get-tuple-element.76), channel_id=1, source_target_pairs={{0,4},{2,6},{4,0},{6,2},{8,12},{10,14},{12,8},{14,10},{16,20},{18,... | collective-permute-start | bytes 1179656 | tf_op jit(solution)/shard_map/ppermute | solution.py:38
  861.9 17.4 %collective-permute-start.56 = (bf16[128,1536]{1,0:T(8,128)(2,1)S(1)}, bf16[128,1536]{1,0:T(8,128)(2,1)S(1)}, u32[]{:S(2)}, u32[]{:S(2)}) collective-permute-start(bf16[128,1536]{1,0:T(8,128)(2,1)S(1)} %get-tuple-element.77), channel_id=1, source_target_pairs={{0,2},{2,0},{4,6},{6,4},{8,10},{10,8},{12,14},{14,12},{16,18},{18,... | collective-permute-start | bytes 1179656 | tf_op jit(solution)/shard_map/ppermute | solution.py:38
  (112 other events, 1194.5 us)
Sparse Core Ops, SparseCore 0:
  28.0 46.3 all-gather.10
  76.0 114.0 all-gather.8
  262.5 43.2 all-gather.14
  334.2 78.0 all-gather.12
  524.3 41.1 reduce-scatter.10
  624.6 73.1 reduce-scatter.8
  700.1 44.3 reduce-scatter.6
  746.9 110.3 reduce-scatter.4

commit v2 on v1

v2 whole, which is shorter than its diff:
```python
import functools

import jax
import jax.numpy as jnp
from jax import lax
from jax.experimental import pallas as pl
from jax.experimental.pallas import tpu as pltpu
from jax.sharding import PartitionSpec as P

DK = 256
DV = 512
PLANE = 4
VMEM_BYTES = 56 * 1024 * 1024

norm_eps = 1e-06
group_floor = 1.0
tanh_scale = 0.7978845608028654
tanh_cubic = 0.044715

bf16 = jnp.bfloat16
f32 = jnp.float32


def shaped(shape, kind):
    return jax.ShapeDtypeStruct(shape, kind)


def cost(flops, bytes_accessed):
    return pl.CostEstimate(flops=int(flops), bytes_accessed=int(bytes_accessed), transcendentals=0)


def params():
    return pltpu.CompilerParams(vmem_limit_bytes=VMEM_BYTES)


ANY = pl.BlockSpec(memory_space=pl.ANY)


def whole(shape):
    return pl.BlockSpec(shape, lambda i: (0,) * len(shape), pipeline_mode=pl.Buffered(1))


def by_slot(*shape):
    return pl.BlockSpec(shape, lambda i: (i,) + (0,) * (len(shape) - 1))


def dot(left, right):
    return jnp.dot(left, right, preferred_element_type=f32)


def dot_nt(left, right):
    return lax.dot_general(left, right, (((1,), (1,)), ((), ())), preferred_element_type=f32)


def dot_tn(left, right):
    return lax.dot_general(left, right, (((0,), (0,)), ((), ())), preferred_element_type=f32)


def decay_table(positions, head):
    spacing = positions[:, None] - positions[None, :]
    log_rate = jnp.log1p(-jnp.exp2(-5.0 - head.astype(f32)))
    kept_spacing = jnp.where(spacing >= 0, spacing, jnp.zeros_like(spacing)).astype(f32)
    powers = jnp.exp(kept_spacing * log_rate)
    return jnp.where(spacing >= 0, powers, jnp.zeros_like(powers))


def copy_kernel(plan, n_in, me_ref, *refs):
    ins, outs, sem = refs[:n_in], refs[n_in:-1], refs[-1]
    copies = [
        pltpu.make_async_copy(source, target, sem.at[i])
        for i, (source, target) in enumerate(plan(me_ref[0], ins, outs))
    ]
    for one in copies:
        one.start()
    for one in copies:
        one.wait()


def place_copies(plan, n_copies, me, ins, out_shapes):
    moved = 2 * sum(2 * s.size for s in out_shapes)
    return pl.pallas_call(
        functools.partial(copy_kernel, plan, len(ins)),
        in_specs=[pl.BlockSpec(memory_space=pltpu.SMEM)] + [pl.BlockSpec(memory_space=pltpu.VMEM)] * len(ins),
        out_specs=[ANY] * len(out_shapes),
        out_shape=out_shapes,
        scratch_shapes=[pltpu.SemaphoreType.DMA((n_copies,))],
        compiler_params=params(),
        cost_estimate=cost(0, moved),
    )(me, *ins)


def lanes(index, size):
    return pl.ds(pl.multiple_of(index * size, size), size)


def cut_columns(me, weights):
    rows = weights[0].shape[0]
    parts = [w.shape[1] // PLANE for w in weights]

    def plan(place, ins, outs):
        copies = []
        for k in range(PLANE):
            at = 0
            for w, part in zip(ins, parts):
                copies.append((w.at[:, lanes(place ^ k, part)], outs[k].at[:, pl.ds(at, part)]))
                at += part
        return copies

    shapes = [shaped((rows, sum(parts)), bf16)] * PLANE
    return place_copies(plan, PLANE * len(parts), me, weights, shapes)


def cut_rows(me, weight):
    depth = weight.shape[0] // PLANE
    place = me[0]
    return [lax.dynamic_slice_in_dim(weight, (place ^ k) * depth, depth, 0) for k in range(PLANE)]


def in_order(blocks, place, axis):
    stacked = jnp.stack(blocks)
    return jnp.concatenate(
        [lax.dynamic_index_in_dim(stacked, place ^ j, 0, keepdims=False) for j in range(PLANE)], axis
    )


def join_weights(me, column_blocks, row_blocks):
    rows, width = column_blocks[0].shape if column_blocks else (row_blocks[0].shape[1], 0)
    tall = PLANE * rows
    if not row_blocks:
        groups, extra = 0, []
    else:
        inner, cols = row_blocks[0].shape
        groups = inner // tall
        aligned = cols % 128 == 0
        extra = row_blocks if aligned else [in_order(row_blocks, me[0], 1)]

    def plan(place, ins, outs):
        copies = []
        for k in range(PLANE):
            if column_blocks:
                copies.append((ins[k], outs[0].at[lanes(place ^ k, rows), pl.ds(0, width)]))
        for k, block in enumerate(ins[len(column_blocks) :]):
            for g in range(groups):
                at = width + g * tall
                if aligned:
                    spot = pl.ds(pl.multiple_of(at + (place ^ k) * cols, cols), cols)
                else:
                    spot = pl.ds(at, tall)
                copies.append((block.at[pl.ds(g * tall, tall)], outs[0].at[:, spot]))
        return copies

    n_copies = len(column_blocks) + len(extra) * groups
    shape = shaped((tall, width + groups * tall), bf16)
    return place_copies(plan, n_copies, me, [*column_blocks, *extra], [shape])[0]


def load_pieces(pieces, held, sem):
    step = pl.program_id(0)
    rows = pieces[0].shape[0]
    copies = [
        pltpu.make_async_copy(piece, held.at[i // 2, pl.ds((i % 2) * rows, rows)], sem.at[i])
        for i, piece in enumerate(pieces)
    ]

    @pl.when(step == 0)
    def start():
        for one in copies:
            one.start()

    for s in range(len(pieces) // 2):

        @pl.when(step == s)
        def arrive(s=s):
            copies[2 * s].wait()
            copies[2 * s + 1].wait()

    return held[step]


def retain_kernel(*refs):
    pieces, (weights, decays) = refs[:8], refs[8:10]
    query_ref, key_ref, value_ref, scores_ref, retained_ref, rows_ref = refs[10:16]
    held, sem, out_sem = refs[16:]
    rows = load_pieces(pieces, held, sem)
    step = pl.program_id(0)
    slot_len = rows.shape[0]
    keep = pltpu.make_async_copy(held.at[step], rows_ref.at[pl.ds(step * slot_len, slot_len)], out_sem)
    keep.start()
    dk, dv = query_ref.shape[1], value_ref.shape[1]
    query_key = dot(rows, weights[:, : 2 * dk]).astype(bf16)
    query, key = query_key[:, :dk], query_key[:, dk:]
    query_ref[...] = query
    key_ref[...] = key
    scores = (dot_nt(query, key) * decays[...]).astype(bf16)
    scores_ref[...] = scores[None]
    value = dot(rows, weights[:, 2 * dk : 2 * dk + dv]).astype(bf16)
    value_ref[...] = value
    retained_ref[...] = dot(scores, value)
    keep.wait()


def retain(pieces, weights, decays, dk, dv):
    rows, width = pieces[0].shape
    slot_len = 2 * rows
    total = PLANE * slot_len
    return pl.pallas_call(
        retain_kernel,
        grid=(PLANE,),
        in_specs=[ANY] * 8 + [whole((width, 2 * dk + dv)), whole((slot_len, slot_len))],
        out_specs=[
            by_slot(slot_len, dk),
            by_slot(slot_len, dk),
            by_slot(slot_len, dv),
            by_slot(1, slot_len, slot_len),
            by_slot(slot_len, dv),
            ANY,
        ],
        out_shape=[
            shaped((total, dk), bf16),
            shaped((total, dk), bf16),
            shaped((total, dv), bf16),
            shaped((PLANE, slot_len, slot_len), bf16),
            shaped((total, dv), f32),
            shaped((total, width), bf16),
        ],
        scratch_shapes=[
            pltpu.VMEM((PLANE, slot_len, width), bf16),
            pltpu.SemaphoreType.DMA((8,)),
            pltpu.SemaphoreType.DMA,
        ],
        compiler_params=params(),
        cost_estimate=cost(2.2 * total * width * (2 * dk + dv), 30e6),
    )(*pieces, weights, decays)


def times_rows(left, right, wide):
    groups = right.shape[1] // wide
    for z in range(right.shape[0] // wide):
        terms = dot(left[:, :wide], right[z * wide : (z + 1) * wide, :wide])
        for g in range(1, groups):
            terms += dot(
                left[:, g * wide : (g + 1) * wide],
                right[z * wide : (z + 1) * wide, g * wide : (g + 1) * wide],
            )
        yield slice(z * wide, (z + 1) * wide), terms


def times_rows_back(left, right, wide):
    made = []
    for g in range(right.shape[1] // wide):
        group = slice(g * wide, (g + 1) * wide)
        terms = dot_nt(left[:, :wide], right[:wide, group])
        for z in range(1, right.shape[0] // wide):
            block = slice(z * wide, (z + 1) * wide)
            terms += dot_nt(left[:, block], right[block, group])
        made.append(terms)
    return made[0] if len(made) == 1 else jnp.concatenate(made, axis=1)


def split_out(terms, near_ref, far_ref, columns):
    rows = near_ref.shape[1]
    near_ref[0, :, columns] = terms[:rows]
    far_ref[0, :, columns] = terms[rows:].astype(bf16)


def gate_out_kernel(wide, rows_ref, weights, out_weights, retained_ref, gate_ref, gated_ref, near_ref, far_ref):
    retained = retained_ref[...]
    scale = lax.rsqrt(jnp.mean(retained * retained, axis=-1, keepdims=True) + group_floor)
    gate = dot(rows_ref[...], weights[...])
    gate_ref[...] = gate
    gated_ref[...] = (gate * jax.nn.sigmoid(gate) * (retained * scale)).astype(bf16)
    for columns, terms in times_rows(gated_ref[...], out_weights[...], wide):
        split_out(terms, near_ref, far_ref, columns)


def gate_out(rows_all, joined, retained, wide):
    total, width = rows_all.shape
    dv = retained.shape[1]
    slot_len = total // PLANE
    rows = slot_len // 2
    return pl.pallas_call(
        functools.partial(gate_out_kernel, wide),
        grid=(PLANE,),
        in_specs=[
            by_slot(slot_len, width),
            pl.BlockSpec((width, dv), lambda i: (0, 2), pipeline_mode=pl.Buffered(1)),
            pl.BlockSpec((width, dv), lambda i: (0, 3), pipeline_mode=pl.Buffered(1)),
            by_slot(slot_len, dv),
        ],
        out_specs=[by_slot(slot_len, dv), by_slot(slot_len, dv), by_slot(1, rows, width), by_slot(1, rows, width)],
        out_shape=[
            shaped((total, dv), f32),
            shaped((total, dv), bf16),
            shaped((PLANE, rows, width), f32),
            shaped((PLANE, rows, width), bf16),
        ],
        compiler_params=params(),
        cost_estimate=cost(4 * total * width * dv, 40e6),
    )(rows_all, joined, joined, retained)


def project_kernel(wide, left, right, near_ref, far_ref):
    for columns, terms in times_rows(left[...], right[...], wide):
        split_out(terms, near_ref, far_ref, columns)


def project(left, right, wide):
    total, inner = left.shape
    width = right.shape[0]
    slot_len = total // PLANE
    rows = slot_len // 2
    return pl.pallas_call(
        functools.partial(project_kernel, wide),
        grid=(PLANE,),
        in_specs=[by_slot(slot_len, inner), whole(right.shape)],
        out_specs=[by_slot(1, rows, width)] * 2,
        out_shape=[shaped((PLANE, rows, width), f32), shaped((PLANE, rows, width), bf16)],
        compiler_params=params(),
        cost_estimate=cost(2 * total * inner * width, 20e6),
    )(left, right)


def back_kernel(left, first, second, near_ref, far_ref):
    dv = second.shape[1]
    narrow = first.shape[1] - dv
    terms = dot_nt(left[:, :dv], first[:, narrow:]) + dot_nt(left[:, dv : 2 * dv], second[...])
    terms += dot_nt(left[:, 2 * dv :], first[:, :narrow])
    split_out(terms, near_ref, far_ref, slice(None))


def project_back(left, joined, dk, dv):
    total, inner = left.shape
    width = joined.shape[0]
    slot_len = total // PLANE
    rows = slot_len // 2
    return pl.pallas_call(
        back_kernel,
        grid=(PLANE,),
        in_specs=[
            by_slot(slot_len, inner),
            whole((width, 2 * dk + dv)),
            pl.BlockSpec((width, dv), lambda i: (0, 2), pipeline_mode=pl.Buffered(1)),
        ],
        out_specs=[by_slot(1, rows, width)] * 2,
        out_shape=[shaped((PLANE, rows, width), f32), shaped((PLANE, rows, width), bf16)],
        compiler_params=params(),
        cost_estimate=cost(2 * total * inner * width, 20e6),
    )(left, joined, joined)


def fold_kernel(spots, n, *refs):
    nears, arriveds = refs[:n], refs[n : 2 * n]
    x_ref, y_ref, keep_x_ref, keep_y_ref = refs[2 * n :]
    half = x_ref.shape[1]

    def summed(k, lo):
        i, j = spots[k]
        return nears[i][j, lo : lo + half] + arriveds[i][j, lo : lo + half].astype(f32)

    x_ref[0] = summed(1, 0).astype(bf16)
    x_ref[1] = summed(3, 0).astype(bf16)
    y_ref[0] = summed(2, half).astype(bf16)
    y_ref[1] = summed(3, half).astype(bf16)
    keep_x_ref[...] = summed(1, half)
    keep_y_ref[...] = summed(2, 0)


def fold_cut(nears, arriveds):
    spots = [(i, j) for i, near in enumerate(nears) for j in range(near.shape[0])]
    _, rows, width = nears[0].shape
    half = rows // 2
    part = width // 4

    def cols(*shape):
        return pl.BlockSpec((*shape, part), lambda i: (0,) * len(shape) + (i,))

    given = [cols(near.shape[0], rows) for near in nears]
    return pl.pallas_call(
        functools.partial(fold_kernel, spots, len(nears)),
        grid=(width // part,),
        in_specs=given + given,
        out_specs=[cols(2, half), cols(2, half), cols(half), cols(half)],
        out_shape=[
            shaped((2, half, width), bf16),
            shaped((2, half, width), bf16),
            shaped((half, width), f32),
            shaped((half, width), f32),
        ],
        compiler_params=params(),
        cost_estimate=cost(1e6, 20e6),
    )(*nears, *arriveds)


def dot_back_kernel(wide, back, right, out_ref):
    out_ref[...] = times_rows_back(back[...], right[...], wide)


def dot_back(back, joined, inner, start, wide):
    total, width = back.shape
    slot_len = total // PLANE
    return pl.pallas_call(
        functools.partial(dot_back_kernel, wide),
        grid=(PLANE,),
        in_specs=[
            by_slot(slot_len, width),
            pl.BlockSpec((width, inner), lambda i: (0, start // inner), pipeline_mode=pl.Buffered(1)),
        ],
        out_specs=by_slot(slot_len, inner),
        out_shape=shaped((total, inner), f32),
        compiler_params=params(),
        cost_estimate=cost(2 * total * width * inner, 20e6),
    )(back, joined)


def hidden_kernel(first, n, n_kept, *refs):
    pieces, (weights, grad_in) = refs[: 2 * n], refs[2 * n : 2 * n + 2]
    act_ref, grad_ref, rows_ref, near_ref, far_ref = refs[2 * n + 2 + n_kept : 2 * n + 7 + n_kept]
    held, sem, out_sem = refs[2 * n + 7 + n_kept :]
    rows = load_pieces(pieces, held, sem)
    step = pl.program_id(0)
    slot_len = rows.shape[0]
    inner = act_ref.shape[1]
    keep = pltpu.make_async_copy(
        held.at[step], rows_ref.at[pl.ds((step + first) * slot_len, slot_len)], out_sem
    )
    keep.start()
    weights = weights[...]
    up = dot(rows, weights[:, :inner])
    value = dot(rows, weights[:, inner:])
    slope = jnp.tanh(tanh_scale * (up + tanh_cubic * (up * up * up)))
    gelu = 0.5 * up * (1.0 + slope)
    act_ref[...] = (gelu * value).astype(bf16)
    rise = 0.5 * (1.0 + slope) + 0.5 * up * (1.0 - slope * slope) * (
        tanh_scale * (1.0 + 3.0 * tanh_cubic * (up * up))
    )
    grad = grad_in[...]
    grad_ref[:, :inner] = (grad * value * rise).astype(bf16)
    grad_ref[:, inner:] = (grad * gelu).astype(bf16)
    split_out(dot_nt(grad_ref[...], weights), near_ref, far_ref, slice(None))
    keep.wait()


def hidden_units(first, pieces, joined, grad_in, kept):
    n = len(pieces) // 2
    rows, width = pieces[0].shape
    slot_len = 2 * rows
    total, inner = grad_in.shape

    def at(cols):
        return pl.BlockSpec((slot_len, cols), lambda i: (i + first, 0))

    return pl.pallas_call(
        functools.partial(hidden_kernel, first, n, len(kept)),
        grid=(n,),
        in_specs=[ANY] * (2 * n)
        + [pl.BlockSpec((width, 2 * inner), lambda i: (0, 0), pipeline_mode=pl.Buffered(1)), at(inner)]
        + [ANY] * len(kept),
        out_specs=[at(inner), at(2 * inner), ANY, by_slot(1, rows, width), by_slot(1, rows, width)],
        out_shape=[
            shaped((total, inner), bf16),
            shaped((total, 2 * inner), bf16),
            shaped((total, width), bf16),
            shaped((n, rows, width), f32),
            shaped((n, rows, width), bf16),
        ],
        scratch_shapes=[
            pltpu.VMEM((n, slot_len, width), bf16),
            pltpu.SemaphoreType.DMA((2 * n,)),
            pltpu.SemaphoreType.DMA,
        ],
        input_output_aliases={2 * n + 2 + i: i for i in range(len(kept))},
        compiler_params=params(),
        cost_estimate=cost(8 * n * slot_len * width * inner, 15e6),
    )(*pieces, joined, grad_in, *kept)


def retain_back_kernel(first, wide, n, n_kept, *refs):
    pieces = refs[: 2 * n]
    out_weights, decays, query, key, value, gate_ref, scores, retained_ref = refs[2 * n : 2 * n + 8]
    grad_ref, rows_ref = refs[2 * n + 8 + n_kept : 2 * n + 10 + n_kept]
    held, sem, out_sem = refs[2 * n + 10 + n_kept :]
    rows = load_pieces(pieces, held, sem)
    step = pl.program_id(0)
    slot_len = rows.shape[0]
    keep = pltpu.make_async_copy(
        held.at[step], rows_ref.at[pl.ds((step + first) * slot_len, slot_len)], out_sem
    )
    keep.start()
    dk, dv = query.shape[1], value.shape[1]
    grad = times_rows_back(rows, out_weights[...], wide)
    retained, gate = retained_ref[...], gate_ref[...]
    scale = lax.rsqrt(jnp.mean(retained * retained, axis=-1, keepdims=True) + group_floor)
    sigma = jax.nn.sigmoid(gate)
    normed = retained * scale
    grad_ref[:, dv : 2 * dv] = (grad * normed * (sigma * (1.0 + gate * (1.0 - sigma)))).astype(bf16)
    grad = grad * (gate * sigma)
    mean = jnp.mean(normed * grad, axis=-1, keepdims=True)
    grad_retained = (scale * (grad - normed * mean)).astype(bf16)
    grad_scores = (dot_nt(grad_retained, value[...]) * decays[...]).astype(bf16)
    grad_ref[:, :dv] = dot_tn(scores[0], grad_retained).astype(bf16)
    grad_ref[:, 2 * dv : 2 * dv + dk] = dot(grad_scores, key[...]).astype(bf16)
    grad_ref[:, 2 * dv + dk :] = dot_tn(grad_scores, query[...]).astype(bf16)
    keep.wait()


def retain_back(first, pieces, joined, decays, query, key, value, gate, scores, retained, kept, wide):
    n = len(pieces) // 2
    rows, width = pieces[0].shape
    slot_len = 2 * rows
    total, dk = query.shape
    dv = value.shape[1]

    def at(cols):
        return pl.BlockSpec((slot_len, cols), lambda i: (i + first, 0))

    return pl.pallas_call(
        functools.partial(retain_back_kernel, first, wide, n, len(kept)),
        grid=(n,),
        in_specs=[ANY] * (2 * n)
        + [
            pl.BlockSpec((width, dv), lambda i: (0, 3), pipeline_mode=pl.Buffered(1)),
            whole((slot_len, slot_len)),
            at(dk),
            at(dk),
            at(dv),
            at(dv),
            pl.BlockSpec((1, slot_len, slot_len), lambda i: (i + first, 0, 0)),
            at(dv),
        ]
        + [ANY] * len(kept),
        out_specs=[at(2 * dk + 2 * dv), ANY],
        out_shape=[shaped((total, 2 * dk + 2 * dv), bf16), shaped((total, width), bf16)],
        scratch_shapes=[
            pltpu.VMEM((n, slot_len, width), bf16),
            pltpu.SemaphoreType.DMA((2 * n,)),
            pltpu.SemaphoreType.DMA,
        ],
        input_output_aliases={2 * n + 8 + i: i for i in range(len(kept))},
        compiler_params=params(),
        cost_estimate=cost(4 * n * slot_len * width * dv, 15e6),
    )(*pieces, joined, decays, query, key, value, gate, scores, retained, *kept)


def grad_kernel(left, right, grad_ref):
    grad_ref[...] = dot_tn(left[...], right[...]).astype(bf16)


def columns_grad(left, right, block, cols):
    total, width = left.shape
    part = width // 4
    return pl.pallas_call(
        grad_kernel,
        grid=(width // part,),
        in_specs=[
            pl.BlockSpec((total, part), lambda i: (0, i)),
            pl.BlockSpec((total, cols), lambda i: (0, block), pipeline_mode=pl.Buffered(1)),
        ],
        out_specs=by_slot(part, cols),
        out_shape=shaped((width, cols), bf16),
        compiler_params=params(),
        cost_estimate=cost(2 * total * width * cols, 20e6),
    )(left, right)


def rows_grad(left, right, wide):
    total, inner = left.shape
    blocks = right.shape[1] // wide
    return pl.pallas_call(
        grad_kernel,
        grid=(blocks,),
        in_specs=[whole((total, inner)), pl.BlockSpec((total, wide), lambda i: (0, i))],
        out_specs=by_slot(inner, wide),
        out_shape=shaped((blocks * inner, wide), bf16),
        compiler_params=params(),
        cost_estimate=cost(2 * total * inner * wide * blocks, 20e6),
    )(left, right)


def place_grads_kernel(n, me_ref, *refs):
    ins, outs, held, sem = refs[:PLANE], refs[PLANE : PLANE + n], refs[-2], refs[-1]
    place = me_ref[0]
    copies = []
    for k in range(PLANE):
        held[k] = ins[k][...].astype(f32)
        at = 0
        for i, out in enumerate(outs):
            part = out.shape[1] // PLANE
            one = pltpu.make_async_copy(
                held.at[k, :, pl.ds(at, part)], out.at[:, lanes(place ^ k, part)], sem.at[k * n + i]
            )
            one.start()
            copies.append(one)
            at += part
    for one in copies:
        one.wait()


def place_columns(me, blocks, widths):
    rows = blocks[0].shape[0]
    n = len(widths)
    return pl.pallas_call(
        functools.partial(place_grads_kernel, n),
        in_specs=[pl.BlockSpec(memory_space=pltpu.SMEM)]
        + [pl.BlockSpec(memory_space=pltpu.VMEM)] * PLANE,
        out_specs=[ANY] * n,
        out_shape=[shaped((rows, PLANE * w), f32) for w in widths],
        scratch_shapes=[
            pltpu.VMEM((PLANE, *blocks[0].shape), f32),
            pltpu.SemaphoreType.DMA((PLANE * n,)),
        ],
        compiler_params=params(),
        cost_estimate=cost(0, 8e6),
    )(me, *blocks)


def place_rows_kernel(me_ref, *refs):
    ins, out, held, sem = refs[:PLANE], refs[PLANE], refs[-2], refs[-1]
    rows = ins[0].shape[0]
    copies = []
    for k in range(PLANE):
        held[k] = ins[k][...].astype(f32)
        one = pltpu.make_async_copy(held.at[k], out.at[lanes(me_ref[0] ^ k, rows), :], sem.at[k])
        one.start()
        copies.append(one)
    for one in copies:
        one.wait()


def place_rows(me, blocks):
    rows, cols = blocks[0].shape
    return pl.pallas_call(
        place_rows_kernel,
        in_specs=[pl.BlockSpec(memory_space=pltpu.SMEM)]
        + [pl.BlockSpec(memory_space=pltpu.VMEM)] * PLANE,
        out_specs=ANY,
        out_shape=shaped((PLANE * rows, cols), f32),
        scratch_shapes=[pltpu.VMEM((PLANE, rows, cols), f32), pltpu.SemaphoreType.DMA((PLANE,))],
        compiler_params=params(),
        cost_estimate=cost(0, 4e6),
    )(me, *blocks)


def hop(value, bits, count):
    return lax.ppermute(value, "dp", [(i, i ^ bits) for i in range(count)])


def swap(value):
    return lax.ppermute(value, "tensor", [(0, 1), (1, 0)])


def trade(blocks, count):
    return [blocks[0]] + [hop(blocks[k], k, count) for k in range(1, PLANE)]


def spread(mine, count, beside=None):
    half = mine.shape[0] // 2
    from_x = hop(mine, 1, count)
    from_y = hop(mine, 2, count)
    pieces = [mine, swap(mine)]
    if beside:
        from_x, from_y = after((from_x, from_y), beside(0, 1, pieces))
    far_a = hop(from_x[:half], 2, count)
    far_b = hop(from_y[half:], 1, count)
    nearer = [from_x, swap(from_x), from_y, swap(from_y)]
    if beside:
        far_a, far_b = after((far_a, far_b), beside(1, 3, nearer))
    far = jnp.concatenate([far_a, far_b])
    far = [far, swap(far)]
    if beside:
        return beside(3, 4, far)
    return pieces + nearer + far


def fold(nears, fars, count, beside=None):
    arriveds = [swap(far) for far in fars]
    to_x, to_y, keep_x, keep_y = fold_cut(nears, arriveds)
    from_x = hop(to_x, 1, count)
    from_y = hop(to_y, 2, count)
    made = None
    if beside:
        made = beside((to_x, to_y))
        from_x, from_y = after((from_x, from_y), made)
    last_y = hop((keep_y + from_x[1].astype(f32)).astype(bf16), 2, count)
    last_x = hop((keep_x + from_y[1].astype(f32)).astype(bf16), 1, count)
    added = jnp.concatenate(
        [from_x[0].astype(f32) + last_y.astype(f32), from_y[0].astype(f32) + last_x.astype(f32)]
    )
    summed = nears[0][0] + arriveds[0][0].astype(f32) + added
    return (summed, made) if beside else summed


def after(values, done):
    return lax.optimization_barrier((values, done))[0]


def on_device(
    tokens,
    lengths,
    w_query,
    w_key,
    w_value,
    w_gate,
    w_out,
    w_ffgate,
    w_ffup,
    w_ffdown,
    gain_attn,
    gain_mlp,
    cotangent,
):
    count = lax.axis_size("dp")
    depth = count // PLANE
    columns = [[q + PLANE * z for z in range(depth)] for q in range(PLANE)]
    place = lax.axis_index("dp")
    me = place % PLANE
    me_scalar = me.reshape(1).astype(jnp.int32)
    core = lax.axis_index("tensor")
    rows, width = tokens.shape
    wide = width // depth
    shard = w_query.shape[0]
    dk = w_query.shape[1] // PLANE
    dv = w_value.shape[1] // PLANE
    inner = w_ffgate.shape[1] // PLANE
    assert dk == DK and dv == DV

    def gather_depth(block):
        return lax.all_gather(block, "dp", axis=0, tiled=True, axis_index_groups=columns)

    def sum_depth(block):
        return lax.psum_scatter(block, "dp", scatter_dimension=0, tiled=True, axis_index_groups=columns)

    attn_cuts = cut_columns(me_scalar, (w_query, w_key, w_value, w_gate)), cut_rows(me_scalar, w_out)
    attn_blocks = [trade(cuts, count) for cuts in attn_cuts]
    attn_own = join_weights(me_scalar, *attn_blocks)
    attn_joined = gather_depth(attn_own)

    gains = jnp.stack([gain_attn, gain_mlp])[None]
    step = 1
    while step < count:
        gains = jnp.concatenate([gains, hop(gains, step, count)])
        step *= 2
    gains = jnp.take(gains, place ^ jnp.arange(count), axis=0).astype(f32)
    gain_first = gains[:, 0].reshape(1, width)
    gain_second = gains[:, 1].reshape(1, width)

    input_rows = tokens.astype(f32)
    first_scale = lax.rsqrt(jnp.mean(input_rows * input_rows, axis=-1, keepdims=True) + norm_eps)
    normed_attn = (input_rows * first_scale * gain_first).astype(bf16)
    attn_pieces = spread(after(normed_attn, attn_own), count)

    ff_cuts = after((cut_columns(me_scalar, (w_ffgate, w_ffup)), cut_rows(me_scalar, w_ffdown)), attn_pieces)
    ff_blocks = [trade(cuts, count) for cuts in ff_cuts]
    ff_own = join_weights(me_scalar, *ff_blocks)
    ff_joined = gather_depth(ff_own)

    local = jnp.arange(rows, dtype=jnp.int32)
    valid_rows = ((core * rows + local) < lengths[0]).astype(f32)[:, None]
    back_rows = valid_rows * cotangent.astype(f32)
    back_all = jnp.concatenate(spread(after(back_rows.astype(bf16), ff_own), count))

    positions = jnp.concatenate([core * rows + local, (1 - core) * rows + local])
    decays = decay_table(positions, core * PLANE + me)
    attn_pieces = after(attn_pieces, back_all)
    query, key, value, scores, retained, attn_all = retain(attn_pieces, attn_joined, decays, dk, dv)
    gate, gated, near, far = gate_out(attn_all, attn_joined, retained, wide)
    hidden = input_rows + fold([near], [far], count)

    second_scale = lax.rsqrt(jnp.mean(hidden * hidden, axis=-1, keepdims=True) + norm_eps)
    normed_mlp = (hidden * second_scale * gain_second).astype(bf16)

    grad_inner = dot_back(back_all, ff_joined, inner, 2 * inner, wide)
    state = {"kept": (), "nears": [], "fars": []}

    def units(lo, hi, pieces):
        *state["kept"], near, far = hidden_units(lo, pieces, ff_joined, grad_inner, state["kept"])
        state["nears"].append(near)
        state["fars"].append(far)
        return state["kept"]

    inner_act, grad_up, mlp_all = spread(normed_mlp, count, units)

    def ff_grads(done):
        act, back, left, right = after((inner_act, back_all, mlp_all, grad_up), done)
        return rows_grad(act, back, wide), columns_grad(left, right, 0, 2 * inner)

    grad_normed, (grad_down, grad_ff) = fold(state["nears"], state["fars"], count, ff_grads)
    down_part = sum_depth(grad_down)
    ff_part = sum_depth(grad_ff)
    scaled = grad_normed * gain_second
    grad_hidden = back_rows + second_scale * (
        scaled
        - hidden * (second_scale * second_scale) * jnp.mean(hidden * scaled, axis=-1, keepdims=True)
    )
    gain_term_mlp = jnp.sum(grad_normed * hidden * second_scale, axis=0)

    state["kept"] = ()

    def heads(lo, hi, pieces):
        state["kept"] = retain_back(
            lo, pieces, attn_joined, decays, query, key, value, gate, scores, retained, state["kept"], wide
        )
        return state["kept"]

    grad_wide, attn_grad_all = spread(grad_hidden.astype(bf16), count, heads)
    out_part = sum_depth(rows_grad(gated, attn_grad_all, wide))
    wide_part = sum_depth(columns_grad(attn_all, grad_wide, 0, 2 * dv + 2 * dk))

    near, far = project_back(grad_wide, attn_joined, dk, dv)
    grad_normed_attn = fold([near], [far], count)
    gain_term_attn = jnp.sum(grad_normed_attn * input_rows * first_scale, axis=0)
    scaled_first = grad_normed_attn * gain_first
    tokens_grad = grad_hidden + first_scale * (
        scaled_first
        - input_rows
        * (first_scale * first_scale)
        * jnp.mean(input_rows * scaled_first, axis=-1, keepdims=True)
    )
    tokens_grad = tokens_grad.astype(bf16)

    down_weights = ff_joined[:, 2 * inner :]
    near, far = project(after(inner_act, attn_grad_all), down_weights, wide)
    output = (valid_rows * (hidden + fold([near], [far], count))).astype(bf16)

    gain_terms = jnp.stack([gain_term_attn, gain_term_mlp])
    bit = count // 2
    while bit >= 1:
        side = (place // bit) % 2
        cut = gain_terms.reshape(2, 2, -1)
        kept = lax.dynamic_index_in_dim(cut, side, 1, keepdims=False)
        sent = lax.dynamic_index_in_dim(cut, 1 - side, 1, keepdims=False)
        gain_terms = kept + hop(sent, bit, count)
        bit //= 2
    cut = gain_terms.reshape(2, 2, -1)
    kept = lax.dynamic_index_in_dim(cut, core, 1, keepdims=False)
    sent = lax.dynamic_index_in_dim(cut, 1 - core, 1, keepdims=False)
    gain_terms = kept + swap(sent)
    wide_part = after(wide_part, (output, tokens_grad, gain_terms))

    def back_columns(block, widths):
        cuts = [lax.dynamic_slice_in_dim(block, (me ^ k) * shard, shard, 0).astype(bf16) for k in range(PLANE)]
        return place_columns(me_scalar, trade(cuts, count), widths)

    def back_rows_of(block):
        cuts = [lax.dynamic_slice_in_dim(block, (me ^ k) * shard, shard, 1).astype(bf16) for k in range(PLANE)]
        return place_rows(me_scalar, trade(cuts, count))

    down_sum = back_rows_of(down_part)
    ffgate_sum, ffup_sum = back_columns(ff_part, (inner, inner))
    out_sum = back_rows_of(out_part)
    value_sum, gate_sum, query_sum, key_sum = back_columns(wide_part, (dv, dv, dk, dk))

    return (
        output,
        tokens_grad,
        query_sum,
        key_sum,
        value_sum,
        gate_sum,
        out_sum,
        ffgate_sum,
        ffup_sum,
        down_sum,
        gain_terms[0],
        gain_terms[1],
    )


def solution(mesh):
    return jax.shard_map(
        on_device,
        mesh=mesh,
        in_specs=(
            P(("dp", "tensor"), None),
            P("dp"),
            P("dp", "tensor"),
            P("dp", "tensor"),
            P("dp", "tensor"),
            P("dp", "tensor"),
            P("tensor", "dp"),
            P("dp", "tensor"),
            P("dp", "tensor"),
            P("tensor", "dp"),
            P("dp"),
            P("dp"),
            P(("dp", "tensor"), None),
        ),
        out_specs=(
            P(("dp", "tensor"), None),
            P(("dp", "tensor"), None),
            P("dp", "tensor"),
            P("dp", "tensor"),
            P("dp", "tensor"),
            P("dp", "tensor"),
            P("tensor", "dp"),
            P("dp", "tensor"),
            P("dp", "tensor"),
            P("tensor", "dp"),
            P(("dp", "tensor")),
            P(("dp", "tensor")),
        ),
        check_vma=False,
    )
```

time: 896 us -> 728 us (0.81)
  Pallas kernels: 0 us -> 236 us
  matrix products: 149 us -> 0 us
  other arithmetic: 154 us -> 43.1 us
  waiting for transfers between devices: 367 us -> 280 us
  local copies, waits for them, and re-layouts: 126 us -> 59.3 us
    pallas_call x0 -> x27, Pallas kernels: none -> 236 us  [the longest x3 37.8 us: hidden_units(): pl.pallas_call(functools.partial(hidden_kernel, first, n, len(kept)), gri...]
    dot_general x20 -> x0, matrix products: 149 us -> none  [the longest x4 51.5 us: dot_nt(): lax.dot_general(left, right, (((1,), (1,)), ((), ())), preferred_element_...]
    another operation x33 -> x0, other arithmetic: 95.6 us -> none
    another operation x14 -> x0, local copies, waits for them, and re-layouts: 46.3 us -> none  [the longest x4 33.5 us: spread(): jnp.stack([near, other], axis=1).reshape(8 * mine.shape[0], mine.shape[1])]
    ppermute x64, waiting for transfers between devices: 273 us -> 235 us  [hop(): return lax.ppermute(value, 'dp', [(i, i ^ bits) for i in range(count)])]
    all_gather x4 -> x2, waiting for transfers between devices: 61.3 us -> 29.5 us  [gather_depth(): lax.all_gather(block, 'dp', axis=0, tiled=True, axis_index_groups=columns)]
    reduce_scatter x4, waiting for transfers between devices: 19.8 us -> 0.01 us  [sum_depth(): lax.psum_scatter(block, 'dp', scatter_dimension=0, tiled=True, axis_index...]
    convert_element_type x24 -> x12, other arithmetic: 34.2 us -> 16.2 us  [the longest x4 6.34 us: fold(): last_y = hop((keep_y + from_x[1].astype(f32)).astype(bf16), 2, count)]
  transfers between devices with their start and end apart: 81 -> 93, of which waited for: 46 -> 39; matrix products, arithmetic and copies ran while one was open for 33% -> 12% of each run, Pallas kernels for 0% -> 29%
where the time goes in v2:
time: 728 us; the launch traced here: 722 us
  waiting for transfers between devices  280 us (38%)
  Pallas kernels  236 us (32%)
  starting transfers between devices  86.3 us (12%)
  local copies, waits for them, and re-layouts  59.3 us (8%)
  other arithmetic  43.1 us (6%)
  between operations  16.5 us (2%)
    ppermute x64, waiting for transfers between devices, hop(): return lax.ppermute(value, 'dp', [(i, i ^ bits) for i in range(count)])  235 us
    ppermute x64, starting transfers between devices, hop(): return lax.ppermute(value, 'dp', [(i, i ^ bits) for i in range(count)])  81.8 us
    pallas_call x3, Pallas kernels, hidden_units(): pl.pallas_call(functools.partial(hidden_kernel, first, n, len(kept)), gri...  37.8 us
    pallas_call x2, Pallas kernels, columns_grad(): pl.pallas_call(grad_kernel, grid=(width // part,), in_specs=[pl.BlockSpec...  32.2 us
    unnamed x142, local copies, waits for them, and re-layouts  31.2 us
    pallas_call x3, Pallas kernels, retain_back(): pl.pallas_call(functools.partial(retain_back_kernel, first, wide, n, len(...  30.5 us
    all_gather x2, waiting for transfers between devices, gather_depth(): lax.all_gather(block, 'dp', axis=0, tiled=True, axis_index_groups=columns)  29.5 us
    pallas_call x4, Pallas kernels, fold_cut(): pl.pallas_call(functools.partial(fold_kernel, spots, len(nears)), grid=(w...  27.1 us
  transfers between devices with their start and end apart: 93, of which 39 were waited for; matrix products, arithmetic and copies ran while one was open for 12% of the time, Pallas kernels for 29%

profile of v2, /device:TPU:0, one launch (start us, length us, event | category | flops | bytes accessed | tf_op | source)
XLA Modules:
  0.0 721.7 jit_solution(10627537786114957609)
XLA Ops:
  9.9 3.0 collective-permute-start.4
  19.7 13.8 %collective-permute-done.7.refs_5_ = bf16[512,128]{1,0:T(8,128)(2,1)S(1)} collective-permute-done((bf16[512,128]{1,0:T(8,128)(2,1)S(1)}, bf16[512,128]{1,0:T(8,128)(2,1)S(1)}, u32[]{:S(2)}, u32[]{:S(2)}) %collective-permute-start.7) | collective-permute-done | bytes 131104 | tf_op jit(solution)/shard_map/ppermute | solution.py:644
  36.2 3.2 collective-permute-done.9.refs_7_
  57.8 6.9 collective-permute-done.3
  68.8 17.5 %collective-permute-done.11.refs_2_ = bf16[256,2048]{1,0:T(8,128)(2,1)S(1)} collective-permute-done((bf16[256,2048]{1,0:T(8,128)(2,1)S(1)}, bf16[256,2048]{1,0:T(8,128)(2,1)S(1)}, u32[]{:S(2)}, u32[]{:S(2)}) %collective-permute-start.11) | collective-permute-done | bytes 1048608 | tf_op jit(solution)/shard_map/ppermute | solution.py:644
  90.0 5.6 collective-permute-done.15
  110.8 13.6 %collective-permute-done.22.refs_6_ = bf16[512,128]{1,0:T(8,128)(2,1)S(1)} collective-permute-done((bf16[512,128]{1,0:T(8,128)(2,1)S(1)}, bf16[512,128]{1,0:T(8,128)(2,1)S(1)}, u32[]{:S(2)}, u32[]{:S(2)}) %collective-permute-start.22) | collective-permute-done | bytes 131104 | tf_op jit(solution)/shard_map/ppermute | solution.py:644
  130.9 22.0 %collective-permute-done.25 = bf16[256,2048]{1,0:T(8,128)(2,1)} collective-permute-done((bf16[256,2048]{1,0:T(8,128)(2,1)S(1)}, bf16[256,2048]{1,0:T(8,128)(2,1)}, u32[]{:S(2)}, u32[]{:S(2)}) %collective-permute-start.25) | collective-permute-done | bytes 1048608 | tf_op jit(solution)/shard_map/ppermute | solution.py:644
  165.6 5.2 collective-permute-done.29
  183.5 11.3 %all-gather.3.cloned.1.call-done.refs_8_.weights.out_weights.refs_2_.refs_4_.first.second = bf16[2048,2048]{1,0:T(8,128)(2,1)} async-done(((bf16[512,2048]{1,0:T(8,128)(2,1)}), bf16[2048,2048]{1,0:T(8,128)(2,1)}) %all-gather.3.cloned.1.call-update) | async-done | bytes 8388624 | tf_op jit(solution)/shard_map/all_gather | solution.py:727
  194.8 17.4 %shard_map.224 = (bf16[2048,256]{1,0:T(8,128)(2,1)}, bf16[2048,256]{1,0:T(8,128)(2,1)}, bf16[2048,512]{1,0:T(8,128)(2,1)}, bf16[4,512,512]{2,1,0:T(8,128)(2,1)},...) custom-call(bf16[256,2048]{1,0:T(8,128)(2,1)} %copy-done.21, bf16[256,2048]{1,0:T(8,128)(2,1)} %collective-permute-done.10.refs_1_, ...), custom_call_target="tpu_custom_call" | custom-call | flops 9448928256 | bytes 30000000 | tf_op jit(solution)/shard_map/pallas_call | solution.py:206
  212.2 16.3 %shard_map.225 = (f32[2048,512]{1,0:T(8,128)}, bf16[2048,512]{1,0:T(8,128)(2,1)}, f32[4,256,2048]{2,1,0:T(8,128)}, bf16[4,256,2048]{2,1,0:T(8,128)(2,1)}) custom-call(bf16[2048,2048]{1,0:T(8,128)(2,1)} %get-tuple-element.137.rows_ref.left, bf16[2048,2048]{1,0:T(8,128)(2,1)} %all-gather.3.cloned.1.call-done.refs_8_.weights.out_weights.refs_2_.refs_4_.first.second, ...), custom_call_target="tpu_custom_call" | custom-call | flops 8589934592 | bytes 40000000 | tf_op jit(solution)/shard_map/pallas_call | solution.py:281
  228.5 7.3 %collective-permute-done.32.refs_1_ = bf16[4,256,2048]{2,1,0:T(8,128)(2,1)S(1)} collective-permute-done((bf16[4,256,2048]{2,1,0:T(8,128)(2,1)}, bf16[4,256,2048]{2,1,0:T(8,128)(2,1)S(1)}, u32[]{:S(2)}, u32[]{:S(2)}) %collective-permute-start.32) | collective-permute-done | bytes 4194336 | tf_op jit(solution)/shard_map/ppermute | solution.py:648
  237.9 6.7 shard_map.226
  247.5 22.5 %collective-permute-done.33 = bf16[2,128,2048]{2,1,0:T(8,128)(2,1)S(1)} collective-permute-done((bf16[2,128,2048]{2,1,0:T(8,128)(2,1)}, bf16[2,128,2048]{2,1,0:T(8,128)(2,1)S(1)}, u32[]{:S(2)}, u32[]{:S(2)}) %collective-permute-start.33) | collective-permute-done | bytes 1048608 | tf_op jit(solution)/shard_map/ppermute | solution.py:644
  274.5 10.1 %collective-permute-done.34 = bf16[128,2048]{1,0:T(8,128)(2,1)S(1)} collective-permute-done((bf16[128,2048]{1,0:T(8,128)(2,1)S(1)}, bf16[128,2048]{1,0:T(8,128)(2,1)S(1)}, u32[]{:S(2)}, u32[]{:S(2)}) %collective-permute-start.34) | collective-permute-done | bytes 524320 | tf_op jit(solution)/shard_map/ppermute | solution.py:644
  291.8 18.2 %all-gather.5.cloned.1.call-done.right.refs_2_.refs_4_ = bf16[2048,1536]{1,0:T(8,128)(2,1)} async-done(((bf16[512,1536]{1,0:T(8,128)(2,1)}), bf16[2048,1536]{1,0:T(8,128)(2,1)}) %all-gather.5.cloned.1.call-update) | async-done | bytes 6291472 | tf_op jit(solution)/shard_map/all_gather | solution.py:727
  309.9 9.2 %shard_map.227.refs_3_.refs_5_ = f32[2048,512]{1,0:T(8,128)} custom-call(bf16[2048,2048]{1,0:T(8,128)(2,1)} %constant_dynamic-update-slice_fusion.7.back.right, bf16[2048,1536]{1,0:T(8,128)(2,1)} %all-gather.5.cloned.1.call-done.right.refs_2_.refs_4_), custom_call_target="tpu_custom_call" | custom-call | flops 4294967296 | bytes 20000000 | tf_op jit(solution)/shard_map/pallas_call | solution.py:401
  319.2 10.9 %shard_map.228 = (bf16[2048,512]{1,0:T(8,128)(2,1)}, bf16[2048,1024]{1,0:T(8,128)(2,1)}, bf16[2048,2048]{1,0:T(8,128)(2,1)}, f32[1,256,2048]{2,1,0:T(8,128)}, bf16[1,256,2048]{2,1,0:T(8,128)(2,1)}) custom-call(bf16[256,2048]{1,0:T(8,128)(2,1)} %multiply_convert_fusion.refs_0_, bf16[256,2048]{1,0:T(8,128)(2,1)} %collective-permute-done.39.refs_1_, ...), custom_call_target="tpu_custom_call" | custom-call | flops 4294967296 | bytes 15000000 | tf_op jit(solution)/shard_map/pallas_call | solution.py:452
  337.8 16.0 %shard_map.229 = (bf16[2048,512]{1,0:T(8,128)(2,1)}, bf16[2048,1024]{1,0:T(8,128)(2,1)}, bf16[2048,2048]{1,0:T(8,128)(2,1)}, f32[2,256,2048]{2,1,0:T(8,128)}, bf16[2,256,2048]{2,1,0:T(8,128)(2,1)}) custom-call(bf16[256,2048]{1,0:T(8,128)(2,1)} %collective-permute-done.37.refs_0_, ...), custom_call_target="tpu_custom_call", output_to_operand_aliasing={{0}: (6, {}), {1}: (7, {}), {2}: (8, {})} | custom-call | flops 8589934592 | bytes 15000000 | tf_op jit(solution)/shard_map/pallas_call | solution.py:452
  357.5 10.9 %shard_map.230 = (bf16[2048,512]{1,0:T(8,128)(2,1)}, bf16[2048,1024]{1,0:T(8,128)(2,1)}, bf16[2048,2048]{1,0:T(8,128)(2,1)}, f32[1,256,2048]{2,1,0:T(8,128)}, bf16[1,256,2048]{2,1,0:T(8,128)(2,1)}) custom-call(bf16[256,2048]{1,0:T(8,128)(2,1)} %copy-done.9, ...), custom_call_target="tpu_custom_call", output_to_operand_aliasing={{0}: (4, {}), {1}: (5, {}), {2}: (6, {})} | custom-call | flops 4294967296 | bytes 15000000 | tf_op jit(solution)/shard_map/pallas_call | solution.py:452
  372.3 6.7 shard_map.231
  378.9 8.8 %shard_map.232 = bf16[2048,512]{1,0:T(8,128)(2,1)} custom-call(bf16[2048,512]{1,0:T(8,128)(2,1)} %get-tuple-element.188.left, bf16[2048,2048]{1,0:T(8,128)(2,1)} %constant_dynamic-update-slice_fusion.7.back.right), custom_call_target="tpu_custom_call" | custom-call | flops 4294967296 | bytes 20000000 | tf_op jit(solution)/shard_map/pallas_call | solution.py:568
  389.0 13.7 %shard_map.233 = bf16[2048,1024]{1,0:T(8,128)(2,1)} custom-call(bf16[2048,2048]{1,0:T(8,128)(2,1)} %get-tuple-element.168.left, bf16[2048,1024]{1,0:T(8,128)(2,1)} %get-tuple-element.169.right), custom_call_target="tpu_custom_call" | custom-call | flops 8589934592 | bytes 20000000 | tf_op jit(solution)/shard_map/pallas_call | solution.py:551
  403.0 10.4 %collective-permute-done.48 = bf16[2,128,2048]{2,1,0:T(8,128)(2,1)} collective-permute-done((bf16[2,128,2048]{2,1,0:T(8,128)(2,1)}, bf16[2,128,2048]{2,1,0:T(8,128)(2,1)}, u32[]{:S(2)}, u32[]{:S(2)}) %collective-permute-start.48) | collective-permute-done | bytes 1048608 | tf_op jit(solution)/shard_map/ppermute | solution.py:644
  418.5 9.6 %collective-permute-done.50 = bf16[128,2048]{1,0:T(8,128)(2,1)S(1)} collective-permute-done((bf16[128,2048]{1,0:T(8,128)(2,1)S(1)}, bf16[128,2048]{1,0:T(8,128)(2,1)S(1)}, u32[]{:S(2)}, u32[]{:S(2)}) %collective-permute-start.50) | collective-permute-done | bytes 524320 | tf_op jit(solution)/shard_map/ppermute | solution.py:644
  438.0 8.4 %shard_map.234 = (bf16[2048,1536]{1,0:T(8,128)(2,1)}, bf16[2048,2048]{1,0:T(8,128)(2,1)}) custom-call(bf16[256,2048]{1,0:T(8,128)(2,1)} %copy-done.3, bf16[256,2048]{1,0:T(8,128)(2,1)} %copy-done.15, bf16[2048,2048]{1,0:T(8,128)(2,1)} %all-gather.3.cloned.1.call-done.refs_8_.weights.out_weights.refs_2_.refs_4_.first.second, ...), custom_call_target="tpu_custom_call" | custom-call | flops 2147483648 | bytes 15000000 | tf_op jit(solution)/shard_map/pallas_call | solution.py:516
  446.4 13.3 %collective-permute-done.52.refs_0_ = bf16[256,2048]{1,0:T(8,128)(2,1)S(1)} collective-permute-done((bf16[256,2048]{1,0:T(8,128)(2,1)S(1)}, bf16[256,2048]{1,0:T(8,128)(2,1)S(1)}, u32[]{:S(2)}, u32[]{:S(2)}) %collective-permute-start.52) | collective-permute-done | bytes 1048608 | tf_op jit(solution)/shard_map/ppermute | solution.py:644
  467.1 13.7 %shard_map.235 = (bf16[2048,1536]{1,0:T(8,128)(2,1)}, bf16[2048,2048]{1,0:T(8,128)(2,1)}) custom-call(bf16[256,2048]{1,0:T(8,128)(2,1)} %copy-done.10, bf16[256,2048]{1,0:T(8,128)(2,1)} %copy-done.23, bf16[256,2048]{1,0:T(8,128)(2,1)} %copy-done.11, bf16[256,2048]{1,0:T(8,128)(2,1)} %copy-done.24, ...), custom_call_target="tpu_custom_call", output_to_operand_aliasing={{0}: (12, {}), {1}: (13, {})} | custom-call | flops 4294967296 | bytes 15000000 | tf_op jit(solution)/shard_map/pallas_call | solution.py:516
  485.7 8.4 %shard_map.236 = (bf16[2048,1536]{1,0:T(8,128)(2,1)}, bf16[2048,2048]{1,0:T(8,128)(2,1)}) custom-call(bf16[256,2048]{1,0:T(8,128)(2,1)} %copy-done.8, bf16[256,2048]{1,0:T(8,128)(2,1)} %copy-done.14, ...), custom_call_target="tpu_custom_call", output_to_operand_aliasing={{0}: (10, {}), {1}: (11, {})} | custom-call | flops 2147483648 | bytes 15000000 | tf_op jit(solution)/shard_map/pallas_call | solution.py:516
  494.1 8.9 %shard_map.243 = bf16[2048,512]{1,0:T(8,128)(2,1)} custom-call(bf16[2048,512]{1,0:T(8,128)(2,1)} %get-tuple-element.207.left, bf16[2048,2048]{1,0:T(8,128)(2,1)} %get-tuple-element.187.right), custom_call_target="tpu_custom_call" | custom-call | flops 4294967296 | bytes 20000000 | tf_op jit(solution)/shard_map/pallas_call | solution.py:568
  503.3 18.8 %shard_map.239 = (f32[4,256,2048]{2,1,0:T(8,128)}, bf16[4,256,2048]{2,1,0:T(8,128)(2,1)}) custom-call(bf16[2048,1536]{1,0:T(8,128)(2,1)} %get-tuple-element.195.left.right, bf16[2048,2048]{1,0:T(8,128)(2,1)} %all-gather.3.cloned.1.call-done.refs_8_.weights.out_weights.refs_2_.refs_4_.first.second, ...), custom_call_target="tpu_custom_call" | custom-call | flops 12884901888 | bytes 20000000 | tf_op jit(solution)/shard_map/pallas_call | solution.py:336
  522.4 18.5 %shard_map.241 = bf16[2048,1536]{1,0:T(8,128)(2,1)} custom-call(bf16[2048,2048]{1,0:T(8,128)(2,1)} %get-tuple-element.137.rows_ref.left, bf16[2048,1536]{1,0:T(8,128)(2,1)} %get-tuple-element.195.left.right), custom_call_target="tpu_custom_call" | custom-call | flops 12884901888 | bytes 20000000 | tf_op jit(solution)/shard_map/pallas_call | solution.py:551
  540.9 3.1 slice.153.right
  544.0 8.9 %shard_map.237 = (f32[4,256,2048]{2,1,0:T(8,128)}, bf16[4,256,2048]{2,1,0:T(8,128)(2,1)}) custom-call(bf16[2048,512]{1,0:T(8,128)(2,1)} %get-tuple-element.188.left, bf16[2048,512]{1,0:T(8,128)(2,1)} %slice.153.right), custom_call_target="tpu_custom_call" | custom-call | flops 4294967296 | bytes 20000000 | tf_op jit(solution)/shard_map/pallas_call | solution.py:312
  553.1 6.7 shard_map.240
  568.7 7.0 shard_map.238
  579.1 7.0 collective-permute-done.66
  591.9 19.5 %collective-permute-done.61 = bf16[2,128,2048]{2,1,0:T(8,128)(2,1)} collective-permute-done((bf16[2,128,2048]{2,1,0:T(8,128)(2,1)}, bf16[2,128,2048]{2,1,0:T(8,128)(2,1)}, u32[]{:S(2)}, u32[]{:S(2)}) %collective-permute-start.61) | collective-permute-done | bytes 1048608 | tf_op jit(solution)/shard_map/ppermute | solution.py:644
  616.6 9.2 %collective-permute-done.67 = bf16[128,2048]{1,0:T(8,128)(2,1)S(1)} collective-permute-done((bf16[128,2048]{1,0:T(8,128)(2,1)S(1)}, bf16[128,2048]{1,0:T(8,128)(2,1)S(1)}, u32[]{:S(2)}, u32[]{:S(2)}) %collective-permute-start.67) | collective-permute-done | bytes 524320 | tf_op jit(solution)/shard_map/ppermute | solution.py:644
  628.8 4.6 fusion.10
  637.1 3.2 collective-permute-done.70
  641.9 3.9 fusion.7
  651.6 9.3 %collective-permute-done.64 = bf16[128,2048]{1,0:T(8,128)(2,1)} collective-permute-done((bf16[128,2048]{1,0:T(8,128)(2,1)}, bf16[128,2048]{1,0:T(8,128)(2,1)}, u32[]{:S(2)}, u32[]{:S(2)}) %collective-permute-start.64) | collective-permute-done | bytes 524320 | tf_op jit(solution)/shard_map/ppermute | solution.py:644
  665.8 3.9 fusion.13
  678.5 6.3 collective-permute-done.82.refs_2_
  694.0 12.8 %collective-permute-done.79.refs_2_ = bf16[512,128]{1,0:T(8,128)(2,1)S(1)} collective-permute-done((bf16[512,128]{1,0:T(8,128)(2,1)S(1)}, bf16[512,128]{1,0:T(8,128)(2,1)S(1)}, u32[]{:S(2)}, u32[]{:S(2)}) %collective-permute-start.79) | collective-permute-done | bytes 131104 | tf_op jit(solution)/shard_map/ppermute | solution.py:644
  711.2 3.2 shard_map.242
  (395 shorter events, 210.1 us)
Async XLA Ops:
  7.2 187.6 %all-gather.3.cloned.1.call-start = ((), (), s32[]{:S(2)}) async-start(), calls=%async_computation.4 | async-start | bytes 10485760 | tf_op jit(solution)/shard_map/all_gather | solution.py:727
  9.9 29.5 %collective-permute-start.4 = (bf16[128,1536]{1,0:T(8,128)(2,1)}, bf16[128,1536]{1,0:T(8,128)(2,1)S(1)}, u32[]{:S(2)}, u32[]{:S(2)}) collective-permute-start(bf16[128,1536]{1,0:T(8,128)(2,1)} %get-tuple-element.112), channel_id=1, source_target_pairs={{0,2},{2,0},{4,6},{6,4},{8,10},{10,8},{12,14},{14,12},{16,18},{18,... | collective-permute-start | bytes 1179656 | tf_op jit(solution)/shard_map/ppermute | solution.py:644
  12.9 26.5 %collective-permute-start.5 = (bf16[128,1536]{1,0:T(8,128)(2,1)}, bf16[128,1536]{1,0:T(8,128)(2,1)S(1)}, u32[]{:S(2)}, u32[]{:S(2)}) collective-permute-start(bf16[128,1536]{1,0:T(8,128)(2,1)} %get-tuple-element.113), channel_id=1, source_target_pairs={{0,4},{2,6},{4,0},{6,2},{8,12},{10,14},{12,8},{14,10},{16,20},{18,... | collective-permute-start | bytes 1179656 | tf_op jit(solution)/shard_map/ppermute | solution.py:644
  14.4 25.0 %collective-permute-start.6 = (bf16[128,1536]{1,0:T(8,128)(2,1)}, bf16[128,1536]{1,0:T(8,128)(2,1)S(1)}, u32[]{:S(2)}, u32[]{:S(2)}) collective-permute-start(bf16[128,1536]{1,0:T(8,128)(2,1)} %get-tuple-element.114), channel_id=1, source_target_pairs={{0,6},{2,4},{4,2},{6,0},{8,14},{10,12},{12,10},{14,8},{16,22},{18,... | collective-permute-start | bytes 1179656 | tf_op jit(solution)/shard_map/ppermute | solution.py:644
  16.2 17.3 %collective-permute-start.7 = (bf16[512,128]{1,0:T(8,128)(2,1)S(1)}, bf16[512,128]{1,0:T(8,128)(2,1)S(1)}, u32[]{:S(2)}, u32[]{:S(2)}) collective-permute-start(bf16[512,128]{1,0:T(8,128)(2,1)S(1)} %get-tuple-element.243), channel_id=1, source_target_pairs={{0,2},{2,0},{4,6},{6,4},{8,10},{10,8},{12,14},{14,12},{16,18},{18,... | collective-permute-start | bytes 393224 | tf_op jit(solution)/shard_map/ppermute | solution.py:644
  18.2 18.0 %collective-permute-start.8 = (bf16[512,128]{1,0:T(8,128)(2,1)S(1)}, bf16[512,128]{1,0:T(8,128)(2,1)S(1)}, u32[]{:S(2)}, u32[]{:S(2)}) collective-permute-start(bf16[512,128]{1,0:T(8,128)(2,1)S(1)} %get-tuple-element.245), channel_id=1, source_target_pairs={{0,4},{2,6},{4,0},{6,2},{8,12},{10,14},{12,8},{14,10},{16,20},{18,... | collective-permute-start | bytes 393224 | tf_op jit(solution)/shard_map/ppermute | solution.py:644
  43.4 266.5 %all-gather.5.cloned.1.call-start = ((), (), s32[]{:S(2)}) async-start(), calls=%async_computation.5 | async-start | bytes 7864320 | tf_op jit(solution)/shard_map/all_gather | solution.py:727
  65.8 20.5 %collective-permute-start.11 = (bf16[256,2048]{1,0:T(8,128)(2,1)S(1)}, bf16[256,2048]{1,0:T(8,128)(2,1)S(1)}, u32[]{:S(2)}, u32[]{:S(2)}) collective-permute-start(bf16[256,2048]{1,0:T(8,128)(2,1)S(1)} %fusion.2.refs_0_), channel_id=1, source_target_pairs={{0,2},{2,0},{4,6},{6,4},{8,10},{10,8},{12,14},{14,12},{16,18},{18,... | collective-permute-start | bytes 3145736 | tf_op jit(solution)/shard_map/ppermute | solution.py:644
  67.3 20.6 %collective-permute-start.13 = (bf16[256,2048]{1,0:T(8,128)(2,1)S(1)}, bf16[256,2048]{1,0:T(8,128)(2,1)S(1)}, u32[]{:S(2)}, u32[]{:S(2)}) collective-permute-start(bf16[256,2048]{1,0:T(8,128)(2,1)S(1)} %fusion.2.refs_0_), channel_id=1, source_target_pairs={{0,4},{2,6},{4,0},{6,2},{8,12},{10,14},{12,8},{14,10},{16,20},{18,... | collective-permute-start | bytes 3145736 | tf_op jit(solution)/shard_map/ppermute | solution.py:644
  104.1 20.2 %collective-permute-start.18 = (bf16[128,1024]{1,0:T(8,128)(2,1)}, bf16[128,1024]{1,0:T(8,128)(2,1)S(1)}, u32[]{:S(2)}, u32[]{:S(2)}) collective-permute-start(bf16[128,1024]{1,0:T(8,128)(2,1)} %get-tuple-element.121), channel_id=1, source_target_pairs={{0,2},{2,0},{4,6},{6,4},{8,10},{10,8},{12,14},{14,12},{16,18},{18,... | collective-permute-start | bytes 786440 | tf_op jit(solution)/shard_map/ppermute | solution.py:644
  104.7 19.6 %collective-permute-start.19 = (bf16[128,1024]{1,0:T(8,128)(2,1)}, bf16[128,1024]{1,0:T(8,128)(2,1)S(1)}, u32[]{:S(2)}, u32[]{:S(2)}) collective-permute-start(bf16[128,1024]{1,0:T(8,128)(2,1)} %get-tuple-element.122), channel_id=1, source_target_pairs={{0,4},{2,6},{4,0},{6,2},{8,12},{10,14},{12,8},{14,10},{16,20},{18,... | collective-permute-start | bytes 786440 | tf_op jit(solution)/shard_map/ppermute | solution.py:644
  106.1 18.3 %collective-permute-start.20 = (bf16[128,1024]{1,0:T(8,128)(2,1)}, bf16[128,1024]{1,0:T(8,128)(2,1)S(1)}, u32[]{:S(2)}, u32[]{:S(2)}) collective-permute-start(bf16[128,1024]{1,0:T(8,128)(2,1)} %get-tuple-element.123), channel_id=1, source_target_pairs={{0,6},{2,4},{4,2},{6,0},{8,14},{10,12},{12,10},{14,8},{16,22},{18,... | collective-permute-start | bytes 786440 | tf_op jit(solution)/shard_map/ppermute | solution.py:644
  107.7 16.7 %collective-permute-start.22 = (bf16[512,128]{1,0:T(8,128)(2,1)S(1)}, bf16[512,128]{1,0:T(8,128)(2,1)S(1)}, u32[]{:S(2)}, u32[]{:S(2)}) collective-permute-start(bf16[512,128]{1,0:T(8,128)(2,1)S(1)} %get-tuple-element.126), channel_id=1, source_target_pairs={{0,4},{2,6},{4,0},{6,2},{8,12},{10,14},{12,8},{14,10},{16,20},{18,... | collective-permute-start | bytes 393224 | tf_op jit(solution)/shard_map/ppermute | solution.py:644
  128.5 24.4 %collective-permute-start.25 = (bf16[256,2048]{1,0:T(8,128)(2,1)S(1)}, bf16[256,2048]{1,0:T(8,128)(2,1)}, u32[]{:S(2)}, u32[]{:S(2)}) collective-permute-start(bf16[256,2048]{1,0:T(8,128)(2,1)S(1)} %fusion.14), channel_id=1, source_target_pairs={{0,2},{2,0},{4,6},{6,4},{8,10},{10,8},{12,14},{14,12},{16,18},{18,... | collective-permute-start | bytes 3145736 | tf_op jit(solution)/shard_map/ppermute | solution.py:644
  130.1 27.4 %collective-permute-start.27 = (bf16[256,2048]{1,0:T(8,128)(2,1)S(1)}, bf16[256,2048]{1,0:T(8,128)(2,1)S(1)}, u32[]{:S(2)}, u32[]{:S(2)}) collective-permute-start(bf16[256,2048]{1,0:T(8,128)(2,1)S(1)} %fusion.14), channel_id=1, source_target_pairs={{0,4},{2,6},{4,0},{6,2},{8,12},{10,14},{12,8},{14,10},{16,20},{18,... | collective-permute-start | bytes 3145736 | tf_op jit(solution)/shard_map/ppermute | solution.py:644
  130.8 30.1 %collective-permute-start.24 = (bf16[256,2048]{1,0:T(8,128)(2,1)S(1)}, bf16[256,2048]{1,0:T(8,128)(2,1)}, u32[]{:S(2)}, u32[]{:S(2)}) collective-permute-start(bf16[256,2048]{1,0:T(8,128)(2,1)S(1)} %fusion.14), channel_id=1, source_target_pairs={{0,1},{1,0},{2,3},{3,2},{4,5},{5,4},{6,7},{7,6},{8,9},{9,8},{10,11... | collective-permute-start | bytes 3145736 | tf_op jit(solution)/shard_map/ppermute | solution.py:648
  153.0 21.2 %collective-permute-start.26 = (bf16[256,2048]{1,0:T(8,128)(2,1)}, bf16[256,2048]{1,0:T(8,128)(2,1)}, u32[]{:S(2)}, u32[]{:S(2)}) collective-permute-start(bf16[256,2048]{1,0:T(8,128)(2,1)} %collective-permute-done.25), channel_id=1, source_target_pairs={{0,1},{1,0},{2,3},{3,2},{4,5},{5,4},{6,7},{7,6},{8,9},{9,8},{10,11... | collective-permute-start | bytes 3145736 | tf_op jit(solution)/shard_map/ppermute | solution.py:648
  160.3 402.0 %reduce-scatter.11.cloned.1.call-start = ((), (), s32[]{:S(2)}) async-start(), calls=%async_computation.9 | async-start | bytes 2621440 | tf_op jit(solution)/shard_map/reduce_scatter | solution.py:730
  244.5 25.4 %collective-permute-start.33 = (bf16[2,128,2048]{2,1,0:T(8,128)(2,1)}, bf16[2,128,2048]{2,1,0:T(8,128)(2,1)S(1)}, u32[]{:S(2)}, u32[]{:S(2)}) collective-permute-start(bf16[2,128,2048]{2,1,0:T(8,128)(2,1)} %get-tuple-element.141), channel_id=1, source_target_pairs={{0,2},{2,0},{4,6},{6,4},{8,10},{10,8},{12,14},{14,12},{16,18},{18,... | collective-permute-start | bytes 3145736 | tf_op jit(solution)/shard_map/ppermute | solution.py:644
  246.0 26.8 %collective-permute-start.35 = (bf16[2,128,2048]{2,1,0:T(8,128)(2,1)}, bf16[2,128,2048]{2,1,0:T(8,128)(2,1)S(1)}, u32[]{:S(2)}, u32[]{:S(2)}) collective-permute-start(bf16[2,128,2048]{2,1,0:T(8,128)(2,1)} %get-tuple-element.143), channel_id=1, source_target_pairs={{0,4},{2,6},{4,0},{6,2},{8,12},{10,14},{12,8},{14,10},{16,20},{18,... | collective-permute-start | bytes 3145736 | tf_op jit(solution)/shard_map/ppermute | solution.py:644
  289.8 29.4 %collective-permute-start.39 = (bf16[256,2048]{1,0:T(8,128)(2,1)}, bf16[256,2048]{1,0:T(8,128)(2,1)}, u32[]{:S(2)}, u32[]{:S(2)}) collective-permute-start(bf16[256,2048]{1,0:T(8,128)(2,1)} %multiply_convert_fusion.refs_0_), channel_id=1, source_target_pairs={{0,1},{1,0},{2,3},{3,2},{4,5},{5,4},{6,7},{7,6},{8,9},{9,8},{10,11... | collective-permute-start | bytes 3145736 | tf_op jit(solution)/shard_map/ppermute | solution.py:648
  289.8 40.3 %collective-permute-start.37 = (bf16[256,2048]{1,0:T(8,128)(2,1)}, bf16[256,2048]{1,0:T(8,128)(2,1)}, u32[]{:S(2)}, u32[]{:S(2)}) collective-permute-start(bf16[256,2048]{1,0:T(8,128)(2,1)} %multiply_convert_fusion.refs_0_), channel_id=1, source_target_pairs={{0,2},{2,0},{4,6},{6,4},{8,10},{10,8},{12,14},{14,12},{16,18},{18,... | collective-permute-start | bytes 3145736 | tf_op jit(solution)/shard_map/ppermute | solution.py:644
  291.3 38.8 %collective-permute-start.38 = (bf16[256,2048]{1,0:T(8,128)(2,1)}, bf16[256,2048]{1,0:T(8,128)(2,1)}, u32[]{:S(2)}, u32[]{:S(2)}) collective-permute-start(bf16[256,2048]{1,0:T(8,128)(2,1)} %multiply_convert_fusion.refs_0_), channel_id=1, source_target_pairs={{0,4},{2,6},{4,0},{6,2},{8,12},{10,14},{12,8},{14,10},{16,20},{18,... | collective-permute-start | bytes 3145736 | tf_op jit(solution)/shard_map/ppermute | solution.py:644
  332.8 20.9 %collective-permute-start.40 = (bf16[128,2048]{1,0:T(8,128)(2,1)S(1)}, bf16[128,2048]{1,0:T(8,128)(2,1)S(1)}, u32[]{:S(2)}, u32[]{:S(2)}) collective-permute-start(bf16[128,2048]{1,0:T(8,128)(2,1)S(1)} %slice.117), channel_id=1, source_target_pairs={{0,4},{2,6},{4,0},{6,2},{8,12},{10,14},{12,8},{14,10},{16,20},{18,... | collective-permute-start | bytes 1572872 | tf_op jit(solution)/shard_map/ppermute | solution.py:644
  334.4 19.4 %collective-permute-start.41 = (bf16[128,2048]{1,0:T(8,128)(2,1)S(1)}, bf16[128,2048]{1,0:T(8,128)(2,1)S(1)}, u32[]{:S(2)}, u32[]{:S(2)}) collective-permute-start(bf16[128,2048]{1,0:T(8,128)(2,1)S(1)} %slice.118), channel_id=1, source_target_pairs={{0,2},{2,0},{4,6},{6,4},{8,10},{10,8},{12,14},{14,12},{16,18},{18,... | collective-permute-start | bytes 1572872 | tf_op jit(solution)/shard_map/ppermute | solution.py:644
  387.8 178.8 %reduce-scatter.9.cloned.1.call-start = ((), (), s32[]{:S(2)}) async-start(), calls=%async_computation.8 | async-start | bytes 5242880 | tf_op jit(solution)/shard_map/reduce_scatter | solution.py:730
  387.8 25.6 %collective-permute-start.48 = (bf16[2,128,2048]{2,1,0:T(8,128)(2,1)}, bf16[2,128,2048]{2,1,0:T(8,128)(2,1)}, u32[]{:S(2)}, u32[]{:S(2)}) collective-permute-start(bf16[2,128,2048]{2,1,0:T(8,128)(2,1)} %get-tuple-element.162), channel_id=1, source_target_pairs={{0,2},{2,0},{4,6},{6,4},{8,10},{10,8},{12,14},{14,12},{16,18},{18,... | collective-permute-start | bytes 3145736 | tf_op jit(solution)/shard_map/ppermute | solution.py:644
  388.4 25.2 %collective-permute-start.49 = (bf16[2,128,2048]{2,1,0:T(8,128)(2,1)}, bf16[2,128,2048]{2,1,0:T(8,128)(2,1)}, u32[]{:S(2)}, u32[]{:S(2)}) collective-permute-start(bf16[2,128,2048]{2,1,0:T(8,128)(2,1)} %get-tuple-element.163), channel_id=1, source_target_pairs={{0,4},{2,6},{4,0},{6,2},{8,12},{10,14},{12,8},{14,10},{16,20},{18,... | collective-permute-start | bytes 3145736 | tf_op jit(solution)/shard_map/ppermute | solution.py:644
  402.7 174.4 %reduce-scatter.7.cloned.1.call-start = ((), (), s32[]{:S(2)}) async-start(), calls=%async_computation.7 | async-start | bytes 2621440 | tf_op jit(solution)/shard_map/reduce_scatter | solution.py:730
  434.1 25.6 %collective-permute-start.52 = (bf16[256,2048]{1,0:T(8,128)(2,1)S(1)}, bf16[256,2048]{1,0:T(8,128)(2,1)S(1)}, u32[]{:S(2)}, u32[]{:S(2)}) collective-permute-start(bf16[256,2048]{1,0:T(8,128)(2,1)S(1)} %get-tuple-element.215.refs_0_), channel_id=1, source_target_pairs={{0,2},{2,0},{4,6},{6,4},{8,10},{10,8},{12,14},{14,12},{16,18},{18,... | collective-permute-start | bytes 3145736 | tf_op jit(solution)/shard_map/ppermute | solution.py:644
  435.6 25.3 %collective-permute-start.53 = (bf16[256,2048]{1,0:T(8,128)(2,1)S(1)}, bf16[256,2048]{1,0:T(8,128)(2,1)S(1)}, u32[]{:S(2)}, u32[]{:S(2)}) collective-permute-start(bf16[256,2048]{1,0:T(8,128)(2,1)S(1)} %get-tuple-element.215.refs_0_), channel_id=1, source_target_pairs={{0,4},{2,6},{4,0},{6,2},{8,12},{10,14},{12,8},{14,10},{16,20},{18,... | collective-permute-start | bytes 3145736 | tf_op jit(solution)/shard_map/ppermute | solution.py:644
  463.1 17.8 %collective-permute-start.55 = (bf16[128,2048]{1,0:T(8,128)(2,1)}, bf16[128,2048]{1,0:T(8,128)(2,1)S(1)}, u32[]{:S(2)}, u32[]{:S(2)}) collective-permute-start(bf16[128,2048]{1,0:T(8,128)(2,1)} %slice.123), channel_id=1, source_target_pairs={{0,4},{2,6},{4,0},{6,2},{8,12},{10,14},{12,8},{14,10},{16,20},{18,... | collective-permute-start | bytes 1572872 | tf_op jit(solution)/shard_map/ppermute | solution.py:644
  503.0 168.3 %reduce-scatter.5.cloned.1.call-start = ((), (), s32[]{:S(2)}) async-start(), calls=%async_computation.6 | async-start | bytes 7864320 | tf_op jit(solution)/shard_map/reduce_scatter | solution.py:730
  522.1 31.0 %collective-permute-start.65 = (bf16[4,256,2048]{2,1,0:T(8,128)(2,1)}, bf16[4,256,2048]{2,1,0:T(8,128)(2,1)}, u32[]{:S(2)}, u32[]{:S(2)}) collective-permute-start(bf16[4,256,2048]{2,1,0:T(8,128)(2,1)} %get-tuple-element.197), channel_id=1, source_target_pairs={{0,1},{1,0},{2,3},{3,2},{4,5},{5,4},{6,7},{7,6},{8,9},{9,8},{10,11... | collective-permute-start | bytes 12582920 | tf_op jit(solution)/shard_map/ppermute | solution.py:648
  559.8 26.3 %collective-permute-start.66 = (bf16[2,128,2048]{2,1,0:T(8,128)(2,1)}, bf16[2,128,2048]{2,1,0:T(8,128)(2,1)}, u32[]{:S(2)}, u32[]{:S(2)}) collective-permute-start(bf16[2,128,2048]{2,1,0:T(8,128)(2,1)} %get-tuple-element.198), channel_id=1, source_target_pairs={{0,2},{2,0},{4,6},{6,4},{8,10},{10,8},{12,14},{14,12},{16,18},{18,... | collective-permute-start | bytes 3145736 | tf_op jit(solution)/shard_map/ppermute | solution.py:644
  561.2 26.8 %collective-permute-start.68 = (bf16[2,128,2048]{2,1,0:T(8,128)(2,1)}, bf16[2,128,2048]{2,1,0:T(8,128)(2,1)}, u32[]{:S(2)}, u32[]{:S(2)}) collective-permute-start(bf16[2,128,2048]{2,1,0:T(8,128)(2,1)} %get-tuple-element.200), channel_id=1, source_target_pairs={{0,4},{2,6},{4,0},{6,2},{8,12},{10,14},{12,8},{14,10},{16,20},{18,... | collective-permute-start | bytes 3145736 | tf_op jit(solution)/shard_map/ppermute | solution.py:644
  564.2 107.1 %collective-permute-start.84 = (bf16[512,128]{1,0:T(8,128)(2,1)}, bf16[512,128]{1,0:T(8,128)(2,1)S(1)}, u32[]{:S(2)}, u32[]{:S(2)}) collective-permute-start(bf16[512,128]{1,0:T(8,128)(2,1)} %get-tuple-element.232), channel_id=1, source_target_pairs={{0,2},{2,0},{4,6},{6,4},{8,10},{10,8},{12,14},{14,12},{16,18},{18,... | collective-permute-start | bytes 393224 | tf_op jit(solution)/shard_map/ppermute | solution.py:644
  565.0 107.9 %collective-permute-start.85 = (bf16[512,128]{1,0:T(8,128)(2,1)}, bf16[512,128]{1,0:T(8,128)(2,1)}, u32[]{:S(2)}, u32[]{:S(2)}) collective-permute-start(bf16[512,128]{1,0:T(8,128)(2,1)} %get-tuple-element.231), channel_id=1, source_target_pairs={{0,4},{2,6},{4,0},{6,2},{8,12},{10,14},{12,8},{14,10},{16,20},{18,... | collective-permute-start | bytes 393224 | tf_op jit(solution)/shard_map/ppermute | solution.py:644
  575.8 35.6 %collective-permute-start.61 = (bf16[2,128,2048]{2,1,0:T(8,128)(2,1)}, bf16[2,128,2048]{2,1,0:T(8,128)(2,1)}, u32[]{:S(2)}, u32[]{:S(2)}) collective-permute-start(bf16[2,128,2048]{2,1,0:T(8,128)(2,1)} %get-tuple-element.191), channel_id=1, source_target_pairs={{0,2},{2,0},{4,6},{6,4},{8,10},{10,8},{12,14},{14,12},{16,18},{18,... | collective-permute-start | bytes 3145736 | tf_op jit(solution)/shard_map/ppermute | solution.py:644
  586.1 29.5 %collective-permute-start.63 = (bf16[2,128,2048]{2,1,0:T(8,128)(2,1)}, bf16[2,128,2048]{2,1,0:T(8,128)(2,1)S(1)}, u32[]{:S(2)}, u32[]{:S(2)}) collective-permute-start(bf16[2,128,2048]{2,1,0:T(8,128)(2,1)} %get-tuple-element.193), channel_id=1, source_target_pairs={{0,4},{2,6},{4,0},{6,2},{8,12},{10,14},{12,8},{14,10},{16,20},{18,... | collective-permute-start | bytes 3145736 | tf_op jit(solution)/shard_map/ppermute | solution.py:644
  588.1 87.5 %collective-permute-start.86 = (bf16[512,128]{1,0:T(8,128)(2,1)}, bf16[512,128]{1,0:T(8,128)(2,1)}, u32[]{:S(2)}, u32[]{:S(2)}) collective-permute-start(bf16[512,128]{1,0:T(8,128)(2,1)} %get-tuple-element.230), channel_id=1, source_target_pairs={{0,6},{2,4},{4,2},{6,0},{8,14},{10,12},{12,10},{14,8},{16,22},{18,... | collective-permute-start | bytes 393224 | tf_op jit(solution)/shard_map/ppermute | solution.py:644
  625.8 21.4 %collective-permute-start.62 = (bf16[128,2048]{1,0:T(8,128)(2,1)}, bf16[128,2048]{1,0:T(8,128)(2,1)}, u32[]{:S(2)}, u32[]{:S(2)}) collective-permute-start(bf16[128,2048]{1,0:T(8,128)(2,1)} %fusion.22), channel_id=1, source_target_pairs={{0,4},{2,6},{4,0},{6,2},{8,12},{10,14},{12,8},{14,10},{16,20},{18,... | collective-permute-start | bytes 1572872 | tf_op jit(solution)/shard_map/ppermute | solution.py:644
  650.8 26.2 %collective-permute-start.81 = (bf16[128,1024]{1,0:T(8,128)(2,1)}, bf16[128,1024]{1,0:T(8,128)(2,1)}, u32[]{:S(2)}, u32[]{:S(2)}) collective-permute-start(bf16[128,1024]{1,0:T(8,128)(2,1)} %get-tuple-element.228), channel_id=1, source_target_pairs={{0,2},{2,0},{4,6},{6,4},{8,10},{10,8},{12,14},{14,12},{16,18},{18,... | collective-permute-start | bytes 786440 | tf_op jit(solution)/shard_map/ppermute | solution.py:644
  675.6 34.5 %collective-permute-start.75 = (bf16[128,1536]{1,0:T(8,128)(2,1)S(1)}, bf16[128,1536]{1,0:T(8,128)(2,1)S(1)}, u32[]{:S(2)}, u32[]{:S(2)}) collective-permute-start(bf16[128,1536]{1,0:T(8,128)(2,1)S(1)} %get-tuple-element.224), channel_id=1, source_target_pairs={{0,2},{2,0},{4,6},{6,4},{8,10},{10,8},{12,14},{14,12},{16,18},{18,... | collective-permute-start | bytes 1179656 | tf_op jit(solution)/shard_map/ppermute | solution.py:644
  677.1 33.1 %collective-permute-start.76 = (bf16[128,1536]{1,0:T(8,128)(2,1)S(1)}, bf16[128,1536]{1,0:T(8,128)(2,1)S(1)}, u32[]{:S(2)}, u32[]{:S(2)}) collective-permute-start(bf16[128,1536]{1,0:T(8,128)(2,1)S(1)} %get-tuple-element.223), channel_id=1, source_target_pairs={{0,4},{2,6},{4,0},{6,2},{8,12},{10,14},{12,8},{14,10},{16,20},{18,... | collective-permute-start | bytes 1179656 | tf_op jit(solution)/shard_map/ppermute | solution.py:644
  684.7 25.4 %collective-permute-start.77 = (bf16[128,1536]{1,0:T(8,128)(2,1)S(1)}, bf16[128,1536]{1,0:T(8,128)(2,1)S(1)}, u32[]{:S(2)}, u32[]{:S(2)}) collective-permute-start(bf16[128,1536]{1,0:T(8,128)(2,1)S(1)} %get-tuple-element.222), channel_id=1, source_target_pairs={{0,6},{2,4},{4,2},{6,0},{8,14},{10,12},{12,10},{14,8},{16,22},{18,... | collective-permute-start | bytes 1179656 | tf_op jit(solution)/shard_map/ppermute | solution.py:644
  687.1 19.7 %collective-permute-start.79 = (bf16[512,128]{1,0:T(8,128)(2,1)S(1)}, bf16[512,128]{1,0:T(8,128)(2,1)S(1)}, u32[]{:S(2)}, u32[]{:S(2)}) collective-permute-start(bf16[512,128]{1,0:T(8,128)(2,1)S(1)} %copy-done.49), channel_id=1, source_target_pairs={{0,4},{2,6},{4,0},{6,2},{8,12},{10,14},{12,8},{14,10},{16,20},{18,... | collective-permute-start | bytes 393224 | tf_op jit(solution)/shard_map/ppermute | solution.py:644
  687.8 19.0 %collective-permute-start.80 = (bf16[512,128]{1,0:T(8,128)(2,1)S(1)}, bf16[512,128]{1,0:T(8,128)(2,1)S(1)}, u32[]{:S(2)}, u32[]{:S(2)}) collective-permute-start(bf16[512,128]{1,0:T(8,128)(2,1)S(1)} %copy-done.48), channel_id=1, source_target_pairs={{0,6},{2,4},{4,2},{6,0},{8,14},{10,12},{12,10},{14,8},{16,22},{18,... | collective-permute-start | bytes 393224 | tf_op jit(solution)/shard_map/ppermute | solution.py:644
  (107 other events, 1233.5 us)
Sparse Core Ops, SparseCore 0:
  43.6 151.1 all-gather.2
  196.4 113.5 all-gather.4
  387.9 40.2 reduce-scatter.10
  430.4 76.0 reduce-scatter.8
  508.7 44.3 reduce-scatter.6
  555.4 110.3 reduce-scatter.4

commit v3 on v2

--- a/solution.py
+++ b/solution.py
@@ -10,7 +10,8 @@
 DK = 256
 DV = 512
 PLANE = 4
-VMEM_BYTES = 56 * 1024 * 1024
+SLOTS = ((0, 1), (1, 3), (3, 4))
+VMEM_BYTES = 62 * 1024 * 1024
 
 norm_eps = 1e-06
 group_floor = 1.0
@@ -93,9 +94,15 @@
     return pl.ds(pl.multiple_of(index * size, size), size)
 
 
-def cut_columns(me, weights):
-    rows = weights[0].shape[0]
-    parts = [w.shape[1] // PLANE for w in weights]
+def cut_weights(me, by_columns, by_rows):
+    rows, cols = by_columns[0].shape[0], by_rows.shape[1]
+    parts = [w.shape[1] // PLANE for w in by_columns]
+    inner = by_rows.shape[0] // PLANE
+    width = sum(parts)
+    aligned = cols % 128 == 0
+    if not aligned:
+        by_rows = jnp.moveaxis(by_rows.reshape(PLANE, inner // rows, rows, cols), 1, 2)
+        by_rows = jnp.moveaxis(by_rows.reshape(PLANE, rows, -1), 0, 1).reshape(rows, -1)
 
     def plan(place, ins, outs):
         copies = []
@@ -104,54 +111,45 @@
             for w, part in zip(ins, parts):
                 copies.append((w.at[:, lanes(place ^ k, part)], outs[k].at[:, pl.ds(at, part)]))
                 at += part
+            if not aligned:
+                copies.append((ins[-1].at[:, lanes(place ^ k, inner)], outs[k].at[:, pl.ds(width, inner)]))
+                continue
+            for block in range(inner // rows):
+                source = pl.ds(pl.multiple_of((place ^ k) * inner + block * rows, rows), rows)
+                copies.append((ins[-1].at[source, :], outs[k].at[:, pl.ds(width + block * cols, cols)]))
         return copies
 
-    shapes = [shaped((rows, sum(parts)), bf16)] * PLANE
-    return place_copies(plan, PLANE * len(parts), me, weights, shapes)
-
-
-def cut_rows(me, weight):
-    depth = weight.shape[0] // PLANE
-    place = me[0]
-    return [lax.dynamic_slice_in_dim(weight, (place ^ k) * depth, depth, 0) for k in range(PLANE)]
-
-
-def in_order(blocks, place, axis):
-    stacked = jnp.stack(blocks)
-    return jnp.concatenate(
-        [lax.dynamic_index_in_dim(stacked, place ^ j, 0, keepdims=False) for j in range(PLANE)], axis
-    )
-
-
-def join_weights(me, column_blocks, row_blocks):
-    rows, width = column_blocks[0].shape if column_blocks else (row_blocks[0].shape[1], 0)
+    shapes = [shaped((rows, width + inner), bf16)] * PLANE
+    n_copies = PLANE * (len(parts) + (inner // rows if aligned else 1))
+    return place_copies(plan, n_copies, me, [*by_columns, by_rows], shapes)
+
+
+def join_weights(me, blocks, width):
+    rows, inner = blocks[0].shape[0], blocks[0].shape[1] - width
     tall = PLANE * rows
-    if not row_blocks:
-        groups, extra = 0, []
-    else:
-        inner, cols = row_blocks[0].shape
-        groups = inner // tall
-        aligned = cols % 128 == 0
-        extra = row_blocks if aligned else [in_order(row_blocks, me[0], 1)]
+    aligned = rows % 128 == 0
+    extra = []
+    if not aligned:
+        parts = jnp.stack([lax.dynamic_index_in_dim(jnp.stack(blocks), me[0] ^ j, 0, keepdims=False) for j in range(PLANE)])
+        parts = parts[:, :, width:].reshape(PLANE, rows, inner // tall, PLANE, rows)
+        extra = [jnp.transpose(parts, (3, 1, 2, 0, 4)).reshape(tall, inner)]
 
     def plan(place, ins, outs):
         copies = []
         for k in range(PLANE):
-            if column_blocks:
-                copies.append((ins[k], outs[0].at[lanes(place ^ k, rows), pl.ds(0, width)]))
-        for k, block in enumerate(ins[len(column_blocks) :]):
-            for g in range(groups):
-                at = width + g * tall
-                if aligned:
-                    spot = pl.ds(pl.multiple_of(at + (place ^ k) * cols, cols), cols)
-                else:
-                    spot = pl.ds(at, tall)
-                copies.append((block.at[pl.ds(g * tall, tall)], outs[0].at[:, spot]))
+            copies.append((ins[k].at[:, pl.ds(0, width)], outs[0].at[lanes(place ^ k, rows), pl.ds(0, width)]))
+            for block in range(inner // rows if aligned else 0):
+                spot = pl.ds(pl.multiple_of(width + (place ^ k) * rows, rows), rows)
+                if block >= PLANE:
+                    spot = pl.ds(pl.multiple_of(width + (block // PLANE) * tall + (place ^ k) * rows, rows), rows)
+                source = ins[k].at[:, pl.ds(width + block * rows, rows)]
+                copies.append((source, outs[0].at[pl.ds((block % PLANE) * rows, rows), spot]))
+        if not aligned:
+            copies.append((ins[PLANE], outs[0].at[:, pl.ds(width, inner)]))
         return copies
 
-    n_copies = len(column_blocks) + len(extra) * groups
-    shape = shaped((tall, width + groups * tall), bf16)
-    return place_copies(plan, n_copies, me, [*column_blocks, *extra], [shape])[0]
+    n_copies = PLANE * (1 + inner // rows) if aligned else PLANE + 1
+    return place_copies(plan, n_copies, me, [*blocks, *extra], [shaped((tall, width + inner), bf16)])[0]
 
 
 def load_pieces(pieces, held, sem):
@@ -263,7 +261,8 @@
     far_ref[0, :, columns] = terms[rows:].astype(bf16)
 
 
-def gate_out_kernel(wide, rows_ref, weights, out_weights, retained_ref, gate_ref, gated_ref, near_ref, far_ref):
+def gate_out_kernel(wide, n_kept, rows_ref, weights, out_weights, retained_ref, *refs):
+    gate_ref, gated_ref, near_ref, far_ref = refs[n_kept:]
     retained = retained_ref[...]
     scale = lax.rsqrt(jnp.mean(retained * retained, axis=-1, keepdims=True) + group_floor)
     gate = dot(rows_ref[...], weights[...])
@@ -273,30 +272,36 @@
         split_out(terms, near_ref, far_ref, columns)
 
 
-def gate_out(rows_all, joined, retained, wide):
+def gate_out(lo, hi, rows_all, joined, retained, kept, wide):
     total, width = rows_all.shape
     dv = retained.shape[1]
     slot_len = total // PLANE
     rows = slot_len // 2
-    return pl.pallas_call(
-        functools.partial(gate_out_kernel, wide),
-        grid=(PLANE,),
+
+    def at(cols):
+        return pl.BlockSpec((slot_len, cols), lambda i: (i + lo, 0))
+
+    return pl.pallas_call(
+        functools.partial(gate_out_kernel, wide, len(kept)),
+        grid=(hi - lo,),
         in_specs=[
-            by_slot(slot_len, width),
+            at(width),
             pl.BlockSpec((width, dv), lambda i: (0, 2), pipeline_mode=pl.Buffered(1)),
             pl.BlockSpec((width, dv), lambda i: (0, 3), pipeline_mode=pl.Buffered(1)),
-            by_slot(slot_len, dv),
-        ],
-        out_specs=[by_slot(slot_len, dv), by_slot(slot_len, dv), by_slot(1, rows, width), by_slot(1, rows, width)],
+            at(dv),
+        ]
+        + [ANY] * len(kept),
+        out_specs=[at(dv), at(dv), by_slot(1, rows, width), by_slot(1, rows, width)],
         out_shape=[
             shaped((total, dv), f32),
             shaped((total, dv), bf16),
-            shaped((PLANE, rows, width), f32),
-            shaped((PLANE, rows, width), bf16),
+            shaped((hi - lo, rows, width), f32),
+            shaped((hi - lo, rows, width), bf16),
         ],
-        compiler_params=params(),
-        cost_estimate=cost(4 * total * width * dv, 40e6),
-    )(rows_all, joined, joined, retained)
+        input_output_aliases={4 + i: i for i in range(len(kept))},
+        compiler_params=params(),
+        cost_estimate=cost((hi - lo) * total * width * dv, (hi - lo) * 10e6),
+    )(rows_all, joined, joined, retained, *kept)
 
 
 def project_kernel(wide, left, right, near_ref, far_ref):
@@ -348,74 +353,38 @@
     )(left, joined, joined)
 
 
-def fold_kernel(spots, n, *refs):
-    nears, arriveds = refs[:n], refs[n : 2 * n]
-    x_ref, y_ref, keep_x_ref, keep_y_ref = refs[2 * n :]
-    half = x_ref.shape[1]
-
-    def summed(k, lo):
-        i, j = spots[k]
-        return nears[i][j, lo : lo + half] + arriveds[i][j, lo : lo + half].astype(f32)
-
-    x_ref[0] = summed(1, 0).astype(bf16)
-    x_ref[1] = summed(3, 0).astype(bf16)
-    y_ref[0] = summed(2, half).astype(bf16)
-    y_ref[1] = summed(3, half).astype(bf16)
-    keep_x_ref[...] = summed(1, half)
-    keep_y_ref[...] = summed(2, 0)
-
-
-def fold_cut(nears, arriveds):
-    spots = [(i, j) for i, near in enumerate(nears) for j in range(near.shape[0])]
+def fold_kernel(*refs):
+    nears, arriveds = refs[:3], refs[3:6]
+    x1_ref, y2_ref, x3_ref, y3_ref, keep_x_ref, keep_y_ref = refs[6:]
+    half = x1_ref.shape[0]
+    targets = ((x1_ref, keep_x_ref), (keep_y_ref, y2_ref), (x3_ref, y3_ref))
+    for near, arrived, (first, second) in zip(nears, arriveds, targets):
+        first[...] = (near[0, :half] + arrived[0, :half].astype(f32)).astype(first.dtype)
+        second[...] = (near[0, half:] + arrived[0, half:].astype(f32)).astype(second.dtype)
+
+
+def fold_cut(slots):
+    nears, arriveds, spots = zip(*slots)
     _, rows, width = nears[0].shape
     half = rows // 2
     part = width // 4
-
-    def cols(*shape):
-        return pl.BlockSpec((*shape, part), lambda i: (0,) * len(shape) + (i,))
-
-    given = [cols(near.shape[0], rows) for near in nears]
-    return pl.pallas_call(
-        functools.partial(fold_kernel, spots, len(nears)),
+    kinds = (bf16, bf16, bf16, bf16, f32, f32)
+    given = [pl.BlockSpec((1, rows, part), lambda i, spot=spot: (spot, 0, i)) for spot in spots]
+    return pl.pallas_call(
+        fold_kernel,
         grid=(width // part,),
         in_specs=given + given,
-        out_specs=[cols(2, half), cols(2, half), cols(half), cols(half)],
-        out_shape=[
-            shaped((2, half, width), bf16),
-            shaped((2, half, width), bf16),
-            shaped((half, width), f32),
-            shaped((half, width), f32),
-        ],
-        compiler_params=params(),
-        cost_estimate=cost(1e6, 20e6),
+        out_specs=[pl.BlockSpec((half, part), lambda i: (0, i))] * len(kinds),
+        out_shape=[shaped((half, width), kind) for kind in kinds],
+        compiler_params=params(),
+        cost_estimate=cost(1e6, 12e6),
     )(*nears, *arriveds)
 
 
-def dot_back_kernel(wide, back, right, out_ref):
-    out_ref[...] = times_rows_back(back[...], right[...], wide)
-
-
-def dot_back(back, joined, inner, start, wide):
-    total, width = back.shape
-    slot_len = total // PLANE
-    return pl.pallas_call(
-        functools.partial(dot_back_kernel, wide),
-        grid=(PLANE,),
-        in_specs=[
-            by_slot(slot_len, width),
-            pl.BlockSpec((width, inner), lambda i: (0, start // inner), pipeline_mode=pl.Buffered(1)),
-        ],
-        out_specs=by_slot(slot_len, inner),
-        out_shape=shaped((total, inner), f32),
-        compiler_params=params(),
-        cost_estimate=cost(2 * total * width * inner, 20e6),
-    )(back, joined)
-
-
-def hidden_kernel(first, n, n_kept, *refs):
-    pieces, (weights, grad_in) = refs[: 2 * n], refs[2 * n : 2 * n + 2]
-    act_ref, grad_ref, rows_ref, near_ref, far_ref = refs[2 * n + 2 + n_kept : 2 * n + 7 + n_kept]
-    held, sem, out_sem = refs[2 * n + 7 + n_kept :]
+def hidden_kernel(first, wide, n, n_kept, *refs):
+    pieces, (weights, down_weights, back) = refs[: 2 * n], refs[2 * n : 2 * n + 3]
+    act_ref, grad_ref, rows_ref, near_ref, far_ref = refs[2 * n + 3 + n_kept : 2 * n + 8 + n_kept]
+    held, sem, out_sem = refs[2 * n + 8 + n_kept :]
     rows = load_pieces(pieces, held, sem)
     step = pl.program_id(0)
     slot_len = rows.shape[0]
@@ -433,27 +402,31 @@
     rise = 0.5 * (1.0 + slope) + 0.5 * up * (1.0 - slope * slope) * (
         tanh_scale * (1.0 + 3.0 * tanh_cubic * (up * up))
     )
-    grad = grad_in[...]
+    grad = times_rows_back(back[...], down_weights[...], wide)
     grad_ref[:, :inner] = (grad * value * rise).astype(bf16)
     grad_ref[:, inner:] = (grad * gelu).astype(bf16)
     split_out(dot_nt(grad_ref[...], weights), near_ref, far_ref, slice(None))
     keep.wait()
 
 
-def hidden_units(first, pieces, joined, grad_in, kept):
+def hidden_units(first, pieces, joined, back, kept, inner, wide):
     n = len(pieces) // 2
     rows, width = pieces[0].shape
     slot_len = 2 * rows
-    total, inner = grad_in.shape
+    total = back.shape[0]
 
     def at(cols):
         return pl.BlockSpec((slot_len, cols), lambda i: (i + first, 0))
 
     return pl.pallas_call(
-        functools.partial(hidden_kernel, first, n, len(kept)),
+        functools.partial(hidden_kernel, first, wide, n, len(kept)),
         grid=(n,),
         in_specs=[ANY] * (2 * n)
-        + [pl.BlockSpec((width, 2 * inner), lambda i: (0, 0), pipeline_mode=pl.Buffered(1)), at(inner)]
+        + [
+            pl.BlockSpec((width, 2 * inner), lambda i: (0, 0), pipeline_mode=pl.Buffered(1)),
+            pl.BlockSpec((width, inner), lambda i: (0, 2), pipeline_mode=pl.Buffered(1)),
+            at(width),
+        ]
         + [ANY] * len(kept),
         out_specs=[at(inner), at(2 * inner), ANY, by_slot(1, rows, width), by_slot(1, rows, width)],
         out_shape=[
@@ -468,10 +441,10 @@
             pltpu.SemaphoreType.DMA((2 * n,)),
             pltpu.SemaphoreType.DMA,
         ],
-        input_output_aliases={2 * n + 2 + i: i for i in range(len(kept))},
-        compiler_params=params(),
-        cost_estimate=cost(8 * n * slot_len * width * inner, 15e6),
-    )(*pieces, joined, grad_in, *kept)
+        input_output_aliases={2 * n + 3 + i: i for i in range(len(kept))},
+        compiler_params=params(),
+        cost_estimate=cost(10 * n * slot_len * width * inner, 15e6),
+    )(*pieces, joined, joined, back, *kept)
 
 
 def retain_back_kernel(first, wide, n, n_kept, *refs):
@@ -671,22 +644,40 @@
     return pieces + nearer + far
 
 
-def fold(nears, fars, count, beside=None):
-    arriveds = [swap(far) for far in fars]
-    to_x, to_y, keep_x, keep_y = fold_cut(nears, arriveds)
-    from_x = hop(to_x, 1, count)
-    from_y = hop(to_y, 2, count)
-    made = None
-    if beside:
-        made = beside((to_x, to_y))
-        from_x, from_y = after((from_x, from_y), made)
-    last_y = hop((keep_y + from_x[1].astype(f32)).astype(bf16), 2, count)
-    last_x = hop((keep_x + from_y[1].astype(f32)).astype(bf16), 1, count)
-    added = jnp.concatenate(
-        [from_x[0].astype(f32) + last_y.astype(f32), from_y[0].astype(f32) + last_x.astype(f32)]
-    )
-    summed = nears[0][0] + arriveds[0][0].astype(f32) + added
-    return (summed, made) if beside else summed
+def fold(groups, count, before=(), first=None, second=None):
+    slots = {}
+
+    def take(lo, near, far):
+        arrived = swap(far)
+        for k in range(near.shape[0]):
+            slots[lo + k] = near, arrived, k
+
+    for group in groups:
+        take(*group)
+    given = after([(near, arrived) for near, arrived, _ in (slots[k] for k in (1, 2, 3))], before)
+    cut = fold_cut([(*pair, slots[k][2]) for k, pair in zip((1, 2, 3), given)])
+    to_x1, to_y2, to_x3, to_y3, keep_x, keep_y = cut
+    half, width = to_x1.shape
+    x1, y2 = hop(to_x1, 1, count), hop(to_y2, 2, count)
+    x3, y3 = hop(to_x3, 1, count), hop(to_y3, 2, count)
+    made = []
+    if first:
+        made.append(first((to_x3, to_y3)))
+        x3, y3 = after((x3, y3), made)
+    if 0 not in slots:
+        take(*made[0][0])
+    near_0, arrived_0, spot = slots[0]
+    to_y, to_x = (keep_y + x3.astype(f32)).astype(bf16), (keep_x + y3.astype(f32)).astype(bf16)
+    last_y, last_x = hop(to_y, 2, count), hop(to_x, 1, count)
+    if second:
+        made.append(second((to_x, to_y), made))
+        last_y, last_x = after((last_y, last_x), made[-1])
+    near_0, arrived_0 = near_0[spot], arrived_0[spot].astype(f32)
+    summed = [
+        near_0[:half] + arrived_0[:half] + (x1.astype(f32) + last_y.astype(f32)),
+        near_0[half:] + arrived_0[half:] + (y2.astype(f32) + last_x.astype(f32)),
+    ]
+    return jnp.concatenate(summed), *made
 
 
 def after(values, done):
@@ -729,9 +720,8 @@
     def sum_depth(block):
         return lax.psum_scatter(block, "dp", scatter_dimension=0, tiled=True, axis_index_groups=columns)
 
-    attn_cuts = cut_columns(me_scalar, (w_query, w_key, w_value, w_gate)), cut_rows(me_scalar, w_out)
-    attn_blocks = [trade(cuts, count) for cuts in attn_cuts]
-    attn_own = join_weights(me_scalar, *attn_blocks)
+    attn_cuts = cut_weights(me_scalar, (w_query, w_key, w_value, w_gate), w_out)
+    attn_own = join_weights(me_scalar, trade(attn_cuts, count), 2 * dk + 2 * dv)
     attn_joined = gather_depth(attn_own)
 
     gains = jnp.stack([gain_attn, gain_mlp])[None]
@@ -748,42 +738,55 @@
     normed_attn = (input_rows * first_scale * gain_first).astype(bf16)
     attn_pieces = spread(after(normed_attn, attn_own), count)
 
-    ff_cuts = after((cut_columns(me_scalar, (w_ffgate, w_ffup)), cut_rows(me_scalar, w_ffdown)), attn_pieces)
-    ff_blocks = [trade(cuts, count) for cuts in ff_cuts]
-    ff_own = join_weights(me_scalar, *ff_blocks)
+    ff_cuts = after(cut_weights(me_scalar, (w_ffgate, w_ffup), w_ffdown), attn_pieces)
+    ff_own = join_weights(me_scalar, trade(ff_cuts, count), 2 * inner)
     ff_joined = gather_depth(ff_own)
 
     local = jnp.arange(rows, dtype=jnp.int32)
     valid_rows = ((core * rows + local) < lengths[0]).astype(f32)[:, None]
     back_rows = valid_rows * cotangent.astype(f32)
-    back_all = jnp.concatenate(spread(after(back_rows.astype(bf16), ff_own), count))
+    back_pieces = spread(after(back_rows.astype(bf16), ff_own), count)
+    back_all = jnp.concatenate(back_pieces)
 
     positions = jnp.concatenate([core * rows + local, (1 - core) * rows + local])
     decays = decay_table(positions, core * PLANE + me)
     attn_pieces = after(attn_pieces, back_all)
     query, key, value, scores, retained, attn_all = retain(attn_pieces, attn_joined, decays, dk, dv)
-    gate, gated, near, far = gate_out(attn_all, attn_joined, retained, wide)
-    hidden = input_rows + fold([near], [far], count)
+    kept, groups = [], []
+    for lo, hi in (SLOTS[1], SLOTS[2]):
+        *kept, near, far = gate_out(lo, hi, attn_all, attn_joined, retained, kept, wide)
+        groups.append((lo, near, far))
+
+    def gate_own(done):
+        lo, hi = SLOTS[0]
+        *made, near, far = gate_out(lo, hi, after(attn_all, done), attn_joined, retained, kept, wide)
+        return (lo, near, far), made
+
+    added, (_, (gate, gated)) = fold(groups, count, first=gate_own)
+    hidden = input_rows + added
 
     second_scale = lax.rsqrt(jnp.mean(hidden * hidden, axis=-1, keepdims=True) + norm_eps)
     normed_mlp = (hidden * second_scale * gain_second).astype(bf16)
 
-    grad_inner = dot_back(back_all, ff_joined, inner, 2 * inner, wide)
-    state = {"kept": (), "nears": [], "fars": []}
+    state = {"kept": (), "groups": []}
 
     def units(lo, hi, pieces):
-        *state["kept"], near, far = hidden_units(lo, pieces, ff_joined, grad_inner, state["kept"])
-        state["nears"].append(near)
-        state["fars"].append(far)
+        if lo == 0:
+            state["own"] = pieces
+            return ()
+        if lo == 1:
+            lo, pieces = 0, state["own"] + pieces
+        *state["kept"], near, far = hidden_units(lo, pieces, ff_joined, back_all, state["kept"], inner, wide)
+        state["groups"].append((lo, near, far))
         return state["kept"]
 
     inner_act, grad_up, mlp_all = spread(normed_mlp, count, units)
-
-    def ff_grads(done):
-        act, back, left, right = after((inner_act, back_all, mlp_all, grad_up), done)
-        return rows_grad(act, back, wide), columns_grad(left, right, 0, 2 * inner)
-
-    grad_normed, (grad_down, grad_ff) = fold(state["nears"], state["fars"], count, ff_grads)
+    grad_down = rows_grad(inner_act, back_all, wide)
+
+    def up_grad(done):
+        return columns_grad(*after((mlp_all, grad_up), done), 0, 2 * inner)
+
+    grad_normed, grad_ff = fold(state["groups"], count, before=grad_down, first=up_grad)
     down_part = sum_depth(grad_down)
     ff_part = sum_depth(grad_ff)
     scaled = grad_normed * gain_second
@@ -793,20 +796,36 @@
     )
     gain_term_mlp = jnp.sum(grad_normed * hidden * second_scale, axis=0)
 
-    state["kept"] = ()
+    state = {"kept": ()}
 
     def heads(lo, hi, pieces):
+        if lo == 3:
+            pieces = after(pieces, down_part)
         state["kept"] = retain_back(
             lo, pieces, attn_joined, decays, query, key, value, gate, scores, retained, state["kept"], wide
         )
-        return state["kept"]
+        if lo > 0:
+            return state["kept"]
+        act = after(inner_act, pieces)
+        state["mlp"] = project(act, ff_joined[:, 2 * inner :], wide)
+        return state["kept"], state["mlp"]
 
     grad_wide, attn_grad_all = spread(grad_hidden.astype(bf16), count, heads)
-    out_part = sum_depth(rows_grad(gated, attn_grad_all, wide))
-    wide_part = sum_depth(columns_grad(attn_all, grad_wide, 0, 2 * dv + 2 * dk))
-
-    near, far = project_back(grad_wide, attn_joined, dk, dv)
-    grad_normed_attn = fold([near], [far], count)
+    grad_out = rows_grad(gated, attn_grad_all, wide)
+    out_part = sum_depth(grad_out)
+
+    def wide_grad(done):
+        return columns_grad(attn_all, after(grad_wide, done), 0, 2 * dv + 2 * dk)
+
+    def back_terms(done, made):
+        return project_back(after(grad_wide, (done, ff_part)), attn_joined, dk, dv)
+
+    mlp_added, grad_wide_weights, (near, far) = fold(
+        [(0, *state["mlp"])], count, before=grad_out, first=wide_grad, second=back_terms
+    )
+    wide_part = sum_depth(grad_wide_weights)
+    output = (valid_rows * (hidden + mlp_added)).astype(bf16)
+    grad_normed_attn, _ = fold([(0, near, far)], count, first=lambda done: out_part)
     gain_term_attn = jnp.sum(grad_normed_attn * input_rows * first_scale, axis=0)
     scaled_first = grad_normed_attn * gain_first
     tokens_grad = grad_hidden + first_scale * (
@@ -816,10 +835,6 @@
         * jnp.mean(input_rows * scaled_first, axis=-1, keepdims=True)
     )
     tokens_grad = tokens_grad.astype(bf16)
-
-    down_weights = ff_joined[:, 2 * inner :]
-    near, far = project(after(inner_act, attn_grad_all), down_weights, wide)
-    output = (valid_rows * (hidden + fold([near], [far], count))).astype(bf16)
 
     gain_terms = jnp.stack([gain_term_attn, gain_term_mlp])
     bit = count // 2
@@ -834,7 +849,6 @@
     kept = lax.dynamic_index_in_dim(cut, core, 1, keepdims=False)
     sent = lax.dynamic_index_in_dim(cut, 1 - core, 1, keepdims=False)
     gain_terms = kept + swap(sent)
-    wide_part = after(wide_part, (output, tokens_grad, gain_terms))
 
     def back_columns(block, widths):
         cuts = [lax.dynamic_slice_in_dim(block, (me ^ k) * shard, shard, 0).astype(bf16) for k in range(PLANE)]
@@ -847,7 +861,8 @@
     down_sum = back_rows_of(down_part)
     ffgate_sum, ffup_sum = back_columns(ff_part, (inner, inner))
     out_sum = back_rows_of(out_part)
-    value_sum, gate_sum, query_sum, key_sum = back_columns(wide_part, (dv, dv, dk, dk))
+    early = output, tokens_grad, gain_terms, down_sum, ffgate_sum, ffup_sum, out_sum
+    value_sum, gate_sum, query_sum, key_sum = back_columns(after(wide_part, early), (dv, dv, dk, dk))
 
     return (
         output,

time: 728 us -> 686 us (0.942)
  waiting for transfers between devices: 280 us -> 253 us
    all_gather x2, waiting for transfers between devices: 29.5 us -> 11 us  [gather_depth(): lax.all_gather(block, 'dp', axis=0, tiled=True, axis_index_groups=columns)]
    ppermute x64 -> x66, waiting for transfers between devices: 235 us -> 228 us  [hop(): return lax.ppermute(value, 'dp', [(i, i ^ bits) for i in range(count)])]
    ppermute x64 -> x66, starting transfers between devices: 81.8 us -> 75.8 us  [hop(): return lax.ppermute(value, 'dp', [(i, i ^ bits) for i in range(count)])]
    convert_element_type x10 -> x14, other arithmetic: 14 us -> 18.1 us  [the longest x4 6.06 us: fold(): near_0, arrived_0 = (near_0[spot], arrived_0[spot].astype(f32))]
    unnamed x142 -> x126, local copies, waits for them, and re-layouts: 31.2 us -> 28.8 us
    ppermute x23 -> x24, waiting for transfers between devices: 15.6 us -> 14.3 us  [swap(): return lax.ppermute(value, 'tensor', [(0, 1), (1, 0)])]
  transfers between devices with their start and end apart: 93 -> 96, of which waited for: 39 -> 45; matrix products, arithmetic and copies ran while one was open for 12% -> 12% of each run, Pallas kernels for 29% -> 30%
where the time goes in v3:
time: 686 us; the launch traced here: 681 us
  waiting for transfers between devices  253 us (37%)
  Pallas kernels  233 us (34%)
  starting transfers between devices  80.3 us (12%)
  local copies, waits for them, and re-layouts  55.8 us (8%)
  other arithmetic  42 us (6%)
  between operations  16.4 us (2%)
    ppermute x66, waiting for transfers between devices, hop(): return lax.ppermute(value, 'dp', [(i, i ^ bits) for i in range(count)])  228 us
    ppermute x66, starting transfers between devices, hop(): return lax.ppermute(value, 'dp', [(i, i ^ bits) for i in range(count)])  75.8 us
    pallas_call x2, Pallas kernels, hidden_units(): pl.pallas_call(functools.partial(hidden_kernel, first, wide, n, len(kept)...  37.8 us
    pallas_call x2, Pallas kernels, columns_grad(): pl.pallas_call(grad_kernel, grid=(width // part,), in_specs=[pl.BlockSpec...  31.9 us
    pallas_call x3, Pallas kernels, retain_back(): pl.pallas_call(functools.partial(retain_back_kernel, first, wide, n, len(...  30.5 us
    unnamed x126, local copies, waits for them, and re-layouts  28.8 us
    pallas_call x4, Pallas kernels, fold_cut(): pl.pallas_call(fold_kernel, grid=(width // part,), in_specs=given + given...  24.2 us
    pallas_call x3, Pallas kernels, gate_out(): pl.pallas_call(functools.partial(gate_out_kernel, wide, len(kept)), grid=...  24.1 us
  transfers between devices with their start and end apart: 96, of which 45 were waited for; matrix products, arithmetic and copies ran while one was open for 12% of the time, Pallas kernels for 30%

profile of v3, /device:TPU:0, one launch (start us, length us, event | category | flops | bytes accessed | tf_op | source)
XLA Modules:
  0.0 680.5 jit_solution(601071060463318025)
XLA Ops:
  7.2 3.1 shard_map.220
  14.9 11.4 %collective-permute-done.4.refs_1_ = bf16[128,2048]{1,0:T(8,128)(2,1)S(1)} collective-permute-done((bf16[128,2048]{1,0:T(8,128)(2,1)}, bf16[128,2048]{1,0:T(8,128)(2,1)S(1)}, u32[]{:S(2)}, u32[]{:S(2)}) %collective-permute-start.4) | collective-permute-done | bytes 524320 | tf_op jit(solution)/shard_map/ppermute | solution.py:617
  26.3 11.9 %collective-permute-done.5.refs_2_ = bf16[128,2048]{1,0:T(8,128)(2,1)S(1)} collective-permute-done((bf16[128,2048]{1,0:T(8,128)(2,1)}, bf16[128,2048]{1,0:T(8,128)(2,1)S(1)}, u32[]{:S(2)}, u32[]{:S(2)}) %collective-permute-start.5) | collective-permute-done | bytes 524320 | tf_op jit(solution)/shard_map/ppermute | solution.py:617
  39.1 3.1 shard_map.221
  56.4 6.0 collective-permute-done.3
  67.3 18.0 %collective-permute-done.8.refs_2_ = bf16[256,2048]{1,0:T(8,128)(2,1)} collective-permute-done((bf16[256,2048]{1,0:T(8,128)(2,1)}, bf16[256,2048]{1,0:T(8,128)(2,1)}, u32[]{:S(2)}, u32[]{:S(2)}) %collective-permute-start.8) | collective-permute-done | bytes 1048608 | tf_op jit(solution)/shard_map/ppermute | solution.py:617
  90.8 4.9 collective-permute-done.12
  108.2 6.2 collective-permute-done.15.refs_1_
  114.4 9.2 %collective-permute-done.16.refs_2_ = bf16[128,1536]{1,0:T(8,128)(2,1)S(1)} collective-permute-done((bf16[128,1536]{1,0:T(8,128)(2,1)}, bf16[128,1536]{1,0:T(8,128)(2,1)S(1)}, u32[]{:S(2)}, u32[]{:S(2)}) %collective-permute-start.16) | collective-permute-done | bytes 393248 | tf_op jit(solution)/shard_map/ppermute | solution.py:617
  128.4 23.7 %collective-permute-done.19 = bf16[256,2048]{1,0:T(8,128)(2,1)} collective-permute-done((bf16[256,2048]{1,0:T(8,128)(2,1)}, bf16[256,2048]{1,0:T(8,128)(2,1)}, u32[]{:S(2)}, u32[]{:S(2)}) %collective-permute-start.19) | collective-permute-done | bytes 1048608 | tf_op jit(solution)/shard_map/ppermute | solution.py:617
  164.9 5.0 collective-permute-done.23
  182.7 9.8 %all-gather.3.cloned.1.call-done.refs_8_.weights.out_weights.refs_2_.refs_4_.first.second = bf16[2048,2048]{1,0:T(8,128)(2,1)} async-done(((bf16[512,2048]{1,0:T(8,128)(2,1)}), bf16[2048,2048]{1,0:T(8,128)(2,1)}) %all-gather.3.cloned.1.call-update) | async-done | bytes 8388624 | tf_op jit(solution)/shard_map/all_gather | solution.py:718
  192.5 17.4 %shard_map.224 = (bf16[2048,256]{1,0:T(8,128)(2,1)}, bf16[2048,256]{1,0:T(8,128)(2,1)}, bf16[2048,512]{1,0:T(8,128)(2,1)}, bf16[4,512,512]{2,1,0:T(8,128)(2,1)},...) custom-call(bf16[256,2048]{1,0:T(8,128)(2,1)} %fusion.2.refs_0_, bf16[256,2048]{1,0:T(8,128)(2,1)} %collective-permute-done.7.refs_1_, ...), custom_call_target="tpu_custom_call" | custom-call | flops 9448928256 | bytes 30000000 | tf_op jit(solution)/shard_map/pallas_call | solution.py:204
  209.9 9.7 %shard_map.225 = (f32[2048,512]{1,0:T(8,128)}, bf16[2048,512]{1,0:T(8,128)(2,1)}, f32[2,256,2048]{2,1,0:T(8,128)}, bf16[2,256,2048]{2,1,0:T(8,128)(2,1)}) custom-call(bf16[2048,2048]{1,0:T(8,128)(2,1)} %get-tuple-element.191.rows_ref.left, bf16[2048,2048]{1,0:T(8,128)(2,1)} %all-gather.3.cloned.1.call-done.refs_8_.weights.out_weights.refs_2_.refs_4_.first.second, ...), custom_call_target="tpu_custom_call" | custom-call | flops 4294967296 | bytes 20000000 | tf_op jit(solution)/shard_map/pallas_call | solution.py:284
  219.7 7.1 %shard_map.226 = (f32[2048,512]{1,0:T(8,128)}, bf16[2048,512]{1,0:T(8,128)(2,1)}, f32[1,256,2048]{2,1,0:T(8,128)}, bf16[1,256,2048]{2,1,0:T(8,128)(2,1)}) custom-call(bf16[2048,2048]{1,0:T(8,128)(2,1)} %get-tuple-element.191.rows_ref.left, ...), custom_call_target="tpu_custom_call", output_to_operand_aliasing={{0}: (4, {}), {1}: (5, {})} | custom-call | flops 2147483648 | bytes 10000000 | tf_op jit(solution)/shard_map/pallas_call | solution.py:284
  229.9 6.0 shard_map.227
  238.9 7.2 %shard_map.228 = (f32[2048,512]{1,0:T(8,128)}, bf16[2048,512]{1,0:T(8,128)(2,1)}, f32[1,256,2048]{2,1,0:T(8,128)}, bf16[1,256,2048]{2,1,0:T(8,128)(2,1)}) custom-call(bf16[2048,2048]{1,0:T(8,128)(2,1)} %get-tuple-element.191.rows_ref.left, ...), custom_call_target="tpu_custom_call", output_to_operand_aliasing={{0}: (4, {}), {1}: (5, {})} | custom-call | flops 2147483648 | bytes 10000000 | tf_op jit(solution)/shard_map/pallas_call | solution.py:284
  247.2 3.7 collective-permute-done.30
  256.6 5.6 collective-permute-done.29
  263.7 9.2 %collective-permute-done.34 = bf16[128,2048]{1,0:T(8,128)(2,1)S(1)} collective-permute-done((bf16[128,2048]{1,0:T(8,128)(2,1)S(1)}, bf16[128,2048]{1,0:T(8,128)(2,1)S(1)}, u32[]{:S(2)}, u32[]{:S(2)}) %collective-permute-start.34) | collective-permute-done | bytes 524320 | tf_op jit(solution)/shard_map/ppermute | solution.py:617
  277.5 22.4 %collective-permute-done.35.refs_2_ = bf16[256,2048]{1,0:T(8,128)(2,1)S(1)} collective-permute-done((bf16[256,2048]{1,0:T(8,128)(2,1)S(1)}, bf16[256,2048]{1,0:T(8,128)(2,1)S(1)}, u32[]{:S(2)}, u32[]{:S(2)}) %collective-permute-start.35) | collective-permute-done | bytes 1048608 | tf_op jit(solution)/shard_map/ppermute | solution.py:617
  307.6 24.9 %shard_map.229 = (bf16[2048,512]{1,0:T(8,128)(2,1)}, bf16[2048,1024]{1,0:T(8,128)(2,1)}, bf16[2048,2048]{1,0:T(8,128)(2,1)}, f32[3,256,2048]{2,1,0:T(8,128)}, bf16[3,256,2048]{2,1,0:T(8,128)(2,1)}) custom-call(bf16[256,2048]{1,0:T(8,128)(2,1)} %copy-done.15, bf16[256,2048]{1,0:T(8,128)(2,1)} %collective-permute-done.39.refs_1_, ...), custom_call_target="tpu_custom_call" | custom-call | flops 16106127360 | bytes 15000000 | tf_op jit(solution)/shard_map/pallas_call | solution.py:421
  336.6 13.0 %shard_map.230 = (bf16[2048,512]{1,0:T(8,128)(2,1)}, bf16[2048,1024]{1,0:T(8,128)(2,1)}, bf16[2048,2048]{1,0:T(8,128)(2,1)}, f32[1,256,2048]{2,1,0:T(8,128)}, bf16[1,256,2048]{2,1,0:T(8,128)(2,1)}) custom-call(bf16[256,2048]{1,0:T(8,128)(2,1)} %copy-done.10, ...), custom_call_target="tpu_custom_call", output_to_operand_aliasing={{0}: (5, {}), {1}: (6, {}), {2}: (7, {})} | custom-call | flops 5368709120 | bytes 15000000 | tf_op jit(solution)/shard_map/pallas_call | solution.py:421
  349.5 8.8 %shard_map.231 = bf16[2048,512]{1,0:T(8,128)(2,1)} custom-call(bf16[2048,512]{1,0:T(8,128)(2,1)} %get-tuple-element.234.left, bf16[2048,2048]{1,0:T(8,128)(2,1)} %constant_dynamic-update-slice_fusion.7.refs_8_.refs_4_.right), custom_call_target="tpu_custom_call" | custom-call | flops 4294967296 | bytes 20000000 | tf_op jit(solution)/shard_map/pallas_call | solution.py:541
  359.7 5.9 collective-permute-done.44.refs_5_
  366.6 5.9 shard_map.232
  376.7 13.4 %shard_map.233 = bf16[2048,1024]{1,0:T(8,128)(2,1)} custom-call(bf16[2048,2048]{1,0:T(8,128)(2,1)} %get-tuple-element.228.left, bf16[2048,1024]{1,0:T(8,128)(2,1)} %get-tuple-element.229.right), custom_call_target="tpu_custom_call" | custom-call | flops 8589934592 | bytes 20000000 | tf_op jit(solution)/shard_map/pallas_call | solution.py:524
  400.4 8.9 %collective-permute-done.50 = bf16[128,2048]{1,0:T(8,128)(2,1)S(1)} collective-permute-done((bf16[128,2048]{1,0:T(8,128)(2,1)S(1)}, bf16[128,2048]{1,0:T(8,128)(2,1)S(1)}, u32[]{:S(2)}, u32[]{:S(2)}) %collective-permute-start.50) | collective-permute-done | bytes 524320 | tf_op jit(solution)/shard_map/ppermute | solution.py:617
  418.0 3.1 slice.166.right
  422.1 8.5 %shard_map.235 = (bf16[2048,1536]{1,0:T(8,128)(2,1)}, bf16[2048,2048]{1,0:T(8,128)(2,1)}) custom-call(bf16[256,2048]{1,0:T(8,128)(2,1)} %copy-done.7, bf16[256,2048]{1,0:T(8,128)(2,1)} %copy-done.13, bf16[2048,2048]{1,0:T(8,128)(2,1)} %all-gather.3.cloned.1.call-done.refs_8_.weights.out_weights.refs_2_.refs_4_.first.second, ...), custom_call_target="tpu_custom_call" | custom-call | flops 2147483648 | bytes 15000000 | tf_op jit(solution)/shard_map/pallas_call | solution.py:489
  430.5 8.9 %shard_map.234 = (f32[4,256,2048]{2,1,0:T(8,128)}, bf16[4,256,2048]{2,1,0:T(8,128)(2,1)}) custom-call(bf16[2048,512]{1,0:T(8,128)(2,1)} %get-tuple-element.234.left, bf16[2048,512]{1,0:T(8,128)(2,1)} %slice.166.right), custom_call_target="tpu_custom_call" | custom-call | flops 4294967296 | bytes 20000000 | tf_op jit(solution)/shard_map/pallas_call | solution.py:317
  450.1 13.6 %shard_map.236 = (bf16[2048,1536]{1,0:T(8,128)(2,1)}, bf16[2048,2048]{1,0:T(8,128)(2,1)}) custom-call(bf16[256,2048]{1,0:T(8,128)(2,1)} %collective-permute-done.53.refs_0_, bf16[256,2048]{1,0:T(8,128)(2,1)} %copy-done.24, bf16[256,2048]{1,0:T(8,128)(2,1)} %collective-permute-done.54.refs_2_, ...), custom_call_target="tpu_custom_call", output_to_operand_aliasing={{0}: (12, {}), {1}: (13, {})} | custom-call | flops 4294967296 | bytes 15000000 | tf_op jit(solution)/shard_map/pallas_call | solution.py:489
  468.5 8.4 %shard_map.237 = (bf16[2048,1536]{1,0:T(8,128)(2,1)}, bf16[2048,2048]{1,0:T(8,128)(2,1)}) custom-call(bf16[256,2048]{1,0:T(8,128)(2,1)} %copy-done.11, bf16[256,2048]{1,0:T(8,128)(2,1)} %collective-permute-done.59.refs_1_, ...), custom_call_target="tpu_custom_call", output_to_operand_aliasing={{0}: (10, {}), {1}: (11, {})} | custom-call | flops 2147483648 | bytes 15000000 | tf_op jit(solution)/shard_map/pallas_call | solution.py:489
  476.9 8.9 %shard_map.238 = bf16[2048,512]{1,0:T(8,128)(2,1)} custom-call(bf16[2048,512]{1,0:T(8,128)(2,1)} %get-tuple-element.199.left, bf16[2048,2048]{1,0:T(8,128)(2,1)} %get-tuple-element.251.right), custom_call_target="tpu_custom_call" | custom-call | flops 4294967296 | bytes 20000000 | tf_op jit(solution)/shard_map/pallas_call | solution.py:541
  486.1 6.1 shard_map.239
  493.3 18.5 %shard_map.240 = bf16[2048,1536]{1,0:T(8,128)(2,1)} custom-call(bf16[2048,2048]{1,0:T(8,128)(2,1)} %get-tuple-element.191.rows_ref.left, bf16[2048,1536]{1,0:T(8,128)(2,1)} %get-tuple-element.267.right.left), custom_call_target="tpu_custom_call" | custom-call | flops 12884901888 | bytes 20000000 | tf_op jit(solution)/shard_map/pallas_call | solution.py:524
  514.8 18.9 %shard_map.241 = (f32[4,256,2048]{2,1,0:T(8,128)}, bf16[4,256,2048]{2,1,0:T(8,128)(2,1)}) custom-call(bf16[2048,1536]{1,0:T(8,128)(2,1)} %get-tuple-element.267.right.left, bf16[2048,2048]{1,0:T(8,128)(2,1)} %all-gather.3.cloned.1.call-done.refs_8_.weights.out_weights.refs_2_.refs_4_.first.second, ...), custom_call_target="tpu_custom_call" | custom-call | flops 12884901888 | bytes 20000000 | tf_op jit(solution)/shard_map/pallas_call | solution.py:341
  540.5 4.2 collective-permute-done.79.refs_2_
  548.5 6.2 shard_map.242
  562.7 11.2 %collective-permute-done.68 = bf16[128,2048]{1,0:T(8,128)(2,1)S(1)} collective-permute-done((bf16[128,2048]{1,0:T(8,128)(2,1)}, bf16[128,2048]{1,0:T(8,128)(2,1)S(1)}, u32[]{:S(2)}, u32[]{:S(2)}) %collective-permute-start.68) | collective-permute-done | bytes 524320 | tf_op jit(solution)/shard_map/ppermute | solution.py:617
  578.7 6.3 collective-permute-done.67
  587.9 8.4 %collective-permute-done.72 = bf16[128,2048]{1,0:T(8,128)(2,1)S(1)} collective-permute-done((bf16[128,2048]{1,0:T(8,128)(2,1)S(1)}, bf16[128,2048]{1,0:T(8,128)(2,1)S(1)}, u32[]{:S(2)}, u32[]{:S(2)}) %collective-permute-start.72) | collective-permute-done | bytes 524320 | tf_op jit(solution)/shard_map/ppermute | solution.py:617
  607.2 6.4 collective-permute-done.63
  618.0 4.9 fusion.25
  642.3 3.9 fusion.7
  652.4 7.9 %collective-permute-done.87.refs_1_ = bf16[128,1536]{1,0:T(8,128)(2,1)S(1)} collective-permute-done((bf16[128,1536]{1,0:T(8,128)(2,1)S(1)}, bf16[128,1536]{1,0:T(8,128)(2,1)S(1)}, u32[]{:S(2)}, u32[]{:S(2)}) %collective-permute-start.87) | collective-permute-done | bytes 393248 | tf_op jit(solution)/shard_map/ppermute | solution.py:617
  660.3 8.7 %collective-permute-done.88.refs_2_ = bf16[128,1536]{1,0:T(8,128)(2,1)S(1)} collective-permute-done((bf16[128,1536]{1,0:T(8,128)(2,1)S(1)}, bf16[128,1536]{1,0:T(8,128)(2,1)S(1)}, u32[]{:S(2)}, u32[]{:S(2)}) %collective-permute-start.88) | collective-permute-done | bytes 393248 | tf_op jit(solution)/shard_map/ppermute | solution.py:617
  670.0 3.2 shard_map.246
  (383 shorter events, 216.8 us)
Async XLA Ops:
  7.2 185.3 %all-gather.3.cloned.1.call-start = ((), (), s32[]{:S(2)}) async-start(), calls=%async_computation.4 | async-start | bytes 10485760 | tf_op jit(solution)/shard_map/all_gather | solution.py:718
  13.3 24.8 %collective-permute-start.5 = (bf16[128,2048]{1,0:T(8,128)(2,1)}, bf16[128,2048]{1,0:T(8,128)(2,1)S(1)}, u32[]{:S(2)}, u32[]{:S(2)}) collective-permute-start(bf16[128,2048]{1,0:T(8,128)(2,1)} %get-tuple-element.155), channel_id=1, source_target_pairs={{0,4},{2,6},{4,0},{6,2},{8,12},{10,14},{12,8},{14,10},{16,20},{18,... | collective-permute-start | bytes 1572872 | tf_op jit(solution)/shard_map/ppermute | solution.py:617
  14.9 23.3 %collective-permute-start.6 = (bf16[128,2048]{1,0:T(8,128)(2,1)}, bf16[128,2048]{1,0:T(8,128)(2,1)S(1)}, u32[]{:S(2)}, u32[]{:S(2)}) collective-permute-start(bf16[128,2048]{1,0:T(8,128)(2,1)} %get-tuple-element.156), channel_id=1, source_target_pairs={{0,6},{2,4},{4,2},{6,0},{8,14},{10,12},{12,10},{14,8},{16,22},{18,... | collective-permute-start | bytes 1572872 | tf_op jit(solution)/shard_map/ppermute | solution.py:617
  42.3 265.3 %all-gather.5.cloned.1.call-start = ((), (), s32[]{:S(2)}) async-start(), calls=%async_computation.5 | async-start | bytes 7864320 | tf_op jit(solution)/shard_map/all_gather | solution.py:718
  64.4 20.9 %collective-permute-start.8 = (bf16[256,2048]{1,0:T(8,128)(2,1)}, bf16[256,2048]{1,0:T(8,128)(2,1)}, u32[]{:S(2)}, u32[]{:S(2)}) collective-permute-start(bf16[256,2048]{1,0:T(8,128)(2,1)} %fusion.2.refs_0_), channel_id=1, source_target_pairs={{0,2},{2,0},{4,6},{6,4},{8,10},{10,8},{12,14},{14,12},{16,18},{18,... | collective-permute-start | bytes 3145736 | tf_op jit(solution)/shard_map/ppermute | solution.py:617
  65.9 21.7 %collective-permute-start.10 = (bf16[256,2048]{1,0:T(8,128)(2,1)}, bf16[256,2048]{1,0:T(8,128)(2,1)}, u32[]{:S(2)}, u32[]{:S(2)}) collective-permute-start(bf16[256,2048]{1,0:T(8,128)(2,1)} %fusion.2.refs_0_), channel_id=1, source_target_pairs={{0,4},{2,6},{4,0},{6,2},{8,12},{10,14},{12,8},{14,10},{16,20},{18,... | collective-permute-start | bytes 3145736 | tf_op jit(solution)/shard_map/ppermute | solution.py:617
  103.7 19.9 %collective-permute-start.16 = (bf16[128,1536]{1,0:T(8,128)(2,1)}, bf16[128,1536]{1,0:T(8,128)(2,1)S(1)}, u32[]{:S(2)}, u32[]{:S(2)}) collective-permute-start(bf16[128,1536]{1,0:T(8,128)(2,1)} %get-tuple-element.164), channel_id=1, source_target_pairs={{0,4},{2,6},{4,0},{6,2},{8,12},{10,14},{12,8},{14,10},{16,20},{18,... | collective-permute-start | bytes 1179656 | tf_op jit(solution)/shard_map/ppermute | solution.py:617
  104.6 19.0 %collective-permute-start.17 = (bf16[128,1536]{1,0:T(8,128)(2,1)}, bf16[128,1536]{1,0:T(8,128)(2,1)}, u32[]{:S(2)}, u32[]{:S(2)}) collective-permute-start(bf16[128,1536]{1,0:T(8,128)(2,1)} %get-tuple-element.165), channel_id=1, source_target_pairs={{0,6},{2,4},{4,2},{6,0},{8,14},{10,12},{12,10},{14,8},{16,22},{18,... | collective-permute-start | bytes 1179656 | tf_op jit(solution)/shard_map/ppermute | solution.py:617
  127.1 25.0 %collective-permute-start.19 = (bf16[256,2048]{1,0:T(8,128)(2,1)}, bf16[256,2048]{1,0:T(8,128)(2,1)}, u32[]{:S(2)}, u32[]{:S(2)}) collective-permute-start(bf16[256,2048]{1,0:T(8,128)(2,1)} %fusion.13), channel_id=1, source_target_pairs={{0,2},{2,0},{4,6},{6,4},{8,10},{10,8},{12,14},{14,12},{16,18},{18,... | collective-permute-start | bytes 3145736 | tf_op jit(solution)/shard_map/ppermute | solution.py:617
  127.2 28.1 %collective-permute-start.21 = (bf16[256,2048]{1,0:T(8,128)(2,1)}, bf16[256,2048]{1,0:T(8,128)(2,1)}, u32[]{:S(2)}, u32[]{:S(2)}) collective-permute-start(bf16[256,2048]{1,0:T(8,128)(2,1)} %fusion.13), channel_id=1, source_target_pairs={{0,4},{2,6},{4,0},{6,2},{8,12},{10,14},{12,8},{14,10},{16,20},{18,... | collective-permute-start | bytes 3145736 | tf_op jit(solution)/shard_map/ppermute | solution.py:617
  128.3 31.9 %collective-permute-start.18 = (bf16[256,2048]{1,0:T(8,128)(2,1)}, bf16[256,2048]{1,0:T(8,128)(2,1)}, u32[]{:S(2)}, u32[]{:S(2)}) collective-permute-start(bf16[256,2048]{1,0:T(8,128)(2,1)} %fusion.13), channel_id=1, source_target_pairs={{0,1},{1,0},{2,3},{3,2},{4,5},{5,4},{6,7},{7,6},{8,9},{9,8},{10,11... | collective-permute-start | bytes 3145736 | tf_op jit(solution)/shard_map/ppermute | solution.py:621
  152.1 21.0 %collective-permute-start.20 = (bf16[256,2048]{1,0:T(8,128)(2,1)}, bf16[256,2048]{1,0:T(8,128)(2,1)}, u32[]{:S(2)}, u32[]{:S(2)}) collective-permute-start(bf16[256,2048]{1,0:T(8,128)(2,1)} %collective-permute-done.19), channel_id=1, source_target_pairs={{0,1},{1,0},{2,3},{3,2},{4,5},{5,4},{6,7},{7,6},{8,9},{9,8},{10,11... | collective-permute-start | bytes 3145736 | tf_op jit(solution)/shard_map/ppermute | solution.py:621
  159.5 306.0 %reduce-scatter.5.cloned.1.call-start = ((), (), s32[]{:S(2)}) async-start(), calls=%async_computation.6 | async-start | bytes 2621440 | tf_op jit(solution)/shard_map/reduce_scatter | solution.py:721
  160.1 17.6 %collective-permute-start.22 = (bf16[256,2048]{1,0:T(8,128)(2,1)}, bf16[256,2048]{1,0:T(8,128)(2,1)S(1)}, u32[]{:S(2)}, u32[]{:S(2)}) collective-permute-start(bf16[256,2048]{1,0:T(8,128)(2,1)} %collective-permute-done.21), channel_id=1, source_target_pairs={{0,1},{1,0},{2,3},{3,2},{4,5},{5,4},{6,7},{7,6},{8,9},{9,8},{10,11... | collective-permute-start | bytes 3145736 | tf_op jit(solution)/shard_map/ppermute | solution.py:621
  246.7 17.0 %collective-permute-start.33 = (bf16[128,2048]{1,0:T(8,128)(2,1)}, bf16[128,2048]{1,0:T(8,128)(2,1)S(1)}, u32[]{:S(2)}, u32[]{:S(2)}) collective-permute-start(bf16[128,2048]{1,0:T(8,128)(2,1)} %get-tuple-element.201), channel_id=1, source_target_pairs={{0,4},{2,6},{4,0},{6,2},{8,12},{10,14},{12,8},{14,10},{16,20},{18,... | collective-permute-start | bytes 1572872 | tf_op jit(solution)/shard_map/ppermute | solution.py:617
  254.0 18.8 %collective-permute-start.34 = (bf16[128,2048]{1,0:T(8,128)(2,1)S(1)}, bf16[128,2048]{1,0:T(8,128)(2,1)S(1)}, u32[]{:S(2)}, u32[]{:S(2)}) collective-permute-start(bf16[128,2048]{1,0:T(8,128)(2,1)S(1)} %add_convert_fusion.6), channel_id=1, source_target_pairs={{0,2},{2,0},{4,6},{6,4},{8,10},{10,8},{12,14},{14,12},{16,18},{18,... | collective-permute-start | bytes 1572872 | tf_op jit(solution)/shard_map/ppermute | solution.py:617
  254.8 19.3 %collective-permute-start.32 = (bf16[128,2048]{1,0:T(8,128)(2,1)S(1)}, bf16[128,2048]{1,0:T(8,128)(2,1)S(1)}, u32[]{:S(2)}, u32[]{:S(2)}) collective-permute-start(bf16[128,2048]{1,0:T(8,128)(2,1)S(1)} %add_convert_fusion.7), channel_id=1, source_target_pairs={{0,4},{2,6},{4,0},{6,2},{8,12},{10,14},{12,8},{14,10},{16,20},{18,... | collective-permute-start | bytes 1572872 | tf_op jit(solution)/shard_map/ppermute | solution.py:617
  275.4 24.5 %collective-permute-start.35 = (bf16[256,2048]{1,0:T(8,128)(2,1)S(1)}, bf16[256,2048]{1,0:T(8,128)(2,1)S(1)}, u32[]{:S(2)}, u32[]{:S(2)}) collective-permute-start(bf16[256,2048]{1,0:T(8,128)(2,1)S(1)} %multiply_convert_fusion.refs_0_), channel_id=1, source_target_pairs={{0,2},{2,0},{4,6},{6,4},{8,10},{10,8},{12,14},{14,12},{16,18},{18,... | collective-permute-start | bytes 3145736 | tf_op jit(solution)/shard_map/ppermute | solution.py:617
  276.0 24.3 %collective-permute-start.36 = (bf16[256,2048]{1,0:T(8,128)(2,1)S(1)}, bf16[256,2048]{1,0:T(8,128)(2,1)}, u32[]{:S(2)}, u32[]{:S(2)}) collective-permute-start(bf16[256,2048]{1,0:T(8,128)(2,1)S(1)} %multiply_convert_fusion.refs_0_), channel_id=1, source_target_pairs={{0,4},{2,6},{4,0},{6,2},{8,12},{10,14},{12,8},{14,10},{16,20},{18,... | collective-permute-start | bytes 3145736 | tf_op jit(solution)/shard_map/ppermute | solution.py:617
  277.5 30.1 %collective-permute-start.39 = (bf16[256,2048]{1,0:T(8,128)(2,1)S(1)}, bf16[256,2048]{1,0:T(8,128)(2,1)}, u32[]{:S(2)}, u32[]{:S(2)}) collective-permute-start(bf16[256,2048]{1,0:T(8,128)(2,1)S(1)} %multiply_convert_fusion.refs_0_), channel_id=1, source_target_pairs={{0,1},{1,0},{2,3},{3,2},{4,5},{5,4},{6,7},{7,6},{8,9},{9,8},{10,11... | collective-permute-start | bytes 3145736 | tf_op jit(solution)/shard_map/ppermute | solution.py:621
  303.5 29.0 %collective-permute-start.37 = (bf16[128,2048]{1,0:T(8,128)(2,1)}, bf16[128,2048]{1,0:T(8,128)(2,1)S(1)}, u32[]{:S(2)}, u32[]{:S(2)}) collective-permute-start(bf16[128,2048]{1,0:T(8,128)(2,1)} %slice.131), channel_id=1, source_target_pairs={{0,4},{2,6},{4,0},{6,2},{8,12},{10,14},{12,8},{14,10},{16,20},{18,... | collective-permute-start | bytes 1572872 | tf_op jit(solution)/shard_map/ppermute | solution.py:617
  305.0 27.6 %collective-permute-start.38 = (bf16[128,2048]{1,0:T(8,128)(2,1)}, bf16[128,2048]{1,0:T(8,128)(2,1)}, u32[]{:S(2)}, u32[]{:S(2)}) collective-permute-start(bf16[128,2048]{1,0:T(8,128)(2,1)} %slice.132), channel_id=1, source_target_pairs={{0,2},{2,0},{4,6},{6,4},{8,10},{10,8},{12,14},{14,12},{16,18},{18,... | collective-permute-start | bytes 1572872 | tf_op jit(solution)/shard_map/ppermute | solution.py:617
  358.4 156.4 %reduce-scatter.7.cloned.1.call-start = ((), (), s32[]{:S(2)}) async-start(), calls=%async_computation.7 | async-start | bytes 5242880 | tf_op jit(solution)/shard_map/reduce_scatter | solution.py:721
  372.6 17.8 %collective-permute-start.46 = (bf16[128,2048]{1,0:T(8,128)(2,1)}, bf16[128,2048]{1,0:T(8,128)(2,1)}, u32[]{:S(2)}, u32[]{:S(2)}) collective-permute-start(bf16[128,2048]{1,0:T(8,128)(2,1)} %get-tuple-element.224), channel_id=1, source_target_pairs={{0,2},{2,0},{4,6},{6,4},{8,10},{10,8},{12,14},{14,12},{16,18},{18,... | collective-permute-start | bytes 1572872 | tf_op jit(solution)/shard_map/ppermute | solution.py:617
  375.6 23.2 %collective-permute-start.45 = (bf16[128,2048]{1,0:T(8,128)(2,1)}, bf16[128,2048]{1,0:T(8,128)(2,1)S(1)}, u32[]{:S(2)}, u32[]{:S(2)}) collective-permute-start(bf16[128,2048]{1,0:T(8,128)(2,1)} %get-tuple-element.222), channel_id=1, source_target_pairs={{0,2},{2,0},{4,6},{6,4},{8,10},{10,8},{12,14},{14,12},{16,18},{18,... | collective-permute-start | bytes 1572872 | tf_op jit(solution)/shard_map/ppermute | solution.py:617
  376.1 24.2 %collective-permute-start.49 = (bf16[128,2048]{1,0:T(8,128)(2,1)}, bf16[128,2048]{1,0:T(8,128)(2,1)S(1)}, u32[]{:S(2)}, u32[]{:S(2)}) collective-permute-start(bf16[128,2048]{1,0:T(8,128)(2,1)} %get-tuple-element.231), channel_id=1, source_target_pairs={{0,4},{2,6},{4,0},{6,2},{8,12},{10,14},{12,8},{14,10},{16,20},{18,... | collective-permute-start | bytes 1572872 | tf_op jit(solution)/shard_map/ppermute | solution.py:617
  390.1 172.5 %reduce-scatter.9.cloned.1.call-start = ((), (), s32[]{:S(2)}) async-start(), calls=%async_computation.8 | async-start | bytes 2621440 | tf_op jit(solution)/shard_map/reduce_scatter | solution.py:721
  416.0 25.7 %collective-permute-start.53 = (bf16[256,2048]{1,0:T(8,128)(2,1)S(1)}, bf16[256,2048]{1,0:T(8,128)(2,1)}, u32[]{:S(2)}, u32[]{:S(2)}) collective-permute-start(bf16[256,2048]{1,0:T(8,128)(2,1)S(1)} %get-tuple-element.298.refs_0_), channel_id=1, source_target_pairs={{0,2},{2,0},{4,6},{6,4},{8,10},{10,8},{12,14},{14,12},{16,18},{18,... | collective-permute-start | bytes 3145736 | tf_op jit(solution)/shard_map/ppermute | solution.py:617
  416.5 25.4 %collective-permute-start.54 = (bf16[256,2048]{1,0:T(8,128)(2,1)S(1)}, bf16[256,2048]{1,0:T(8,128)(2,1)}, u32[]{:S(2)}, u32[]{:S(2)}) collective-permute-start(bf16[256,2048]{1,0:T(8,128)(2,1)S(1)} %get-tuple-element.298.refs_0_), channel_id=1, source_target_pairs={{0,4},{2,6},{4,0},{6,2},{8,12},{10,14},{12,8},{14,10},{16,20},{18,... | collective-permute-start | bytes 3145736 | tf_op jit(solution)/shard_map/ppermute | solution.py:617
  446.2 17.6 %collective-permute-start.55 = (bf16[128,2048]{1,0:T(8,128)(2,1)}, bf16[128,2048]{1,0:T(8,128)(2,1)S(1)}, u32[]{:S(2)}, u32[]{:S(2)}) collective-permute-start(bf16[128,2048]{1,0:T(8,128)(2,1)} %slice.142), channel_id=1, source_target_pairs={{0,4},{2,6},{4,0},{6,2},{8,12},{10,14},{12,8},{14,10},{16,20},{18,... | collective-permute-start | bytes 1572872 | tf_op jit(solution)/shard_map/ppermute | solution.py:617
  465.0 21.1 %collective-permute-start.52 = (bf16[4,256,2048]{2,1,0:T(8,128)(2,1)}, bf16[4,256,2048]{2,1,0:T(8,128)(2,1)}, u32[]{:S(2)}, u32[]{:S(2)}) collective-permute-start(bf16[4,256,2048]{2,1,0:T(8,128)(2,1)} %get-tuple-element.236), channel_id=1, source_target_pairs={{0,1},{1,0},{2,3},{3,2},{4,5},{5,4},{6,7},{7,6},{8,9},{9,8},{10,11... | collective-permute-start | bytes 12582920 | tf_op jit(solution)/shard_map/ppermute | solution.py:621
  485.8 160.4 %reduce-scatter.11.cloned.1.call-start = ((), (), s32[]{:S(2)}) async-start(), calls=%async_computation.9 | async-start | bytes 7864320 | tf_op jit(solution)/shard_map/reduce_scatter | solution.py:721
  492.2 19.6 %collective-permute-start.61 = (bf16[128,2048]{1,0:T(8,128)(2,1)}, bf16[128,2048]{1,0:T(8,128)(2,1)S(1)}, u32[]{:S(2)}, u32[]{:S(2)}) collective-permute-start(bf16[128,2048]{1,0:T(8,128)(2,1)} %get-tuple-element.260), channel_id=1, source_target_pairs={{0,2},{2,0},{4,6},{6,4},{8,10},{10,8},{12,14},{14,12},{16,18},{18,... | collective-permute-start | bytes 1572872 | tf_op jit(solution)/shard_map/ppermute | solution.py:617
  493.0 18.8 %collective-permute-start.62 = (bf16[128,2048]{1,0:T(8,128)(2,1)}, bf16[128,2048]{1,0:T(8,128)(2,1)S(1)}, u32[]{:S(2)}, u32[]{:S(2)}) collective-permute-start(bf16[128,2048]{1,0:T(8,128)(2,1)} %get-tuple-element.261), channel_id=1, source_target_pairs={{0,4},{2,6},{4,0},{6,2},{8,12},{10,14},{12,8},{14,10},{16,20},{18,... | collective-permute-start | bytes 1572872 | tf_op jit(solution)/shard_map/ppermute | solution.py:617
  547.4 69.0 %collective-permute-start.60 = (bf16[128,2048]{1,0:T(8,128)(2,1)}, bf16[128,2048]{1,0:T(8,128)(2,1)}, u32[]{:S(2)}, u32[]{:S(2)}) collective-permute-start(bf16[128,2048]{1,0:T(8,128)(2,1)} %get-tuple-element.258), channel_id=1, source_target_pairs={{0,2},{2,0},{4,6},{6,4},{8,10},{10,8},{12,14},{14,12},{16,18},{18,... | collective-permute-start | bytes 1572872 | tf_op jit(solution)/shard_map/ppermute | solution.py:617
  554.7 19.1 %collective-permute-start.68 = (bf16[128,2048]{1,0:T(8,128)(2,1)}, bf16[128,2048]{1,0:T(8,128)(2,1)S(1)}, u32[]{:S(2)}, u32[]{:S(2)}) collective-permute-start(bf16[128,2048]{1,0:T(8,128)(2,1)} %get-tuple-element.281), channel_id=1, source_target_pairs={{0,2},{2,0},{4,6},{6,4},{8,10},{10,8},{12,14},{14,12},{16,18},{18,... | collective-permute-start | bytes 1572872 | tf_op jit(solution)/shard_map/ppermute | solution.py:617
  555.8 18.0 %collective-permute-start.69 = (bf16[128,2048]{1,0:T(8,128)(2,1)}, bf16[128,2048]{1,0:T(8,128)(2,1)}, u32[]{:S(2)}, u32[]{:S(2)}) collective-permute-start(bf16[128,2048]{1,0:T(8,128)(2,1)} %get-tuple-element.282), channel_id=1, source_target_pairs={{0,4},{2,6},{4,0},{6,2},{8,12},{10,14},{12,8},{14,10},{16,20},{18,... | collective-permute-start | bytes 1572872 | tf_op jit(solution)/shard_map/ppermute | solution.py:617
  561.0 24.1 %collective-permute-start.67 = (bf16[128,2048]{1,0:T(8,128)(2,1)}, bf16[128,2048]{1,0:T(8,128)(2,1)S(1)}, u32[]{:S(2)}, u32[]{:S(2)}) collective-permute-start(bf16[128,2048]{1,0:T(8,128)(2,1)} %get-tuple-element.279), channel_id=1, source_target_pairs={{0,2},{2,0},{4,6},{6,4},{8,10},{10,8},{12,14},{14,12},{16,18},{18,... | collective-permute-start | bytes 1572872 | tf_op jit(solution)/shard_map/ppermute | solution.py:617
  561.7 25.5 %collective-permute-start.71 = (bf16[128,2048]{1,0:T(8,128)(2,1)}, bf16[128,2048]{1,0:T(8,128)(2,1)}, u32[]{:S(2)}, u32[]{:S(2)}) collective-permute-start(bf16[128,2048]{1,0:T(8,128)(2,1)} %get-tuple-element.284), channel_id=1, source_target_pairs={{0,4},{2,6},{4,0},{6,2},{8,12},{10,14},{12,8},{14,10},{16,20},{18,... | collective-permute-start | bytes 1572872 | tf_op jit(solution)/shard_map/ppermute | solution.py:617
  575.0 21.3 %collective-permute-start.72 = (bf16[128,2048]{1,0:T(8,128)(2,1)S(1)}, bf16[128,2048]{1,0:T(8,128)(2,1)S(1)}, u32[]{:S(2)}, u32[]{:S(2)}) collective-permute-start(bf16[128,2048]{1,0:T(8,128)(2,1)S(1)} %add_convert_fusion), channel_id=1, source_target_pairs={{0,2},{2,0},{4,6},{6,4},{8,10},{10,8},{12,14},{14,12},{16,18},{18,... | collective-permute-start | bytes 1572872 | tf_op jit(solution)/shard_map/ppermute | solution.py:617
  576.1 21.5 %collective-permute-start.70 = (bf16[128,2048]{1,0:T(8,128)(2,1)S(1)}, bf16[128,2048]{1,0:T(8,128)(2,1)S(1)}, u32[]{:S(2)}, u32[]{:S(2)}) collective-permute-start(bf16[128,2048]{1,0:T(8,128)(2,1)S(1)} %add_convert_fusion.1), channel_id=1, source_target_pairs={{0,4},{2,6},{4,0},{6,2},{8,12},{10,14},{12,8},{14,10},{16,20},{18,... | collective-permute-start | bytes 1572872 | tf_op jit(solution)/shard_map/ppermute | solution.py:617
  585.8 31.3 %collective-permute-start.65 = (bf16[128,2048]{1,0:T(8,128)(2,1)}, bf16[128,2048]{1,0:T(8,128)(2,1)S(1)}, u32[]{:S(2)}, u32[]{:S(2)}) collective-permute-start(bf16[128,2048]{1,0:T(8,128)(2,1)} %get-tuple-element.271), channel_id=1, source_target_pairs={{0,4},{2,6},{4,0},{6,2},{8,12},{10,14},{12,8},{14,10},{16,20},{18,... | collective-permute-start | bytes 1572872 | tf_op jit(solution)/shard_map/ppermute | solution.py:617
  587.2 18.6 %collective-permute-start.64 = (bf16[128,2048]{1,0:T(8,128)(2,1)}, bf16[128,2048]{1,0:T(8,128)(2,1)S(1)}, u32[]{:S(2)}, u32[]{:S(2)}) collective-permute-start(bf16[128,2048]{1,0:T(8,128)(2,1)} %add_convert_fusion.2), channel_id=1, source_target_pairs={{0,2},{2,0},{4,6},{6,4},{8,10},{10,8},{12,14},{14,12},{16,18},{18,... | collective-permute-start | bytes 1572872 | tf_op jit(solution)/shard_map/ppermute | solution.py:617
  596.3 17.3 %collective-permute-start.63 = (bf16[128,2048]{1,0:T(8,128)(2,1)}, bf16[128,2048]{1,0:T(8,128)(2,1)S(1)}, u32[]{:S(2)}, u32[]{:S(2)}) collective-permute-start(bf16[128,2048]{1,0:T(8,128)(2,1)} %add_convert_fusion.3), channel_id=1, source_target_pairs={{0,4},{2,6},{4,0},{6,2},{8,12},{10,14},{12,8},{14,10},{16,20},{18,... | collective-permute-start | bytes 1572872 | tf_op jit(solution)/shard_map/ppermute | solution.py:617
  605.8 20.6 %collective-permute-start.84 = (bf16[512,128]{1,0:T(8,128)(2,1)}, bf16[512,128]{1,0:T(8,128)(2,1)S(1)}, u32[]{:S(2)}, u32[]{:S(2)}) collective-permute-start(bf16[512,128]{1,0:T(8,128)(2,1)} %get-tuple-element.322), channel_id=1, source_target_pairs={{0,2},{2,0},{4,6},{6,4},{8,10},{10,8},{12,14},{14,12},{16,18},{18,... | collective-permute-start | bytes 393224 | tf_op jit(solution)/shard_map/ppermute | solution.py:617
  616.5 16.9 %collective-permute-start.81 = (bf16[128,1024]{1,0:T(8,128)(2,1)}, bf16[128,1024]{1,0:T(8,128)(2,1)}, u32[]{:S(2)}, u32[]{:S(2)}) collective-permute-start(bf16[128,1024]{1,0:T(8,128)(2,1)} %get-tuple-element.318), channel_id=1, source_target_pairs={{0,2},{2,0},{4,6},{6,4},{8,10},{10,8},{12,14},{14,12},{16,18},{18,... | collective-permute-start | bytes 786440 | tf_op jit(solution)/shard_map/ppermute | solution.py:617
  649.4 19.7 %collective-permute-start.88 = (bf16[128,1536]{1,0:T(8,128)(2,1)S(1)}, bf16[128,1536]{1,0:T(8,128)(2,1)S(1)}, u32[]{:S(2)}, u32[]{:S(2)}) collective-permute-start(bf16[128,1536]{1,0:T(8,128)(2,1)S(1)} %get-tuple-element.313), channel_id=1, source_target_pairs={{0,4},{2,6},{4,0},{6,2},{8,12},{10,14},{12,8},{14,10},{16,20},{18,... | collective-permute-start | bytes 1179656 | tf_op jit(solution)/shard_map/ppermute | solution.py:617
  650.6 18.5 %collective-permute-start.89 = (bf16[128,1536]{1,0:T(8,128)(2,1)S(1)}, bf16[128,1536]{1,0:T(8,128)(2,1)S(1)}, u32[]{:S(2)}, u32[]{:S(2)}) collective-permute-start(bf16[128,1536]{1,0:T(8,128)(2,1)S(1)} %get-tuple-element.312), channel_id=1, source_target_pairs={{0,6},{2,4},{4,2},{6,0},{8,14},{10,12},{12,10},{14,8},{16,22},{18,... | collective-permute-start | bytes 1179656 | tf_op jit(solution)/shard_map/ppermute | solution.py:617
  (102 other events, 1215.7 us)
Sparse Core Ops, SparseCore 0:
  42.4 150.0 all-gather.2
  194.0 113.5 all-gather.4
  358.5 42.0 reduce-scatter.4
  402.9 76.0 reduce-scatter.6
  485.9 40.9 reduce-scatter.8
  529.1 110.3 reduce-scatter.10

commit v4 on v3

--- a/solution.py
+++ b/solution.py
@@ -175,62 +175,6 @@
     return held[step]
 
 
-def retain_kernel(*refs):
-    pieces, (weights, decays) = refs[:8], refs[8:10]
-    query_ref, key_ref, value_ref, scores_ref, retained_ref, rows_ref = refs[10:16]
-    held, sem, out_sem = refs[16:]
-    rows = load_pieces(pieces, held, sem)
-    step = pl.program_id(0)
-    slot_len = rows.shape[0]
-    keep = pltpu.make_async_copy(held.at[step], rows_ref.at[pl.ds(step * slot_len, slot_len)], out_sem)
-    keep.start()
-    dk, dv = query_ref.shape[1], value_ref.shape[1]
-    query_key = dot(rows, weights[:, : 2 * dk]).astype(bf16)
-    query, key = query_key[:, :dk], query_key[:, dk:]
-    query_ref[...] = query
-    key_ref[...] = key
-    scores = (dot_nt(query, key) * decays[...]).astype(bf16)
-    scores_ref[...] = scores[None]
-    value = dot(rows, weights[:, 2 * dk : 2 * dk + dv]).astype(bf16)
-    value_ref[...] = value
-    retained_ref[...] = dot(scores, value)
-    keep.wait()
-
-
-def retain(pieces, weights, decays, dk, dv):
-    rows, width = pieces[0].shape
-    slot_len = 2 * rows
-    total = PLANE * slot_len
-    return pl.pallas_call(
-        retain_kernel,
-        grid=(PLANE,),
-        in_specs=[ANY] * 8 + [whole((width, 2 * dk + dv)), whole((slot_len, slot_len))],
-        out_specs=[
-            by_slot(slot_len, dk),
-            by_slot(slot_len, dk),
-            by_slot(slot_len, dv),
-            by_slot(1, slot_len, slot_len),
-            by_slot(slot_len, dv),
-            ANY,
-        ],
-        out_shape=[
-            shaped((total, dk), bf16),
-            shaped((total, dk), bf16),
-            shaped((total, dv), bf16),
-            shaped((PLANE, slot_len, slot_len), bf16),
-            shaped((total, dv), f32),
-            shaped((total, width), bf16),
-        ],
-        scratch_shapes=[
-            pltpu.VMEM((PLANE, slot_len, width), bf16),
-            pltpu.SemaphoreType.DMA((8,)),
-            pltpu.SemaphoreType.DMA,
-        ],
-        compiler_params=params(),
-        cost_estimate=cost(2.2 * total * width * (2 * dk + dv), 30e6),
-    )(*pieces, weights, decays)
-
-
 def times_rows(left, right, wide):
     groups = right.shape[1] // wide
     for z in range(right.shape[0] // wide):
@@ -255,58 +199,170 @@
     return made[0] if len(made) == 1 else jnp.concatenate(made, axis=1)
 
 
-def split_out(terms, near_ref, far_ref, columns):
+def split_out(terms, near_ref, far_refs, columns):
     rows = near_ref.shape[1]
     near_ref[0, :, columns] = terms[:rows]
-    far_ref[0, :, columns] = terms[rows:].astype(bf16)
-
-
-def gate_out_kernel(wide, n_kept, rows_ref, weights, out_weights, retained_ref, *refs):
-    gate_ref, gated_ref, near_ref, far_ref = refs[n_kept:]
-    retained = retained_ref[...]
+    far = terms[rows:].astype(bf16)
+    for slot, far_ref in enumerate(far_refs):
+
+        @pl.when(pl.program_id(0) == slot)
+        def put(far_ref=far_ref):
+            far_ref[:, columns] = far
+
+
+def split_specs(n, rows, width):
+    fars = [pl.BlockSpec((rows, width), lambda i: (0, 0), pipeline_mode=pl.Buffered(1))] * n
+    return [by_slot(1, rows, width), *fars]
+
+
+def split_shapes(n, rows, width):
+    return [shaped((n, rows, width), f32)] + [shaped((rows, width), bf16)] * n
+
+
+def weave(place, own, others, target, width, sem):
+    planes, full = 4, own.shape[1]
+    shard = own.shape[0] // planes
+    copies = []
+    for plane in range(planes):
+        top = plane * PLANE * shard
+        for k in range(PLANE):
+            if k == 0:
+                source = own.at[pl.ds(plane * shard, shard)]
+            else:
+                source = others.at[pl.ds((plane * (PLANE - 1) + k - 1) * shard, shard)]
+            spot = pl.ds(pl.multiple_of(top + (place ^ k) * shard, shard), shard)
+            moves = [(source.at[:, pl.ds(0, width)], target.at[spot, pl.ds(0, width)])]
+            spot = pl.ds(pl.multiple_of(width + (place ^ k) * shard, shard), shard)
+            for a in range((full - width) // shard):
+                piece = source.at[:, pl.ds(width + a * shard, shard)]
+                moves.append((piece, target.at[pl.ds(top + a * shard, shard), spot]))
+            copies += [pltpu.make_async_copy(*move, sem.at[plane, k, n]) for n, move in enumerate(moves)]
+    return copies
+
+
+def retain_kernel(first, wide, n, n_kept, woven, *refs):
+    pieces, refs = refs[: 2 * n], refs[2 * n :]
+    if woven:
+        place_ref, own, others, decays = refs[:4]
+        refs = refs[4:]
+    else:
+        weights, decays = refs[:2]
+        refs = refs[2 + n_kept :]
+    query_ref, key_ref, value_ref, gate_ref, scores_ref, retained_ref, gated_ref, rows_ref = refs[:8]
+    near_ref, *far_refs = refs[8 : 9 + n]
+    if woven:
+        joined_ref, held, sem, out_sem, weights, weights_sem, joined_sem = refs[9 + n :]
+    else:
+        held, sem, out_sem = refs[9 + n :]
+    step = pl.program_id(0)
+    dk, dv = query_ref.shape[1], value_ref.shape[1]
+    if woven:
+        copies = weave(place_ref[0], own, others, weights, 2 * dk + 2 * dv, weights_sem)
+        keep_weights = pltpu.make_async_copy(weights, joined_ref, joined_sem)
+
+        @pl.when(step == 0)
+        def bring():
+            for one in copies:
+                one.start()
+
+    rows = load_pieces(pieces, held, sem)
+    slot_len = rows.shape[0]
+    keep = pltpu.make_async_copy(
+        held.at[step], rows_ref.at[pl.ds((step + first) * slot_len, slot_len)], out_sem
+    )
+    keep.start()
+    if woven:
+
+        @pl.when(step == 0)
+        def brought():
+            for one in copies:
+                one.wait()
+            keep_weights.start()
+
+    query_key = dot(rows, weights[:, : 2 * dk]).astype(bf16)
+    query, key = query_key[:, :dk], query_key[:, dk:]
+    query_ref[...] = query
+    key_ref[...] = key
+    scores = (dot_nt(query, key) * decays[...]).astype(bf16)
+    scores_ref[...] = scores[None]
+    value = dot(rows, weights[:, 2 * dk : 2 * dk + dv]).astype(bf16)
+    value_ref[...] = value
+    retained = dot(scores, value)
+    retained_ref[...] = retained
     scale = lax.rsqrt(jnp.mean(retained * retained, axis=-1, keepdims=True) + group_floor)
-    gate = dot(rows_ref[...], weights[...])
+    gate = dot(rows, weights[:, 2 * dk + dv : 2 * dk + 2 * dv])
     gate_ref[...] = gate
     gated_ref[...] = (gate * jax.nn.sigmoid(gate) * (retained * scale)).astype(bf16)
-    for columns, terms in times_rows(gated_ref[...], out_weights[...], wide):
-        split_out(terms, near_ref, far_ref, columns)
-
-
-def gate_out(lo, hi, rows_all, joined, retained, kept, wide):
-    total, width = rows_all.shape
-    dv = retained.shape[1]
-    slot_len = total // PLANE
-    rows = slot_len // 2
+    for columns, terms in times_rows(gated_ref[...], weights[:, 2 * dk + 2 * dv :], wide):
+        split_out(terms, near_ref, far_refs, columns)
+    keep.wait()
+    if woven:
+
+        @pl.when(step == n - 1)
+        def kept():
+            keep_weights.wait()
+
+
+def retain(first, pieces, weights, decays, kept, dk, dv, wide, place=None):
+    n = len(pieces) // 2
+    rows, width = pieces[0].shape
+    slot_len = 2 * rows
+    total = PLANE * slot_len
 
     def at(cols):
-        return pl.BlockSpec((slot_len, cols), lambda i: (i + lo, 0))
-
-    return pl.pallas_call(
-        functools.partial(gate_out_kernel, wide, len(kept)),
-        grid=(hi - lo,),
-        in_specs=[
-            at(width),
-            pl.BlockSpec((width, dv), lambda i: (0, 2), pipeline_mode=pl.Buffered(1)),
-            pl.BlockSpec((width, dv), lambda i: (0, 3), pipeline_mode=pl.Buffered(1)),
-            at(dv),
+        return pl.BlockSpec((slot_len, cols), lambda i: (i + first, 0))
+
+    kept_specs = [at(dk), at(dk), at(dv), at(dv), None, at(dv), at(dv), ANY]
+    kept_specs[4] = pl.BlockSpec((1, slot_len, slot_len), lambda i: (i + first, 0, 0))
+    out_specs = kept_specs + split_specs(n, rows, width)
+    out_shape = [
+        shaped((total, dk), bf16),
+        shaped((total, dk), bf16),
+        shaped((total, dv), bf16),
+        shaped((total, dv), f32),
+        shaped((PLANE, slot_len, slot_len), bf16),
+        shaped((total, dv), f32),
+        shaped((total, dv), bf16),
+        shaped((total, width), bf16),
+        *split_shapes(n, rows, width),
+    ]
+    scratch_shapes = [
+        pltpu.VMEM((n, slot_len, width), bf16),
+        pltpu.SemaphoreType.DMA((2 * n,)),
+        pltpu.SemaphoreType.DMA,
+    ]
+    if place is None:
+        given = [weights, decays]
+        in_specs = [whole(weights.shape), whole((slot_len, slot_len))]
+    else:
+        assert not kept
+        given = [place, *weights, decays]
+        in_specs = [pl.BlockSpec(memory_space=pltpu.SMEM), ANY, ANY, whole((slot_len, slot_len))]
+        full = weights[0].shape[1]
+        shard = weights[0].shape[0] // 4
+        out_specs.append(ANY)
+        out_shape.append(shaped((width, full), bf16))
+        scratch_shapes += [
+            pltpu.VMEM((width, full), bf16),
+            pltpu.SemaphoreType.DMA((4, PLANE, 1 + (full - 2 * dk - 2 * dv) // shard)),
+            pltpu.SemaphoreType.DMA,
         ]
-        + [ANY] * len(kept),
-        out_specs=[at(dv), at(dv), by_slot(1, rows, width), by_slot(1, rows, width)],
-        out_shape=[
-            shaped((total, dv), f32),
-            shaped((total, dv), bf16),
-            shaped((hi - lo, rows, width), f32),
-            shaped((hi - lo, rows, width), bf16),
-        ],
-        input_output_aliases={4 + i: i for i in range(len(kept))},
-        compiler_params=params(),
-        cost_estimate=cost((hi - lo) * total * width * dv, (hi - lo) * 10e6),
-    )(rows_all, joined, joined, retained, *kept)
-
-
-def project_kernel(wide, left, right, near_ref, far_ref):
+    return pl.pallas_call(
+        functools.partial(retain_kernel, first, wide, n, len(kept), place is not None),
+        grid=(n,),
+        in_specs=[ANY] * (2 * n) + in_specs + [ANY] * len(kept),
+        out_specs=out_specs,
+        out_shape=out_shape,
+        scratch_shapes=scratch_shapes,
+        input_output_aliases={2 * n + len(given) + i: i for i in range(len(kept))},
+        compiler_params=params(),
+        cost_estimate=cost(2.2 * n * slot_len * width * (2 * dk + 3 * dv), 15e6),
+    )(*pieces, *given, *kept)
+
+
+def project_kernel(wide, left, right, near_ref, *far_refs):
     for columns, terms in times_rows(left[...], right[...], wide):
-        split_out(terms, near_ref, far_ref, columns)
+        split_out(terms, near_ref, far_refs, columns)
 
 
 def project(left, right, wide):
@@ -318,19 +374,19 @@
         functools.partial(project_kernel, wide),
         grid=(PLANE,),
         in_specs=[by_slot(slot_len, inner), whole(right.shape)],
-        out_specs=[by_slot(1, rows, width)] * 2,
-        out_shape=[shaped((PLANE, rows, width), f32), shaped((PLANE, rows, width), bf16)],
+        out_specs=split_specs(PLANE, rows, width),
+        out_shape=split_shapes(PLANE, rows, width),
         compiler_params=params(),
         cost_estimate=cost(2 * total * inner * width, 20e6),
     )(left, right)
 
 
-def back_kernel(left, first, second, near_ref, far_ref):
+def back_kernel(left, first, second, near_ref, *far_refs):
     dv = second.shape[1]
     narrow = first.shape[1] - dv
     terms = dot_nt(left[:, :dv], first[:, narrow:]) + dot_nt(left[:, dv : 2 * dv], second[...])
     terms += dot_nt(left[:, 2 * dv :], first[:, :narrow])
-    split_out(terms, near_ref, far_ref, slice(None))
+    split_out(terms, near_ref, far_refs, slice(None))
 
 
 def project_back(left, joined, dk, dv):
@@ -346,8 +402,8 @@
             whole((width, 2 * dk + dv)),
             pl.BlockSpec((width, dv), lambda i: (0, 2), pipeline_mode=pl.Buffered(1)),
         ],
-        out_specs=[by_slot(1, rows, width)] * 2,
-        out_shape=[shaped((PLANE, rows, width), f32), shaped((PLANE, rows, width), bf16)],
+        out_specs=split_specs(PLANE, rows, width),
+        out_shape=split_shapes(PLANE, rows, width),
         compiler_params=params(),
         cost_estimate=cost(2 * total * inner * width, 20e6),
     )(left, joined, joined)
@@ -359,8 +415,8 @@
     half = x1_ref.shape[0]
     targets = ((x1_ref, keep_x_ref), (keep_y_ref, y2_ref), (x3_ref, y3_ref))
     for near, arrived, (first, second) in zip(nears, arriveds, targets):
-        first[...] = (near[0, :half] + arrived[0, :half].astype(f32)).astype(first.dtype)
-        second[...] = (near[0, half:] + arrived[0, half:].astype(f32)).astype(second.dtype)
+        first[...] = (near[0, :half] + arrived[:half].astype(f32)).astype(first.dtype)
+        second[...] = (near[0, half:] + arrived[half:].astype(f32)).astype(second.dtype)
 
 
 def fold_cut(slots):
@@ -370,10 +426,11 @@
     part = width // 4
     kinds = (bf16, bf16, bf16, bf16, f32, f32)
     given = [pl.BlockSpec((1, rows, part), lambda i, spot=spot: (spot, 0, i)) for spot in spots]
+    given += [pl.BlockSpec((rows, part), lambda i: (0, i))] * len(spots)
     return pl.pallas_call(
         fold_kernel,
         grid=(width // part,),
-        in_specs=given + given,
+        in_specs=given,
         out_specs=[pl.BlockSpec((half, part), lambda i: (0, i))] * len(kinds),
         out_shape=[shaped((half, width), kind) for kind in kinds],
         compiler_params=params(),
@@ -383,8 +440,8 @@
 
 def hidden_kernel(first, wide, n, n_kept, *refs):
     pieces, (weights, down_weights, back) = refs[: 2 * n], refs[2 * n : 2 * n + 3]
-    act_ref, grad_ref, rows_ref, near_ref, far_ref = refs[2 * n + 3 + n_kept : 2 * n + 8 + n_kept]
-    held, sem, out_sem = refs[2 * n + 8 + n_kept :]
+    act_ref, grad_ref, rows_ref, near_ref, *far_refs = refs[2 * n + 3 + n_kept : 3 * n + 7 + n_kept]
+    held, sem, out_sem = refs[3 * n + 7 + n_kept :]
     rows = load_pieces(pieces, held, sem)
     step = pl.program_id(0)
     slot_len = rows.shape[0]
@@ -405,7 +462,7 @@
     grad = times_rows_back(back[...], down_weights[...], wide)
     grad_ref[:, :inner] = (grad * value * rise).astype(bf16)
     grad_ref[:, inner:] = (grad * gelu).astype(bf16)
-    split_out(dot_nt(grad_ref[...], weights), near_ref, far_ref, slice(None))
+    split_out(dot_nt(grad_ref[...], weights), near_ref, far_refs, slice(None))
     keep.wait()
 
 
@@ -428,13 +485,12 @@
             at(width),
         ]
         + [ANY] * len(kept),
-        out_specs=[at(inner), at(2 * inner), ANY, by_slot(1, rows, width), by_slot(1, rows, width)],
+        out_specs=[at(inner), at(2 * inner), ANY, *split_specs(n, rows, width)],
         out_shape=[
             shaped((total, inner), bf16),
             shaped((total, 2 * inner), bf16),
             shaped((total, width), bf16),
-            shaped((n, rows, width), f32),
-            shaped((n, rows, width), bf16),
+            *split_shapes(n, rows, width),
         ],
         scratch_shapes=[
             pltpu.VMEM((n, slot_len, width), bf16),
@@ -535,6 +591,62 @@
     )(left, right)
 
 
+def places_grad_kernel(me_ref, left, right, own, others, held, sem):
+    step = pl.program_id(0)
+    slot = step % 2
+    held[slot] = dot_tn(left[...], right[...]).astype(bf16)
+    shard = held.shape[1] // PLANE
+
+    def each(step, slot, act):
+        def copy(j, target):
+            return pltpu.make_async_copy(held.at[slot, pl.ds(j * shard, shard)], target, sem.at[slot, j])
+
+        for j in range(PLANE):
+            k = me_ref[0] ^ j
+
+            @pl.when(k == 0)
+            def here(j=j):
+                act(copy(j, own.at[pl.ds(pl.multiple_of(step * shard, shard), shard)]))
+
+            @pl.when(k != 0)
+            def there(j=j, k=k):
+                at = pl.multiple_of((step * (PLANE - 1) + k - 1) * shard, shard)
+                act(copy(j, others.at[pl.ds(at, shard)]))
+
+    each(step, slot, lambda one: one.start())
+
+    @pl.when(step > 0)
+    def before():
+        each(step - 1, 1 - slot, lambda one: one.wait())
+
+    @pl.when(step == pl.num_programs(0) - 1)
+    def last():
+        each(step, slot, lambda one: one.wait())
+
+
+def places_grad(me, left, right, depth):
+    total, width = left.shape
+    cols = right.shape[1]
+    part = width // depth
+    return pl.pallas_call(
+        places_grad_kernel,
+        grid=(depth,),
+        in_specs=[
+            pl.BlockSpec(memory_space=pltpu.SMEM),
+            pl.BlockSpec((total, part), lambda i: (0, i)),
+            whole((total, cols)),
+        ],
+        out_specs=[ANY, ANY],
+        out_shape=[
+            shaped((width // PLANE, cols), bf16),
+            shaped((width // PLANE * (PLANE - 1), cols), bf16),
+        ],
+        scratch_shapes=[pltpu.VMEM((2, part, cols), bf16), pltpu.SemaphoreType.DMA((2, PLANE))],
+        compiler_params=params(),
+        cost_estimate=cost(2 * total * width * cols, 20e6),
+    )(me, left, right)
+
+
 def rows_grad(left, right, wide):
     total, inner = left.shape
     blocks = right.shape[1] // wide
@@ -644,35 +756,37 @@
     return pieces + nearer + far
 
 
-def fold(groups, count, before=(), first=None, second=None):
+def fold(groups, count, before=None, first=None, second=None):
     slots = {}
 
-    def take(lo, near, far):
-        arrived = swap(far)
-        for k in range(near.shape[0]):
-            slots[lo + k] = near, arrived, k
+    def take(lo, near, *fars):
+        for k, far in enumerate(fars):
+            slots[lo + k] = near, swap(far), k
 
     for group in groups:
         take(*group)
-    given = after([(near, arrived) for near, arrived, _ in (slots[k] for k in (1, 2, 3))], before)
+    given = [(near, arrived) for near, arrived, _ in (slots[k] for k in (1, 2, 3))]
+    made = []
+    if before:
+        made.append(before(slots[1][1]))
+        given = after(given, made)
     cut = fold_cut([(*pair, slots[k][2]) for k, pair in zip((1, 2, 3), given)])
     to_x1, to_y2, to_x3, to_y3, keep_x, keep_y = cut
     half, width = to_x1.shape
     x1, y2 = hop(to_x1, 1, count), hop(to_y2, 2, count)
     x3, y3 = hop(to_x3, 1, count), hop(to_y3, 2, count)
-    made = []
     if first:
         made.append(first((to_x3, to_y3)))
         x3, y3 = after((x3, y3), made)
     if 0 not in slots:
-        take(*made[0][0])
+        take(*made[-1][0])
     near_0, arrived_0, spot = slots[0]
     to_y, to_x = (keep_y + x3.astype(f32)).astype(bf16), (keep_x + y3.astype(f32)).astype(bf16)
     last_y, last_x = hop(to_y, 2, count), hop(to_x, 1, count)
     if second:
-        made.append(second((to_x, to_y), made))
+        made.append(second((to_x, to_y)))
         last_y, last_x = after((last_y, last_x), made[-1])
-    near_0, arrived_0 = near_0[spot], arrived_0[spot].astype(f32)
+    near_0, arrived_0 = near_0[spot], arrived_0.astype(f32)
     summed = [
         near_0[:half] + arrived_0[:half] + (x1.astype(f32) + last_y.astype(f32)),
         near_0[half:] + arrived_0[half:] + (y2.astype(f32) + last_x.astype(f32)),
@@ -721,8 +835,15 @@
         return lax.psum_scatter(block, "dp", scatter_dimension=0, tiled=True, axis_index_groups=columns)
 
     attn_cuts = cut_weights(me_scalar, (w_query, w_key, w_value, w_gate), w_out)
-    attn_own = join_weights(me_scalar, trade(attn_cuts, count), 2 * dk + 2 * dv)
-    attn_joined = gather_depth(attn_own)
+    attn_blocks = trade(attn_cuts, count)
+    attn_width = 2 * dk + 2 * dv
+    if depth == 4:
+        own_gathered = gather_depth(attn_cuts[0])
+        attn_own = jnp.concatenate(attn_blocks[1:])
+        attn_weights = own_gathered, gather_depth(attn_own)
+    else:
+        attn_own = join_weights(me_scalar, attn_blocks, attn_width)
+        attn_joined = gather_depth(attn_own)
 
     gains = jnp.stack([gain_attn, gain_mlp])[None]
     step = 1
@@ -751,18 +872,21 @@
     positions = jnp.concatenate([core * rows + local, (1 - core) * rows + local])
     decays = decay_table(positions, core * PLANE + me)
     attn_pieces = after(attn_pieces, back_all)
-    query, key, value, scores, retained, attn_all = retain(attn_pieces, attn_joined, decays, dk, dv)
     kept, groups = [], []
-    for lo, hi in (SLOTS[1], SLOTS[2]):
-        *kept, near, far = gate_out(lo, hi, attn_all, attn_joined, retained, kept, wide)
-        groups.append((lo, near, far))
-
-    def gate_own(done):
-        lo, hi = SLOTS[0]
-        *made, near, far = gate_out(lo, hi, after(attn_all, done), attn_joined, retained, kept, wide)
-        return (lo, near, far), made
-
-    added, (_, (gate, gated)) = fold(groups, count, first=gate_own)
+    if depth == 4:
+        *kept, attn_joined = retain(1, attn_pieces[2:], attn_weights, decays, kept, dk, dv, wide, me_scalar)
+    else:
+        kept = retain(1, attn_pieces[2:], attn_joined, decays, kept, dk, dv, wide)
+    kept, terms = kept[:8], kept[8:]
+    groups.append((1, *terms))
+
+    def retain_own(done):
+        pieces = after(attn_pieces[:2], done)
+        made = retain(0, pieces, attn_joined, decays, kept, dk, dv, wide)
+        return (0, *made[8:]), made[:8]
+
+    added, (_, made) = fold(groups, count, first=retain_own)
+    query, key, value, gate, scores, retained, gated, attn_all = made
     hidden = input_rows + added
 
     second_scale = lax.rsqrt(jnp.mean(hidden * hidden, axis=-1, keepdims=True) + norm_eps)
@@ -776,17 +900,20 @@
             return ()
         if lo == 1:
             lo, pieces = 0, state["own"] + pieces
-        *state["kept"], near, far = hidden_units(lo, pieces, ff_joined, back_all, state["kept"], inner, wide)
-        state["groups"].append((lo, near, far))
+        made = hidden_units(lo, pieces, ff_joined, back_all, state["kept"], inner, wide)
+        state["kept"] = made[:3]
+        state["groups"].append((lo, *made[3:]))
         return state["kept"]
 
     inner_act, grad_up, mlp_all = spread(normed_mlp, count, units)
-    grad_down = rows_grad(inner_act, back_all, wide)
+
+    def down_grad(_):
+        return rows_grad(inner_act, back_all, wide)
 
     def up_grad(done):
         return columns_grad(*after((mlp_all, grad_up), done), 0, 2 * inner)
 
-    grad_normed, grad_ff = fold(state["groups"], count, before=grad_down, first=up_grad)
+    grad_normed, grad_down, grad_ff = fold(state["groups"], count, down_grad, up_grad)
     down_part = sum_depth(grad_down)
     ff_part = sum_depth(grad_ff)
     scaled = grad_normed * gain_second
@@ -814,18 +941,17 @@
     grad_out = rows_grad(gated, attn_grad_all, wide)
     out_part = sum_depth(grad_out)
 
-    def wide_grad(done):
-        return columns_grad(attn_all, after(grad_wide, done), 0, 2 * dv + 2 * dk)
-
-    def back_terms(done, made):
+    own_grad, others_grad = places_grad(me_scalar, attn_all, after(grad_wide, grad_out), depth)
+
+    def back_terms(done):
         return project_back(after(grad_wide, (done, ff_part)), attn_joined, dk, dv)
 
-    mlp_added, grad_wide_weights, (near, far) = fold(
-        [(0, *state["mlp"])], count, before=grad_out, first=wide_grad, second=back_terms
-    )
-    wide_part = sum_depth(grad_wide_weights)
+    mlp_added, _, attn_terms = fold([(0, *state["mlp"])], count, lambda _: others_grad, back_terms)
+    others_part = sum_depth(others_grad)
     output = (valid_rows * (hidden + mlp_added)).astype(bf16)
-    grad_normed_attn, _ = fold([(0, near, far)], count, first=lambda done: out_part)
+    grad_normed_attn, *_ = fold([(0, *attn_terms)], count, lambda _: mlp_added, lambda _: out_part)
+    own_grad = after(own_grad, grad_normed_attn)
+    own_part = sum_depth(own_grad)
     gain_term_attn = jnp.sum(grad_normed_attn * input_rows * first_scale, axis=0)
     scaled_first = grad_normed_attn * gain_first
     tokens_grad = grad_hidden + first_scale * (
@@ -836,9 +962,23 @@
     )
     tokens_grad = tokens_grad.astype(bf16)
 
+    def back_columns(block, widths):
+        cuts = [lax.dynamic_slice_in_dim(block, (me ^ k) * shard, shard, 0).astype(bf16) for k in range(PLANE)]
+        return place_columns(me_scalar, trade(cuts, count), widths)
+
+    def back_rows_of(block):
+        cuts = [lax.dynamic_slice_in_dim(block, (me ^ k) * shard, shard, 1).astype(bf16) for k in range(PLANE)]
+        return place_rows(me_scalar, trade(cuts, count))
+
+    down_sum = back_rows_of(down_part)
+    ffgate_sum, ffup_sum = back_columns(ff_part, (inner, inner))
+    out_sum = back_rows_of(out_part)
+    blocks = [hop(others_part[k * shard : (k + 1) * shard], k + 1, count) for k in range(PLANE - 1)]
     gain_terms = jnp.stack([gain_term_attn, gain_term_mlp])
     bit = count // 2
     while bit >= 1:
+        if bit == PLANE // 2:
+            gain_terms = after(gain_terms, blocks)
         side = (place // bit) % 2
         cut = gain_terms.reshape(2, 2, -1)
         kept = lax.dynamic_index_in_dim(cut, side, 1, keepdims=False)
@@ -849,20 +989,10 @@
     kept = lax.dynamic_index_in_dim(cut, core, 1, keepdims=False)
     sent = lax.dynamic_index_in_dim(cut, 1 - core, 1, keepdims=False)
     gain_terms = kept + swap(sent)
-
-    def back_columns(block, widths):
-        cuts = [lax.dynamic_slice_in_dim(block, (me ^ k) * shard, shard, 0).astype(bf16) for k in range(PLANE)]
-        return place_columns(me_scalar, trade(cuts, count), widths)
-
-    def back_rows_of(block):
-        cuts = [lax.dynamic_slice_in_dim(block, (me ^ k) * shard, shard, 1).astype(bf16) for k in range(PLANE)]
-        return place_rows(me_scalar, trade(cuts, count))
-
-    down_sum = back_rows_of(down_part)
-    ffgate_sum, ffup_sum = back_columns(ff_part, (inner, inner))
-    out_sum = back_rows_of(out_part)
     early = output, tokens_grad, gain_terms, down_sum, ffgate_sum, ffup_sum, out_sum
-    value_sum, gate_sum, query_sum, key_sum = back_columns(after(wide_part, early), (dv, dv, dk, dk))
+    value_sum, gate_sum, query_sum, key_sum = place_columns(
+        me_scalar, [after(own_part, (blocks, early)), *blocks], (dv, dv, dk, dk)
+    )
 
     return (
         output,

time: 686 us -> 664 us (0.968)
  waiting for transfers between devices: 253 us -> 226 us
    ppermute x66, waiting for transfers between devices: 228 us -> 207 us  [hop(): return lax.ppermute(value, 'dp', [(i, i ^ bits) for i in range(count)])]
    pallas_call x8 -> x7, Pallas kernels: 65.7 us -> 85.4 us  [the longest x2 42.6 us: retain(): pl.pallas_call(functools.partial(retain_kernel, first, wide, n, len(kept)...]
    pallas_call x2 -> x1, Pallas kernels: 31.9 us -> 13.3 us  [columns_grad(): pl.pallas_call(grad_kernel, grid=(width // part,), in_specs=[pl.BlockSpec...]
    all_gather x2 -> x3, waiting for transfers between devices: 11 us -> 0.01 us  [gather_depth(): lax.all_gather(block, 'dp', axis=0, tiled=True, axis_index_groups=columns)]
    unnamed x126 -> x116, local copies, waits for them, and re-layouts: 28.8 us -> 23.5 us
    ppermute x24 -> x33, waiting for transfers between devices: 14.3 us -> 19.4 us  [swap(): return lax.ppermute(value, 'tensor', [(0, 1), (1, 0)])]
  transfers between devices with their start and end apart: 96 -> 107, of which waited for: 45 -> 45; matrix products, arithmetic and copies ran while one was open for 12% -> 13% of each run, Pallas kernels for 30% -> 32%
where the time goes in v4:
time: 664 us; the launch traced here: 658 us
  Pallas kernels  237 us (36%)
  waiting for transfers between devices  226 us (34%)
  starting transfers between devices  85.9 us (13%)
  local copies, waits for them, and re-layouts  52 us (8%)
  other arithmetic  40.2 us (6%)
  between operations  16.3 us (2%)
    ppermute x66, waiting for transfers between devices, hop(): return lax.ppermute(value, 'dp', [(i, i ^ bits) for i in range(count)])  207 us
    ppermute x66, starting transfers between devices, hop(): return lax.ppermute(value, 'dp', [(i, i ^ bits) for i in range(count)])  79.6 us
    pallas_call x2, Pallas kernels, retain(): pl.pallas_call(functools.partial(retain_kernel, first, wide, n, len(kept)...  42.6 us
    pallas_call x2, Pallas kernels, hidden_units(): pl.pallas_call(functools.partial(hidden_kernel, first, wide, n, len(kept)...  39.1 us
    pallas_call x3, Pallas kernels, retain_back(): pl.pallas_call(functools.partial(retain_back_kernel, first, wide, n, len(...  30.4 us
    pallas_call x4, Pallas kernels, fold_cut(): pl.pallas_call(fold_kernel, grid=(width // part,), in_specs=given, out_sp...  24.2 us
    unnamed x116, local copies, waits for them, and re-layouts  23.5 us
    pallas_call x1, Pallas kernels, project_back(): pl.pallas_call(back_kernel, grid=(PLANE,), in_specs=[by_slot(slot_len, in...  20.4 us
  transfers between devices with their start and end apart: 107, of which 45 were waited for; matrix products, arithmetic and copies ran while one was open for 13% of the time, Pallas kernels for 32%

profile of v4, /device:TPU:0, one launch (start us, length us, event | category | flops | bytes accessed | tf_op | source)
XLA Modules:
  0.0 657.8 jit_solution(3780703292484976082)
XLA Ops:
  7.2 3.1 shard_map.220
  10.4 3.0 collective-permute-start.4
  15.0 11.4 %collective-permute-done.4 = bf16[128,2048]{1,0:T(8,128)(2,1)S(1)} collective-permute-done((bf16[128,2048]{1,0:T(8,128)(2,1)}, bf16[128,2048]{1,0:T(8,128)(2,1)S(1)}, u32[]{:S(2)}, u32[]{:S(2)}) %collective-permute-start.4) | collective-permute-done | bytes 524320 | tf_op jit(solution)/shard_map/ppermute | solution.py:729
  27.2 11.0 %collective-permute-done.5 = bf16[128,2048]{1,0:T(8,128)(2,1)S(1)} collective-permute-done((bf16[128,2048]{1,0:T(8,128)(2,1)}, bf16[128,2048]{1,0:T(8,128)(2,1)S(1)}, u32[]{:S(2)}, u32[]{:S(2)}) %collective-permute-start.5) | collective-permute-done | bytes 524320 | tf_op jit(solution)/shard_map/ppermute | solution.py:729
  60.4 18.4 %collective-permute-done.8.refs_0_ = bf16[256,2048]{1,0:T(8,128)(2,1)} collective-permute-done((bf16[256,2048]{1,0:T(8,128)(2,1)}, bf16[256,2048]{1,0:T(8,128)(2,1)}, u32[]{:S(2)}, u32[]{:S(2)}) %collective-permute-start.8) | collective-permute-done | bytes 1048608 | tf_op jit(solution)/shard_map/ppermute | solution.py:729
  84.1 6.1 collective-permute-done.12
  102.9 6.2 collective-permute-done.15.refs_1_
  109.1 8.5 %collective-permute-done.17.refs_3_ = bf16[128,1536]{1,0:T(8,128)(2,1)} collective-permute-done((bf16[128,1536]{1,0:T(8,128)(2,1)}, bf16[128,1536]{1,0:T(8,128)(2,1)}, u32[]{:S(2)}, u32[]{:S(2)}) %collective-permute-start.17) | collective-permute-done | bytes 393248 | tf_op jit(solution)/shard_map/ppermute | solution.py:729
  123.5 22.0 %collective-permute-done.19 = bf16[256,2048]{1,0:T(8,128)(2,1)} collective-permute-done((bf16[256,2048]{1,0:T(8,128)(2,1)}, bf16[256,2048]{1,0:T(8,128)(2,1)}, u32[]{:S(2)}, u32[]{:S(2)}) %collective-permute-start.19) | collective-permute-done | bytes 1048608 | tf_op jit(solution)/shard_map/ppermute | solution.py:729
  159.3 4.0 collective-permute-done.23
  163.3 2.8 collective-permute-done.24
  176.9 29.2 %shard_map.223 = (bf16[2048,256]{1,0:T(8,128)(2,1)}, bf16[2048,256]{1,0:T(8,128)(2,1)}, bf16[2048,512]{1,0:T(8,128)(2,1)}, f32[2048,512]{1,0:T(8,128)}, bf16[4,5...) custom-call(bf16[256,2048]{1,0:T(8,128)(2,1)} %collective-permute-do, ...), custom_call_target="tpu_custom_call" | custom-call | flops 14173391872 | bytes 15000000 | tf_op jit(solution)/shard_map/pallas_call | solution.py:350
  212.4 6.0 shard_map.224
  220.9 13.4 %shard_map.225 = (bf16[2048,256]{1,0:T(8,128)(2,1)}, bf16[2048,256]{1,0:T(8,128)(2,1)}, bf16[2048,512]{1,0:T(8,128)(2,1)}, f32[2048,512]{1,0:T(8,128)}, bf16[4,5...) custom-call(bf16[256,2048]{1,0:T(8,128)(2,1)} %fusion.2.refs_0_, ...), custom_call_target="tpu_custom_call", output_to_operand_aliasing={{0}: (4, {}), {1}: (5, {}), {2}: (6, {}), {3}: (7, {}), {4}... | custom-call | flops 4724464128 | bytes 15000000 | tf_op jit(solution)/shard_map/pallas_call | solution.py:350
  240.5 8.9 %collective-permute-done.30 = bf16[128,2048]{1,0:T(8,128)(2,1)S(1)} collective-permute-done((bf16[128,2048]{1,0:T(8,128)(2,1)}, bf16[128,2048]{1,0:T(8,128)(2,1)S(1)}, u32[]{:S(2)}, u32[]{:S(2)}) %collective-permute-start.30) | collective-permute-done | bytes 524320 | tf_op jit(solution)/shard_map/ppermute | solution.py:729
  249.6 10.6 %collective-permute-done.35 = bf16[128,2048]{1,0:T(8,128)(2,1)S(1)} collective-permute-done((bf16[128,2048]{1,0:T(8,128)(2,1)S(1)}, bf16[128,2048]{1,0:T(8,128)(2,1)S(1)}, u32[]{:S(2)}, u32[]{:S(2)}) %collective-permute-start.35) | collective-permute-done | bytes 524320 | tf_op jit(solution)/shard_map/ppermute | solution.py:729
  264.5 21.8 %collective-permute-done.36.refs_2_ = bf16[256,2048]{1,0:T(8,128)(2,1)S(1)} collective-permute-done((bf16[256,2048]{1,0:T(8,128)(2,1)S(1)}, bf16[256,2048]{1,0:T(8,128)(2,1)S(1)}, u32[]{:S(2)}, u32[]{:S(2)}) %collective-permute-start.36) | collective-permute-done | bytes 1048608 | tf_op jit(solution)/shard_map/ppermute | solution.py:729
  292.7 26.1 %shard_map.226 = (bf16[2048,512]{1,0:T(8,128)(2,1)}, bf16[2048,1024]{1,0:T(8,128)(2,1)}, bf16[2048,2048]{1,0:T(8,128)(2,1)}, f32[3,256,2048]{2,1,0:T(8,128)}, bf...) custom-call(bf16[256,2048]{1,0:T(8,128)(2,1)} %copy-done.17, ...), custom_call_target="tpu_custom_call" | custom-call | flops 16106127360 | bytes 15000000 | tf_op jit(solution)/shard_map/pallas_call | solution.py:478
  320.1 2.8 collective-permute-done.43.refs_1_
  322.9 13.0 %shard_map.227 = (bf16[2048,512]{1,0:T(8,128)(2,1)}, bf16[2048,1024]{1,0:T(8,128)(2,1)}, bf16[2048,2048]{1,0:T(8,128)(2,1)}, f32[1,256,2048]{2,1,0:T(8,128)}, bf16[256,2048]{1,0:T(8,128)(2,1)}) custom-call(bf16[256,2048]{1,0:T(8,128)(2,1)} %copy-done.10, ...), custom_call_target="tpu_custom_call", output_to_operand_aliasing={{0}: (5, {}), {1}: (6, {}), {2}: (7, {})} | custom-call | flops 5368709120 | bytes 15000000 | tf_op jit(solution)/shard_map/pallas_call | solution.py:478
  335.9 8.8 %shard_map.228 = bf16[2048,512]{1,0:T(8,128)(2,1)} custom-call(bf16[2048,512]{1,0:T(8,128)(2,1)} %get-tuple-element.250.left, bf16[2048,2048]{1,0:T(8,128)(2,1)} %constant_dynamic-update-slice_fusion.10.refs_8_.refs_4_.right), custom_call_target="tpu_custom_call" | custom-call | flops 4294967296 | bytes 20000000 | tf_op jit(solution)/shard_map/pallas_call | solution.py:653
  347.8 2.8 collective-permute-done.46.refs_4_
  350.8 6.1 shard_map.229
  361.1 13.3 %shard_map.230 = bf16[2048,1024]{1,0:T(8,128)(2,1)} custom-call(bf16[2048,2048]{1,0:T(8,128)(2,1)} %get-tuple-element.244.left, bf16[2048,1024]{1,0:T(8,128)(2,1)} %get-tuple-element.245.right), custom_call_target="tpu_custom_call" | custom-call | flops 8589934592 | bytes 20000000 | tf_op jit(solution)/shard_map/pallas_call | solution.py:580
  380.0 3.3 collective-permute-done.48
  385.0 8.8 %collective-permute-done.53 = bf16[128,2048]{1,0:T(8,128)(2,1)S(1)} collective-permute-done((bf16[128,2048]{1,0:T(8,128)(2,1)S(1)}, bf16[128,2048]{1,0:T(8,128)(2,1)S(1)}, u32[]{:S(2)}, u32[]{:S(2)}) %collective-permute-start.53) | collective-permute-done | bytes 524320 | tf_op jit(solution)/shard_map/ppermute | solution.py:729
  401.9 3.1 slice.181.right
  405.0 8.5 %shard_map.232 = (bf16[2048,1536]{1,0:T(8,128)(2,1)}, bf16[2048,2048]{1,0:T(8,128)(2,1)}) custom-call(bf16[256,2048]{1,0:T(8,128)(2,1)} %copy-done.7, bf16[256,2048]{1,0:T(8,128)(2,1)} %collective-permute-done.54.refs_1_, bf16[2048,2048]{1,0:T(8,128)(2,1)} %get-tuple-element.193.refs_2_.refs_4_.first.second, f32[512,512]{1,0:T(8,128)} %fusion.12.refs_9_.refs_3_.refs_5_, ...), custom_call_target="tpu_custom_call" | custom-call | flops 2147483648 | bytes 15000000 | tf_op jit(solution)/shard_map/pallas_call | solution.py:545
  413.5 12.4 %shard_map.231 = (f32[4,256,2048]{2,1,0:T(8,128)}, bf16[256,2048]{1,0:T(8,128)(2,1)}, bf16[256,2048]{1,0:T(8,128)(2,1)}, bf16[256,2048]{1,0:T(8,128)(2,1)}, bf16[256,2048]{1,0:T(8,128)(2,1)}) custom-call(bf16[2048,512]{1,0:T(8,128)(2,1)} %get-tuple-element.250.left, bf16[2048,512]{1,0:T(8,128)(2,1)} %slice.181.right), custom_call_target="tpu_custom_call" | custom-call | flops 4294967296 | bytes 20000000 | tf_op jit(solution)/shard_map/pallas_call | solution.py:373
  434.3 13.6 %shard_map.233 = (bf16[2048,1536]{1,0:T(8,128)(2,1)}, bf16[2048,2048]{1,0:T(8,128)(2,1)}) custom-call(bf16[256,2048]{1,0:T(8,128)(2,1)} %collective-permute-done.59.refs_0_, bf16[256,2048]{1,0:T(8,128)(2,1)} %copy-done.22, bf16[256,2048]{1,0:T(8,128)(2,1)} %collective-permute-done.60.refs_2_, ...), custom_call_target="tpu_custom_call", output_to_operand_aliasing={{0}: (12, {}), {1}: (13, {})} | custom-call | flops 4294967296 | bytes 15000000 | tf_op jit(solution)/shard_map/pallas_call | solution.py:545
  449.1 2.7 collective-permute-done.65.refs_1_
  451.9 8.4 %shard_map.234 = (bf16[2048,1536]{1,0:T(8,128)(2,1)}, bf16[2048,2048]{1,0:T(8,128)(2,1)}) custom-call(bf16[256,2048]{1,0:T(8,128)(2,1)} %copy-done.11, bf16[256,2048]{1,0:T(8,128)(2,1)} %collective-permute-done.65.refs_1_, bf16[2048,2048]{1,0:T(8,128)(2,1)} %get-tuple-element.193.refs_2_.refs_4_.first.second, ...), custom_call_target="tpu_custom_call", output_to_operand_aliasing={{0}: (10, {}), {1}: (11, {})} | custom-call | flops 2147483648 | bytes 15000000 | tf_op jit(solution)/shard_map/pallas_call | solution.py:545
  460.3 8.8 %shard_map.235 = bf16[2048,512]{1,0:T(8,128)(2,1)} custom-call(bf16[2048,512]{1,0:T(8,128)(2,1)} %get-tuple-element.212.left, bf16[2048,2048]{1,0:T(8,128)(2,1)} %get-tuple-element.267.right), custom_call_target="tpu_custom_call" | custom-call | flops 4294967296 | bytes 20000000 | tf_op jit(solution)/shard_map/pallas_call | solution.py:653
  469.2 18.7 %shard_map.236 = (bf16[512,1536]{1,0:T(8,128)(2,1)}, bf16[1536,1536]{1,0:T(8,128)(2,1)}) custom-call(s32[1]{0:T(128)} %bitcast.6.me_ref.refs_6_, bf16[2048,2048]{1,0:T(8,128)(2,1)} %get-tuple-element.213.left, bf16[2048,1536]{1,0:T(8,128)(2,1)} %get-tuple-element.280.right.left), custom_call_target="tpu_custom_call" | custom-call | flops 12884901888 | bytes 20000000 | tf_op jit(solution)/shard_map/pallas_call | solution.py:631
  490.9 3.1 collective-permute-done.57.refs_4_
  494.0 6.2 shard_map.237
  504.3 20.4 %shard_map.238 = (f32[4,256,2048]{2,1,0:T(8,128)}, bf16[256,2048]{1,0:T(8,128)(2,1)}, bf16[256,2048]{1,0:T(8,128)(2,1)}, bf16[256,2048]{1,0:T(8,128)(2,1)}, bf16[256,2048]{1,0:T(8,128)(2,1)}) custom-call(bf16[2048,1536]{1,0:T(8,128)(2,1)} %get-tuple-element.280.right.left, bf16[2048,2048]{1,0:T(8,128)(2,1)} %get-tuple-element.193.refs_2_.refs_4_.first.second, ...), custom_call_target="tpu_custom_call" | custom-call | flops 12884901888 | bytes 20000000 | tf_op jit(solution)/shard_map/pallas_call | solution.py:397
  531.5 7.8 %collective-permute-done.71 = bf16[128,2048]{1,0:T(8,128)(2,1)S(1)} collective-permute-done((bf16[128,2048]{1,0:T(8,128)(2,1)S(1)}, bf16[128,2048]{1,0:T(8,128)(2,1)S(1)}, u32[]{:S(2)}, u32[]{:S(2)}) %collective-permute-start.71) | collective-permute-done | bytes 524320 | tf_op jit(solution)/shard_map/ppermute | solution.py:729
  540.5 3.5 fusion.19
  545.0 5.9 shard_map.239
  555.1 11.0 %collective-permute-done.77 = bf16[128,2048]{1,0:T(8,128)(2,1)S(1)} collective-permute-done((bf16[128,2048]{1,0:T(8,128)(2,1)}, bf16[128,2048]{1,0:T(8,128)(2,1)S(1)}, u32[]{:S(2)}, u32[]{:S(2)}) %collective-permute-start.77) | collective-permute-done | bytes 524320 | tf_op jit(solution)/shard_map/ppermute | solution.py:729
  582.3 6.4 collective-permute-done.81
  598.3 2.9 collective-permute-start.85
  610.5 8.3 %collective-permute-done.94.refs_2_ = bf16[128,1024]{1,0:T(8,128)(2,1)S(1)} collective-permute-done((bf16[128,1024]{1,0:T(8,128)(2,1)S(1)}, bf16[128,1024]{1,0:T(8,128)(2,1)S(1)}, u32[]{:S(2)}, u32[]{:S(2)}) %collective-permute-start.94) | collective-permute-done | bytes 262176 | tf_op jit(solution)/shard_map/ppermute | solution.py:729
  628.0 6.7 %collective-permute-done.83.refs_2_ = bf16[128,1536]{1,0:T(8,128)(2,1)} collective-permute-done((bf16[128,1536]{1,0:T(8,128)(2,1)S(1)}, bf16[128,1536]{1,0:T(8,128)(2,1)}, u32[]{:S(2)}, u32[]{:S(2)}) %collective-permute-start.83) | collective-permute-done | bytes 393248 | tf_op jit(solution)/shard_map/ppermute | solution.py:729
  636.3 3.4 multiply_convert_fusion
  643.5 3.6 fusion.7
  647.6 3.2 shard_map.243
  (395 shorter events, 201.7 us)
Async XLA Ops:
  7.2 169.7 %all-gather.4.cloned.1.call-start = ((), (), s32[]{:S(2)}) async-start(), calls=%async_computation.5 | async-start | bytes 2621440 | tf_op jit(solution)/shard_map/all_gather | solution.py:832
  10.4 166.5 %all-gather.6.cloned.1.call-start = ((), (), s32[]{:S(2)}) async-start(), calls=%async_computation.6 | async-start | bytes 7864320 | tf_op jit(solution)/shard_map/all_gather | solution.py:832
  13.4 24.8 %collective-permute-start.5 = (bf16[128,2048]{1,0:T(8,128)(2,1)}, bf16[128,2048]{1,0:T(8,128)(2,1)S(1)}, u32[]{:S(2)}, u32[]{:S(2)}) collective-permute-start(bf16[128,2048]{1,0:T(8,128)(2,1)} %get-tuple-element.164), channel_id=1, source_target_pairs={{0,4},{2,6},{4,0},{6,2},{8,12},{10,14},{12,8},{14,10},{16,20},{18,... | collective-permute-start | bytes 1572872 | tf_op jit(solution)/shard_map/ppermute | solution.py:729
  14.9 24.1 %collective-permute-start.6 = (bf16[128,2048]{1,0:T(8,128)(2,1)}, bf16[128,2048]{1,0:T(8,128)(2,1)S(1)}, u32[]{:S(2)}, u32[]{:S(2)}) collective-permute-start(bf16[128,2048]{1,0:T(8,128)(2,1)} %get-tuple-element.165), channel_id=1, source_target_pairs={{0,6},{2,4},{4,2},{6,0},{8,14},{10,12},{12,10},{14,8},{16,22},{18,... | collective-permute-start | bytes 1572872 | tf_op jit(solution)/shard_map/ppermute | solution.py:729
  39.9 252.8 %all-gather.8.cloned.1.call-start = ((), (), s32[]{:S(2)}) async-start(), calls=%async_computation.7 | async-start | bytes 7864320 | tf_op jit(solution)/shard_map/all_gather | solution.py:832
  57.6 21.2 %collective-permute-start.8 = (bf16[256,2048]{1,0:T(8,128)(2,1)}, bf16[256,2048]{1,0:T(8,128)(2,1)}, u32[]{:S(2)}, u32[]{:S(2)}) collective-permute-start(bf16[256,2048]{1,0:T(8,128)(2,1)} %fusion.2.refs_0_), channel_id=1, source_target_pairs={{0,2},{2,0},{4,6},{6,4},{8,10},{10,8},{12,14},{14,12},{16,18},{18,... | collective-permute-start | bytes 3145736 | tf_op jit(solution)/shard_map/ppermute | solution.py:729
  58.9 23.4 %collective-permute-start.10 = (bf16[256,2048]{1,0:T(8,128)(2,1)}, bf16[256,2048]{1,0:T(8,128)(2,1)}, u32[]{:S(2)}, u32[]{:S(2)}) collective-permute-start(bf16[256,2048]{1,0:T(8,128)(2,1)} %fusion.2.refs_0_), channel_id=1, source_target_pairs={{0,4},{2,6},{4,0},{6,2},{8,12},{10,14},{12,8},{14,10},{16,20},{18,... | collective-permute-start | bytes 3145736 | tf_op jit(solution)/shard_map/ppermute | solution.py:729
  98.0 19.6 %collective-permute-start.17 = (bf16[128,1536]{1,0:T(8,128)(2,1)}, bf16[128,1536]{1,0:T(8,128)(2,1)}, u32[]{:S(2)}, u32[]{:S(2)}) collective-permute-start(bf16[128,1536]{1,0:T(8,128)(2,1)} %get-tuple-element.174), channel_id=1, source_target_pairs={{0,6},{2,4},{4,2},{6,0},{8,14},{10,12},{12,10},{14,8},{16,22},{18,... | collective-permute-start | bytes 1179656 | tf_op jit(solution)/shard_map/ppermute | solution.py:729
  120.4 25.2 %collective-permute-start.19 = (bf16[256,2048]{1,0:T(8,128)(2,1)}, bf16[256,2048]{1,0:T(8,128)(2,1)}, u32[]{:S(2)}, u32[]{:S(2)}) collective-permute-start(bf16[256,2048]{1,0:T(8,128)(2,1)} %fusion.11), channel_id=1, source_target_pairs={{0,2},{2,0},{4,6},{6,4},{8,10},{10,8},{12,14},{14,12},{16,18},{18,... | collective-permute-start | bytes 3145736 | tf_op jit(solution)/shard_map/ppermute | solution.py:729
  122.4 27.4 %collective-permute-start.21 = (bf16[256,2048]{1,0:T(8,128)(2,1)}, bf16[256,2048]{1,0:T(8,128)(2,1)}, u32[]{:S(2)}, u32[]{:S(2)}) collective-permute-start(bf16[256,2048]{1,0:T(8,128)(2,1)} %fusion.11), channel_id=1, source_target_pairs={{0,4},{2,6},{4,0},{6,2},{8,12},{10,14},{12,8},{14,10},{16,20},{18,... | collective-permute-start | bytes 3145736 | tf_op jit(solution)/shard_map/ppermute | solution.py:729
  123.4 31.2 %collective-permute-start.18 = (bf16[256,2048]{1,0:T(8,128)(2,1)}, bf16[256,2048]{1,0:T(8,128)(2,1)}, u32[]{:S(2)}, u32[]{:S(2)}) collective-permute-start(bf16[256,2048]{1,0:T(8,128)(2,1)} %fusion.11), channel_id=1, source_target_pairs={{0,1},{1,0},{2,3},{3,2},{4,5},{5,4},{6,7},{7,6},{8,9},{9,8},{10,11... | collective-permute-start | bytes 3145736 | tf_op jit(solution)/shard_map/ppermute | solution.py:733
  145.6 21.7 %collective-permute-start.20 = (bf16[256,2048]{1,0:T(8,128)(2,1)}, bf16[256,2048]{1,0:T(8,128)(2,1)}, u32[]{:S(2)}, u32[]{:S(2)}) collective-permute-start(bf16[256,2048]{1,0:T(8,128)(2,1)} %collective-permute-done.19), channel_id=1, source_target_pairs={{0,1},{1,0},{2,3},{3,2},{4,5},{5,4},{6,7},{7,6},{8,9},{9,8},{10,11... | collective-permute-start | bytes 3145736 | tf_op jit(solution)/shard_map/ppermute | solution.py:733
  154.5 294.6 %reduce-scatter.6.cloned.1.call-start = ((), (), s32[]{:S(2)}) async-start(), calls=%async_computation.8 | async-start | bytes 2621440 | tf_op jit(solution)/shard_map/reduce_scatter | solution.py:835
  154.5 17.4 %collective-permute-start.22 = (bf16[256,2048]{1,0:T(8,128)(2,1)}, bf16[256,2048]{1,0:T(8,128)(2,1)S(1)}, u32[]{:S(2)}, u32[]{:S(2)}) collective-permute-start(bf16[256,2048]{1,0:T(8,128)(2,1)} %collective-permute-done.21), channel_id=1, source_target_pairs={{0,1},{1,0},{2,3},{3,2},{4,5},{5,4},{6,7},{7,6},{8,9},{9,8},{10,11... | collective-permute-start | bytes 3145736 | tf_op jit(solution)/shard_map/ppermute | solution.py:733
  218.3 17.7 %collective-permute-start.31 = (bf16[128,2048]{1,0:T(8,128)(2,1)}, bf16[128,2048]{1,0:T(8,128)(2,1)S(1)}, u32[]{:S(2)}, u32[]{:S(2)}) collective-permute-start(bf16[128,2048]{1,0:T(8,128)(2,1)} %get-tuple-element.189), channel_id=1, source_target_pairs={{0,2},{2,0},{4,6},{6,4},{8,10},{10,8},{12,14},{14,12},{16,18},{18,... | collective-permute-start | bytes 1572872 | tf_op jit(solution)/shard_map/ppermute | solution.py:729
  237.5 22.7 %collective-permute-start.35 = (bf16[128,2048]{1,0:T(8,128)(2,1)S(1)}, bf16[128,2048]{1,0:T(8,128)(2,1)S(1)}, u32[]{:S(2)}, u32[]{:S(2)}) collective-permute-start(bf16[128,2048]{1,0:T(8,128)(2,1)S(1)} %add_convert_fusion.6), channel_id=1, source_target_pairs={{0,2},{2,0},{4,6},{6,4},{8,10},{10,8},{12,14},{14,12},{16,18},{18,... | collective-permute-start | bytes 1572872 | tf_op jit(solution)/shard_map/ppermute | solution.py:729
  239.4 20.8 %collective-permute-start.33 = (bf16[128,2048]{1,0:T(8,128)(2,1)S(1)}, bf16[128,2048]{1,0:T(8,128)(2,1)S(1)}, u32[]{:S(2)}, u32[]{:S(2)}) collective-permute-start(bf16[128,2048]{1,0:T(8,128)(2,1)S(1)} %add_convert_fusion.7), channel_id=1, source_target_pairs={{0,4},{2,6},{4,0},{6,2},{8,12},{10,14},{12,8},{14,10},{16,20},{18,... | collective-permute-start | bytes 1572872 | tf_op jit(solution)/shard_map/ppermute | solution.py:729
  261.5 24.9 %collective-permute-start.36 = (bf16[256,2048]{1,0:T(8,128)(2,1)S(1)}, bf16[256,2048]{1,0:T(8,128)(2,1)S(1)}, u32[]{:S(2)}, u32[]{:S(2)}) collective-permute-start(bf16[256,2048]{1,0:T(8,128)(2,1)S(1)} %multiply_convert_fusion.1.refs_0_), channel_id=1, source_target_pairs={{0,2},{2,0},{4,6},{6,4},{8,10},{10,8},{12,14},{14,12},{16,18},{18,... | collective-permute-start | bytes 3145736 | tf_op jit(solution)/shard_map/ppermute | solution.py:729
  263.3 24.3 %collective-permute-start.37 = (bf16[256,2048]{1,0:T(8,128)(2,1)S(1)}, bf16[256,2048]{1,0:T(8,128)(2,1)}, u32[]{:S(2)}, u32[]{:S(2)}) collective-permute-start(bf16[256,2048]{1,0:T(8,128)(2,1)S(1)} %multiply_convert_fusion.1.refs_0_), channel_id=1, source_target_pairs={{0,4},{2,6},{4,0},{6,2},{8,12},{10,14},{12,8},{14,10},{16,20},{18,... | collective-permute-start | bytes 3145736 | tf_op jit(solution)/shard_map/ppermute | solution.py:729
  264.5 28.2 %collective-permute-start.40 = (bf16[256,2048]{1,0:T(8,128)(2,1)S(1)}, bf16[256,2048]{1,0:T(8,128)(2,1)}, u32[]{:S(2)}, u32[]{:S(2)}) collective-permute-start(bf16[256,2048]{1,0:T(8,128)(2,1)S(1)} %multiply_convert_fusion.1.refs_0_), channel_id=1, source_target_pairs={{0,1},{1,0},{2,3},{3,2},{4,5},{5,4},{6,7},{7,6},{8,9},{9,8},{10,11... | collective-permute-start | bytes 3145736 | tf_op jit(solution)/shard_map/ppermute | solution.py:733
  290.9 28.0 %collective-permute-start.38 = (bf16[128,2048]{1,0:T(8,128)(2,1)}, bf16[128,2048]{1,0:T(8,128)(2,1)S(1)}, u32[]{:S(2)}, u32[]{:S(2)}) collective-permute-start(bf16[128,2048]{1,0:T(8,128)(2,1)} %slice.141), channel_id=1, source_target_pairs={{0,4},{2,6},{4,0},{6,2},{8,12},{10,14},{12,8},{14,10},{16,20},{18,... | collective-permute-start | bytes 1572872 | tf_op jit(solution)/shard_map/ppermute | solution.py:729
  292.1 26.8 %collective-permute-start.39 = (bf16[128,2048]{1,0:T(8,128)(2,1)}, bf16[128,2048]{1,0:T(8,128)(2,1)}, u32[]{:S(2)}, u32[]{:S(2)}) collective-permute-start(bf16[128,2048]{1,0:T(8,128)(2,1)} %slice.142), channel_id=1, source_target_pairs={{0,2},{2,0},{4,6},{6,4},{8,10},{10,8},{12,14},{14,12},{16,18},{18,... | collective-permute-start | bytes 1572872 | tf_op jit(solution)/shard_map/ppermute | solution.py:729
  344.7 159.6 %reduce-scatter.8.cloned.1.call-start = ((), (), s32[]{:S(2)}) async-start(), calls=%async_computation.9 | async-start | bytes 5242880 | tf_op jit(solution)/shard_map/reduce_scatter | solution.py:835
  346.4 33.3 %collective-permute-start.44 = (bf16[256,2048]{1,0:T(8,128)(2,1)}, bf16[256,2048]{1,0:T(8,128)(2,1)S(1)}, u32[]{:S(2)}, u32[]{:S(2)}) collective-permute-start(bf16[256,2048]{1,0:T(8,128)(2,1)} %get-tuple-element.227), channel_id=1, source_target_pairs={{0,1},{1,0},{2,3},{3,2},{4,5},{5,4},{6,7},{7,6},{8,9},{9,8},{10,11... | collective-permute-start | bytes 3145736 | tf_op jit(solution)/shard_map/ppermute | solution.py:733
  357.0 17.7 %collective-permute-start.49 = (bf16[128,2048]{1,0:T(8,128)(2,1)}, bf16[128,2048]{1,0:T(8,128)(2,1)}, u32[]{:S(2)}, u32[]{:S(2)}) collective-permute-start(bf16[128,2048]{1,0:T(8,128)(2,1)} %get-tuple-element.240), channel_id=1, source_target_pairs={{0,2},{2,0},{4,6},{6,4},{8,10},{10,8},{12,14},{14,12},{16,18},{18,... | collective-permute-start | bytes 1572872 | tf_op jit(solution)/shard_map/ppermute | solution.py:729
  359.3 24.0 %collective-permute-start.48 = (bf16[128,2048]{1,0:T(8,128)(2,1)}, bf16[128,2048]{1,0:T(8,128)(2,1)S(1)}, u32[]{:S(2)}, u32[]{:S(2)}) collective-permute-start(bf16[128,2048]{1,0:T(8,128)(2,1)} %get-tuple-element.238), channel_id=1, source_target_pairs={{0,2},{2,0},{4,6},{6,4},{8,10},{10,8},{12,14},{14,12},{16,18},{18,... | collective-permute-start | bytes 1572872 | tf_op jit(solution)/shard_map/ppermute | solution.py:729
  359.8 25.1 %collective-permute-start.52 = (bf16[128,2048]{1,0:T(8,128)(2,1)}, bf16[128,2048]{1,0:T(8,128)(2,1)}, u32[]{:S(2)}, u32[]{:S(2)}) collective-permute-start(bf16[128,2048]{1,0:T(8,128)(2,1)} %get-tuple-element.247), channel_id=1, source_target_pairs={{0,4},{2,6},{4,0},{6,2},{8,12},{10,14},{12,8},{14,10},{16,20},{18,... | collective-permute-start | bytes 1572872 | tf_op jit(solution)/shard_map/ppermute | solution.py:729
  374.4 180.7 %reduce-scatter.10.cloned.1.call-start = ((), (), s32[]{:S(2)}) async-start(), calls=%async_computation.10 | async-start | bytes 2621440 | tf_op jit(solution)/shard_map/reduce_scatter | solution.py:835
  376.2 17.5 %collective-permute-start.53 = (bf16[128,2048]{1,0:T(8,128)(2,1)S(1)}, bf16[128,2048]{1,0:T(8,128)(2,1)S(1)}, u32[]{:S(2)}, u32[]{:S(2)}) collective-permute-start(bf16[128,2048]{1,0:T(8,128)(2,1)S(1)} %add_convert_fusion.4), channel_id=1, source_target_pairs={{0,2},{2,0},{4,6},{6,4},{8,10},{10,8},{12,14},{14,12},{16,18},{18,... | collective-permute-start | bytes 1572872 | tf_op jit(solution)/shard_map/ppermute | solution.py:729
  400.7 25.7 %collective-permute-start.59 = (bf16[256,2048]{1,0:T(8,128)(2,1)S(1)}, bf16[256,2048]{1,0:T(8,128)(2,1)}, u32[]{:S(2)}, u32[]{:S(2)}) collective-permute-start(bf16[256,2048]{1,0:T(8,128)(2,1)S(1)} %get-tuple-element.318.refs_0_), channel_id=1, source_target_pairs={{0,2},{2,0},{4,6},{6,4},{8,10},{10,8},{12,14},{14,12},{16,18},{18,... | collective-permute-start | bytes 3145736 | tf_op jit(solution)/shard_map/ppermute | solution.py:729
  401.4 25.4 %collective-permute-start.60 = (bf16[256,2048]{1,0:T(8,128)(2,1)S(1)}, bf16[256,2048]{1,0:T(8,128)(2,1)}, u32[]{:S(2)}, u32[]{:S(2)}) collective-permute-start(bf16[256,2048]{1,0:T(8,128)(2,1)S(1)} %get-tuple-element.318.refs_0_), channel_id=1, source_target_pairs={{0,4},{2,6},{4,0},{6,2},{8,12},{10,14},{12,8},{14,10},{16,20},{18,... | collective-permute-start | bytes 3145736 | tf_op jit(solution)/shard_map/ppermute | solution.py:729
  469.1 132.2 %reduce-scatter.14.cloned.1.call-start = ((), (), s32[]{:S(2)}) async-start(), calls=%async_computation.12 | async-start | bytes 5898240 | tf_op jit(solution)/shard_map/reduce_scatter | solution.py:835
  487.9 159.7 %reduce-scatter.12.cloned.1.call-start = ((), (), s32[]{:S(2)}) async-start(), calls=%async_computation.11 | async-start | bytes 1966080 | tf_op jit(solution)/shard_map/reduce_scatter | solution.py:835
  489.3 40.1 %collective-permute-start.55 = (bf16[256,2048]{1,0:T(8,128)(2,1)}, bf16[256,2048]{1,0:T(8,128)(2,1)}, u32[]{:S(2)}, u32[]{:S(2)}) collective-permute-start(bf16[256,2048]{1,0:T(8,128)(2,1)} %get-tuple-element.252), channel_id=1, source_target_pairs={{0,1},{1,0},{2,3},{3,2},{4,5},{5,4},{6,7},{7,6},{8,9},{9,8},{10,11... | collective-permute-start | bytes 3145736 | tf_op jit(solution)/shard_map/ppermute | solution.py:733
  500.2 24.5 %collective-permute-start.67 = (bf16[128,2048]{1,0:T(8,128)(2,1)}, bf16[128,2048]{1,0:T(8,128)(2,1)}, u32[]{:S(2)}, u32[]{:S(2)}) collective-permute-start(bf16[128,2048]{1,0:T(8,128)(2,1)} %get-tuple-element.278), channel_id=1, source_target_pairs={{0,2},{2,0},{4,6},{6,4},{8,10},{10,8},{12,14},{14,12},{16,18},{18,... | collective-permute-start | bytes 1572872 | tf_op jit(solution)/shard_map/ppermute | solution.py:729
  500.7 23.9 %collective-permute-start.68 = (bf16[128,2048]{1,0:T(8,128)(2,1)}, bf16[128,2048]{1,0:T(8,128)(2,1)}, u32[]{:S(2)}, u32[]{:S(2)}) collective-permute-start(bf16[128,2048]{1,0:T(8,128)(2,1)} %get-tuple-element.279), channel_id=1, source_target_pairs={{0,4},{2,6},{4,0},{6,2},{8,12},{10,14},{12,8},{14,10},{16,20},{18,... | collective-permute-start | bytes 1572872 | tf_op jit(solution)/shard_map/ppermute | solution.py:729
  502.1 27.4 %collective-permute-start.66 = (bf16[128,2048]{1,0:T(8,128)(2,1)}, bf16[128,2048]{1,0:T(8,128)(2,1)S(1)}, u32[]{:S(2)}, u32[]{:S(2)}) collective-permute-start(bf16[128,2048]{1,0:T(8,128)(2,1)} %get-tuple-element.276), channel_id=1, source_target_pairs={{0,2},{2,0},{4,6},{6,4},{8,10},{10,8},{12,14},{14,12},{16,18},{18,... | collective-permute-start | bytes 1572872 | tf_op jit(solution)/shard_map/ppermute | solution.py:729
  503.4 26.5 %collective-permute-start.70 = (bf16[128,2048]{1,0:T(8,128)(2,1)}, bf16[128,2048]{1,0:T(8,128)(2,1)}, u32[]{:S(2)}, u32[]{:S(2)}) collective-permute-start(bf16[128,2048]{1,0:T(8,128)(2,1)} %get-tuple-element.287), channel_id=1, source_target_pairs={{0,4},{2,6},{4,0},{6,2},{8,12},{10,14},{12,8},{14,10},{16,20},{18,... | collective-permute-start | bytes 1572872 | tf_op jit(solution)/shard_map/ppermute | solution.py:729
  553.8 24.7 %collective-permute-start.72 = (bf16[256,2048]{1,0:T(8,128)(2,1)}, bf16[256,2048]{1,0:T(8,128)(2,1)S(1)}, u32[]{:S(2)}, u32[]{:S(2)}) collective-permute-start(bf16[256,2048]{1,0:T(8,128)(2,1)} %get-tuple-element.282), channel_id=1, source_target_pairs={{0,1},{1,0},{2,3},{3,2},{4,5},{5,4},{6,7},{7,6},{8,9},{9,8},{10,11... | collective-permute-start | bytes 3145736 | tf_op jit(solution)/shard_map/ppermute | solution.py:733
  553.8 26.4 %collective-permute-start.76 = (bf16[128,2048]{1,0:T(8,128)(2,1)}, bf16[128,2048]{1,0:T(8,128)(2,1)}, u32[]{:S(2)}, u32[]{:S(2)}) collective-permute-start(bf16[128,2048]{1,0:T(8,128)(2,1)} %get-tuple-element.296), channel_id=1, source_target_pairs={{0,2},{2,0},{4,6},{6,4},{8,10},{10,8},{12,14},{14,12},{16,18},{18,... | collective-permute-start | bytes 1572872 | tf_op jit(solution)/shard_map/ppermute | solution.py:729
  554.4 26.8 %collective-permute-start.80 = (bf16[128,2048]{1,0:T(8,128)(2,1)}, bf16[128,2048]{1,0:T(8,128)(2,1)}, u32[]{:S(2)}, u32[]{:S(2)}) collective-permute-start(bf16[128,2048]{1,0:T(8,128)(2,1)} %get-tuple-element.301), channel_id=1, source_target_pairs={{0,4},{2,6},{4,0},{6,2},{8,12},{10,14},{12,8},{14,10},{16,20},{18,... | collective-permute-start | bytes 1572872 | tf_op jit(solution)/shard_map/ppermute | solution.py:729
  570.0 18.7 %collective-permute-start.81 = (bf16[128,2048]{1,0:T(8,128)(2,1)}, bf16[128,2048]{1,0:T(8,128)(2,1)}, u32[]{:S(2)}, u32[]{:S(2)}) collective-permute-start(bf16[128,2048]{1,0:T(8,128)(2,1)} %add_convert_fusion), channel_id=1, source_target_pairs={{0,2},{2,0},{4,6},{6,4},{8,10},{10,8},{12,14},{14,12},{16,18},{18,... | collective-permute-start | bytes 1572872 | tf_op jit(solution)/shard_map/ppermute | solution.py:729
  572.4 18.1 %collective-permute-start.79 = (bf16[128,2048]{1,0:T(8,128)(2,1)}, bf16[128,2048]{1,0:T(8,128)(2,1)S(1)}, u32[]{:S(2)}, u32[]{:S(2)}) collective-permute-start(bf16[128,2048]{1,0:T(8,128)(2,1)} %add_convert_fusion.1), channel_id=1, source_target_pairs={{0,4},{2,6},{4,0},{6,2},{8,12},{10,14},{12,8},{14,10},{16,20},{18,... | collective-permute-start | bytes 1572872 | tf_op jit(solution)/shard_map/ppermute | solution.py:729
  588.7 18.8 %collective-permute-start.93 = (bf16[128,1024]{1,0:T(8,128)(2,1)}, bf16[128,1024]{1,0:T(8,128)(2,1)S(1)}, u32[]{:S(2)}, u32[]{:S(2)}) collective-permute-start(bf16[128,1024]{1,0:T(8,128)(2,1)} %get-tuple-element.337), channel_id=1, source_target_pairs={{0,2},{2,0},{4,6},{6,4},{8,10},{10,8},{12,14},{14,12},{16,18},{18,... | collective-permute-start | bytes 786440 | tf_op jit(solution)/shard_map/ppermute | solution.py:729
  605.5 19.9 %collective-permute-start.95 = (bf16[128,1024]{1,0:T(8,128)(2,1)}, bf16[128,1024]{1,0:T(8,128)(2,1)}, u32[]{:S(2)}, u32[]{:S(2)}) collective-permute-start(bf16[128,1024]{1,0:T(8,128)(2,1)} %get-tuple-element.335), channel_id=1, source_target_pairs={{0,6},{2,4},{4,2},{6,0},{8,14},{10,12},{12,10},{14,8},{16,22},{18,... | collective-permute-start | bytes 786440 | tf_op jit(solution)/shard_map/ppermute | solution.py:729
  606.9 21.0 %collective-permute-start.82 = (bf16[128,1536]{1,0:T(8,128)(2,1)}, bf16[128,1536]{1,0:T(8,128)(2,1)}, u32[]{:S(2)}, u32[]{:S(2)}) collective-permute-start(bf16[128,1536]{1,0:T(8,128)(2,1)} %get-tuple-element.334), channel_id=1, source_target_pairs={{0,2},{2,0},{4,6},{6,4},{8,10},{10,8},{12,14},{14,12},{16,18},{18,... | collective-permute-start | bytes 1179656 | tf_op jit(solution)/shard_map/ppermute | solution.py:729
  607.5 27.2 %collective-permute-start.83 = (bf16[128,1536]{1,0:T(8,128)(2,1)S(1)}, bf16[128,1536]{1,0:T(8,128)(2,1)}, u32[]{:S(2)}, u32[]{:S(2)}) collective-permute-start(bf16[128,1536]{1,0:T(8,128)(2,1)S(1)} %get-tuple-element.333), channel_id=1, source_target_pairs={{0,4},{2,6},{4,0},{6,2},{8,12},{10,14},{12,8},{14,10},{16,20},{18,... | collective-permute-start | bytes 1179656 | tf_op jit(solution)/shard_map/ppermute | solution.py:729
  609.0 25.7 %collective-permute-start.84 = (bf16[128,1536]{1,0:T(8,128)(2,1)S(1)}, bf16[128,1536]{1,0:T(8,128)(2,1)}, u32[]{:S(2)}, u32[]{:S(2)}) collective-permute-start(bf16[128,1536]{1,0:T(8,128)(2,1)S(1)} %get-tuple-element.332), channel_id=1, source_target_pairs={{0,6},{2,4},{4,2},{6,0},{8,14},{10,12},{12,10},{14,8},{16,22},{18,... | collective-permute-start | bytes 1179656 | tf_op jit(solution)/shard_map/ppermute | solution.py:729
  (107 other events, 1047.2 us)
Sparse Core Ops, SparseCore 0:
  10.5 48.8 all-gather.3
  60.9 114.0 all-gather.5
  176.6 113.5 all-gather.7
  344.8 44.3 reduce-scatter.5
  391.5 76.0 reduce-scatter.7
  469.8 44.4 reduce-scatter.9
  516.6 84.6 reduce-scatter.13
  603.7 35.8 reduce-scatter.11

commit v5 on v4

--- a/solution.py
+++ b/solution.py
@@ -11,7 +11,6 @@
 DV = 512
 PLANE = 4
 SLOTS = ((0, 1), (1, 3), (3, 4))
-VMEM_BYTES = 62 * 1024 * 1024
 
 norm_eps = 1e-06
 group_floor = 1.0
@@ -30,8 +29,8 @@
     return pl.CostEstimate(flops=int(flops), bytes_accessed=int(bytes_accessed), transcendentals=0)
 
 
-def params():
-    return pltpu.CompilerParams(vmem_limit_bytes=VMEM_BYTES)
+def params(mib=62):
+    return pltpu.CompilerParams(vmem_limit_bytes=mib * 1024 * 1024)
 
 
 ANY = pl.BlockSpec(memory_space=pl.ANY)
@@ -215,8 +214,8 @@
     return [by_slot(1, rows, width), *fars]
 
 
-def split_shapes(n, rows, width):
-    return [shaped((n, rows, width), f32)] + [shaped((rows, width), bf16)] * n
+def split_shapes(n, rows, width, place=shaped):
+    return [place((n, rows, width), f32)] + [place((rows, width), bf16)] * n
 
 
 def weave(place, own, others, target, width, sem):
@@ -365,7 +364,7 @@
         split_out(terms, near_ref, far_refs, columns)
 
 
-def project(left, right, wide):
+def project(left, right, block, wide):
     total, inner = left.shape
     width = right.shape[0]
     slot_len = total // PLANE
@@ -373,7 +372,10 @@
     return pl.pallas_call(
         functools.partial(project_kernel, wide),
         grid=(PLANE,),
-        in_specs=[by_slot(slot_len, inner), whole(right.shape)],
+        in_specs=[
+            by_slot(slot_len, inner),
+            pl.BlockSpec((width, inner), lambda i: (0, block), pipeline_mode=pl.Buffered(1)),
+        ],
         out_specs=split_specs(PLANE, rows, width),
         out_shape=split_shapes(PLANE, rows, width),
         compiler_params=params(),
@@ -439,9 +441,9 @@
 
 
 def hidden_kernel(first, wide, n, n_kept, *refs):
-    pieces, (weights, down_weights, back) = refs[: 2 * n], refs[2 * n : 2 * n + 3]
-    act_ref, grad_ref, rows_ref, near_ref, *far_refs = refs[2 * n + 3 + n_kept : 3 * n + 7 + n_kept]
-    held, sem, out_sem = refs[3 * n + 7 + n_kept :]
+    pieces, (joined, back) = refs[: 2 * n], refs[2 * n : 2 * n + 2]
+    act_ref, grad_ref, rows_ref, near_ref, *far_refs = refs[2 * n + 2 + n_kept : 3 * n + 6 + n_kept]
+    held, sem, out_sem = refs[3 * n + 6 + n_kept :]
     rows = load_pieces(pieces, held, sem)
     step = pl.program_id(0)
     slot_len = rows.shape[0]
@@ -450,7 +452,7 @@
         held.at[step], rows_ref.at[pl.ds((step + first) * slot_len, slot_len)], out_sem
     )
     keep.start()
-    weights = weights[...]
+    weights, down_weights = joined[:, : 2 * inner], joined[:, 2 * inner :]
     up = dot(rows, weights[:, :inner])
     value = dot(rows, weights[:, inner:])
     slope = jnp.tanh(tanh_scale * (up + tanh_cubic * (up * up * up)))
@@ -459,7 +461,7 @@
     rise = 0.5 * (1.0 + slope) + 0.5 * up * (1.0 - slope * slope) * (
         tanh_scale * (1.0 + 3.0 * tanh_cubic * (up * up))
     )
-    grad = times_rows_back(back[...], down_weights[...], wide)
+    grad = times_rows_back(back[...], down_weights, wide)
     grad_ref[:, :inner] = (grad * value * rise).astype(bf16)
     grad_ref[:, inner:] = (grad * gelu).astype(bf16)
     split_out(dot_nt(grad_ref[...], weights), near_ref, far_refs, slice(None))
@@ -480,27 +482,26 @@
         grid=(n,),
         in_specs=[ANY] * (2 * n)
         + [
-            pl.BlockSpec((width, 2 * inner), lambda i: (0, 0), pipeline_mode=pl.Buffered(1)),
-            pl.BlockSpec((width, inner), lambda i: (0, 2), pipeline_mode=pl.Buffered(1)),
+            pl.BlockSpec(memory_space=pltpu.VMEM),
             at(width),
         ]
         + [ANY] * len(kept),
         out_specs=[at(inner), at(2 * inner), ANY, *split_specs(n, rows, width)],
         out_shape=[
-            shaped((total, inner), bf16),
-            shaped((total, 2 * inner), bf16),
-            shaped((total, width), bf16),
-            *split_shapes(n, rows, width),
+            pltpu.HBM((total, inner), bf16),
+            pltpu.HBM((total, 2 * inner), bf16),
+            pltpu.HBM((total, width), bf16),
+            *split_shapes(n, rows, width, pltpu.HBM),
         ],
         scratch_shapes=[
             pltpu.VMEM((n, slot_len, width), bf16),
             pltpu.SemaphoreType.DMA((2 * n,)),
             pltpu.SemaphoreType.DMA,
         ],
-        input_output_aliases={2 * n + 3 + i: i for i in range(len(kept))},
-        compiler_params=params(),
+        input_output_aliases={2 * n + 2 + i: i for i in range(len(kept))},
+        compiler_params=params(44),
         cost_estimate=cost(10 * n * slot_len * width * inner, 15e6),
-    )(*pieces, joined, joined, back, *kept)
+    )(*pieces, joined, back, *kept)
 
 
 def retain_back_kernel(first, wide, n, n_kept, *refs):
@@ -723,6 +724,69 @@
         compiler_params=params(),
         cost_estimate=cost(0, 4e6),
     )(me, *blocks)
+
+
+def cut_sums(me, columns, rows):
+    width = columns.shape[1]
+    shard = columns.shape[0] // PLANE
+    blocks = [r.shape[0] // shard for r in rows]
+
+    def plan(place, ins, outs):
+        copies = []
+        for k in range(PLANE):
+            copies.append((ins[0].at[lanes(place ^ k, shard), :], outs[k].at[:, pl.ds(0, width)]))
+            at = width
+            for r, count in zip(ins[1:], blocks):
+                for a in range(count):
+                    source = r.at[pl.ds(a * shard, shard), lanes(place ^ k, shard)]
+                    copies.append((source, outs[k].at[:, pl.ds(at, shard)]))
+                    at += shard
+        return copies
+
+    shapes = [shaped((shard, width + shard * sum(blocks)), bf16)] * PLANE
+    return place_copies(plan, PLANE * (1 + sum(blocks)), me, [columns, *rows], shapes)
+
+
+def place_sums_kernel(parts, blocks, me_ref, *refs):
+    ins, outs, held, sem = refs[:PLANE], refs[PLANE:-2], refs[-2], refs[-1]
+    place = me_ref[0]
+    shard = ins[0].shape[0]
+    copies = []
+    for k in range(PLANE):
+        held[k] = ins[k][...].astype(f32)
+        at = 0
+        moves = []
+        for out, part in zip(outs, parts):
+            moves.append((held.at[k, :, pl.ds(at, part)], out.at[:, lanes(place ^ k, part)]))
+            at += part
+        for out, count in zip(outs[len(parts) :], blocks):
+            for a in range(count):
+                spot = pl.multiple_of((place ^ k) * count * shard + a * shard, shard)
+                moves.append((held.at[k, :, pl.ds(at, shard)], out.at[pl.ds(spot, shard), :]))
+                at += shard
+        for n, move in enumerate(moves):
+            copies.append(pltpu.make_async_copy(*move, sem.at[k, n]))
+            copies[-1].start()
+    for one in copies:
+        one.wait()
+
+
+def place_sums(me, pieces, parts, inners):
+    shard, full = pieces[0].shape
+    blocks = [inner // shard for inner in inners]
+    return pl.pallas_call(
+        functools.partial(place_sums_kernel, parts, blocks),
+        in_specs=[pl.BlockSpec(memory_space=pltpu.SMEM)] + [pl.BlockSpec(memory_space=pltpu.VMEM)] * PLANE,
+        out_specs=[ANY] * (len(parts) + len(blocks)),
+        out_shape=[shaped((shard, PLANE * part), f32) for part in parts]
+        + [shaped((PLANE * inner, shard), f32) for inner in inners],
+        scratch_shapes=[
+            pltpu.VMEM((PLANE, shard, full), f32),
+            pltpu.SemaphoreType.DMA((PLANE, len(parts) + sum(blocks))),
+        ],
+        compiler_params=params(),
+        cost_estimate=cost(0, 8e6),
+    )(me, *pieces)
 
 
 def hop(value, bits, count):
@@ -934,7 +998,7 @@
         if lo > 0:
             return state["kept"]
         act = after(inner_act, pieces)
-        state["mlp"] = project(act, ff_joined[:, 2 * inner :], wide)
+        state["mlp"] = project(act, ff_joined, 2, wide)
         return state["kept"], state["mlp"]
 
     grad_wide, attn_grad_all = spread(grad_hidden.astype(bf16), count, heads)
@@ -949,7 +1013,11 @@
     mlp_added, _, attn_terms = fold([(0, *state["mlp"])], count, lambda _: others_grad, back_terms)
     others_part = sum_depth(others_grad)
     output = (valid_rows * (hidden + mlp_added)).astype(bf16)
-    grad_normed_attn, *_ = fold([(0, *attn_terms)], count, lambda _: mlp_added, lambda _: out_part)
+    if shard % 128 == 0:
+        sums = trade(cut_sums(me_scalar, ff_part, (down_part, out_part)), count)
+    else:
+        sums = out_part
+    grad_normed_attn, *_ = fold([(0, *attn_terms)], count, lambda _: mlp_added, lambda _: sums)
     own_grad = after(own_grad, grad_normed_attn)
     own_part = sum_depth(own_grad)
     gain_term_attn = jnp.sum(grad_normed_attn * input_rows * first_scale, axis=0)
@@ -970,22 +1038,23 @@
         cuts = [lax.dynamic_slice_in_dim(block, (me ^ k) * shard, shard, 1).astype(bf16) for k in range(PLANE)]
         return place_rows(me_scalar, trade(cuts, count))
 
-    down_sum = back_rows_of(down_part)
-    ffgate_sum, ffup_sum = back_columns(ff_part, (inner, inner))
-    out_sum = back_rows_of(out_part)
+    if shard % 128 == 0:
+        ffgate_sum, ffup_sum, down_sum, out_sum = place_sums(me_scalar, sums, (inner, inner), (inner, dv))
+    else:
+        down_sum, out_sum = back_rows_of(down_part), back_rows_of(out_part)
+        ffgate_sum, ffup_sum = back_columns(ff_part, (inner, inner))
+    others_part = after(others_part, (tokens_grad, output))
     blocks = [hop(others_part[k * shard : (k + 1) * shard], k + 1, count) for k in range(PLANE - 1)]
     gain_terms = jnp.stack([gain_term_attn, gain_term_mlp])
     bit = count // 2
     while bit >= 1:
-        if bit == PLANE // 2:
-            gain_terms = after(gain_terms, blocks)
         side = (place // bit) % 2
         cut = gain_terms.reshape(2, 2, -1)
         kept = lax.dynamic_index_in_dim(cut, side, 1, keepdims=False)
         sent = lax.dynamic_index_in_dim(cut, 1 - side, 1, keepdims=False)
         gain_terms = kept + hop(sent, bit, count)
         bit //= 2
-    cut = gain_terms.reshape(2, 2, -1)
+    cut = after(gain_terms, blocks).reshape(2, 2, -1)
     kept = lax.dynamic_index_in_dim(cut, core, 1, keepdims=False)
     sent = lax.dynamic_index_in_dim(cut, 1 - core, 1, keepdims=False)
     gain_terms = kept + swap(sent)

time: 664 us -> 653 us (0.983)
  waiting for transfers between devices: 226 us -> 239 us
  local copies, waits for them, and re-layouts: 52 us -> 40.9 us
  starting transfers between devices: 85.9 us -> 76.6 us
    ppermute x66 -> x60, starting transfers between devices: 79.6 us -> 69.8 us  [hop(): return lax.ppermute(value, 'dp', [(i, i ^ bits) for i in range(count)])]
    ppermute x66 -> x60, waiting for transfers between devices: 207 us -> 215 us  [hop(): return lax.ppermute(value, 'dp', [(i, i ^ bits) for i in range(count)])]
    unnamed x116 -> x94, local copies, waits for them, and re-layouts: 23.5 us -> 22 us
  transfers between devices with their start and end apart: 107 -> 101, of which waited for: 45 -> 51; matrix products, arithmetic and copies ran while one was open for 13% -> 12% of each run, Pallas kernels for 32% -> 32%
where the time goes in v5:
time: 653 us; the launch traced here: 647 us
  waiting for transfers between devices  239 us (37%)
  Pallas kernels  234 us (36%)
  starting transfers between devices  76.6 us (12%)
  local copies, waits for them, and re-layouts  40.9 us (6%)
  other arithmetic  40 us (6%)
  between operations  16.1 us (2%)
    ppermute x60, waiting for transfers between devices, hop(): return lax.ppermute(value, 'dp', [(i, i ^ bits) for i in range(count)])  215 us
    ppermute x60, starting transfers between devices, hop(): return lax.ppermute(value, 'dp', [(i, i ^ bits) for i in range(count)])  69.8 us
    pallas_call x2, Pallas kernels, retain(): pl.pallas_call(functools.partial(retain_kernel, first, wide, n, len(kept)...  43.1 us
    pallas_call x2, Pallas kernels, hidden_units(): pl.pallas_call(functools.partial(hidden_kernel, first, wide, n, len(kept)...  35.7 us
    pallas_call x3, Pallas kernels, retain_back(): pl.pallas_call(functools.partial(retain_back_kernel, first, wide, n, len(...  30.3 us
    pallas_call x4, Pallas kernels, fold_cut(): pl.pallas_call(fold_kernel, grid=(width // part,), in_specs=given, out_sp...  24.1 us
    unnamed x94, local copies, waits for them, and re-layouts  22 us
    pallas_call x1, Pallas kernels, project_back(): pl.pallas_call(back_kernel, grid=(PLANE,), in_specs=[by_slot(slot_len, in...  20.4 us
  transfers between devices with their start and end apart: 101, of which 51 were waited for; matrix products, arithmetic and copies ran while one was open for 12% of the time, Pallas kernels for 32%

profile of v5, /device:TPU:0, one launch (start us, length us, event | category | flops | bytes accessed | tf_op | source)
XLA Modules:
  0.0 646.7 jit_solution(13434012527124700084)
XLA Ops:
  7.2 3.1 shard_map.220
  10.4 3.0 collective-permute-start.4
  15.0 11.4 %collective-permute-done.4 = bf16[128,2048]{1,0:T(8,128)(2,1)S(1)} collective-permute-done((bf16[128,2048]{1,0:T(8,128)(2,1)}, bf16[128,2048]{1,0:T(8,128)(2,1)S(1)}, u32[]{:S(2)}, u32[]{:S(2)}) %collective-permute-start.4) | collective-permute-done | bytes 524320 | tf_op jit(solution)/shard_map/ppermute | solution.py:793
  27.2 11.0 %collective-permute-done.5 = bf16[128,2048]{1,0:T(8,128)(2,1)S(1)} collective-permute-done((bf16[128,2048]{1,0:T(8,128)(2,1)}, bf16[128,2048]{1,0:T(8,128)(2,1)S(1)}, u32[]{:S(2)}, u32[]{:S(2)}) %collective-permute-start.5) | collective-permute-done | bytes 524320 | tf_op jit(solution)/shard_map/ppermute | solution.py:793
  60.4 18.4 %collective-permute-done.8.refs_0_ = bf16[256,2048]{1,0:T(8,128)(2,1)} collective-permute-done((bf16[256,2048]{1,0:T(8,128)(2,1)}, bf16[256,2048]{1,0:T(8,128)(2,1)}, u32[]{:S(2)}, u32[]{:S(2)}) %collective-permute-start.8) | collective-permute-done | bytes 1048608 | tf_op jit(solution)/shard_map/ppermute | solution.py:793
  84.1 6.2 collective-permute-done.12
  102.9 6.2 collective-permute-done.15.refs_1_
  109.1 8.5 %collective-permute-done.17.refs_3_ = bf16[128,1536]{1,0:T(8,128)(2,1)} collective-permute-done((bf16[128,1536]{1,0:T(8,128)(2,1)}, bf16[128,1536]{1,0:T(8,128)(2,1)}, u32[]{:S(2)}, u32[]{:S(2)}) %collective-permute-start.17) | collective-permute-done | bytes 393248 | tf_op jit(solution)/shard_map/ppermute | solution.py:793
  123.5 22.0 %collective-permute-done.19 = bf16[256,2048]{1,0:T(8,128)(2,1)} collective-permute-done((bf16[256,2048]{1,0:T(8,128)(2,1)}, bf16[256,2048]{1,0:T(8,128)(2,1)}, u32[]{:S(2)}, u32[]{:S(2)}) %collective-permute-start.19) | collective-permute-done | bytes 1048608 | tf_op jit(solution)/shard_map/ppermute | solution.py:793
  159.2 4.0 collective-permute-done.23
  176.8 29.6 %shard_map.223 = (bf16[2048,256]{1,0:T(8,128)(2,1)}, bf16[2048,256]{1,0:T(8,128)(2,1)}, bf16[2048,512]{1,0:T(8,128)(2,1)}, f32[2048,512]{1,0:T(8,128)}, bf16[4,5...) custom-call(bf16[256,2048]{1,0:T(8,128)(2,1)} %collective-permute-do, ...), custom_call_target="tpu_custom_call" | custom-call | flops 14173391872 | bytes 15000000 | tf_op jit(solution)/shard_map/pallas_call | solution.py:349
  212.7 6.0 shard_map.224
  221.3 13.5 %shard_map.225 = (bf16[2048,256]{1,0:T(8,128)(2,1)}, bf16[2048,256]{1,0:T(8,128)(2,1)}, bf16[2048,512]{1,0:T(8,128)(2,1)}, f32[2048,512]{1,0:T(8,128)}, bf16[4,5...) custom-call(bf16[256,2048]{1,0:T(8,128)(2,1)} %fusion.2.refs_0_, ...), custom_call_target="tpu_custom_call", output_to_operand_aliasing={{0}: (4, {}), {1}: (5, {}), {2}: (6, {}), {3}: (7, {}), {4}... | custom-call | flops 4724464128 | bytes 15000000 | tf_op jit(solution)/shard_map/pallas_call | solution.py:349
  240.9 8.9 %collective-permute-done.30 = bf16[128,2048]{1,0:T(8,128)(2,1)S(1)} collective-permute-done((bf16[128,2048]{1,0:T(8,128)(2,1)}, bf16[128,2048]{1,0:T(8,128)(2,1)S(1)}, u32[]{:S(2)}, u32[]{:S(2)}) %collective-permute-start.30) | collective-permute-done | bytes 524320 | tf_op jit(solution)/shard_map/ppermute | solution.py:793
  250.0 10.6 %collective-permute-done.35 = bf16[128,2048]{1,0:T(8,128)(2,1)S(1)} collective-permute-done((bf16[128,2048]{1,0:T(8,128)(2,1)S(1)}, bf16[128,2048]{1,0:T(8,128)(2,1)S(1)}, u32[]{:S(2)}, u32[]{:S(2)}) %collective-permute-start.35) | collective-permute-done | bytes 524320 | tf_op jit(solution)/shard_map/ppermute | solution.py:793
  265.0 21.9 %collective-permute-done.36.refs_2_ = bf16[256,2048]{1,0:T(8,128)(2,1)S(1)} collective-permute-done((bf16[256,2048]{1,0:T(8,128)(2,1)S(1)}, bf16[256,2048]{1,0:T(8,128)(2,1)S(1)}, u32[]{:S(2)}, u32[]{:S(2)}) %collective-permute-start.36) | collective-permute-done | bytes 1048608 | tf_op jit(solution)/shard_map/ppermute | solution.py:793
  292.3 26.1 %shard_map.226 = (bf16[2048,512]{1,0:T(8,128)(2,1)}, bf16[2048,1024]{1,0:T(8,128)(2,1)}, bf16[2048,2048]{1,0:T(8,128)(2,1)}, f32[3,256,2048]{2,1,0:T(8,128)}, bf...) custom-call(bf16[256,2048]{1,0:T(8,128)(2,1)S(1)} %multiply_convert_fusion.1.refs_0_, ...), custom_call_target="tpu_custom_call" | custom-call | flops 16106127360 | bytes 15000000 | tf_op jit(solution)/shard_map/pallas_call | solution.py:480
  323.3 9.7 %shard_map.227 = (bf16[2048,512]{1,0:T(8,128)(2,1)}, bf16[2048,1024]{1,0:T(8,128)(2,1)}, bf16[2048,2048]{1,0:T(8,128)(2,1)}, f32[1,256,2048]{2,1,0:T(8,128)}, bf16[256,2048]{1,0:T(8,128)(2,1)}) custom-call(bf16[256,2048]{1,0:T(8,128)(2,1)S(1)} %constant_dynamic-update-slice_fusion.19.refs_0_, ...), custom_call_target="tpu_custom_call", output_to_operand_aliasing={{0}: (4, {}), {1}: (5, {}), {2}: (6, {})} | custom-call | flops 5368709120 | bytes 15000000 | tf_op jit(solution)/shard_map/pallas_call | solution.py:480
  333.0 8.8 %shard_map.228 = bf16[2048,512]{1,0:T(8,128)(2,1)} custom-call(bf16[2048,512]{1,0:T(8,128)(2,1)} %get-tuple-element.257.left, bf16[2048,2048]{1,0:T(8,128)(2,1)} %constant_dynamic-update-slice_fusion.10.refs_7_.refs_3_.right), custom_call_target="tpu_custom_call" | custom-call | flops 4294967296 | bytes 20000000 | tf_op jit(solution)/shard_map/pallas_call | solution.py:654
  347.9 6.1 shard_map.229
  358.2 13.3 %shard_map.230 = bf16[2048,1024]{1,0:T(8,128)(2,1)} custom-call(bf16[2048,2048]{1,0:T(8,128)(2,1)} %get-tuple-element.251.left, bf16[2048,1024]{1,0:T(8,128)(2,1)} %get-tuple-element.252.right), custom_call_target="tpu_custom_call" | custom-call | flops 8589934592 | bytes 20000000 | tf_op jit(solution)/shard_map/pallas_call | solution.py:581
  377.2 3.1 collective-permute-done.48
  381.9 9.0 %collective-permute-done.53 = bf16[128,2048]{1,0:T(8,128)(2,1)S(1)} collective-permute-done((bf16[128,2048]{1,0:T(8,128)(2,1)S(1)}, bf16[128,2048]{1,0:T(8,128)(2,1)S(1)}, u32[]{:S(2)}, u32[]{:S(2)}) %collective-permute-start.53) | collective-permute-done | bytes 524320 | tf_op jit(solution)/shard_map/ppermute | solution.py:793
  400.4 8.4 %shard_map.232 = (bf16[2048,1536]{1,0:T(8,128)(2,1)}, bf16[2048,2048]{1,0:T(8,128)(2,1)}) custom-call(bf16[256,2048]{1,0:T(8,128)(2,1)} %copy-done.6, bf16[256,2048]{1,0:T(8,128)(2,1)} %collective-permute-done.54.refs_1_, bf16[2048,2048]{1,0:T(8,128)(2,1)} %get-tuple-element.200.refs_2_.refs_4_.first.second, f32[512,512]{1,0:T(8,128)} %fusion.12.refs_9_.refs_3_.refs_5_, ...), custom_call_target="tpu_custom_call" | custom-call | flops 2147483648 | bytes 15000000 | tf_op jit(solution)/shard_map/pallas_call | solution.py:546
  408.8 12.4 %shard_map.231 = (f32[4,256,2048]{2,1,0:T(8,128)}, bf16[256,2048]{1,0:T(8,128)(2,1)}, bf16[256,2048]{1,0:T(8,128)(2,1)}, bf16[256,2048]{1,0:T(8,128)(2,1)}, bf16[256,2048]{1,0:T(8,128)(2,1)}) custom-call(bf16[2048,512]{1,0:T(8,128)(2,1)} %get-tuple-element.257.left, bf16[2048,1536]{1,0:T(8,128)(2,1)} %all-gather.8.cloned.1.call-done.refs_6_.refs_2_.right), custom_call_target="tpu_custom_call" | custom-call | flops 4294967296 | bytes 20000000 | tf_op jit(solution)/shard_map/pallas_call | solution.py:372
  431.2 13.6 %shard_map.233 = (bf16[2048,1536]{1,0:T(8,128)(2,1)}, bf16[2048,2048]{1,0:T(8,128)(2,1)}) custom-call(bf16[256,2048]{1,0:T(8,128)(2,1)} %collective-permute-done.59.refs_0_, bf16[256,2048]{1,0:T(8,128)(2,1)} %copy-done.18, bf16[256,2048]{1,0:T(8,128)(2,1)} %collective-permute-done.60.refs_2_, ...), custom_call_target="tpu_custom_call", output_to_operand_aliasing={{0}: (12, {}), {1}: (13, {})} | custom-call | flops 4294967296 | bytes 15000000 | tf_op jit(solution)/shard_map/pallas_call | solution.py:546
  448.8 8.3 %shard_map.234 = (bf16[2048,1536]{1,0:T(8,128)(2,1)}, bf16[2048,2048]{1,0:T(8,128)(2,1)}) custom-call(bf16[256,2048]{1,0:T(8,128)(2,1)} %copy-done.10, bf16[256,2048]{1,0:T(8,128)(2,1)} %collective-permute-done.65.refs_1_, bf16[2048,2048]{1,0:T(8,128)(2,1)} %get-tuple-element.200.refs_2_.refs_4_.first.second, ...), custom_call_target="tpu_custom_call", output_to_operand_aliasing={{0}: (10, {}), {1}: (11, {})} | custom-call | flops 2147483648 | bytes 15000000 | tf_op jit(solution)/shard_map/pallas_call | solution.py:546
  457.1 8.9 %shard_map.235 = bf16[2048,512]{1,0:T(8,128)(2,1)} custom-call(bf16[2048,512]{1,0:T(8,128)(2,1)} %get-tuple-element.219.left, bf16[2048,2048]{1,0:T(8,128)(2,1)} %get-tuple-element.274.right), custom_call_target="tpu_custom_call" | custom-call | flops 4294967296 | bytes 20000000 | tf_op jit(solution)/shard_map/pallas_call | solution.py:654
  466.2 18.6 %shard_map.236 = (bf16[512,1536]{1,0:T(8,128)(2,1)}, bf16[1536,1536]{1,0:T(8,128)(2,1)}) custom-call(s32[1]{0:T(128)} %bitcast.6.me_ref.refs_6_, bf16[2048,2048]{1,0:T(8,128)(2,1)} %get-tuple-element.220.left, bf16[2048,1536]{1,0:T(8,128)(2,1)} %get-tuple-element.287.right.left), custom_call_target="tpu_custom_call" | custom-call | flops 12884901888 | bytes 20000000 | tf_op jit(solution)/shard_map/pallas_call | solution.py:632
  487.9 3.1 collective-permute-done.57.refs_4_
  491.0 6.0 shard_map.237
  501.1 20.4 %shard_map.238 = (f32[4,256,2048]{2,1,0:T(8,128)}, bf16[256,2048]{1,0:T(8,128)(2,1)}, bf16[256,2048]{1,0:T(8,128)(2,1)}, bf16[256,2048]{1,0:T(8,128)(2,1)}, bf16[256,2048]{1,0:T(8,128)(2,1)}) custom-call(bf16[2048,1536]{1,0:T(8,128)(2,1)} %get-tuple-element.287.right.left, bf16[2048,2048]{1,0:T(8,128)(2,1)} %get-tuple-element.200.refs_2_.refs_4_.first.second, ...), custom_call_target="tpu_custom_call" | custom-call | flops 12884901888 | bytes 20000000 | tf_op jit(solution)/shard_map/pallas_call | solution.py:399
  528.3 2.8 convert_element_type.176
  531.1 3.2 shard_map.240
  541.2 4.5 fusion.19
  547.5 6.0 shard_map.239
  555.4 11.5 %collective-permute-done.80.refs_2_ = bf16[128,2048]{1,0:T(8,128)(2,1)} collective-permute-done((bf16[128,2048]{1,0:T(8,128)(2,1)}, bf16[128,2048]{1,0:T(8,128)(2,1)}, u32[]{:S(2)}, u32[]{:S(2)}) %collective-permute-start.80) | collective-permute-done | bytes 524320 | tf_op jit(solution)/shard_map/ppermute | solution.py:793
  568.4 6.0 collective-permute-done.77
  574.4 3.7 collective-permute-done.78
  585.5 3.7 collective-permute-done.83
  589.2 5.3 collective-permute-done.84
  594.5 3.2 collective-permute-done.82
  600.5 3.1 collective-permute-start.88
  606.4 3.5 fusion.7
  616.8 11.5 %collective-permute-done.91 = f32[2,128]{1,0:T(2,128)S(1)} collective-permute-done((f32[2,128]{1,0:T(2,128)S(1)}, f32[2,128]{1,0:T(2,128)S(1)}, u32[]{:S(2)}, u32[]{:S(2)}) %collective-permute-start.91) | collective-permute-done | bytes 1056 | tf_op jit(solution)/shard_map/ppermute | solution.py:793
  628.8 4.1 shard_map.241
  633.4 3.0 reduce-scatter.12.cloned.1.call-done.refs_0_
  636.5 3.2 shard_map.242
  (356 shorter events, 192.4 us)
Async XLA Ops:
  7.2 169.7 %all-gather.4.cloned.1.call-start = ((), (), s32[]{:S(2)}) async-start(), calls=%async_computation.5 | async-start | bytes 2621440 | tf_op jit(solution)/shard_map/all_gather | solution.py:896
  10.4 166.5 %all-gather.6.cloned.1.call-start = ((), (), s32[]{:S(2)}) async-start(), calls=%async_computation.6 | async-start | bytes 7864320 | tf_op jit(solution)/shard_map/all_gather | solution.py:896
  13.4 24.8 %collective-permute-start.5 = (bf16[128,2048]{1,0:T(8,128)(2,1)}, bf16[128,2048]{1,0:T(8,128)(2,1)S(1)}, u32[]{:S(2)}, u32[]{:S(2)}) collective-permute-start(bf16[128,2048]{1,0:T(8,128)(2,1)} %get-tuple-element.171), channel_id=1, source_target_pairs={{0,4},{2,6},{4,0},{6,2},{8,12},{10,14},{12,8},{14,10},{16,20},{18,... | collective-permute-start | bytes 1572872 | tf_op jit(solution)/shard_map/ppermute | solution.py:793
  14.9 24.1 %collective-permute-start.6 = (bf16[128,2048]{1,0:T(8,128)(2,1)}, bf16[128,2048]{1,0:T(8,128)(2,1)S(1)}, u32[]{:S(2)}, u32[]{:S(2)}) collective-permute-start(bf16[128,2048]{1,0:T(8,128)(2,1)} %get-tuple-element.172), channel_id=1, source_target_pairs={{0,6},{2,4},{4,2},{6,0},{8,14},{10,12},{12,10},{14,8},{16,22},{18,... | collective-permute-start | bytes 1572872 | tf_op jit(solution)/shard_map/ppermute | solution.py:793
  39.9 252.1 %all-gather.8.cloned.1.call-start = ((), (), s32[]{:S(2)}) async-start(), calls=%async_computation.7 | async-start | bytes 7864320 | tf_op jit(solution)/shard_map/all_gather | solution.py:896
  57.6 21.2 %collective-permute-start.8 = (bf16[256,2048]{1,0:T(8,128)(2,1)}, bf16[256,2048]{1,0:T(8,128)(2,1)}, u32[]{:S(2)}, u32[]{:S(2)}) collective-permute-start(bf16[256,2048]{1,0:T(8,128)(2,1)} %fusion.2.refs_0_), channel_id=1, source_target_pairs={{0,2},{2,0},{4,6},{6,4},{8,10},{10,8},{12,14},{14,12},{16,18},{18,... | collective-permute-start | bytes 3145736 | tf_op jit(solution)/shard_map/ppermute | solution.py:793
  58.9 23.3 %collective-permute-start.10 = (bf16[256,2048]{1,0:T(8,128)(2,1)}, bf16[256,2048]{1,0:T(8,128)(2,1)}, u32[]{:S(2)}, u32[]{:S(2)}) collective-permute-start(bf16[256,2048]{1,0:T(8,128)(2,1)} %fusion.2.refs_0_), channel_id=1, source_target_pairs={{0,4},{2,6},{4,0},{6,2},{8,12},{10,14},{12,8},{14,10},{16,20},{18,... | collective-permute-start | bytes 3145736 | tf_op jit(solution)/shard_map/ppermute | solution.py:793
  98.0 19.6 %collective-permute-start.17 = (bf16[128,1536]{1,0:T(8,128)(2,1)}, bf16[128,1536]{1,0:T(8,128)(2,1)}, u32[]{:S(2)}, u32[]{:S(2)}) collective-permute-start(bf16[128,1536]{1,0:T(8,128)(2,1)} %get-tuple-element.181), channel_id=1, source_target_pairs={{0,6},{2,4},{4,2},{6,0},{8,14},{10,12},{12,10},{14,8},{16,22},{18,... | collective-permute-start | bytes 1179656 | tf_op jit(solution)/shard_map/ppermute | solution.py:793
  120.4 25.2 %collective-permute-start.19 = (bf16[256,2048]{1,0:T(8,128)(2,1)}, bf16[256,2048]{1,0:T(8,128)(2,1)}, u32[]{:S(2)}, u32[]{:S(2)}) collective-permute-start(bf16[256,2048]{1,0:T(8,128)(2,1)} %fusion.11), channel_id=1, source_target_pairs={{0,2},{2,0},{4,6},{6,4},{8,10},{10,8},{12,14},{14,12},{16,18},{18,... | collective-permute-start | bytes 3145736 | tf_op jit(solution)/shard_map/ppermute | solution.py:793
  122.4 27.4 %collective-permute-start.21 = (bf16[256,2048]{1,0:T(8,128)(2,1)}, bf16[256,2048]{1,0:T(8,128)(2,1)}, u32[]{:S(2)}, u32[]{:S(2)}) collective-permute-start(bf16[256,2048]{1,0:T(8,128)(2,1)} %fusion.11), channel_id=1, source_target_pairs={{0,4},{2,6},{4,0},{6,2},{8,12},{10,14},{12,8},{14,10},{16,20},{18,... | collective-permute-start | bytes 3145736 | tf_op jit(solution)/shard_map/ppermute | solution.py:793
  123.4 31.2 %collective-permute-start.18 = (bf16[256,2048]{1,0:T(8,128)(2,1)}, bf16[256,2048]{1,0:T(8,128)(2,1)}, u32[]{:S(2)}, u32[]{:S(2)}) collective-permute-start(bf16[256,2048]{1,0:T(8,128)(2,1)} %fusion.11), channel_id=1, source_target_pairs={{0,1},{1,0},{2,3},{3,2},{4,5},{5,4},{6,7},{7,6},{8,9},{9,8},{10,11... | collective-permute-start | bytes 3145736 | tf_op jit(solution)/shard_map/ppermute | solution.py:797
  145.6 21.7 %collective-permute-start.20 = (bf16[256,2048]{1,0:T(8,128)(2,1)}, bf16[256,2048]{1,0:T(8,128)(2,1)}, u32[]{:S(2)}, u32[]{:S(2)}) collective-permute-start(bf16[256,2048]{1,0:T(8,128)(2,1)} %collective-permute-done.19), channel_id=1, source_target_pairs={{0,1},{1,0},{2,3},{3,2},{4,5},{5,4},{6,7},{7,6},{8,9},{9,8},{10,11... | collective-permute-start | bytes 3145736 | tf_op jit(solution)/shard_map/ppermute | solution.py:797
  154.4 291.6 %reduce-scatter.6.cloned.1.call-start = ((), (), s32[]{:S(2)}) async-start(), calls=%async_computation.8 | async-start | bytes 2621440 | tf_op jit(solution)/shard_map/reduce_scatter | solution.py:899
  154.5 17.4 %collective-permute-start.22 = (bf16[256,2048]{1,0:T(8,128)(2,1)}, bf16[256,2048]{1,0:T(8,128)(2,1)S(1)}, u32[]{:S(2)}, u32[]{:S(2)}) collective-permute-start(bf16[256,2048]{1,0:T(8,128)(2,1)} %collective-permute-done.21), channel_id=1, source_target_pairs={{0,1},{1,0},{2,3},{3,2},{4,5},{5,4},{6,7},{7,6},{8,9},{9,8},{10,11... | collective-permute-start | bytes 3145736 | tf_op jit(solution)/shard_map/ppermute | solution.py:797
  218.7 17.8 %collective-permute-start.31 = (bf16[128,2048]{1,0:T(8,128)(2,1)}, bf16[128,2048]{1,0:T(8,128)(2,1)S(1)}, u32[]{:S(2)}, u32[]{:S(2)}) collective-permute-start(bf16[128,2048]{1,0:T(8,128)(2,1)} %get-tuple-element.196), channel_id=1, source_target_pairs={{0,2},{2,0},{4,6},{6,4},{8,10},{10,8},{12,14},{14,12},{16,18},{18,... | collective-permute-start | bytes 1572872 | tf_op jit(solution)/shard_map/ppermute | solution.py:793
  237.9 22.7 %collective-permute-start.35 = (bf16[128,2048]{1,0:T(8,128)(2,1)S(1)}, bf16[128,2048]{1,0:T(8,128)(2,1)S(1)}, u32[]{:S(2)}, u32[]{:S(2)}) collective-permute-start(bf16[128,2048]{1,0:T(8,128)(2,1)S(1)} %add_convert_fusion.6), channel_id=1, source_target_pairs={{0,2},{2,0},{4,6},{6,4},{8,10},{10,8},{12,14},{14,12},{16,18},{18,... | collective-permute-start | bytes 1572872 | tf_op jit(solution)/shard_map/ppermute | solution.py:793
  239.8 20.8 %collective-permute-start.33 = (bf16[128,2048]{1,0:T(8,128)(2,1)S(1)}, bf16[128,2048]{1,0:T(8,128)(2,1)S(1)}, u32[]{:S(2)}, u32[]{:S(2)}) collective-permute-start(bf16[128,2048]{1,0:T(8,128)(2,1)S(1)} %add_convert_fusion.7), channel_id=1, source_target_pairs={{0,4},{2,6},{4,0},{6,2},{8,12},{10,14},{12,8},{14,10},{16,20},{18,... | collective-permute-start | bytes 1572872 | tf_op jit(solution)/shard_map/ppermute | solution.py:793
  262.0 24.9 %collective-permute-start.36 = (bf16[256,2048]{1,0:T(8,128)(2,1)S(1)}, bf16[256,2048]{1,0:T(8,128)(2,1)S(1)}, u32[]{:S(2)}, u32[]{:S(2)}) collective-permute-start(bf16[256,2048]{1,0:T(8,128)(2,1)S(1)} %multiply_convert_fusion.1.refs_0_), channel_id=1, source_target_pairs={{0,2},{2,0},{4,6},{6,4},{8,10},{10,8},{12,14},{14,12},{16,18},{18,... | collective-permute-start | bytes 3145736 | tf_op jit(solution)/shard_map/ppermute | solution.py:793
  263.8 24.2 %collective-permute-start.37 = (bf16[256,2048]{1,0:T(8,128)(2,1)S(1)}, bf16[256,2048]{1,0:T(8,128)(2,1)S(1)}, u32[]{:S(2)}, u32[]{:S(2)}) collective-permute-start(bf16[256,2048]{1,0:T(8,128)(2,1)S(1)} %multiply_convert_fusion.1.refs_0_), channel_id=1, source_target_pairs={{0,4},{2,6},{4,0},{6,2},{8,12},{10,14},{12,8},{14,10},{16,20},{18,... | collective-permute-start | bytes 3145736 | tf_op jit(solution)/shard_map/ppermute | solution.py:793
  265.0 27.0 %collective-permute-start.40 = (bf16[256,2048]{1,0:T(8,128)(2,1)S(1)}, bf16[256,2048]{1,0:T(8,128)(2,1)}, u32[]{:S(2)}, u32[]{:S(2)}) collective-permute-start(bf16[256,2048]{1,0:T(8,128)(2,1)S(1)} %multiply_convert_fusion.1.refs_0_), channel_id=1, source_target_pairs={{0,1},{1,0},{2,3},{3,2},{4,5},{5,4},{6,7},{7,6},{8,9},{9,8},{10,11... | collective-permute-start | bytes 3145736 | tf_op jit(solution)/shard_map/ppermute | solution.py:797
  290.2 28.2 %collective-permute-start.38 = (bf16[128,2048]{1,0:T(8,128)(2,1)}, bf16[128,2048]{1,0:T(8,128)(2,1)}, u32[]{:S(2)}, u32[]{:S(2)}) collective-permute-start(bf16[128,2048]{1,0:T(8,128)(2,1)} %slice.138), channel_id=1, source_target_pairs={{0,4},{2,6},{4,0},{6,2},{8,12},{10,14},{12,8},{14,10},{16,20},{18,... | collective-permute-start | bytes 1572872 | tf_op jit(solution)/shard_map/ppermute | solution.py:793
  291.4 27.0 %collective-permute-start.39 = (bf16[128,2048]{1,0:T(8,128)(2,1)}, bf16[128,2048]{1,0:T(8,128)(2,1)}, u32[]{:S(2)}, u32[]{:S(2)}) collective-permute-start(bf16[128,2048]{1,0:T(8,128)(2,1)} %slice.139), channel_id=1, source_target_pairs={{0,2},{2,0},{4,6},{6,4},{8,10},{10,8},{12,14},{14,12},{16,18},{18,... | collective-permute-start | bytes 1572872 | tf_op jit(solution)/shard_map/ppermute | solution.py:793
  341.8 159.3 %reduce-scatter.8.cloned.1.call-start = ((), (), s32[]{:S(2)}) async-start(), calls=%async_computation.9 | async-start | bytes 5242880 | tf_op jit(solution)/shard_map/reduce_scatter | solution.py:899
  343.5 33.4 %collective-permute-start.44 = (bf16[256,2048]{1,0:T(8,128)(2,1)}, bf16[256,2048]{1,0:T(8,128)(2,1)S(1)}, u32[]{:S(2)}, u32[]{:S(2)}) collective-permute-start(bf16[256,2048]{1,0:T(8,128)(2,1)} %get-tuple-element.234), channel_id=1, source_target_pairs={{0,1},{1,0},{2,3},{3,2},{4,5},{5,4},{6,7},{7,6},{8,9},{9,8},{10,11... | collective-permute-start | bytes 3145736 | tf_op jit(solution)/shard_map/ppermute | solution.py:797
  354.0 17.9 %collective-permute-start.49 = (bf16[128,2048]{1,0:T(8,128)(2,1)}, bf16[128,2048]{1,0:T(8,128)(2,1)}, u32[]{:S(2)}, u32[]{:S(2)}) collective-permute-start(bf16[128,2048]{1,0:T(8,128)(2,1)} %get-tuple-element.247), channel_id=1, source_target_pairs={{0,2},{2,0},{4,6},{6,4},{8,10},{10,8},{12,14},{14,12},{16,18},{18,... | collective-permute-start | bytes 1572872 | tf_op jit(solution)/shard_map/ppermute | solution.py:793
  356.3 24.0 %collective-permute-start.48 = (bf16[128,2048]{1,0:T(8,128)(2,1)}, bf16[128,2048]{1,0:T(8,128)(2,1)S(1)}, u32[]{:S(2)}, u32[]{:S(2)}) collective-permute-start(bf16[128,2048]{1,0:T(8,128)(2,1)} %get-tuple-element.245), channel_id=1, source_target_pairs={{0,2},{2,0},{4,6},{6,4},{8,10},{10,8},{12,14},{14,12},{16,18},{18,... | collective-permute-start | bytes 1572872 | tf_op jit(solution)/shard_map/ppermute | solution.py:793
  357.6 24.3 %collective-permute-start.52 = (bf16[128,2048]{1,0:T(8,128)(2,1)}, bf16[128,2048]{1,0:T(8,128)(2,1)}, u32[]{:S(2)}, u32[]{:S(2)}) collective-permute-start(bf16[128,2048]{1,0:T(8,128)(2,1)} %get-tuple-element.254), channel_id=1, source_target_pairs={{0,4},{2,6},{4,0},{6,2},{8,12},{10,14},{12,8},{14,10},{16,20},{18,... | collective-permute-start | bytes 1572872 | tf_op jit(solution)/shard_map/ppermute | solution.py:793
  371.5 159.6 %reduce-scatter.10.cloned.1.call-start = ((), (), s32[]{:S(2)}) async-start(), calls=%async_computation.10 | async-start | bytes 2621440 | tf_op jit(solution)/shard_map/reduce_scatter | solution.py:899
  397.6 25.7 %collective-permute-start.59 = (bf16[256,2048]{1,0:T(8,128)(2,1)S(1)}, bf16[256,2048]{1,0:T(8,128)(2,1)}, u32[]{:S(2)}, u32[]{:S(2)}) collective-permute-start(bf16[256,2048]{1,0:T(8,128)(2,1)S(1)} %get-tuple-element.332.refs_0_), channel_id=1, source_target_pairs={{0,2},{2,0},{4,6},{6,4},{8,10},{10,8},{12,14},{14,12},{16,18},{18,... | collective-permute-start | bytes 3145736 | tf_op jit(solution)/shard_map/ppermute | solution.py:793
  398.5 25.4 %collective-permute-start.60 = (bf16[256,2048]{1,0:T(8,128)(2,1)S(1)}, bf16[256,2048]{1,0:T(8,128)(2,1)}, u32[]{:S(2)}, u32[]{:S(2)}) collective-permute-start(bf16[256,2048]{1,0:T(8,128)(2,1)S(1)} %get-tuple-element.332.refs_0_), channel_id=1, source_target_pairs={{0,4},{2,6},{4,0},{6,2},{8,12},{10,14},{12,8},{14,10},{16,20},{18,... | collective-permute-start | bytes 3145736 | tf_op jit(solution)/shard_map/ppermute | solution.py:793
  466.0 144.8 %reduce-scatter.14.cloned.1.call-start = ((), (), s32[]{:S(2)}) async-start(), calls=%async_computation.12 | async-start | bytes 5898240 | tf_op jit(solution)/shard_map/reduce_scatter | solution.py:899
  484.9 151.5 %reduce-scatter.12.cloned.1.call-start = ((), (), s32[]{:S(2)}) async-start(), calls=%async_computation.11 | async-start | bytes 1966080 | tf_op jit(solution)/shard_map/reduce_scatter | solution.py:899
  486.3 41.3 %collective-permute-start.55 = (bf16[256,2048]{1,0:T(8,128)(2,1)}, bf16[256,2048]{1,0:T(8,128)(2,1)}, u32[]{:S(2)}, u32[]{:S(2)}) collective-permute-start(bf16[256,2048]{1,0:T(8,128)(2,1)} %get-tuple-element.259), channel_id=1, source_target_pairs={{0,1},{1,0},{2,3},{3,2},{4,5},{5,4},{6,7},{7,6},{8,9},{9,8},{10,11... | collective-permute-start | bytes 3145736 | tf_op jit(solution)/shard_map/ppermute | solution.py:797
  497.0 24.5 %collective-permute-start.67 = (bf16[128,2048]{1,0:T(8,128)(2,1)}, bf16[128,2048]{1,0:T(8,128)(2,1)}, u32[]{:S(2)}, u32[]{:S(2)}) collective-permute-start(bf16[128,2048]{1,0:T(8,128)(2,1)} %get-tuple-element.285), channel_id=1, source_target_pairs={{0,2},{2,0},{4,6},{6,4},{8,10},{10,8},{12,14},{14,12},{16,18},{18,... | collective-permute-start | bytes 1572872 | tf_op jit(solution)/shard_map/ppermute | solution.py:793
  498.3 23.2 %collective-permute-start.68 = (bf16[128,2048]{1,0:T(8,128)(2,1)}, bf16[128,2048]{1,0:T(8,128)(2,1)}, u32[]{:S(2)}, u32[]{:S(2)}) collective-permute-start(bf16[128,2048]{1,0:T(8,128)(2,1)} %get-tuple-element.286), channel_id=1, source_target_pairs={{0,4},{2,6},{4,0},{6,2},{8,12},{10,14},{12,8},{14,10},{16,20},{18,... | collective-permute-start | bytes 1572872 | tf_op jit(solution)/shard_map/ppermute | solution.py:793
  499.0 28.7 %collective-permute-start.66 = (bf16[128,2048]{1,0:T(8,128)(2,1)}, bf16[128,2048]{1,0:T(8,128)(2,1)S(1)}, u32[]{:S(2)}, u32[]{:S(2)}) collective-permute-start(bf16[128,2048]{1,0:T(8,128)(2,1)} %get-tuple-element.283), channel_id=1, source_target_pairs={{0,2},{2,0},{4,6},{6,4},{8,10},{10,8},{12,14},{14,12},{16,18},{18,... | collective-permute-start | bytes 1572872 | tf_op jit(solution)/shard_map/ppermute | solution.py:793
  500.3 27.9 %collective-permute-start.70 = (bf16[128,2048]{1,0:T(8,128)(2,1)}, bf16[128,2048]{1,0:T(8,128)(2,1)}, u32[]{:S(2)}, u32[]{:S(2)}) collective-permute-start(bf16[128,2048]{1,0:T(8,128)(2,1)} %get-tuple-element.294), channel_id=1, source_target_pairs={{0,4},{2,6},{4,0},{6,2},{8,12},{10,14},{12,8},{14,10},{16,20},{18,... | collective-permute-start | bytes 1572872 | tf_op jit(solution)/shard_map/ppermute | solution.py:793
  527.7 18.0 %collective-permute-start.73 = (bf16[256,2048]{1,0:T(8,128)(2,1)}, bf16[256,2048]{1,0:T(8,128)(2,1)}, u32[]{:S(2)}, u32[]{:S(2)}) collective-permute-start(bf16[256,2048]{1,0:T(8,128)(2,1)} %get-tuple-element.290), channel_id=1, source_target_pairs={{0,1},{1,0},{2,3},{3,2},{4,5},{5,4},{6,7},{7,6},{8,9},{9,8},{10,11... | collective-permute-start | bytes 3145736 | tf_op jit(solution)/shard_map/ppermute | solution.py:797
  527.7 19.8 %collective-permute-start.74 = (bf16[256,2048]{1,0:T(8,128)(2,1)}, bf16[256,2048]{1,0:T(8,128)(2,1)}, u32[]{:S(2)}, u32[]{:S(2)}) collective-permute-start(bf16[256,2048]{1,0:T(8,128)(2,1)} %get-tuple-element.291), channel_id=1, source_target_pairs={{0,1},{1,0},{2,3},{3,2},{4,5},{5,4},{6,7},{7,6},{8,9},{9,8},{10,11... | collective-permute-start | bytes 3145736 | tf_op jit(solution)/shard_map/ppermute | solution.py:797
  528.2 19.3 %collective-permute-start.75 = (bf16[256,2048]{1,0:T(8,128)(2,1)}, bf16[256,2048]{1,0:T(8,128)(2,1)}, u32[]{:S(2)}, u32[]{:S(2)}) collective-permute-start(bf16[256,2048]{1,0:T(8,128)(2,1)} %get-tuple-element.292), channel_id=1, source_target_pairs={{0,1},{1,0},{2,3},{3,2},{4,5},{5,4},{6,7},{7,6},{8,9},{9,8},{10,11... | collective-permute-start | bytes 3145736 | tf_op jit(solution)/shard_map/ppermute | solution.py:797
  537.0 18.3 %collective-permute-start.79 = (bf16[128,2048]{1,0:T(8,128)(2,1)}, bf16[128,2048]{1,0:T(8,128)(2,1)S(1)}, u32[]{:S(2)}, u32[]{:S(2)}) collective-permute-start(bf16[128,2048]{1,0:T(8,128)(2,1)} %get-tuple-element.308), channel_id=1, source_target_pairs={{0,2},{2,0},{4,6},{6,4},{8,10},{10,8},{12,14},{14,12},{16,18},{18,... | collective-permute-start | bytes 1572872 | tf_op jit(solution)/shard_map/ppermute | solution.py:793
  540.6 26.2 %collective-permute-start.80 = (bf16[128,2048]{1,0:T(8,128)(2,1)}, bf16[128,2048]{1,0:T(8,128)(2,1)}, u32[]{:S(2)}, u32[]{:S(2)}) collective-permute-start(bf16[128,2048]{1,0:T(8,128)(2,1)} %get-tuple-element.309), channel_id=1, source_target_pairs={{0,4},{2,6},{4,0},{6,2},{8,12},{10,14},{12,8},{14,10},{16,20},{18,... | collective-permute-start | bytes 1572872 | tf_op jit(solution)/shard_map/ppermute | solution.py:793
  545.7 22.1 %collective-permute-start.81 = (bf16[128,2048]{1,0:T(8,128)(2,1)}, bf16[128,2048]{1,0:T(8,128)(2,1)}, u32[]{:S(2)}, u32[]{:S(2)}) collective-permute-start(bf16[128,2048]{1,0:T(8,128)(2,1)} %get-tuple-element.310), channel_id=1, source_target_pairs={{0,6},{2,4},{4,2},{6,0},{8,14},{10,12},{12,10},{14,8},{16,22},{18,... | collective-permute-start | bytes 1572872 | tf_op jit(solution)/shard_map/ppermute | solution.py:793
  553.5 20.9 %collective-permute-start.77 = (bf16[128,2048]{1,0:T(8,128)(2,1)}, bf16[128,2048]{1,0:T(8,128)(2,1)}, u32[]{:S(2)}, u32[]{:S(2)}) collective-permute-start(bf16[128,2048]{1,0:T(8,128)(2,1)} %get-tuple-element.305), channel_id=1, source_target_pairs={{0,2},{2,0},{4,6},{6,4},{8,10},{10,8},{12,14},{14,12},{16,18},{18,... | collective-permute-start | bytes 1572872 | tf_op jit(solution)/shard_map/ppermute | solution.py:793
  554.6 23.4 %collective-permute-start.78 = (bf16[128,2048]{1,0:T(8,128)(2,1)}, bf16[128,2048]{1,0:T(8,128)(2,1)}, u32[]{:S(2)}, u32[]{:S(2)}) collective-permute-start(bf16[128,2048]{1,0:T(8,128)(2,1)} %get-tuple-element.306), channel_id=1, source_target_pairs={{0,4},{2,6},{4,0},{6,2},{8,12},{10,14},{12,8},{14,10},{16,20},{18,... | collective-permute-start | bytes 1572872 | tf_op jit(solution)/shard_map/ppermute | solution.py:793
  555.3 28.5 %collective-permute-start.72 = (bf16[256,2048]{1,0:T(8,128)(2,1)}, bf16[256,2048]{1,0:T(8,128)(2,1)S(1)}, u32[]{:S(2)}, u32[]{:S(2)}) collective-permute-start(bf16[256,2048]{1,0:T(8,128)(2,1)} %get-tuple-element.289), channel_id=1, source_target_pairs={{0,1},{1,0},{2,3},{3,2},{4,5},{5,4},{6,7},{7,6},{8,9},{9,8},{10,11... | collective-permute-start | bytes 3145736 | tf_op jit(solution)/shard_map/ppermute | solution.py:797
  566.8 18.7 %collective-permute-start.76 = (bf16[128,2048]{1,0:T(8,128)(2,1)}, bf16[128,2048]{1,0:T(8,128)(2,1)S(1)}, u32[]{:S(2)}, u32[]{:S(2)}) collective-permute-start(bf16[128,2048]{1,0:T(8,128)(2,1)} %get-tuple-element.303), channel_id=1, source_target_pairs={{0,2},{2,0},{4,6},{6,4},{8,10},{10,8},{12,14},{14,12},{16,18},{18,... | collective-permute-start | bytes 1572872 | tf_op jit(solution)/shard_map/ppermute | solution.py:793
  567.9 21.3 %collective-permute-start.83 = (bf16[128,2048]{1,0:T(8,128)(2,1)}, bf16[128,2048]{1,0:T(8,128)(2,1)S(1)}, u32[]{:S(2)}, u32[]{:S(2)}) collective-permute-start(bf16[128,2048]{1,0:T(8,128)(2,1)} %get-tuple-element.312), channel_id=1, source_target_pairs={{0,4},{2,6},{4,0},{6,2},{8,12},{10,14},{12,8},{14,10},{16,20},{18,... | collective-permute-start | bytes 1572872 | tf_op jit(solution)/shard_map/ppermute | solution.py:793
  (90 other events, 943.4 us)
Sparse Core Ops, SparseCore 0:
  10.5 48.8 all-gather.3
  60.9 114.0 all-gather.5
  176.6 113.5 all-gather.7
  341.9 44.3 reduce-scatter.5
  388.5 76.0 reduce-scatter.7
  466.8 44.3 reduce-scatter.9
  513.6 84.5 reduce-scatter.13
  600.6 35.8 reduce-scatter.11

commit v6 on v5

--- a/solution.py
+++ b/solution.py
@@ -500,7 +500,7 @@
         ],
         input_output_aliases={2 * n + 2 + i: i for i in range(len(kept))},
         compiler_params=params(44),
-        cost_estimate=cost(10 * n * slot_len * width * inner, 15e6),
+        cost_estimate=cost(10 * n * slot_len * width * inner, 15e6 if n > 1 else 60e6),
     )(*pieces, joined, back, *kept)
 
 
@@ -662,17 +662,17 @@
     )(left, right)
 
 
-def place_grads_kernel(n, me_ref, *refs):
-    ins, outs, held, sem = refs[:PLANE], refs[PLANE : PLANE + n], refs[-2], refs[-1]
+def place_grads_kernel(n, ks, n_kept, me_ref, *refs):
+    ins, outs, held, sem = refs[: len(ks)], refs[len(ks) + n_kept : -2], refs[-2], refs[-1]
     place = me_ref[0]
     copies = []
-    for k in range(PLANE):
-        held[k] = ins[k][...].astype(f32)
+    for b, k in enumerate(ks):
+        held[b] = ins[b][...].astype(f32)
         at = 0
         for i, out in enumerate(outs):
             part = out.shape[1] // PLANE
             one = pltpu.make_async_copy(
-                held.at[k, :, pl.ds(at, part)], out.at[:, lanes(place ^ k, part)], sem.at[k * n + i]
+                held.at[b, :, pl.ds(at, part)], out.at[:, lanes(place ^ k, part)], sem.at[b * n + i]
             )
             one.start()
             copies.append(one)
@@ -681,22 +681,24 @@
         one.wait()
 
 
-def place_columns(me, blocks, widths):
+def place_columns(me, blocks, widths, ks=tuple(range(PLANE)), kept=()):
     rows = blocks[0].shape[0]
     n = len(widths)
     return pl.pallas_call(
-        functools.partial(place_grads_kernel, n),
+        functools.partial(place_grads_kernel, n, ks, len(kept)),
         in_specs=[pl.BlockSpec(memory_space=pltpu.SMEM)]
-        + [pl.BlockSpec(memory_space=pltpu.VMEM)] * PLANE,
+        + [pl.BlockSpec(memory_space=pltpu.VMEM)] * len(ks)
+        + [ANY] * len(kept),
         out_specs=[ANY] * n,
         out_shape=[shaped((rows, PLANE * w), f32) for w in widths],
         scratch_shapes=[
-            pltpu.VMEM((PLANE, *blocks[0].shape), f32),
-            pltpu.SemaphoreType.DMA((PLANE * n,)),
+            pltpu.VMEM((len(ks), *blocks[0].shape), f32),
+            pltpu.SemaphoreType.DMA((len(ks) * n,)),
         ],
+        input_output_aliases={1 + len(ks) + i: i for i in range(len(kept))},
         compiler_params=params(),
         cost_estimate=cost(0, 8e6),
-    )(me, *blocks)
+    )(me, *blocks, *kept)
 
 
 def place_rows_kernel(me_ref, *refs):
@@ -801,15 +803,34 @@
     return [blocks[0]] + [hop(blocks[k], k, count) for k in range(1, PLANE)]
 
 
+def halves_kernel(first, second, top_ref, bottom_ref):
+    top_ref[...] = first[...]
+    bottom_ref[...] = second[...]
+
+
+def halves(first, second):
+    rows, width = first.shape
+    half, part = rows // 2, width // 2
+    out = pl.BlockSpec((half, part), lambda i: (0, i))
+    return pl.pallas_call(
+        halves_kernel,
+        grid=(2,),
+        in_specs=[out, pl.BlockSpec((half, part), lambda i: (1, i))],
+        out_specs=[out, out],
+        out_shape=[pltpu.HBM((half, width), bf16)] * 2,
+        compiler_params=params(),
+        cost_estimate=cost(0, 4e6),
+    )(first, second)
+
+
 def spread(mine, count, beside=None):
-    half = mine.shape[0] // 2
     from_x = hop(mine, 1, count)
     from_y = hop(mine, 2, count)
     pieces = [mine, swap(mine)]
     if beside:
         from_x, from_y = after((from_x, from_y), beside(0, 1, pieces))
-    far_a = hop(from_x[:half], 2, count)
-    far_b = hop(from_y[half:], 1, count)
+    top, bottom = halves(from_x, from_y)
+    far_a, far_b = hop(top, 2, count), hop(bottom, 1, count)
     nearer = [from_x, swap(from_x), from_y, swap(from_y)]
     if beside:
         far_a, far_b = after((far_a, far_b), beside(1, 3, nearer))
@@ -1059,9 +1080,9 @@
     sent = lax.dynamic_index_in_dim(cut, 1 - core, 1, keepdims=False)
     gain_terms = kept + swap(sent)
     early = output, tokens_grad, gain_terms, down_sum, ffgate_sum, ffup_sum, out_sum
-    value_sum, gate_sum, query_sum, key_sum = place_columns(
-        me_scalar, [after(own_part, (blocks, early)), *blocks], (dv, dv, dk, dk)
-    )
+    begun = place_columns(me_scalar, blocks, (dv, dv, dk, dk), (1, 2, 3))
+    own_part = after(own_part, (begun, early))
+    value_sum, gate_sum, query_sum, key_sum = place_columns(me_scalar, [own_part], (dv, dv, dk, dk), (0,), begun)
 
     return (
         output,

time: 653 us -> 645 us (0.988)
  local copies, waits for them, and re-layouts: 40.9 us -> 29.2 us
  Pallas kernels: 234 us -> 243 us
    slice x8 -> x0, local copies, waits for them, and re-layouts: 11.3 us -> none  [the longest x4 5.67 us: spread(): far_b = hop(from_y[half:], 1, count)]
    pallas_call x1 -> x6, Pallas kernels: 3.19 us -> 12.8 us  [the longest x4 8.11 us: halves(): pl.pallas_call(halves_kernel, grid=(2,), in_specs=[out, pl.BlockSpec((hal...]
    unnamed x94 -> x96, local copies, waits for them, and re-layouts: 22 us -> 22.7 us
  transfers between devices with their start and end apart: 101 -> 101, of which waited for: 51 -> 54; matrix products, arithmetic and copies ran while one was open for 12% -> 10% of each run, Pallas kernels for 32% -> 34%
where the time goes in v6:
time: 645 us; the launch traced here: 639 us
  Pallas kernels  243 us (38%)
  waiting for transfers between devices  239 us (37%)
  starting transfers between devices  73 us (11%)
  other arithmetic  38 us (6%)
  local copies, waits for them, and re-layouts  29.2 us (5%)
  between operations  16.1 us (2%)
    ppermute x60, waiting for transfers between devices, hop(): return lax.ppermute(value, 'dp', [(i, i ^ bits) for i in range(count)])  215 us
    ppermute x60, starting transfers between devices, hop(): return lax.ppermute(value, 'dp', [(i, i ^ bits) for i in range(count)])  66.9 us
    pallas_call x2, Pallas kernels, retain(): pl.pallas_call(functools.partial(retain_kernel, first, wide, n, len(kept)...  42.1 us
    pallas_call x2, Pallas kernels, hidden_units(): pl.pallas_call(functools.partial(hidden_kernel, first, wide, n, len(kept)...  35.8 us
    pallas_call x3, Pallas kernels, retain_back(): pl.pallas_call(functools.partial(retain_back_kernel, first, wide, n, len(...  30.4 us
    pallas_call x4, Pallas kernels, fold_cut(): pl.pallas_call(fold_kernel, grid=(width // part,), in_specs=given, out_sp...  23.9 us
    unnamed x96, local copies, waits for them, and re-layouts  22.7 us
    pallas_call x1, Pallas kernels, project_back(): pl.pallas_call(back_kernel, grid=(PLANE,), in_specs=[by_slot(slot_len, in...  20.4 us
  transfers between devices with their start and end apart: 101, of which 54 were waited for; matrix products, arithmetic and copies ran while one was open for 10% of the time, Pallas kernels for 34%

profile of v6, /device:TPU:0, one launch (start us, length us, event | category | flops | bytes accessed | tf_op | source)
XLA Modules:
  0.0 639.1 jit_solution(12993583093984636437)
XLA Ops:
  7.2 3.1 shard_map.220
  10.4 3.0 collective-permute-start.4
  15.0 11.4 %collective-permute-done.4 = bf16[128,2048]{1,0:T(8,128)(2,1)S(1)} collective-permute-done((bf16[128,2048]{1,0:T(8,128)(2,1)}, bf16[128,2048]{1,0:T(8,128)(2,1)S(1)}, u32[]{:S(2)}, u32[]{:S(2)}) %collective-permute-start.4) | collective-permute-done | bytes 524320 | tf_op jit(solution)/shard_map/ppermute | solution.py:795
  27.2 11.0 %collective-permute-done.5 = bf16[128,2048]{1,0:T(8,128)(2,1)S(1)} collective-permute-done((bf16[128,2048]{1,0:T(8,128)(2,1)}, bf16[128,2048]{1,0:T(8,128)(2,1)S(1)}, u32[]{:S(2)}, u32[]{:S(2)}) %collective-permute-start.5) | collective-permute-done | bytes 524320 | tf_op jit(solution)/shard_map/ppermute | solution.py:795
  59.5 17.2 %collective-permute-done.10.second.refs_2_ = bf16[256,2048]{1,0:T(8,128)(2,1)S(1)} collective-permute-done((bf16[256,2048]{1,0:T(8,128)(2,1)S(1)}, bf16[256,2048]{1,0:T(8,128)(2,1)S(1)}, u32[]{:S(2)}, u32[]{:S(2)}) %collective-permute-start.10) | collective-permute-done | bytes 1048608 | tf_op jit(solution)/shard_map/ppermute | solution.py:795
  82.6 7.3 %collective-permute-done.12 = bf16[128,2048]{1,0:T(8,128)(2,1)S(1)} collective-permute-done((bf16[128,2048]{1,0:T(8,128)(2,1)}, bf16[128,2048]{1,0:T(8,128)(2,1)S(1)}, u32[]{:S(2)}, u32[]{:S(2)}) %collective-permute-start.12) | collective-permute-done | bytes 524320 | tf_op jit(solution)/shard_map/ppermute | solution.py:795
  101.0 6.2 collective-permute-done.15.refs_1_
  107.2 9.1 %collective-permute-done.16.refs_2_ = bf16[128,1536]{1,0:T(8,128)(2,1)S(1)} collective-permute-done((bf16[128,1536]{1,0:T(8,128)(2,1)}, bf16[128,1536]{1,0:T(8,128)(2,1)S(1)}, u32[]{:S(2)}, u32[]{:S(2)}) %collective-permute-start.16) | collective-permute-done | bytes 393248 | tf_op jit(solution)/shard_map/ppermute | solution.py:795
  121.9 22.1 %collective-permute-done.19.first = bf16[256,2048]{1,0:T(8,128)(2,1)} collective-permute-done((bf16[256,2048]{1,0:T(8,128)(2,1)}, bf16[256,2048]{1,0:T(8,128)(2,1)}, u32[]{:S(2)}, u32[]{:S(2)}) %collective-permute-start.19) | collective-permute-done | bytes 1048608 | tf_op jit(solution)/shard_map/ppermute | solution.py:795
  156.9 5.2 collective-permute-done.23
  172.3 2.8 all-gather.6.cloned.1.call-done.refs_8_
  175.0 28.8 %shard_map.225 = (bf16[2048,256]{1,0:T(8,128)(2,1)}, bf16[2048,256]{1,0:T(8,128)(2,1)}, bf16[2048,512]{1,0:T(8,128)(2,1)}, f32[2048,512]{1,0:T(8,128)}, bf16[4,5...) custom-call(bf16[256,2048]{1,0:T(8,128)(2,1)} %collective-permute-do, ...), custom_call_target="tpu_custom_call" | custom-call | flops 14173391872 | bytes 15000000 | tf_op jit(solution)/shard_map/pallas_call | solution.py:349
  209.9 5.9 shard_map.226
  218.8 13.3 %shard_map.227 = (bf16[2048,256]{1,0:T(8,128)(2,1)}, bf16[2048,256]{1,0:T(8,128)(2,1)}, bf16[2048,512]{1,0:T(8,128)(2,1)}, f32[2048,512]{1,0:T(8,128)}, bf16[4,5...) custom-call(bf16[256,2048]{1,0:T(8,128)(2,1)} %copy-done.8, ...), custom_call_target="tpu_custom_call", output_to_operand_aliasing={{0}: (4, {}), {1}: (5, {}), {2}: (6, {}), {3}: (7, {}), {4}... | custom-call | flops 4724464128 | bytes 15000000 | tf_op jit(solution)/shard_map/pallas_call | solution.py:349
  238.3 8.9 %collective-permute-done.30 = bf16[128,2048]{1,0:T(8,128)(2,1)S(1)} collective-permute-done((bf16[128,2048]{1,0:T(8,128)(2,1)}, bf16[128,2048]{1,0:T(8,128)(2,1)S(1)}, u32[]{:S(2)}, u32[]{:S(2)}) %collective-permute-start.30) | collective-permute-done | bytes 524320 | tf_op jit(solution)/shard_map/ppermute | solution.py:795
  247.8 10.2 %collective-permute-done.35 = bf16[128,2048]{1,0:T(8,128)(2,1)S(1)} collective-permute-done((bf16[128,2048]{1,0:T(8,128)(2,1)S(1)}, bf16[128,2048]{1,0:T(8,128)(2,1)S(1)}, u32[]{:S(2)}, u32[]{:S(2)}) %collective-permute-start.35) | collective-permute-done | bytes 524320 | tf_op jit(solution)/shard_map/ppermute | solution.py:795
  261.7 22.6 %collective-permute-done.36.first.refs_2_ = bf16[256,2048]{1,0:T(8,128)(2,1)} collective-permute-done((bf16[256,2048]{1,0:T(8,128)(2,1)S(1)}, bf16[256,2048]{1,0:T(8,128)(2,1)}, u32[]{:S(2)}, u32[]{:S(2)}) %collective-permute-start.36) | collective-permute-done | bytes 1048608 | tf_op jit(solution)/shard_map/ppermute | solution.py:795
  290.2 26.1 %shard_map.229 = (bf16[2048,512]{1,0:T(8,128)(2,1)}, bf16[2048,1024]{1,0:T(8,128)(2,1)}, bf16[2048,2048]{1,0:T(8,128)(2,1)}, f32[3,256,2048]{2,1,0:T(8,128)}, bf...) custom-call(bf16[256,2048]{1,0:T(8,128)(2,1)S(1)} %multiply_convert_fusion.1.refs_0_, ...), custom_call_target="tpu_custom_call" | custom-call | flops 16106127360 | bytes 15000000 | tf_op jit(solution)/shard_map/pallas_call | solution.py:480
  319.2 9.7 %shard_map.230 = (bf16[2048,512]{1,0:T(8,128)(2,1)}, bf16[2048,1024]{1,0:T(8,128)(2,1)}, bf16[2048,2048]{1,0:T(8,128)(2,1)}, f32[1,256,2048]{2,1,0:T(8,128)}, bf16[256,2048]{1,0:T(8,128)(2,1)}) custom-call(bf16[256,2048]{1,0:T(8,128)(2,1)S(1)} %constant_dynamic-update-slice_fusion.19.refs_0_, ...), custom_call_target="tpu_custom_call", output_to_operand_aliasing={{0}: (4, {}), {1}: (5, {}), {2}: (6, {})} | custom-call | flops 5368709120 | bytes 60000000 | tf_op jit(solution)/shard_map/pallas_call | solution.py:480
  328.9 8.8 %shard_map.231 = bf16[2048,512]{1,0:T(8,128)(2,1)} custom-call(bf16[2048,512]{1,0:T(8,128)(2,1)} %get-tuple-element.275.left, bf16[2048,2048]{1,0:T(8,128)(2,1)} %constant_dynamic-update-slice_fusion.10.refs_7_.refs_3_.right), custom_call_target="tpu_custom_call" | custom-call | flops 4294967296 | bytes 20000000 | tf_op jit(solution)/shard_map/pallas_call | solution.py:654
  340.8 2.8 collective-permute-done.46.refs_4_
  343.8 5.9 shard_map.232
  353.9 13.3 %shard_map.233 = bf16[2048,1024]{1,0:T(8,128)(2,1)} custom-call(bf16[2048,2048]{1,0:T(8,128)(2,1)} %get-tuple-element.269.left, bf16[2048,1024]{1,0:T(8,128)(2,1)} %get-tuple-element.270.right), custom_call_target="tpu_custom_call" | custom-call | flops 8589934592 | bytes 20000000 | tf_op jit(solution)/shard_map/pallas_call | solution.py:581
  377.6 8.8 %collective-permute-done.53 = bf16[128,2048]{1,0:T(8,128)(2,1)S(1)} collective-permute-done((bf16[128,2048]{1,0:T(8,128)(2,1)S(1)}, bf16[128,2048]{1,0:T(8,128)(2,1)S(1)}, u32[]{:S(2)}, u32[]{:S(2)}) %collective-permute-start.53) | collective-permute-done | bytes 524320 | tf_op jit(solution)/shard_map/ppermute | solution.py:795
  396.3 8.4 %shard_map.235 = (bf16[2048,1536]{1,0:T(8,128)(2,1)}, bf16[2048,2048]{1,0:T(8,128)(2,1)}) custom-call(bf16[256,2048]{1,0:T(8,128)(2,1)} %copy-done.6, bf16[256,2048]{1,0:T(8,128)(2,1)} %collective-permute-done.54.refs_1_, bf16[2048,2048]{1,0:T(8,128)(2,1)} %get-tuple-element.216.refs_2_.refs_4_.first.second, f32[512,512]{1,0:T(8,128)} %fusion.12.refs_9_.refs_3_.refs_5_, ...), custom_call_target="tpu_custom_call" | custom-call | flops 2147483648 | bytes 15000000 | tf_op jit(solution)/shard_map/pallas_call | solution.py:546
  404.7 12.4 %shard_map.234 = (f32[4,256,2048]{2,1,0:T(8,128)}, bf16[256,2048]{1,0:T(8,128)(2,1)}, bf16[256,2048]{1,0:T(8,128)(2,1)}, bf16[256,2048]{1,0:T(8,128)(2,1)}, bf16[256,2048]{1,0:T(8,128)(2,1)}) custom-call(bf16[2048,512]{1,0:T(8,128)(2,1)} %get-tuple-element.275.left, bf16[2048,1536]{1,0:T(8,128)(2,1)} %all-gather.8.cloned.1.call-done.refs_6_.refs_2_.right), custom_call_target="tpu_custom_call" | custom-call | flops 4294967296 | bytes 20000000 | tf_op jit(solution)/shard_map/pallas_call | solution.py:372
  426.1 13.6 %shard_map.237 = (bf16[2048,1536]{1,0:T(8,128)(2,1)}, bf16[2048,2048]{1,0:T(8,128)(2,1)}) custom-call(bf16[256,2048]{1,0:T(8,128)(2,1)} %collective-permute-done.59.first.refs_0_, bf16[256,2048]{1,0:T(8,128)(2,1)} %copy-done.19, bf16[256,2048]{1,0:T(8,128)(2,1)} %collective-permute-done.60.second.refs_2_, ...), custom_call_target="tpu_custom_call", output_to_operand_aliasing={{0}: (12, {}), {1}: (13, {})} | custom-call | flops 4294967296 | bytes 15000000 | tf_op jit(solution)/shard_map/pallas_call | solution.py:546
  443.8 8.4 %shard_map.238 = (bf16[2048,1536]{1,0:T(8,128)(2,1)}, bf16[2048,2048]{1,0:T(8,128)(2,1)}) custom-call(bf16[256,2048]{1,0:T(8,128)(2,1)} %copy-done.10, bf16[256,2048]{1,0:T(8,128)(2,1)} %collective-permute-done.65.refs_1_, bf16[2048,2048]{1,0:T(8,128)(2,1)} %get-tuple-element.216.refs_2_.refs_4_.first.second, ...), custom_call_target="tpu_custom_call", output_to_operand_aliasing={{0}: (10, {}), {1}: (11, {})} | custom-call | flops 2147483648 | bytes 15000000 | tf_op jit(solution)/shard_map/pallas_call | solution.py:546
  452.1 8.9 %shard_map.239 = bf16[2048,512]{1,0:T(8,128)(2,1)} custom-call(bf16[2048,512]{1,0:T(8,128)(2,1)} %get-tuple-element.235.left, bf16[2048,2048]{1,0:T(8,128)(2,1)} %get-tuple-element.294.right), custom_call_target="tpu_custom_call" | custom-call | flops 4294967296 | bytes 20000000 | tf_op jit(solution)/shard_map/pallas_call | solution.py:654
  461.3 18.6 %shard_map.240 = (bf16[512,1536]{1,0:T(8,128)(2,1)}, bf16[1536,1536]{1,0:T(8,128)(2,1)}) custom-call(s32[1]{0:T(128)} %bitcast.6.me_ref.refs_6_, bf16[2048,2048]{1,0:T(8,128)(2,1)} %get-tuple-element.236.left, bf16[2048,1536]{1,0:T(8,128)(2,1)} %get-tuple-element.307.right.left), custom_call_target="tpu_custom_call" | custom-call | flops 12884901888 | bytes 20000000 | tf_op jit(solution)/shard_map/pallas_call | solution.py:632
  486.6 6.0 shard_map.241
  496.8 20.4 %shard_map.242 = (f32[4,256,2048]{2,1,0:T(8,128)}, bf16[256,2048]{1,0:T(8,128)(2,1)}, bf16[256,2048]{1,0:T(8,128)(2,1)}, bf16[256,2048]{1,0:T(8,128)(2,1)}, bf16[256,2048]{1,0:T(8,128)(2,1)}) custom-call(bf16[2048,1536]{1,0:T(8,128)(2,1)} %get-tuple-element.307.right.left, bf16[2048,2048]{1,0:T(8,128)(2,1)} %get-tuple-element.216.refs_2_.refs_4_.first.second, ...), custom_call_target="tpu_custom_call" | custom-call | flops 12884901888 | bytes 20000000 | tf_op jit(solution)/shard_map/pallas_call | solution.py:399
  522.8 2.8 convert_element_type.176
  525.6 3.2 shard_map.244
  528.8 3.5 collective-permute-done.71
  536.1 4.4 fusion.19
  542.7 6.0 shard_map.243
  550.3 11.0 %collective-permute-done.80.refs_2_ = bf16[128,2048]{1,0:T(8,128)(2,1)} collective-permute-done((bf16[128,2048]{1,0:T(8,128)(2,1)}, bf16[128,2048]{1,0:T(8,128)(2,1)}, u32[]{:S(2)}, u32[]{:S(2)}) %collective-permute-start.80) | collective-permute-done | bytes 524320 | tf_op jit(solution)/shard_map/ppermute | solution.py:795
  563.6 6.0 collective-permute-done.77
  569.6 3.0 collective-permute-done.78
  580.7 3.0 collective-permute-done.83
  583.7 5.8 collective-permute-done.84
  589.5 2.9 collective-permute-done.82
  595.5 4.4 collective-permute-done.88
  600.0 3.5 fusion.7
  610.7 11.0 %collective-permute-done.91 = f32[2,128]{1,0:T(2,128)S(1)} collective-permute-done((f32[2,128]{1,0:T(2,128)S(1)}, f32[2,128]{1,0:T(2,128)S(1)}, u32[]{:S(2)}, u32[]{:S(2)}) %collective-permute-start.91) | collective-permute-done | bytes 1056 | tf_op jit(solution)/shard_map/ppermute | solution.py:795
  622.6 4.1 shard_map.246
  626.7 2.8 shard_map.245
  (355 shorter events, 185.1 us)
Async XLA Ops:
  7.2 165.1 %all-gather.4.cloned.1.call-start = ((), (), s32[]{:S(2)}) async-start(), calls=%async_computation.5 | async-start | bytes 2621440 | tf_op jit(solution)/shard_map/all_gather | solution.py:917
  10.4 164.6 %all-gather.6.cloned.1.call-start = ((), (), s32[]{:S(2)}) async-start(), calls=%async_computation.6 | async-start | bytes 7864320 | tf_op jit(solution)/shard_map/all_gather | solution.py:917
  13.4 24.8 %collective-permute-start.5 = (bf16[128,2048]{1,0:T(8,128)(2,1)}, bf16[128,2048]{1,0:T(8,128)(2,1)S(1)}, u32[]{:S(2)}, u32[]{:S(2)}) collective-permute-start(bf16[128,2048]{1,0:T(8,128)(2,1)} %get-tuple-element.183), channel_id=1, source_target_pairs={{0,4},{2,6},{4,0},{6,2},{8,12},{10,14},{12,8},{14,10},{16,20},{18,... | collective-permute-start | bytes 1572872 | tf_op jit(solution)/shard_map/ppermute | solution.py:795
  14.9 24.1 %collective-permute-start.6 = (bf16[128,2048]{1,0:T(8,128)(2,1)}, bf16[128,2048]{1,0:T(8,128)(2,1)S(1)}, u32[]{:S(2)}, u32[]{:S(2)}) collective-permute-start(bf16[128,2048]{1,0:T(8,128)(2,1)} %get-tuple-element.184), channel_id=1, source_target_pairs={{0,6},{2,4},{4,2},{6,0},{8,14},{10,12},{12,10},{14,8},{16,22},{18,... | collective-permute-start | bytes 1572872 | tf_op jit(solution)/shard_map/ppermute | solution.py:795
  39.9 250.3 %all-gather.8.cloned.1.call-start = ((), (), s32[]{:S(2)}) async-start(), calls=%async_computation.7 | async-start | bytes 7864320 | tf_op jit(solution)/shard_map/all_gather | solution.py:917
  56.6 20.1 %collective-permute-start.10 = (bf16[256,2048]{1,0:T(8,128)(2,1)S(1)}, bf16[256,2048]{1,0:T(8,128)(2,1)S(1)}, u32[]{:S(2)}, u32[]{:S(2)}) collective-permute-start(bf16[256,2048]{1,0:T(8,128)(2,1)S(1)} %fusion.2.refs_0_), channel_id=1, source_target_pairs={{0,4},{2,6},{4,0},{6,2},{8,12},{10,14},{12,8},{14,10},{16,20},{18,... | collective-permute-start | bytes 3145736 | tf_op jit(solution)/shard_map/ppermute | solution.py:795
  58.2 20.3 %collective-permute-start.8 = (bf16[256,2048]{1,0:T(8,128)(2,1)S(1)}, bf16[256,2048]{1,0:T(8,128)(2,1)}, u32[]{:S(2)}, u32[]{:S(2)}) collective-permute-start(bf16[256,2048]{1,0:T(8,128)(2,1)S(1)} %fusion.2.refs_0_), channel_id=1, source_target_pairs={{0,2},{2,0},{4,6},{6,4},{8,10},{10,8},{12,14},{14,12},{16,18},{18,... | collective-permute-start | bytes 3145736 | tf_op jit(solution)/shard_map/ppermute | solution.py:795
  96.5 19.9 %collective-permute-start.16 = (bf16[128,1536]{1,0:T(8,128)(2,1)}, bf16[128,1536]{1,0:T(8,128)(2,1)S(1)}, u32[]{:S(2)}, u32[]{:S(2)}) collective-permute-start(bf16[128,1536]{1,0:T(8,128)(2,1)} %get-tuple-element.194), channel_id=1, source_target_pairs={{0,4},{2,6},{4,0},{6,2},{8,12},{10,14},{12,8},{14,10},{16,20},{18,... | collective-permute-start | bytes 1179656 | tf_op jit(solution)/shard_map/ppermute | solution.py:795
  97.6 18.7 %collective-permute-start.17 = (bf16[128,1536]{1,0:T(8,128)(2,1)}, bf16[128,1536]{1,0:T(8,128)(2,1)}, u32[]{:S(2)}, u32[]{:S(2)}) collective-permute-start(bf16[128,1536]{1,0:T(8,128)(2,1)} %get-tuple-element.195), channel_id=1, source_target_pairs={{0,6},{2,4},{4,2},{6,0},{8,14},{10,12},{12,10},{14,8},{16,22},{18,... | collective-permute-start | bytes 1179656 | tf_op jit(solution)/shard_map/ppermute | solution.py:795
  119.8 24.1 %collective-permute-start.19 = (bf16[256,2048]{1,0:T(8,128)(2,1)}, bf16[256,2048]{1,0:T(8,128)(2,1)}, u32[]{:S(2)}, u32[]{:S(2)}) collective-permute-start(bf16[256,2048]{1,0:T(8,128)(2,1)} %fusion.11), channel_id=1, source_target_pairs={{0,2},{2,0},{4,6},{6,4},{8,10},{10,8},{12,14},{14,12},{16,18},{18,... | collective-permute-start | bytes 3145736 | tf_op jit(solution)/shard_map/ppermute | solution.py:795
  120.2 25.1 %collective-permute-start.21 = (bf16[256,2048]{1,0:T(8,128)(2,1)}, bf16[256,2048]{1,0:T(8,128)(2,1)}, u32[]{:S(2)}, u32[]{:S(2)}) collective-permute-start(bf16[256,2048]{1,0:T(8,128)(2,1)} %fusion.11), channel_id=1, source_target_pairs={{0,4},{2,6},{4,0},{6,2},{8,12},{10,14},{12,8},{14,10},{16,20},{18,... | collective-permute-start | bytes 3145736 | tf_op jit(solution)/shard_map/ppermute | solution.py:795
  121.7 30.5 %collective-permute-start.18 = (bf16[256,2048]{1,0:T(8,128)(2,1)}, bf16[256,2048]{1,0:T(8,128)(2,1)}, u32[]{:S(2)}, u32[]{:S(2)}) collective-permute-start(bf16[256,2048]{1,0:T(8,128)(2,1)} %fusion.11), channel_id=1, source_target_pairs={{0,1},{1,0},{2,3},{3,2},{4,5},{5,4},{6,7},{7,6},{8,9},{9,8},{10,11... | collective-permute-start | bytes 3145736 | tf_op jit(solution)/shard_map/ppermute | solution.py:799
  143.9 19.8 %collective-permute-start.20 = (bf16[256,2048]{1,0:T(8,128)(2,1)}, bf16[256,2048]{1,0:T(8,128)(2,1)}, u32[]{:S(2)}, u32[]{:S(2)}) collective-permute-start(bf16[256,2048]{1,0:T(8,128)(2,1)} %collective-permute-done.19.first), channel_id=1, source_target_pairs={{0,1},{1,0},{2,3},{3,2},{4,5},{5,4},{6,7},{7,6},{8,9},{9,8},{10,11... | collective-permute-start | bytes 3145736 | tf_op jit(solution)/shard_map/ppermute | solution.py:799
  152.1 288.9 %reduce-scatter.6.cloned.1.call-start = ((), (), s32[]{:S(2)}) async-start(), calls=%async_computation.8 | async-start | bytes 2621440 | tf_op jit(solution)/shard_map/reduce_scatter | solution.py:920
  215.9 17.6 %collective-permute-start.31 = (bf16[128,2048]{1,0:T(8,128)(2,1)}, bf16[128,2048]{1,0:T(8,128)(2,1)S(1)}, u32[]{:S(2)}, u32[]{:S(2)}) collective-permute-start(bf16[128,2048]{1,0:T(8,128)(2,1)} %get-tuple-element.212), channel_id=1, source_target_pairs={{0,2},{2,0},{4,6},{6,4},{8,10},{10,8},{12,14},{14,12},{16,18},{18,... | collective-permute-start | bytes 1572872 | tf_op jit(solution)/shard_map/ppermute | solution.py:795
  235.0 23.0 %collective-permute-start.35 = (bf16[128,2048]{1,0:T(8,128)(2,1)S(1)}, bf16[128,2048]{1,0:T(8,128)(2,1)S(1)}, u32[]{:S(2)}, u32[]{:S(2)}) collective-permute-start(bf16[128,2048]{1,0:T(8,128)(2,1)S(1)} %add_convert_fusion.6), channel_id=1, source_target_pairs={{0,2},{2,0},{4,6},{6,4},{8,10},{10,8},{12,14},{14,12},{16,18},{18,... | collective-permute-start | bytes 1572872 | tf_op jit(solution)/shard_map/ppermute | solution.py:795
  236.5 21.7 %collective-permute-start.33 = (bf16[128,2048]{1,0:T(8,128)(2,1)S(1)}, bf16[128,2048]{1,0:T(8,128)(2,1)S(1)}, u32[]{:S(2)}, u32[]{:S(2)}) collective-permute-start(bf16[128,2048]{1,0:T(8,128)(2,1)S(1)} %add_convert_fusion.7), channel_id=1, source_target_pairs={{0,4},{2,6},{4,0},{6,2},{8,12},{10,14},{12,8},{14,10},{16,20},{18,... | collective-permute-start | bytes 1572872 | tf_op jit(solution)/shard_map/ppermute | solution.py:795
  259.6 24.7 %collective-permute-start.36 = (bf16[256,2048]{1,0:T(8,128)(2,1)S(1)}, bf16[256,2048]{1,0:T(8,128)(2,1)}, u32[]{:S(2)}, u32[]{:S(2)}) collective-permute-start(bf16[256,2048]{1,0:T(8,128)(2,1)S(1)} %multiply_convert_fusion.1.refs_0_), channel_id=1, source_target_pairs={{0,2},{2,0},{4,6},{6,4},{8,10},{10,8},{12,14},{14,12},{16,18},{18,... | collective-permute-start | bytes 3145736 | tf_op jit(solution)/shard_map/ppermute | solution.py:795
  261.1 24.3 %collective-permute-start.37 = (bf16[256,2048]{1,0:T(8,128)(2,1)S(1)}, bf16[256,2048]{1,0:T(8,128)(2,1)}, u32[]{:S(2)}, u32[]{:S(2)}) collective-permute-start(bf16[256,2048]{1,0:T(8,128)(2,1)S(1)} %multiply_convert_fusion.1.refs_0_), channel_id=1, source_target_pairs={{0,4},{2,6},{4,0},{6,2},{8,12},{10,14},{12,8},{14,10},{16,20},{18,... | collective-permute-start | bytes 3145736 | tf_op jit(solution)/shard_map/ppermute | solution.py:795
  261.7 28.5 %collective-permute-start.40 = (bf16[256,2048]{1,0:T(8,128)(2,1)S(1)}, bf16[256,2048]{1,0:T(8,128)(2,1)}, u32[]{:S(2)}, u32[]{:S(2)}) collective-permute-start(bf16[256,2048]{1,0:T(8,128)(2,1)S(1)} %multiply_convert_fusion.1.refs_0_), channel_id=1, source_target_pairs={{0,1},{1,0},{2,3},{3,2},{4,5},{5,4},{6,7},{7,6},{8,9},{9,8},{10,11... | collective-permute-start | bytes 3145736 | tf_op jit(solution)/shard_map/ppermute | solution.py:799
  288.0 28.3 %collective-permute-start.38 = (bf16[128,2048]{1,0:T(8,128)(2,1)}, bf16[128,2048]{1,0:T(8,128)(2,1)S(1)}, u32[]{:S(2)}, u32[]{:S(2)}) collective-permute-start(bf16[128,2048]{1,0:T(8,128)(2,1)} %get-tuple-element.243), channel_id=1, source_target_pairs={{0,4},{2,6},{4,0},{6,2},{8,12},{10,14},{12,8},{14,10},{16,20},{18,... | collective-permute-start | bytes 1572872 | tf_op jit(solution)/shard_map/ppermute | solution.py:795
  288.5 27.8 %collective-permute-start.39 = (bf16[128,2048]{1,0:T(8,128)(2,1)}, bf16[128,2048]{1,0:T(8,128)(2,1)S(1)}, u32[]{:S(2)}, u32[]{:S(2)}) collective-permute-start(bf16[128,2048]{1,0:T(8,128)(2,1)} %get-tuple-element.244), channel_id=1, source_target_pairs={{0,2},{2,0},{4,6},{6,4},{8,10},{10,8},{12,14},{14,12},{16,18},{18,... | collective-permute-start | bytes 1572872 | tf_op jit(solution)/shard_map/ppermute | solution.py:795
  337.7 159.1 %reduce-scatter.8.cloned.1.call-start = ((), (), s32[]{:S(2)}) async-start(), calls=%async_computation.9 | async-start | bytes 5242880 | tf_op jit(solution)/shard_map/reduce_scatter | solution.py:920
  339.4 34.0 %collective-permute-start.44 = (bf16[256,2048]{1,0:T(8,128)(2,1)}, bf16[256,2048]{1,0:T(8,128)(2,1)S(1)}, u32[]{:S(2)}, u32[]{:S(2)}) collective-permute-start(bf16[256,2048]{1,0:T(8,128)(2,1)} %get-tuple-element.252), channel_id=1, source_target_pairs={{0,1},{1,0},{2,3},{3,2},{4,5},{5,4},{6,7},{7,6},{8,9},{9,8},{10,11... | collective-permute-start | bytes 3145736 | tf_op jit(solution)/shard_map/ppermute | solution.py:799
  349.7 17.9 %collective-permute-start.49 = (bf16[128,2048]{1,0:T(8,128)(2,1)}, bf16[128,2048]{1,0:T(8,128)(2,1)}, u32[]{:S(2)}, u32[]{:S(2)}) collective-permute-start(bf16[128,2048]{1,0:T(8,128)(2,1)} %get-tuple-element.265), channel_id=1, source_target_pairs={{0,2},{2,0},{4,6},{6,4},{8,10},{10,8},{12,14},{14,12},{16,18},{18,... | collective-permute-start | bytes 1572872 | tf_op jit(solution)/shard_map/ppermute | solution.py:795
  352.8 23.3 %collective-permute-start.48 = (bf16[128,2048]{1,0:T(8,128)(2,1)}, bf16[128,2048]{1,0:T(8,128)(2,1)S(1)}, u32[]{:S(2)}, u32[]{:S(2)}) collective-permute-start(bf16[128,2048]{1,0:T(8,128)(2,1)} %get-tuple-element.263), channel_id=1, source_target_pairs={{0,2},{2,0},{4,6},{6,4},{8,10},{10,8},{12,14},{14,12},{16,18},{18,... | collective-permute-start | bytes 1572872 | tf_op jit(solution)/shard_map/ppermute | solution.py:795
  353.3 24.3 %collective-permute-start.52 = (bf16[128,2048]{1,0:T(8,128)(2,1)}, bf16[128,2048]{1,0:T(8,128)(2,1)}, u32[]{:S(2)}, u32[]{:S(2)}) collective-permute-start(bf16[128,2048]{1,0:T(8,128)(2,1)} %get-tuple-element.272), channel_id=1, source_target_pairs={{0,4},{2,6},{4,0},{6,2},{8,12},{10,14},{12,8},{14,10},{16,20},{18,... | collective-permute-start | bytes 1572872 | tf_op jit(solution)/shard_map/ppermute | solution.py:795
  367.2 158.4 %reduce-scatter.10.cloned.1.call-start = ((), (), s32[]{:S(2)}) async-start(), calls=%async_computation.10 | async-start | bytes 2621440 | tf_op jit(solution)/shard_map/reduce_scatter | solution.py:920
  393.5 25.7 %collective-permute-start.59 = (bf16[256,2048]{1,0:T(8,128)(2,1)S(1)}, bf16[256,2048]{1,0:T(8,128)(2,1)}, u32[]{:S(2)}, u32[]{:S(2)}) collective-permute-start(bf16[256,2048]{1,0:T(8,128)(2,1)S(1)} %get-tuple-element.356.refs_0_), channel_id=1, source_target_pairs={{0,2},{2,0},{4,6},{6,4},{8,10},{10,8},{12,14},{14,12},{16,18},{18,... | collective-permute-start | bytes 3145736 | tf_op jit(solution)/shard_map/ppermute | solution.py:795
  394.5 25.4 %collective-permute-start.60 = (bf16[256,2048]{1,0:T(8,128)(2,1)S(1)}, bf16[256,2048]{1,0:T(8,128)(2,1)}, u32[]{:S(2)}, u32[]{:S(2)}) collective-permute-start(bf16[256,2048]{1,0:T(8,128)(2,1)S(1)} %get-tuple-element.356.refs_0_), channel_id=1, source_target_pairs={{0,4},{2,6},{4,0},{6,2},{8,12},{10,14},{12,8},{14,10},{16,20},{18,... | collective-permute-start | bytes 3145736 | tf_op jit(solution)/shard_map/ppermute | solution.py:795
  461.1 143.6 %reduce-scatter.14.cloned.1.call-start = ((), (), s32[]{:S(2)}) async-start(), calls=%async_computation.12 | async-start | bytes 5898240 | tf_op jit(solution)/shard_map/reduce_scatter | solution.py:920
  480.0 150.1 %reduce-scatter.12.cloned.1.call-start = ((), (), s32[]{:S(2)}) async-start(), calls=%async_computation.11 | async-start | bytes 1966080 | tf_op jit(solution)/shard_map/reduce_scatter | solution.py:920
  481.3 40.9 %collective-permute-start.55 = (bf16[256,2048]{1,0:T(8,128)(2,1)}, bf16[256,2048]{1,0:T(8,128)(2,1)}, u32[]{:S(2)}, u32[]{:S(2)}) collective-permute-start(bf16[256,2048]{1,0:T(8,128)(2,1)} %get-tuple-element.277), channel_id=1, source_target_pairs={{0,1},{1,0},{2,3},{3,2},{4,5},{5,4},{6,7},{7,6},{8,9},{9,8},{10,11... | collective-permute-start | bytes 3145736 | tf_op jit(solution)/shard_map/ppermute | solution.py:799
  492.7 24.5 %collective-permute-start.67 = (bf16[128,2048]{1,0:T(8,128)(2,1)}, bf16[128,2048]{1,0:T(8,128)(2,1)}, u32[]{:S(2)}, u32[]{:S(2)}) collective-permute-start(bf16[128,2048]{1,0:T(8,128)(2,1)} %get-tuple-element.305), channel_id=1, source_target_pairs={{0,2},{2,0},{4,6},{6,4},{8,10},{10,8},{12,14},{14,12},{16,18},{18,... | collective-permute-start | bytes 1572872 | tf_op jit(solution)/shard_map/ppermute | solution.py:795
  492.9 24.3 %collective-permute-start.68 = (bf16[128,2048]{1,0:T(8,128)(2,1)}, bf16[128,2048]{1,0:T(8,128)(2,1)}, u32[]{:S(2)}, u32[]{:S(2)}) collective-permute-start(bf16[128,2048]{1,0:T(8,128)(2,1)} %get-tuple-element.306), channel_id=1, source_target_pairs={{0,4},{2,6},{4,0},{6,2},{8,12},{10,14},{12,8},{14,10},{16,20},{18,... | collective-permute-start | bytes 1572872 | tf_op jit(solution)/shard_map/ppermute | solution.py:795
  493.7 28.4 %collective-permute-start.66 = (bf16[128,2048]{1,0:T(8,128)(2,1)}, bf16[128,2048]{1,0:T(8,128)(2,1)S(1)}, u32[]{:S(2)}, u32[]{:S(2)}) collective-permute-start(bf16[128,2048]{1,0:T(8,128)(2,1)} %get-tuple-element.303), channel_id=1, source_target_pairs={{0,2},{2,0},{4,6},{6,4},{8,10},{10,8},{12,14},{14,12},{16,18},{18,... | collective-permute-start | bytes 1572872 | tf_op jit(solution)/shard_map/ppermute | solution.py:795
  494.8 27.9 %collective-permute-start.70 = (bf16[128,2048]{1,0:T(8,128)(2,1)}, bf16[128,2048]{1,0:T(8,128)(2,1)}, u32[]{:S(2)}, u32[]{:S(2)}) collective-permute-start(bf16[128,2048]{1,0:T(8,128)(2,1)} %get-tuple-element.314), channel_id=1, source_target_pairs={{0,4},{2,6},{4,0},{6,2},{8,12},{10,14},{12,8},{14,10},{16,20},{18,... | collective-permute-start | bytes 1572872 | tf_op jit(solution)/shard_map/ppermute | solution.py:795
  522.2 18.4 %collective-permute-start.73 = (bf16[256,2048]{1,0:T(8,128)(2,1)}, bf16[256,2048]{1,0:T(8,128)(2,1)}, u32[]{:S(2)}, u32[]{:S(2)}) collective-permute-start(bf16[256,2048]{1,0:T(8,128)(2,1)} %get-tuple-element.310), channel_id=1, source_target_pairs={{0,1},{1,0},{2,3},{3,2},{4,5},{5,4},{6,7},{7,6},{8,9},{9,8},{10,11... | collective-permute-start | bytes 3145736 | tf_op jit(solution)/shard_map/ppermute | solution.py:799
  522.2 20.5 %collective-permute-start.74 = (bf16[256,2048]{1,0:T(8,128)(2,1)}, bf16[256,2048]{1,0:T(8,128)(2,1)}, u32[]{:S(2)}, u32[]{:S(2)}) collective-permute-start(bf16[256,2048]{1,0:T(8,128)(2,1)} %get-tuple-element.311), channel_id=1, source_target_pairs={{0,1},{1,0},{2,3},{3,2},{4,5},{5,4},{6,7},{7,6},{8,9},{9,8},{10,11... | collective-permute-start | bytes 3145736 | tf_op jit(solution)/shard_map/ppermute | solution.py:799
  522.7 20.0 %collective-permute-start.75 = (bf16[256,2048]{1,0:T(8,128)(2,1)}, bf16[256,2048]{1,0:T(8,128)(2,1)}, u32[]{:S(2)}, u32[]{:S(2)}) collective-permute-start(bf16[256,2048]{1,0:T(8,128)(2,1)} %get-tuple-element.312), channel_id=1, source_target_pairs={{0,1},{1,0},{2,3},{3,2},{4,5},{5,4},{6,7},{7,6},{8,9},{9,8},{10,11... | collective-permute-start | bytes 3145736 | tf_op jit(solution)/shard_map/ppermute | solution.py:799
  532.3 17.9 %collective-permute-start.79 = (bf16[128,2048]{1,0:T(8,128)(2,1)}, bf16[128,2048]{1,0:T(8,128)(2,1)S(1)}, u32[]{:S(2)}, u32[]{:S(2)}) collective-permute-start(bf16[128,2048]{1,0:T(8,128)(2,1)} %get-tuple-element.328), channel_id=1, source_target_pairs={{0,2},{2,0},{4,6},{6,4},{8,10},{10,8},{12,14},{14,12},{16,18},{18,... | collective-permute-start | bytes 1572872 | tf_op jit(solution)/shard_map/ppermute | solution.py:795
  535.2 26.1 %collective-permute-start.80 = (bf16[128,2048]{1,0:T(8,128)(2,1)}, bf16[128,2048]{1,0:T(8,128)(2,1)}, u32[]{:S(2)}, u32[]{:S(2)}) collective-permute-start(bf16[128,2048]{1,0:T(8,128)(2,1)} %get-tuple-element.329), channel_id=1, source_target_pairs={{0,4},{2,6},{4,0},{6,2},{8,12},{10,14},{12,8},{14,10},{16,20},{18,... | collective-permute-start | bytes 1572872 | tf_op jit(solution)/shard_map/ppermute | solution.py:795
  540.6 22.2 %collective-permute-start.81 = (bf16[128,2048]{1,0:T(8,128)(2,1)}, bf16[128,2048]{1,0:T(8,128)(2,1)}, u32[]{:S(2)}, u32[]{:S(2)}) collective-permute-start(bf16[128,2048]{1,0:T(8,128)(2,1)} %get-tuple-element.330), channel_id=1, source_target_pairs={{0,6},{2,4},{4,2},{6,0},{8,14},{10,12},{12,10},{14,8},{16,22},{18,... | collective-permute-start | bytes 1572872 | tf_op jit(solution)/shard_map/ppermute | solution.py:795
  548.6 20.9 %collective-permute-start.77 = (bf16[128,2048]{1,0:T(8,128)(2,1)}, bf16[128,2048]{1,0:T(8,128)(2,1)}, u32[]{:S(2)}, u32[]{:S(2)}) collective-permute-start(bf16[128,2048]{1,0:T(8,128)(2,1)} %get-tuple-element.325), channel_id=1, source_target_pairs={{0,2},{2,0},{4,6},{6,4},{8,10},{10,8},{12,14},{14,12},{16,18},{18,... | collective-permute-start | bytes 1572872 | tf_op jit(solution)/shard_map/ppermute | solution.py:795
  549.3 23.3 %collective-permute-start.78 = (bf16[128,2048]{1,0:T(8,128)(2,1)}, bf16[128,2048]{1,0:T(8,128)(2,1)}, u32[]{:S(2)}, u32[]{:S(2)}) collective-permute-start(bf16[128,2048]{1,0:T(8,128)(2,1)} %get-tuple-element.326), channel_id=1, source_target_pairs={{0,4},{2,6},{4,0},{6,2},{8,12},{10,14},{12,8},{14,10},{16,20},{18,... | collective-permute-start | bytes 1572872 | tf_op jit(solution)/shard_map/ppermute | solution.py:795
  550.2 28.9 %collective-permute-start.72 = (bf16[256,2048]{1,0:T(8,128)(2,1)}, bf16[256,2048]{1,0:T(8,128)(2,1)S(1)}, u32[]{:S(2)}, u32[]{:S(2)}) collective-permute-start(bf16[256,2048]{1,0:T(8,128)(2,1)} %get-tuple-element.309), channel_id=1, source_target_pairs={{0,1},{1,0},{2,3},{3,2},{4,5},{5,4},{6,7},{7,6},{8,9},{9,8},{10,11... | collective-permute-start | bytes 3145736 | tf_op jit(solution)/shard_map/ppermute | solution.py:799
  561.3 19.4 %collective-permute-start.76 = (bf16[128,2048]{1,0:T(8,128)(2,1)}, bf16[128,2048]{1,0:T(8,128)(2,1)S(1)}, u32[]{:S(2)}, u32[]{:S(2)}) collective-permute-start(bf16[128,2048]{1,0:T(8,128)(2,1)} %get-tuple-element.323), channel_id=1, source_target_pairs={{0,2},{2,0},{4,6},{6,4},{8,10},{10,8},{12,14},{14,12},{16,18},{18,... | collective-permute-start | bytes 1572872 | tf_op jit(solution)/shard_map/ppermute | solution.py:795
  562.8 20.9 %collective-permute-start.83 = (bf16[128,2048]{1,0:T(8,128)(2,1)}, bf16[128,2048]{1,0:T(8,128)(2,1)S(1)}, u32[]{:S(2)}, u32[]{:S(2)}) collective-permute-start(bf16[128,2048]{1,0:T(8,128)(2,1)} %get-tuple-element.332), channel_id=1, source_target_pairs={{0,4},{2,6},{4,0},{6,2},{8,12},{10,14},{12,8},{14,10},{16,20},{18,... | collective-permute-start | bytes 1572872 | tf_op jit(solution)/shard_map/ppermute | solution.py:795
  (91 other events, 884.6 us)
Sparse Core Ops, SparseCore 0:
  10.5 48.8 all-gather.3
  60.9 114.0 all-gather.5
  176.6 113.5 all-gather.7
  337.8 42.0 reduce-scatter.5
  382.2 76.0 reduce-scatter.7
  461.2 43.5 reduce-scatter.9
  507.2 84.5 reduce-scatter.13
  594.2 35.8 reduce-scatter.11

commit v7 on v6

--- a/solution.py
+++ b/solution.py
@@ -76,12 +76,13 @@
         one.wait()
 
 
-def place_copies(plan, n_copies, me, ins, out_shapes):
+def place_copies(plan, n_copies, me, ins, out_shapes, any_in=False):
     moved = 2 * sum(2 * s.size for s in out_shapes)
     return pl.pallas_call(
         functools.partial(copy_kernel, plan, len(ins)),
-        in_specs=[pl.BlockSpec(memory_space=pltpu.SMEM)] + [pl.BlockSpec(memory_space=pltpu.VMEM)] * len(ins),
-        out_specs=[ANY] * len(out_shapes),
+        in_specs=[pl.BlockSpec(memory_space=pltpu.SMEM)]
+        + [ANY if any_in else pl.BlockSpec(memory_space=pltpu.VMEM)] * len(ins),
+        out_specs=[pl.BlockSpec(memory_space=pltpu.VMEM) if any_in else ANY] * len(out_shapes),
         out_shape=out_shapes,
         scratch_shapes=[pltpu.SemaphoreType.DMA((n_copies,))],
         compiler_params=params(),
@@ -121,6 +122,26 @@
     shapes = [shaped((rows, width + inner), bf16)] * PLANE
     n_copies = PLANE * (len(parts) + (inner // rows if aligned else 1))
     return place_copies(plan, n_copies, me, [*by_columns, by_rows], shapes)
+
+
+def own_weights(me, by_columns, by_rows):
+    rows, cols = by_columns[0].shape[0], by_rows.shape[1]
+    parts = [w.shape[1] // PLANE for w in by_columns]
+    inner = by_rows.shape[0] // PLANE
+    width = sum(parts)
+
+    def plan(place, ins, outs):
+        copies, at = [], 0
+        for w, part in zip(ins, parts):
+            copies.append((w.at[:, lanes(place, part)], outs[0].at[:, pl.ds(at, part)]))
+            at += part
+        for block in range(inner // rows):
+            source = pl.ds(pl.multiple_of(place * inner + block * rows, rows), rows)
+            copies.append((ins[-1].at[source, :], outs[0].at[:, pl.ds(width + block * cols, cols)]))
+        return copies
+
+    shape = shaped((rows, width + inner), bf16)
+    return place_copies(plan, len(parts) + inner // rows, me, [*by_columns, by_rows], [shape], any_in=True)[0]
 
 
 def join_weights(me, blocks, width):
@@ -923,7 +944,7 @@
     attn_blocks = trade(attn_cuts, count)
     attn_width = 2 * dk + 2 * dv
     if depth == 4:
-        own_gathered = gather_depth(attn_cuts[0])
+        own_gathered = gather_depth(own_weights(me_scalar, (w_query, w_key, w_value, w_gate), w_out))
         attn_own = jnp.concatenate(attn_blocks[1:])
         attn_weights = own_gathered, gather_depth(attn_own)
     else:

time: 645 us -> 645 us (level)
    pallas_call x4 -> x5, Pallas kernels: 11.7 us -> 13.6 us  [place_copies(): pl.pallas_call(functools.partial(copy_kernel, plan, len(ins)), in_specs=[...]
  transfers between devices with their start and end apart: 101 -> 101, of which waited for: 54 -> 55; matrix products, arithmetic and copies ran while one was open for 10% -> 10% of each run, Pallas kernels for 34% -> 35%
where the time goes in v7:
time: 645 us; the launch traced here: 639 us
  Pallas kernels  245 us (38%)
  waiting for transfers between devices  238 us (37%)
  starting transfers between devices  72.2 us (11%)
  other arithmetic  38 us (6%)
  local copies, waits for them, and re-layouts  29.2 us (5%)
  between operations  16.1 us (2%)
    ppermute x60, waiting for transfers between devices, hop(): return lax.ppermute(value, 'dp', [(i, i ^ bits) for i in range(count)])  215 us
    ppermute x60, starting transfers between devices, hop(): return lax.ppermute(value, 'dp', [(i, i ^ bits) for i in range(count)])  66.1 us
    pallas_call x2, Pallas kernels, retain(): pl.pallas_call(functools.partial(retain_kernel, first, wide, n, len(kept)...  42.1 us
    pallas_call x2, Pallas kernels, hidden_units(): pl.pallas_call(functools.partial(hidden_kernel, first, wide, n, len(kept)...  35.8 us
    pallas_call x3, Pallas kernels, retain_back(): pl.pallas_call(functools.partial(retain_back_kernel, first, wide, n, len(...  30.4 us
    pallas_call x4, Pallas kernels, fold_cut(): pl.pallas_call(fold_kernel, grid=(width // part,), in_specs=given, out_sp...  23.9 us
    unnamed x96, local copies, waits for them, and re-layouts  22.7 us
    pallas_call x1, Pallas kernels, project_back(): pl.pallas_call(back_kernel, grid=(PLANE,), in_specs=[by_slot(slot_len, in...  20.4 us
  transfers between devices with their start and end apart: 101, of which 55 were waited for; matrix products, arithmetic and copies ran while one was open for 10% of the time, Pallas kernels for 35%

profile of v7, /device:TPU:0, one launch (start us, length us, event | category | flops | bytes accessed | tf_op | source)
XLA Modules:
  0.0 638.7 jit_solution(7009398106551780113)
XLA Ops:
  9.2 3.1 shard_map.220
  12.3 3.0 collective-permute-start.4
  16.9 11.4 %collective-permute-done.4 = bf16[128,2048]{1,0:T(8,128)(2,1)S(1)} collective-permute-done((bf16[128,2048]{1,0:T(8,128)(2,1)}, bf16[128,2048]{1,0:T(8,128)(2,1)S(1)}, u32[]{:S(2)}, u32[]{:S(2)}) %collective-permute-start.4) | collective-permute-done | bytes 524320 | tf_op jit(solution)/shard_map/ppermute | solution.py:816
  29.1 11.0 %collective-permute-done.5 = bf16[128,2048]{1,0:T(8,128)(2,1)S(1)} collective-permute-done((bf16[128,2048]{1,0:T(8,128)(2,1)}, bf16[128,2048]{1,0:T(8,128)(2,1)S(1)}, u32[]{:S(2)}, u32[]{:S(2)}) %collective-permute-start.5) | collective-permute-done | bytes 524320 | tf_op jit(solution)/shard_map/ppermute | solution.py:816
  61.7 17.4 %collective-permute-done.10.second.refs_2_ = bf16[256,2048]{1,0:T(8,128)(2,1)S(1)} collective-permute-done((bf16[256,2048]{1,0:T(8,128)(2,1)S(1)}, bf16[256,2048]{1,0:T(8,128)(2,1)S(1)}, u32[]{:S(2)}, u32[]{:S(2)}) %collective-permute-start.10) | collective-permute-done | bytes 1048608 | tf_op jit(solution)/shard_map/ppermute | solution.py:816
  85.2 6.5 %collective-permute-done.12 = bf16[128,2048]{1,0:T(8,128)(2,1)S(1)} collective-permute-done((bf16[128,2048]{1,0:T(8,128)(2,1)}, bf16[128,2048]{1,0:T(8,128)(2,1)S(1)}, u32[]{:S(2)}, u32[]{:S(2)}) %collective-permute-start.12) | collective-permute-done | bytes 524320 | tf_op jit(solution)/shard_map/ppermute | solution.py:816
  103.2 6.2 collective-permute-done.15.refs_1_
  109.4 8.9 %collective-permute-done.16.refs_2_ = bf16[128,1536]{1,0:T(8,128)(2,1)S(1)} collective-permute-done((bf16[128,1536]{1,0:T(8,128)(2,1)}, bf16[128,1536]{1,0:T(8,128)(2,1)S(1)}, u32[]{:S(2)}, u32[]{:S(2)}) %collective-permute-start.16) | collective-permute-done | bytes 393248 | tf_op jit(solution)/shard_map/ppermute | solution.py:816
  123.1 22.7 %collective-permute-done.19.first = bf16[256,2048]{1,0:T(8,128)(2,1)} collective-permute-done((bf16[256,2048]{1,0:T(8,128)(2,1)}, bf16[256,2048]{1,0:T(8,128)(2,1)}, u32[]{:S(2)}, u32[]{:S(2)}) %collective-permute-start.19) | collective-permute-done | bytes 1048608 | tf_op jit(solution)/shard_map/ppermute | solution.py:816
  158.5 5.1 collective-permute-done.23
  174.6 28.9 %shard_map.226 = (bf16[2048,256]{1,0:T(8,128)(2,1)}, bf16[2048,256]{1,0:T(8,128)(2,1)}, bf16[2048,512]{1,0:T(8,128)(2,1)}, f32[2048,512]{1,0:T(8,128)}, bf16[4,5...) custom-call(bf16[256,2048]{1,0:T(8,128)(2,1)} %collective-permute-do, ...), custom_call_target="tpu_custom_call" | custom-call | flops 14173391872 | bytes 15000000 | tf_op jit(solution)/shard_map/pallas_call | solution.py:370
  209.5 5.9 shard_map.227
  218.4 13.3 %shard_map.228 = (bf16[2048,256]{1,0:T(8,128)(2,1)}, bf16[2048,256]{1,0:T(8,128)(2,1)}, bf16[2048,512]{1,0:T(8,128)(2,1)}, f32[2048,512]{1,0:T(8,128)}, bf16[4,5...) custom-call(bf16[256,2048]{1,0:T(8,128)(2,1)} %copy-done.8, ...), custom_call_target="tpu_custom_call", output_to_operand_aliasing={{0}: (4, {}), {1}: (5, {}), {2}: (6, {}), {3}: (7, {}), {4}... | custom-call | flops 4724464128 | bytes 15000000 | tf_op jit(solution)/shard_map/pallas_call | solution.py:370
  237.9 8.9 %collective-permute-done.30 = bf16[128,2048]{1,0:T(8,128)(2,1)S(1)} collective-permute-done((bf16[128,2048]{1,0:T(8,128)(2,1)}, bf16[128,2048]{1,0:T(8,128)(2,1)S(1)}, u32[]{:S(2)}, u32[]{:S(2)}) %collective-permute-start.30) | collective-permute-done | bytes 524320 | tf_op jit(solution)/shard_map/ppermute | solution.py:816
  247.4 10.2 %collective-permute-done.35 = bf16[128,2048]{1,0:T(8,128)(2,1)S(1)} collective-permute-done((bf16[128,2048]{1,0:T(8,128)(2,1)S(1)}, bf16[128,2048]{1,0:T(8,128)(2,1)S(1)}, u32[]{:S(2)}, u32[]{:S(2)}) %collective-permute-start.35) | collective-permute-done | bytes 524320 | tf_op jit(solution)/shard_map/ppermute | solution.py:816
  261.3 22.6 %collective-permute-done.36.first.refs_2_ = bf16[256,2048]{1,0:T(8,128)(2,1)} collective-permute-done((bf16[256,2048]{1,0:T(8,128)(2,1)S(1)}, bf16[256,2048]{1,0:T(8,128)(2,1)}, u32[]{:S(2)}, u32[]{:S(2)}) %collective-permute-start.36) | collective-permute-done | bytes 1048608 | tf_op jit(solution)/shard_map/ppermute | solution.py:816
  289.8 26.1 %shard_map.230 = (bf16[2048,512]{1,0:T(8,128)(2,1)}, bf16[2048,1024]{1,0:T(8,128)(2,1)}, bf16[2048,2048]{1,0:T(8,128)(2,1)}, f32[3,256,2048]{2,1,0:T(8,128)}, bf...) custom-call(bf16[256,2048]{1,0:T(8,128)(2,1)S(1)} %multiply_convert_fusion.1.refs_0_, ...), custom_call_target="tpu_custom_call" | custom-call | flops 16106127360 | bytes 15000000 | tf_op jit(solution)/shard_map/pallas_call | solution.py:501
  318.8 9.7 %shard_map.231 = (bf16[2048,512]{1,0:T(8,128)(2,1)}, bf16[2048,1024]{1,0:T(8,128)(2,1)}, bf16[2048,2048]{1,0:T(8,128)(2,1)}, f32[1,256,2048]{2,1,0:T(8,128)}, bf16[256,2048]{1,0:T(8,128)(2,1)}) custom-call(bf16[256,2048]{1,0:T(8,128)(2,1)S(1)} %constant_dynamic-update-slice_fusion.19.refs_0_, ...), custom_call_target="tpu_custom_call", output_to_operand_aliasing={{0}: (4, {}), {1}: (5, {}), {2}: (6, {})} | custom-call | flops 5368709120 | bytes 60000000 | tf_op jit(solution)/shard_map/pallas_call | solution.py:501
  328.4 8.8 %shard_map.232 = bf16[2048,512]{1,0:T(8,128)(2,1)} custom-call(bf16[2048,512]{1,0:T(8,128)(2,1)} %get-tuple-element.273.left, bf16[2048,2048]{1,0:T(8,128)(2,1)} %constant_dynamic-update-slice_fusion.10.refs_7_.refs_3_.right), custom_call_target="tpu_custom_call" | custom-call | flops 4294967296 | bytes 20000000 | tf_op jit(solution)/shard_map/pallas_call | solution.py:675
  340.4 2.8 collective-permute-done.46.refs_4_
  343.4 5.9 shard_map.233
  353.5 13.3 %shard_map.234 = bf16[2048,1024]{1,0:T(8,128)(2,1)} custom-call(bf16[2048,2048]{1,0:T(8,128)(2,1)} %get-tuple-element.267.left, bf16[2048,1024]{1,0:T(8,128)(2,1)} %get-tuple-element.268.right), custom_call_target="tpu_custom_call" | custom-call | flops 8589934592 | bytes 20000000 | tf_op jit(solution)/shard_map/pallas_call | solution.py:602
  377.2 8.8 %collective-permute-done.53 = bf16[128,2048]{1,0:T(8,128)(2,1)S(1)} collective-permute-done((bf16[128,2048]{1,0:T(8,128)(2,1)S(1)}, bf16[128,2048]{1,0:T(8,128)(2,1)S(1)}, u32[]{:S(2)}, u32[]{:S(2)}) %collective-permute-start.53) | collective-permute-done | bytes 524320 | tf_op jit(solution)/shard_map/ppermute | solution.py:816
  395.9 8.4 %shard_map.236 = (bf16[2048,1536]{1,0:T(8,128)(2,1)}, bf16[2048,2048]{1,0:T(8,128)(2,1)}) custom-call(bf16[256,2048]{1,0:T(8,128)(2,1)} %copy-done.6, bf16[256,2048]{1,0:T(8,128)(2,1)} %collective-permute-done.54.refs_1_, bf16[2048,2048]{1,0:T(8,128)(2,1)} %get-tuple-element.214.refs_2_.refs_4_.first.second, f32[512,512]{1,0:T(8,128)} %fusion.12.refs_9_.refs_3_.refs_5_, ...), custom_call_target="tpu_custom_call" | custom-call | flops 2147483648 | bytes 15000000 | tf_op jit(solution)/shard_map/pallas_call | solution.py:567
  404.3 12.4 %shard_map.235 = (f32[4,256,2048]{2,1,0:T(8,128)}, bf16[256,2048]{1,0:T(8,128)(2,1)}, bf16[256,2048]{1,0:T(8,128)(2,1)}, bf16[256,2048]{1,0:T(8,128)(2,1)}, bf16[256,2048]{1,0:T(8,128)(2,1)}) custom-call(bf16[2048,512]{1,0:T(8,128)(2,1)} %get-tuple-element.273.left, bf16[2048,1536]{1,0:T(8,128)(2,1)} %all-gather.8.cloned.1.call-done.refs_6_.refs_2_.right), custom_call_target="tpu_custom_call" | custom-call | flops 4294967296 | bytes 20000000 | tf_op jit(solution)/shard_map/pallas_call | solution.py:393
  425.7 13.6 %shard_map.238 = (bf16[2048,1536]{1,0:T(8,128)(2,1)}, bf16[2048,2048]{1,0:T(8,128)(2,1)}) custom-call(bf16[256,2048]{1,0:T(8,128)(2,1)} %collective-permute-done.59.first.refs_0_, bf16[256,2048]{1,0:T(8,128)(2,1)} %copy-done.19, bf16[256,2048]{1,0:T(8,128)(2,1)} %collective-permute-done.60.second.refs_2_, ...), custom_call_target="tpu_custom_call", output_to_operand_aliasing={{0}: (12, {}), {1}: (13, {})} | custom-call | flops 4294967296 | bytes 15000000 | tf_op jit(solution)/shard_map/pallas_call | solution.py:567
  440.6 2.7 collective-permute-done.65.refs_1_
  443.4 8.4 %shard_map.239 = (bf16[2048,1536]{1,0:T(8,128)(2,1)}, bf16[2048,2048]{1,0:T(8,128)(2,1)}) custom-call(bf16[256,2048]{1,0:T(8,128)(2,1)} %copy-done.10, bf16[256,2048]{1,0:T(8,128)(2,1)} %collective-permute-done.65.refs_1_, bf16[2048,2048]{1,0:T(8,128)(2,1)} %get-tuple-element.214.refs_2_.refs_4_.first.second, ...), custom_call_target="tpu_custom_call", output_to_operand_aliasing={{0}: (10, {}), {1}: (11, {})} | custom-call | flops 2147483648 | bytes 15000000 | tf_op jit(solution)/shard_map/pallas_call | solution.py:567
  451.7 8.9 %shard_map.240 = bf16[2048,512]{1,0:T(8,128)(2,1)} custom-call(bf16[2048,512]{1,0:T(8,128)(2,1)} %get-tuple-element.233.left, bf16[2048,2048]{1,0:T(8,128)(2,1)} %get-tuple-element.292.right), custom_call_target="tpu_custom_call" | custom-call | flops 4294967296 | bytes 20000000 | tf_op jit(solution)/shard_map/pallas_call | solution.py:675
  460.9 18.6 %shard_map.241 = (bf16[512,1536]{1,0:T(8,128)(2,1)}, bf16[1536,1536]{1,0:T(8,128)(2,1)}) custom-call(s32[1]{0:T(128)} %bitcast.6.me_ref.refs_6_, bf16[2048,2048]{1,0:T(8,128)(2,1)} %get-tuple-element.234.left, bf16[2048,1536]{1,0:T(8,128)(2,1)} %get-tuple-element.305.right.left), custom_call_target="tpu_custom_call" | custom-call | flops 12884901888 | bytes 20000000 | tf_op jit(solution)/shard_map/pallas_call | solution.py:653
  486.2 6.0 shard_map.242
  496.4 20.4 %shard_map.243 = (f32[4,256,2048]{2,1,0:T(8,128)}, bf16[256,2048]{1,0:T(8,128)(2,1)}, bf16[256,2048]{1,0:T(8,128)(2,1)}, bf16[256,2048]{1,0:T(8,128)(2,1)}, bf16[256,2048]{1,0:T(8,128)(2,1)}) custom-call(bf16[2048,1536]{1,0:T(8,128)(2,1)} %get-tuple-element.305.right.left, bf16[2048,2048]{1,0:T(8,128)(2,1)} %get-tuple-element.214.refs_2_.refs_4_.first.second, ...), custom_call_target="tpu_custom_call" | custom-call | flops 12884901888 | bytes 20000000 | tf_op jit(solution)/shard_map/pallas_call | solution.py:420
  522.4 2.8 convert_element_type.176
  525.2 3.2 shard_map.245
  528.3 3.5 collective-permute-done.71
  535.7 4.4 fusion.19
  542.3 6.0 shard_map.244
  549.9 11.1 %collective-permute-done.80.refs_2_ = bf16[128,2048]{1,0:T(8,128)(2,1)} collective-permute-done((bf16[128,2048]{1,0:T(8,128)(2,1)}, bf16[128,2048]{1,0:T(8,128)(2,1)}, u32[]{:S(2)}, u32[]{:S(2)}) %collective-permute-start.80) | collective-permute-done | bytes 524320 | tf_op jit(solution)/shard_map/ppermute | solution.py:816
  563.2 6.0 collective-permute-done.77
  569.2 3.0 collective-permute-done.78
  580.3 3.0 collective-permute-done.83
  583.3 5.8 collective-permute-done.84
  589.1 2.9 collective-permute-done.82
  595.1 4.4 collective-permute-done.88
  599.6 3.5 fusion.7
  610.4 11.0 %collective-permute-done.91 = f32[2,128]{1,0:T(2,128)S(1)} collective-permute-done((f32[2,128]{1,0:T(2,128)S(1)}, f32[2,128]{1,0:T(2,128)S(1)}, u32[]{:S(2)}, u32[]{:S(2)}) %collective-permute-start.91) | collective-permute-done | bytes 1056 | tf_op jit(solution)/shard_map/ppermute | solution.py:816
  622.2 4.1 shard_map.247
  626.3 2.8 shard_map.246
  (356 shorter events, 185.1 us)
Async XLA Ops:
  7.2 166.1 %all-gather.4.cloned.1.call-start = ((), (), s32[]{:S(2)}) async-start(), calls=%async_computation.5 | async-start | bytes 2621440 | tf_op jit(solution)/shard_map/all_gather | solution.py:938
  9.2 165.4 %all-gather.6.cloned.1.call-start = ((), (), s32[]{:S(2)}) async-start(), calls=%async_computation.6 | async-start | bytes 7864320 | tf_op jit(solution)/shard_map/all_gather | solution.py:938
  15.3 24.8 %collective-permute-start.5 = (bf16[128,2048]{1,0:T(8,128)(2,1)}, bf16[128,2048]{1,0:T(8,128)(2,1)S(1)}, u32[]{:S(2)}, u32[]{:S(2)}) collective-permute-start(bf16[128,2048]{1,0:T(8,128)(2,1)} %get-tuple-element.182), channel_id=1, source_target_pairs={{0,4},{2,6},{4,0},{6,2},{8,12},{10,14},{12,8},{14,10},{16,20},{18,... | collective-permute-start | bytes 1572872 | tf_op jit(solution)/shard_map/ppermute | solution.py:816
  16.9 24.1 %collective-permute-start.6 = (bf16[128,2048]{1,0:T(8,128)(2,1)}, bf16[128,2048]{1,0:T(8,128)(2,1)S(1)}, u32[]{:S(2)}, u32[]{:S(2)}) collective-permute-start(bf16[128,2048]{1,0:T(8,128)(2,1)} %get-tuple-element.183), channel_id=1, source_target_pairs={{0,6},{2,4},{4,2},{6,0},{8,14},{10,12},{12,10},{14,8},{16,22},{18,... | collective-permute-start | bytes 1572872 | tf_op jit(solution)/shard_map/ppermute | solution.py:816
  41.9 247.9 %all-gather.8.cloned.1.call-start = ((), (), s32[]{:S(2)}) async-start(), calls=%async_computation.7 | async-start | bytes 7864320 | tf_op jit(solution)/shard_map/all_gather | solution.py:938
  59.0 20.1 %collective-permute-start.10 = (bf16[256,2048]{1,0:T(8,128)(2,1)S(1)}, bf16[256,2048]{1,0:T(8,128)(2,1)S(1)}, u32[]{:S(2)}, u32[]{:S(2)}) collective-permute-start(bf16[256,2048]{1,0:T(8,128)(2,1)S(1)} %fusion.2.refs_0_), channel_id=1, source_target_pairs={{0,4},{2,6},{4,0},{6,2},{8,12},{10,14},{12,8},{14,10},{16,20},{18,... | collective-permute-start | bytes 3145736 | tf_op jit(solution)/shard_map/ppermute | solution.py:816
  60.6 19.8 %collective-permute-start.8 = (bf16[256,2048]{1,0:T(8,128)(2,1)S(1)}, bf16[256,2048]{1,0:T(8,128)(2,1)}, u32[]{:S(2)}, u32[]{:S(2)}) collective-permute-start(bf16[256,2048]{1,0:T(8,128)(2,1)S(1)} %fusion.2.refs_0_), channel_id=1, source_target_pairs={{0,2},{2,0},{4,6},{6,4},{8,10},{10,8},{12,14},{14,12},{16,18},{18,... | collective-permute-start | bytes 3145736 | tf_op jit(solution)/shard_map/ppermute | solution.py:816
  98.4 19.9 %collective-permute-start.16 = (bf16[128,1536]{1,0:T(8,128)(2,1)}, bf16[128,1536]{1,0:T(8,128)(2,1)S(1)}, u32[]{:S(2)}, u32[]{:S(2)}) collective-permute-start(bf16[128,1536]{1,0:T(8,128)(2,1)} %get-tuple-element.193), channel_id=1, source_target_pairs={{0,4},{2,6},{4,0},{6,2},{8,12},{10,14},{12,8},{14,10},{16,20},{18,... | collective-permute-start | bytes 1179656 | tf_op jit(solution)/shard_map/ppermute | solution.py:816
  99.3 19.0 %collective-permute-start.17 = (bf16[128,1536]{1,0:T(8,128)(2,1)}, bf16[128,1536]{1,0:T(8,128)(2,1)}, u32[]{:S(2)}, u32[]{:S(2)}) collective-permute-start(bf16[128,1536]{1,0:T(8,128)(2,1)} %get-tuple-element.194), channel_id=1, source_target_pairs={{0,6},{2,4},{4,2},{6,0},{8,14},{10,12},{12,10},{14,8},{16,22},{18,... | collective-permute-start | bytes 1179656 | tf_op jit(solution)/shard_map/ppermute | solution.py:816
  121.8 24.0 %collective-permute-start.19 = (bf16[256,2048]{1,0:T(8,128)(2,1)}, bf16[256,2048]{1,0:T(8,128)(2,1)}, u32[]{:S(2)}, u32[]{:S(2)}) collective-permute-start(bf16[256,2048]{1,0:T(8,128)(2,1)} %fusion.11), channel_id=1, source_target_pairs={{0,2},{2,0},{4,6},{6,4},{8,10},{10,8},{12,14},{14,12},{16,18},{18,... | collective-permute-start | bytes 3145736 | tf_op jit(solution)/shard_map/ppermute | solution.py:816
  122.7 24.4 %collective-permute-start.21 = (bf16[256,2048]{1,0:T(8,128)(2,1)}, bf16[256,2048]{1,0:T(8,128)(2,1)}, u32[]{:S(2)}, u32[]{:S(2)}) collective-permute-start(bf16[256,2048]{1,0:T(8,128)(2,1)} %fusion.11), channel_id=1, source_target_pairs={{0,4},{2,6},{4,0},{6,2},{8,12},{10,14},{12,8},{14,10},{16,20},{18,... | collective-permute-start | bytes 3145736 | tf_op jit(solution)/shard_map/ppermute | solution.py:816
  123.0 30.9 %collective-permute-start.18 = (bf16[256,2048]{1,0:T(8,128)(2,1)}, bf16[256,2048]{1,0:T(8,128)(2,1)}, u32[]{:S(2)}, u32[]{:S(2)}) collective-permute-start(bf16[256,2048]{1,0:T(8,128)(2,1)} %fusion.11), channel_id=1, source_target_pairs={{0,1},{1,0},{2,3},{3,2},{4,5},{5,4},{6,7},{7,6},{8,9},{9,8},{10,11... | collective-permute-start | bytes 3145736 | tf_op jit(solution)/shard_map/ppermute | solution.py:820
  145.8 19.0 %collective-permute-start.20 = (bf16[256,2048]{1,0:T(8,128)(2,1)}, bf16[256,2048]{1,0:T(8,128)(2,1)}, u32[]{:S(2)}, u32[]{:S(2)}) collective-permute-start(bf16[256,2048]{1,0:T(8,128)(2,1)} %collective-permute-done.19.first), channel_id=1, source_target_pairs={{0,1},{1,0},{2,3},{3,2},{4,5},{5,4},{6,7},{7,6},{8,9},{9,8},{10,11... | collective-permute-start | bytes 3145736 | tf_op jit(solution)/shard_map/ppermute | solution.py:820
  153.7 286.9 %reduce-scatter.6.cloned.1.call-start = ((), (), s32[]{:S(2)}) async-start(), calls=%async_computation.8 | async-start | bytes 2621440 | tf_op jit(solution)/shard_map/reduce_scatter | solution.py:941
  215.5 17.6 %collective-permute-start.31 = (bf16[128,2048]{1,0:T(8,128)(2,1)}, bf16[128,2048]{1,0:T(8,128)(2,1)S(1)}, u32[]{:S(2)}, u32[]{:S(2)}) collective-permute-start(bf16[128,2048]{1,0:T(8,128)(2,1)} %get-tuple-element.210), channel_id=1, source_target_pairs={{0,2},{2,0},{4,6},{6,4},{8,10},{10,8},{12,14},{14,12},{16,18},{18,... | collective-permute-start | bytes 1572872 | tf_op jit(solution)/shard_map/ppermute | solution.py:816
  234.6 23.0 %collective-permute-start.35 = (bf16[128,2048]{1,0:T(8,128)(2,1)S(1)}, bf16[128,2048]{1,0:T(8,128)(2,1)S(1)}, u32[]{:S(2)}, u32[]{:S(2)}) collective-permute-start(bf16[128,2048]{1,0:T(8,128)(2,1)S(1)} %add_convert_fusion.6), channel_id=1, source_target_pairs={{0,2},{2,0},{4,6},{6,4},{8,10},{10,8},{12,14},{14,12},{16,18},{18,... | collective-permute-start | bytes 1572872 | tf_op jit(solution)/shard_map/ppermute | solution.py:816
  236.1 21.7 %collective-permute-start.33 = (bf16[128,2048]{1,0:T(8,128)(2,1)S(1)}, bf16[128,2048]{1,0:T(8,128)(2,1)S(1)}, u32[]{:S(2)}, u32[]{:S(2)}) collective-permute-start(bf16[128,2048]{1,0:T(8,128)(2,1)S(1)} %add_convert_fusion.7), channel_id=1, source_target_pairs={{0,4},{2,6},{4,0},{6,2},{8,12},{10,14},{12,8},{14,10},{16,20},{18,... | collective-permute-start | bytes 1572872 | tf_op jit(solution)/shard_map/ppermute | solution.py:816
  259.2 24.7 %collective-permute-start.36 = (bf16[256,2048]{1,0:T(8,128)(2,1)S(1)}, bf16[256,2048]{1,0:T(8,128)(2,1)}, u32[]{:S(2)}, u32[]{:S(2)}) collective-permute-start(bf16[256,2048]{1,0:T(8,128)(2,1)S(1)} %multiply_convert_fusion.1.refs_0_), channel_id=1, source_target_pairs={{0,2},{2,0},{4,6},{6,4},{8,10},{10,8},{12,14},{14,12},{16,18},{18,... | collective-permute-start | bytes 3145736 | tf_op jit(solution)/shard_map/ppermute | solution.py:816
  260.7 24.3 %collective-permute-start.37 = (bf16[256,2048]{1,0:T(8,128)(2,1)S(1)}, bf16[256,2048]{1,0:T(8,128)(2,1)}, u32[]{:S(2)}, u32[]{:S(2)}) collective-permute-start(bf16[256,2048]{1,0:T(8,128)(2,1)S(1)} %multiply_convert_fusion.1.refs_0_), channel_id=1, source_target_pairs={{0,4},{2,6},{4,0},{6,2},{8,12},{10,14},{12,8},{14,10},{16,20},{18,... | collective-permute-start | bytes 3145736 | tf_op jit(solution)/shard_map/ppermute | solution.py:816
  261.3 28.5 %collective-permute-start.40 = (bf16[256,2048]{1,0:T(8,128)(2,1)S(1)}, bf16[256,2048]{1,0:T(8,128)(2,1)}, u32[]{:S(2)}, u32[]{:S(2)}) collective-permute-start(bf16[256,2048]{1,0:T(8,128)(2,1)S(1)} %multiply_convert_fusion.1.refs_0_), channel_id=1, source_target_pairs={{0,1},{1,0},{2,3},{3,2},{4,5},{5,4},{6,7},{7,6},{8,9},{9,8},{10,11... | collective-permute-start | bytes 3145736 | tf_op jit(solution)/shard_map/ppermute | solution.py:820
  287.6 28.3 %collective-permute-start.38 = (bf16[128,2048]{1,0:T(8,128)(2,1)}, bf16[128,2048]{1,0:T(8,128)(2,1)S(1)}, u32[]{:S(2)}, u32[]{:S(2)}) collective-permute-start(bf16[128,2048]{1,0:T(8,128)(2,1)} %get-tuple-element.241), channel_id=1, source_target_pairs={{0,4},{2,6},{4,0},{6,2},{8,12},{10,14},{12,8},{14,10},{16,20},{18,... | collective-permute-start | bytes 1572872 | tf_op jit(solution)/shard_map/ppermute | solution.py:816
  288.1 27.8 %collective-permute-start.39 = (bf16[128,2048]{1,0:T(8,128)(2,1)}, bf16[128,2048]{1,0:T(8,128)(2,1)S(1)}, u32[]{:S(2)}, u32[]{:S(2)}) collective-permute-start(bf16[128,2048]{1,0:T(8,128)(2,1)} %get-tuple-element.242), channel_id=1, source_target_pairs={{0,2},{2,0},{4,6},{6,4},{8,10},{10,8},{12,14},{14,12},{16,18},{18,... | collective-permute-start | bytes 1572872 | tf_op jit(solution)/shard_map/ppermute | solution.py:816
  337.3 159.1 %reduce-scatter.8.cloned.1.call-start = ((), (), s32[]{:S(2)}) async-start(), calls=%async_computation.9 | async-start | bytes 5242880 | tf_op jit(solution)/shard_map/reduce_scatter | solution.py:941
  339.0 34.0 %collective-permute-start.44 = (bf16[256,2048]{1,0:T(8,128)(2,1)}, bf16[256,2048]{1,0:T(8,128)(2,1)S(1)}, u32[]{:S(2)}, u32[]{:S(2)}) collective-permute-start(bf16[256,2048]{1,0:T(8,128)(2,1)} %get-tuple-element.250), channel_id=1, source_target_pairs={{0,1},{1,0},{2,3},{3,2},{4,5},{5,4},{6,7},{7,6},{8,9},{9,8},{10,11... | collective-permute-start | bytes 3145736 | tf_op jit(solution)/shard_map/ppermute | solution.py:820
  349.3 17.9 %collective-permute-start.49 = (bf16[128,2048]{1,0:T(8,128)(2,1)}, bf16[128,2048]{1,0:T(8,128)(2,1)}, u32[]{:S(2)}, u32[]{:S(2)}) collective-permute-start(bf16[128,2048]{1,0:T(8,128)(2,1)} %get-tuple-element.263), channel_id=1, source_target_pairs={{0,2},{2,0},{4,6},{6,4},{8,10},{10,8},{12,14},{14,12},{16,18},{18,... | collective-permute-start | bytes 1572872 | tf_op jit(solution)/shard_map/ppermute | solution.py:816
  352.3 23.3 %collective-permute-start.48 = (bf16[128,2048]{1,0:T(8,128)(2,1)}, bf16[128,2048]{1,0:T(8,128)(2,1)S(1)}, u32[]{:S(2)}, u32[]{:S(2)}) collective-permute-start(bf16[128,2048]{1,0:T(8,128)(2,1)} %get-tuple-element.261), channel_id=1, source_target_pairs={{0,2},{2,0},{4,6},{6,4},{8,10},{10,8},{12,14},{14,12},{16,18},{18,... | collective-permute-start | bytes 1572872 | tf_op jit(solution)/shard_map/ppermute | solution.py:816
  352.9 24.3 %collective-permute-start.52 = (bf16[128,2048]{1,0:T(8,128)(2,1)}, bf16[128,2048]{1,0:T(8,128)(2,1)}, u32[]{:S(2)}, u32[]{:S(2)}) collective-permute-start(bf16[128,2048]{1,0:T(8,128)(2,1)} %get-tuple-element.270), channel_id=1, source_target_pairs={{0,4},{2,6},{4,0},{6,2},{8,12},{10,14},{12,8},{14,10},{16,20},{18,... | collective-permute-start | bytes 1572872 | tf_op jit(solution)/shard_map/ppermute | solution.py:816
  366.8 158.3 %reduce-scatter.10.cloned.1.call-start = ((), (), s32[]{:S(2)}) async-start(), calls=%async_computation.10 | async-start | bytes 2621440 | tf_op jit(solution)/shard_map/reduce_scatter | solution.py:941
  393.1 25.7 %collective-permute-start.59 = (bf16[256,2048]{1,0:T(8,128)(2,1)S(1)}, bf16[256,2048]{1,0:T(8,128)(2,1)}, u32[]{:S(2)}, u32[]{:S(2)}) collective-permute-start(bf16[256,2048]{1,0:T(8,128)(2,1)S(1)} %get-tuple-element.354.refs_0_), channel_id=1, source_target_pairs={{0,2},{2,0},{4,6},{6,4},{8,10},{10,8},{12,14},{14,12},{16,18},{18,... | collective-permute-start | bytes 3145736 | tf_op jit(solution)/shard_map/ppermute | solution.py:816
  394.1 25.4 %collective-permute-start.60 = (bf16[256,2048]{1,0:T(8,128)(2,1)S(1)}, bf16[256,2048]{1,0:T(8,128)(2,1)}, u32[]{:S(2)}, u32[]{:S(2)}) collective-permute-start(bf16[256,2048]{1,0:T(8,128)(2,1)S(1)} %get-tuple-element.354.refs_0_), channel_id=1, source_target_pairs={{0,4},{2,6},{4,0},{6,2},{8,12},{10,14},{12,8},{14,10},{16,20},{18,... | collective-permute-start | bytes 3145736 | tf_op jit(solution)/shard_map/ppermute | solution.py:816
  460.7 143.6 %reduce-scatter.14.cloned.1.call-start = ((), (), s32[]{:S(2)}) async-start(), calls=%async_computation.12 | async-start | bytes 5898240 | tf_op jit(solution)/shard_map/reduce_scatter | solution.py:941
  479.6 150.1 %reduce-scatter.12.cloned.1.call-start = ((), (), s32[]{:S(2)}) async-start(), calls=%async_computation.11 | async-start | bytes 1966080 | tf_op jit(solution)/shard_map/reduce_scatter | solution.py:941
  480.8 40.9 %collective-permute-start.55 = (bf16[256,2048]{1,0:T(8,128)(2,1)}, bf16[256,2048]{1,0:T(8,128)(2,1)}, u32[]{:S(2)}, u32[]{:S(2)}) collective-permute-start(bf16[256,2048]{1,0:T(8,128)(2,1)} %get-tuple-element.275), channel_id=1, source_target_pairs={{0,1},{1,0},{2,3},{3,2},{4,5},{5,4},{6,7},{7,6},{8,9},{9,8},{10,11... | collective-permute-start | bytes 3145736 | tf_op jit(solution)/shard_map/ppermute | solution.py:820
  492.3 24.5 %collective-permute-start.67 = (bf16[128,2048]{1,0:T(8,128)(2,1)}, bf16[128,2048]{1,0:T(8,128)(2,1)}, u32[]{:S(2)}, u32[]{:S(2)}) collective-permute-start(bf16[128,2048]{1,0:T(8,128)(2,1)} %get-tuple-element.303), channel_id=1, source_target_pairs={{0,2},{2,0},{4,6},{6,4},{8,10},{10,8},{12,14},{14,12},{16,18},{18,... | collective-permute-start | bytes 1572872 | tf_op jit(solution)/shard_map/ppermute | solution.py:816
  492.5 24.3 %collective-permute-start.68 = (bf16[128,2048]{1,0:T(8,128)(2,1)}, bf16[128,2048]{1,0:T(8,128)(2,1)}, u32[]{:S(2)}, u32[]{:S(2)}) collective-permute-start(bf16[128,2048]{1,0:T(8,128)(2,1)} %get-tuple-element.304), channel_id=1, source_target_pairs={{0,4},{2,6},{4,0},{6,2},{8,12},{10,14},{12,8},{14,10},{16,20},{18,... | collective-permute-start | bytes 1572872 | tf_op jit(solution)/shard_map/ppermute | solution.py:816
  493.3 28.4 %collective-permute-start.66 = (bf16[128,2048]{1,0:T(8,128)(2,1)}, bf16[128,2048]{1,0:T(8,128)(2,1)S(1)}, u32[]{:S(2)}, u32[]{:S(2)}) collective-permute-start(bf16[128,2048]{1,0:T(8,128)(2,1)} %get-tuple-element.301), channel_id=1, source_target_pairs={{0,2},{2,0},{4,6},{6,4},{8,10},{10,8},{12,14},{14,12},{16,18},{18,... | collective-permute-start | bytes 1572872 | tf_op jit(solution)/shard_map/ppermute | solution.py:816
  494.4 27.9 %collective-permute-start.70 = (bf16[128,2048]{1,0:T(8,128)(2,1)}, bf16[128,2048]{1,0:T(8,128)(2,1)}, u32[]{:S(2)}, u32[]{:S(2)}) collective-permute-start(bf16[128,2048]{1,0:T(8,128)(2,1)} %get-tuple-element.312), channel_id=1, source_target_pairs={{0,4},{2,6},{4,0},{6,2},{8,12},{10,14},{12,8},{14,10},{16,20},{18,... | collective-permute-start | bytes 1572872 | tf_op jit(solution)/shard_map/ppermute | solution.py:816
  521.8 18.4 %collective-permute-start.73 = (bf16[256,2048]{1,0:T(8,128)(2,1)}, bf16[256,2048]{1,0:T(8,128)(2,1)}, u32[]{:S(2)}, u32[]{:S(2)}) collective-permute-start(bf16[256,2048]{1,0:T(8,128)(2,1)} %get-tuple-element.308), channel_id=1, source_target_pairs={{0,1},{1,0},{2,3},{3,2},{4,5},{5,4},{6,7},{7,6},{8,9},{9,8},{10,11... | collective-permute-start | bytes 3145736 | tf_op jit(solution)/shard_map/ppermute | solution.py:820
  521.8 20.5 %collective-permute-start.74 = (bf16[256,2048]{1,0:T(8,128)(2,1)}, bf16[256,2048]{1,0:T(8,128)(2,1)}, u32[]{:S(2)}, u32[]{:S(2)}) collective-permute-start(bf16[256,2048]{1,0:T(8,128)(2,1)} %get-tuple-element.309), channel_id=1, source_target_pairs={{0,1},{1,0},{2,3},{3,2},{4,5},{5,4},{6,7},{7,6},{8,9},{9,8},{10,11... | collective-permute-start | bytes 3145736 | tf_op jit(solution)/shard_map/ppermute | solution.py:820
  522.3 20.0 %collective-permute-start.75 = (bf16[256,2048]{1,0:T(8,128)(2,1)}, bf16[256,2048]{1,0:T(8,128)(2,1)}, u32[]{:S(2)}, u32[]{:S(2)}) collective-permute-start(bf16[256,2048]{1,0:T(8,128)(2,1)} %get-tuple-element.310), channel_id=1, source_target_pairs={{0,1},{1,0},{2,3},{3,2},{4,5},{5,4},{6,7},{7,6},{8,9},{9,8},{10,11... | collective-permute-start | bytes 3145736 | tf_op jit(solution)/shard_map/ppermute | solution.py:820
  531.9 17.9 %collective-permute-start.79 = (bf16[128,2048]{1,0:T(8,128)(2,1)}, bf16[128,2048]{1,0:T(8,128)(2,1)S(1)}, u32[]{:S(2)}, u32[]{:S(2)}) collective-permute-start(bf16[128,2048]{1,0:T(8,128)(2,1)} %get-tuple-element.326), channel_id=1, source_target_pairs={{0,2},{2,0},{4,6},{6,4},{8,10},{10,8},{12,14},{14,12},{16,18},{18,... | collective-permute-start | bytes 1572872 | tf_op jit(solution)/shard_map/ppermute | solution.py:816
  534.8 26.1 %collective-permute-start.80 = (bf16[128,2048]{1,0:T(8,128)(2,1)}, bf16[128,2048]{1,0:T(8,128)(2,1)}, u32[]{:S(2)}, u32[]{:S(2)}) collective-permute-start(bf16[128,2048]{1,0:T(8,128)(2,1)} %get-tuple-element.327), channel_id=1, source_target_pairs={{0,4},{2,6},{4,0},{6,2},{8,12},{10,14},{12,8},{14,10},{16,20},{18,... | collective-permute-start | bytes 1572872 | tf_op jit(solution)/shard_map/ppermute | solution.py:816
  540.2 22.2 %collective-permute-start.81 = (bf16[128,2048]{1,0:T(8,128)(2,1)}, bf16[128,2048]{1,0:T(8,128)(2,1)}, u32[]{:S(2)}, u32[]{:S(2)}) collective-permute-start(bf16[128,2048]{1,0:T(8,128)(2,1)} %get-tuple-element.328), channel_id=1, source_target_pairs={{0,6},{2,4},{4,2},{6,0},{8,14},{10,12},{12,10},{14,8},{16,22},{18,... | collective-permute-start | bytes 1572872 | tf_op jit(solution)/shard_map/ppermute | solution.py:816
  548.2 20.9 %collective-permute-start.77 = (bf16[128,2048]{1,0:T(8,128)(2,1)}, bf16[128,2048]{1,0:T(8,128)(2,1)}, u32[]{:S(2)}, u32[]{:S(2)}) collective-permute-start(bf16[128,2048]{1,0:T(8,128)(2,1)} %get-tuple-element.323), channel_id=1, source_target_pairs={{0,2},{2,0},{4,6},{6,4},{8,10},{10,8},{12,14},{14,12},{16,18},{18,... | collective-permute-start | bytes 1572872 | tf_op jit(solution)/shard_map/ppermute | solution.py:816
  548.9 23.3 %collective-permute-start.78 = (bf16[128,2048]{1,0:T(8,128)(2,1)}, bf16[128,2048]{1,0:T(8,128)(2,1)}, u32[]{:S(2)}, u32[]{:S(2)}) collective-permute-start(bf16[128,2048]{1,0:T(8,128)(2,1)} %get-tuple-element.324), channel_id=1, source_target_pairs={{0,4},{2,6},{4,0},{6,2},{8,12},{10,14},{12,8},{14,10},{16,20},{18,... | collective-permute-start | bytes 1572872 | tf_op jit(solution)/shard_map/ppermute | solution.py:816
  549.8 28.9 %collective-permute-start.72 = (bf16[256,2048]{1,0:T(8,128)(2,1)}, bf16[256,2048]{1,0:T(8,128)(2,1)S(1)}, u32[]{:S(2)}, u32[]{:S(2)}) collective-permute-start(bf16[256,2048]{1,0:T(8,128)(2,1)} %get-tuple-element.307), channel_id=1, source_target_pairs={{0,1},{1,0},{2,3},{3,2},{4,5},{5,4},{6,7},{7,6},{8,9},{9,8},{10,11... | collective-permute-start | bytes 3145736 | tf_op jit(solution)/shard_map/ppermute | solution.py:820
  560.9 19.4 %collective-permute-start.76 = (bf16[128,2048]{1,0:T(8,128)(2,1)}, bf16[128,2048]{1,0:T(8,128)(2,1)S(1)}, u32[]{:S(2)}, u32[]{:S(2)}) collective-permute-start(bf16[128,2048]{1,0:T(8,128)(2,1)} %get-tuple-element.321), channel_id=1, source_target_pairs={{0,2},{2,0},{4,6},{6,4},{8,10},{10,8},{12,14},{14,12},{16,18},{18,... | collective-permute-start | bytes 1572872 | tf_op jit(solution)/shard_map/ppermute | solution.py:816
  562.4 20.9 %collective-permute-start.83 = (bf16[128,2048]{1,0:T(8,128)(2,1)}, bf16[128,2048]{1,0:T(8,128)(2,1)S(1)}, u32[]{:S(2)}, u32[]{:S(2)}) collective-permute-start(bf16[128,2048]{1,0:T(8,128)(2,1)} %get-tuple-element.330), channel_id=1, source_target_pairs={{0,4},{2,6},{4,0},{6,2},{8,12},{10,14},{12,8},{14,10},{16,20},{18,... | collective-permute-start | bytes 1572872 | tf_op jit(solution)/shard_map/ppermute | solution.py:816
  (91 other events, 881.7 us)
Sparse Core Ops, SparseCore 0:
  10.2 48.7 all-gather.3
  60.6 113.9 all-gather.5
  176.2 113.5 all-gather.7
  337.4 42.0 reduce-scatter.5
  381.8 76.0 reduce-scatter.7
  460.8 43.5 reduce-scatter.9
  506.8 84.5 reduce-scatter.13
  593.9 35.7 reduce-scatter.11
